TPU v7x, 32 devices: a whole 2x2x4 slice. The times are simulated.
32 devices in a mesh: pipe: 4 (over x, core), tx: 4 (over z), ty: 2 (over y).
Axes of the slice: x: 2, y: 2, z: 4, core: 2. Of those that a mesh axis runs over, the one named last changes fastest.
Arguments:
- stored: bfloat16 [4, 2, 4, 2, 256, 512], P('pipe', None, 'tx', 'ty'), may hold values from -6 to 6
- cotangent: bfloat16 [2, 4, 2, 256, 512], P(None, 'tx', 'ty'), may hold values from -6 to 6
- weight: bfloat16 [4, 512, 512], P('pipe'), may hold values from -0.25 to 0.25
- local_edges: bfloat16 [2, 4, 2, 2, 2, 128, 128], P(None, 'tx', 'ty'), may hold values from -0.21875 to 0.21875
- halo_edges: bfloat16 [2, 4, 2, 4, 2, 128, 128], P(None, 'tx', 'ty'), may hold values from -0.21875 to 0.21875
- pattern: int32 [2, 4, 2, 2, 6], P(None, 'tx', 'ty'), may hold values 0 or 1
- pick: int32 [2, 4, 2, 4], P(None, 'tx', 'ty'), may hold values from 0 to 1
Outputs:
- grad_weight: float32 [4, 512, 512], P('pipe', ('tx', 'ty'))
- grad_input: bfloat16 [4, 2, 4, 2, 256, 512], P('pipe', None, 'tx', 'ty')
Inputs may be any that keep to these rules, and one draw needn't show every extreme that they name: `pattern`: 1 where a block of edges is present, 0 where it is absent. `pick`: a block index of the sending tile.
All inputs are finite; a program needn't handle non-finite values.
Results may differ from a plain program's by a relative error of at most 0.015.
Values may be sent and summed in bfloat16 or wider, within the bound.
No kernel may reach another device: no remote copies, remote signals or barrier semaphores. Data moves between devices by JAX's collectives and lax.ppermute only.
A program may use at most 64 MiB of HBM per device.

v0:
```python
import math

import jax
import jax.numpy as jnp
from jax import lax
from jax.sharding import PartitionSpec as P


def shifted(value, axis, steps):
    count = lax.axis_size(axis)
    leading, last = (max(0, -steps), min(count, count - steps))
    return lax.ppermute(value, axis, [(source, source + steps) for source in range(leading, last)])


def silu_slope(value):
    sigma = jax.nn.sigmoid(value)
    return sigma * (1.0 + value * (1.0 - sigma))


def take_entry(array, index):
    return lax.dynamic_index_in_dim(array, index, 0, keepdims=False)


def per_device(stored, cotangent, weight, local_edges, halo_edges, pattern, pick):
    sections = lax.axis_size("pipe")
    section = lax.axis_index("pipe")
    stashed = stored[0, :, 0, 0]
    given = cotangent[:, 0, 0]
    matrix = weight[0]
    batches, nodes, width = stashed.shape
    blocks = local_edges.shape[3]
    block_size = local_edges.shape[5]
    block_mask = pattern[:, 0, 0].astype(jnp.bfloat16)
    local_masked = local_edges[:, 0, 0] * block_mask[:, :, :blocks, None, None]
    halo_masked = (
        halo_edges[:, 0, 0] * jnp.swapaxes(block_mask[:, :, blocks:], 1, 2)[:, :, :, None, None]
    )
    placing = (
        pick[:, 0, 0][:, :, None] == jnp.arange(blocks, dtype=jnp.int32)[None, None, :]
    ).astype(jnp.float32)
    carried = jnp.zeros((nodes, width), jnp.bfloat16)
    results = jnp.zeros((batches, nodes, width), jnp.bfloat16)
    weight_total = jnp.zeros((width, width), jnp.float32)
    rounds = sections + batches - 1
    for step in range(rounds):
        offset_batch = step - (sections - 1 - section)
        active = (offset_batch >= 0) & (offset_batch < batches)
        batch = jnp.clip(offset_batch, 0, batches - 1)
        upstream = jnp.where(section == sections - 1, take_entry(given, batch), carried)
        features = take_entry(stashed, batch)
        pre_activation = jnp.dot(features, matrix, preferred_element_type=jnp.float32)
        slope_grad = (upstream.astype(jnp.float32) * silu_slope(pre_activation)).astype(
            jnp.bfloat16
        )
        message_grad = lax.dot_general(
            slope_grad, matrix, (((1,), (1,)), ((), ())), preferred_element_type=jnp.float32
        ).astype(jnp.bfloat16)
        grad_blocks = message_grad.reshape(blocks, block_size, width)
        inner = jnp.einsum(
            "bcij,bik->cjk",
            take_entry(local_masked, batch),
            grad_blocks,
            preferred_element_type=jnp.float32,
        )
        outward = jnp.einsum(
            "ebij,bik->ejk",
            take_entry(halo_masked, batch),
            grad_blocks,
            preferred_element_type=jnp.float32,
        ).astype(jnp.bfloat16)
        arrived = jnp.stack(
            [
                shifted(outward[0], "tx", -1),
                shifted(outward[1], "tx", 1),
                shifted(outward[2], "ty", -1),
                shifted(outward[3], "ty", 1),
            ]
        ).astype(jnp.float32)
        placed = jnp.einsum(
            "ec,ejk->cjk", take_entry(placing, batch), arrived, precision=lax.Precision.HIGHEST
        )
        total = upstream.astype(jnp.float32) + (inner + placed).reshape(nodes, width)
        features, slope_grad, result = (features, slope_grad, total.astype(jnp.bfloat16))
        results = jnp.where(
            active, lax.dynamic_update_index_in_dim(results, result, batch, 0), results
        )
        product = lax.dot_general(
            features, slope_grad, (((0,), (0,)), ((), ())), preferred_element_type=jnp.float32
        )
        weight_total = weight_total + jnp.where(active, product, 0.0)
        if step + 1 < rounds:
            carried = shifted(result, "pipe", -1)
    scale = 1.0 / math.sqrt(batches * nodes * lax.axis_size("tx") * lax.axis_size("ty"))
    summed = lax.psum_scatter(weight_total, ("tx", "ty"), scatter_dimension=0, tiled=True)
    return ((summed * scale)[None], results[None, :, None, None])


def solution(mesh):
    in_specs = (
        P("pipe", None, "tx", "ty", None, None),
        P(None, "tx", "ty", None, None),
        P("pipe", None, None),
        P(None, "tx", "ty", None, None, None, None),
        P(None, "tx", "ty", None, None, None, None),
        P(None, "tx", "ty", None, None),
        P(None, "tx", "ty", None),
    )
    out_specs = (P("pipe", ("tx", "ty"), None), P("pipe", None, "tx", "ty", None, None))
    return jax.shard_map(
        per_device, mesh=mesh, in_specs=in_specs, out_specs=out_specs, check_vma=False
    )
```

profile of v0, /device:TPU:0, one launch (start us, length us, event | category | flops | bytes accessed | tf_op | source)
XLA Modules:
  0.0 185.7 jit_solution(3022474468966165510)
XLA Ops:
  8.2 1.6 fusion.24
  13.4 4.9 %collective-permute-start.3 = (bf16[128,512]{1,0:T(8,128)(2,1)S(1)}, bf16[128,512]{1,0:T(8,128)(2,1)S(1)}, u32[]{:S(2)}, u32[]{:S(2)}) collective-permute-start(bf16[128,512]{1,0:T(8,128)(2,1)S(1)} %get-tuple-element.21), channel_id=1, source_target_pairs={{0,1},{2,3},{4,5},{6,7},{8,9},{10,11},{12,13},{14,15},{16,17},{18,... | collective-permute-start | bytes 393224 | tf_op jit(solution)/shard_map/ppermute | solution.py:12
  18.3 1.3 collective-permute-start.2
  19.6 4.6 %collective-permute-start.1 = (bf16[128,512]{1,0:T(8,128)(2,1)S(1)}, bf16[128,512]{1,0:T(8,128)(2,1)S(1)}, u32[]{:S(2)}, u32[]{:S(2)}) collective-permute-start(bf16[128,512]{1,0:T(8,128)(2,1)S(1)} %get-tuple-element.23), channel_id=1, source_target_pairs={{0,2},{2,4},{4,6},{1,3},{3,5},{5,7},{8,10},{10,12},{12,14},{9,11},... | collective-permute-start | bytes 393224 | tf_op jit(solution)/shard_map/ppermute | solution.py:12
  28.5 1.3 collective-permute-start.4
  30.6 1.3 collective-permute-done.4
  33.3 1.3 collective-permute-start.5
  34.6 4.6 %collective-permute-start.8 = (bf16[128,512]{1,0:T(8,128)(2,1)S(1)}, bf16[128,512]{1,0:T(8,128)(2,1)S(1)}, u32[]{:S(2)}, u32[]{:S(2)}) collective-permute-start(bf16[128,512]{1,0:T(8,128)(2,1)S(1)} %get-tuple-element.17), channel_id=1, source_target_pairs={{0,1},{2,3},{4,5},{6,7},{8,9},{10,11},{12,13},{14,15},{16,17},{18,... | collective-permute-start | bytes 393224 | tf_op jit(solution)/shard_map/ppermute | solution.py:12
  39.2 1.3 collective-permute-start.7
  40.5 5.0 %collective-permute-start.6 = (bf16[128,512]{1,0:T(8,128)(2,1)S(1)}, bf16[128,512]{1,0:T(8,128)(2,1)S(1)}, u32[]{:S(2)}, u32[]{:S(2)}) collective-permute-start(bf16[128,512]{1,0:T(8,128)(2,1)S(1)} %get-tuple-element.19), channel_id=1, source_target_pairs={{0,2},{2,4},{4,6},{1,3},{3,5},{5,7},{8,10},{10,12},{12,14},{9,11},... | collective-permute-start | bytes 393224 | tf_op jit(solution)/shard_map/ppermute | solution.py:12
  46.0 1.9 %collective-permute-done.6 = bf16[128,512]{1,0:T(8,128)(2,1)S(1)} collective-permute-done((bf16[128,512]{1,0:T(8,128)(2,1)S(1)}, bf16[128,512]{1,0:T(8,128)(2,1)S(1)}, u32[]{:S(2)}, u32[]{:S(2)}) %collective-permute-start.6) | collective-permute-done | bytes 131104 | tf_op jit(solution)/shard_map/ppermute | solution.py:12
  53.1 3.9 %collective-permute-done.9 = bf16[256,512]{1,0:T(8,128)(2,1)} collective-permute-done((bf16[256,512]{1,0:T(8,128)(2,1)}, bf16[256,512]{1,0:T(8,128)(2,1)}, u32[]{:S(2)}, u32[]{:S(2)}) %collective-permute-start.9) | collective-permute-done | bytes 262176 | tf_op jit(solution)/shard_map/ppermute | solution.py:12
  57.0 1.4 fusion.18
  59.2 1.4 collective-permute-start.10
  60.6 4.3 %collective-permute-start.13 = (bf16[128,512]{1,0:T(8,128)(2,1)S(1)}, bf16[128,512]{1,0:T(8,128)(2,1)S(1)}, u32[]{:S(2)}, u32[]{:S(2)}) collective-permute-start(bf16[128,512]{1,0:T(8,128)(2,1)S(1)} %get-tuple-element.13), channel_id=1, source_target_pairs={{0,1},{2,3},{4,5},{6,7},{8,9},{10,11},{12,13},{14,15},{16,17},{18,... | collective-permute-start | bytes 393224 | tf_op jit(solution)/shard_map/ppermute | solution.py:12
  64.9 1.3 collective-permute-start.12
  66.2 4.7 %collective-permute-start.11 = (bf16[128,512]{1,0:T(8,128)(2,1)S(1)}, bf16[128,512]{1,0:T(8,128)(2,1)S(1)}, u32[]{:S(2)}, u32[]{:S(2)}) collective-permute-start(bf16[128,512]{1,0:T(8,128)(2,1)S(1)} %get-tuple-element.15), channel_id=1, source_target_pairs={{0,2},{2,4},{4,6},{1,3},{3,5},{5,7},{8,10},{10,12},{12,14},{9,11},... | collective-permute-start | bytes 393224 | tf_op jit(solution)/shard_map/ppermute | solution.py:12
  71.7 1.6 collective-permute-done.11
  75.4 1.3 collective-permute-start.14
  77.1 4.9 %collective-permute-done.14 = bf16[256,512]{1,0:T(8,128)(2,1)S(1)} collective-permute-done((bf16[256,512]{1,0:T(8,128)(2,1)S(1)}, bf16[256,512]{1,0:T(8,128)(2,1)S(1)}, u32[]{:S(2)}, u32[]{:S(2)}) %collective-permute-start.14) | collective-permute-done | bytes 262176 | tf_op jit(solution)/shard_map/ppermute | solution.py:12
  83.1 1.3 collective-permute-start.15
  84.4 4.3 %collective-permute-start.18 = (bf16[128,512]{1,0:T(8,128)(2,1)S(1)}, bf16[128,512]{1,0:T(8,128)(2,1)S(1)}, u32[]{:S(2)}, u32[]{:S(2)}) collective-permute-start(bf16[128,512]{1,0:T(8,128)(2,1)S(1)} %get-tuple-element.9), channel_id=1, source_target_pairs={{0,1},{2,3},{4,5},{6,7},{8,9},{10,11},{12,13},{14,15},{16,17},{18,... | collective-permute-start | bytes 393224 | tf_op jit(solution)/shard_map/ppermute | solution.py:12
  88.7 1.3 collective-permute-start.17
  90.0 4.7 %collective-permute-start.16 = (bf16[128,512]{1,0:T(8,128)(2,1)S(1)}, bf16[128,512]{1,0:T(8,128)(2,1)S(1)}, u32[]{:S(2)}, u32[]{:S(2)}) collective-permute-start(bf16[128,512]{1,0:T(8,128)(2,1)S(1)} %get-tuple-element.11), channel_id=1, source_target_pairs={{0,2},{2,4},{4,6},{1,3},{3,5},{5,7},{8,10},{10,12},{12,14},{9,11},... | collective-permute-start | bytes 393224 | tf_op jit(solution)/shard_map/ppermute | solution.py:12
  95.6 1.6 collective-permute-done.16
  99.9 4.9 %collective-permute-done.19 = bf16[256,512]{1,0:T(8,128)(2,1)S(1)} collective-permute-done((bf16[256,512]{1,0:T(8,128)(2,1)S(1)}, bf16[256,512]{1,0:T(8,128)(2,1)S(1)}, u32[]{:S(2)}, u32[]{:S(2)}) %collective-permute-start.19) | collective-permute-done | bytes 262176 | tf_op jit(solution)/shard_map/ppermute | solution.py:12
  105.6 1.3 fusion
  108.9 4.3 %collective-permute-start.23 = (bf16[128,512]{1,0:T(8,128)(2,1)S(1)}, bf16[128,512]{1,0:T(8,128)(2,1)S(1)}, u32[]{:S(2)}, u32[]{:S(2)}) collective-permute-start(bf16[128,512]{1,0:T(8,128)(2,1)S(1)} %get-tuple-element.5), channel_id=1, source_target_pairs={{0,1},{2,3},{4,5},{6,7},{8,9},{10,11},{12,13},{14,15},{16,17},{18,... | collective-permute-start | bytes 393224 | tf_op jit(solution)/shard_map/ppermute | solution.py:12
  114.5 4.7 %collective-permute-start.21 = (bf16[128,512]{1,0:T(8,128)(2,1)S(1)}, bf16[128,512]{1,0:T(8,128)(2,1)S(1)}, u32[]{:S(2)}, u32[]{:S(2)}) collective-permute-start(bf16[128,512]{1,0:T(8,128)(2,1)S(1)} %get-tuple-element.7), channel_id=1, source_target_pairs={{0,2},{2,4},{4,6},{1,3},{3,5},{5,7},{8,10},{10,12},{12,14},{9,11},... | collective-permute-start | bytes 393224 | tf_op jit(solution)/shard_map/ppermute | solution.py:12
  120.1 3.0 %collective-permute-done.21 = bf16[128,512]{1,0:T(8,128)(2,1)S(1)} collective-permute-done((bf16[128,512]{1,0:T(8,128)(2,1)S(1)}, bf16[128,512]{1,0:T(8,128)(2,1)S(1)}, u32[]{:S(2)}, u32[]{:S(2)}) %collective-permute-start.21) | collective-permute-done | bytes 131104 | tf_op jit(solution)/shard_map/ppermute | solution.py:12
  125.2 52.2 %reduce-scatter.2.cloned.1.call-done = f32[64,512]{1,0:T(8,128)} async-done(((f32[512,512]{1,0:T(8,128)}), f32[64,512]{1,0:T(8,128)}) %reduce-scatter.2.cloned.1.call-update) | async-done | bytes 131088 | tf_op jit(solution)/shard_map/reduce_scatter | solution.py:94
  177.3 1.6 multiply_bitcast_fusion
  (116 shorter events, 32.0 us)
Async XLA Ops:
  7.2 1.1 copy-start
  7.2 170.1 %reduce-scatter.2.cloned.1.call-start = ((), (), s32[]{:S(2)}) async-start(), calls=%async_computation.1 | async-start | bytes 1179648 | tf_op jit(solution)/shard_map/reduce_scatter | solution.py:94
  8.2 1.6 copy-start.1
  9.9 1.1 copy-start.7
  11.4 12.8 %copy-start.13 = (bf16[2,1,1,2,2,128,128]{6,5,4,3,2,1,0:T(8,128)(2,1)S(1)}, bf16[2,1,1,2,2,128,128]{6,5,4,3,2,1,0:T(8,128)(2,1)}, u32[]{:S(2)}) copy-start(bf16[2,1,1,2,2,128,128]{6,5,4,3,2,1,0:T(8,128)(2,1)} %param.10) | copy-start | bytes 786436
  12.1 13.8 %collective-permute-start = (bf16[128,512]{1,0:T(8,128)(2,1)}, bf16[128,512]{1,0:T(8,128)(2,1)S(1)}, u32[]{:S(2)}, u32[]{:S(2)}) collective-permute-start(bf16[128,512]{1,0:T(8,128)(2,1)} %get-tuple-element.20), channel_id=1, source_target_pairs={{2,0},{4,2},{6,4},{3,1},{5,3},{7,5},{10,8},{12,10},{14,12},{11,9},... | collective-permute-start | bytes 393224 | tf_op jit(solution)/shard_map/ppermute | solution.py:12
  13.4 12.6 %collective-permute-start.3 = (bf16[128,512]{1,0:T(8,128)(2,1)S(1)}, bf16[128,512]{1,0:T(8,128)(2,1)S(1)}, u32[]{:S(2)}, u32[]{:S(2)}) collective-permute-start(bf16[128,512]{1,0:T(8,128)(2,1)S(1)} %get-tuple-element.21), channel_id=1, source_target_pairs={{0,1},{2,3},{4,5},{6,7},{8,9},{10,11},{12,13},{14,15},{16,17},{18,... | collective-permute-start | bytes 393224 | tf_op jit(solution)/shard_map/ppermute | solution.py:12
  18.3 7.7 %collective-permute-start.2 = (bf16[128,512]{1,0:T(8,128)(2,1)S(1)}, bf16[128,512]{1,0:T(8,128)(2,1)S(1)}, u32[]{:S(2)}, u32[]{:S(2)}) collective-permute-start(bf16[128,512]{1,0:T(8,128)(2,1)S(1)} %get-tuple-element.22), channel_id=1, source_target_pairs={{1,0},{3,2},{5,4},{7,6},{9,8},{11,10},{13,12},{15,14},{17,16},{19,... | collective-permute-start | bytes 393224 | tf_op jit(solution)/shard_map/ppermute | solution.py:12
  19.6 7.1 %collective-permute-start.1 = (bf16[128,512]{1,0:T(8,128)(2,1)S(1)}, bf16[128,512]{1,0:T(8,128)(2,1)S(1)}, u32[]{:S(2)}, u32[]{:S(2)}) collective-permute-start(bf16[128,512]{1,0:T(8,128)(2,1)S(1)} %get-tuple-element.23), channel_id=1, source_target_pairs={{0,2},{2,4},{4,6},{1,3},{3,5},{5,7},{8,10},{10,12},{12,14},{9,11},... | collective-permute-start | bytes 393224 | tf_op jit(solution)/shard_map/ppermute | solution.py:12
  28.5 3.4 %collective-permute-start.4 = (bf16[256,512]{1,0:T(8,128)(2,1)S(1)}, bf16[256,512]{1,0:T(8,128)(2,1)S(1)}, u32[]{:S(2)}, u32[]{:S(2)}) collective-permute-start(bf16[256,512]{1,0:T(8,128)(2,1)S(1)} %fusion.25), channel_id=1, source_target_pairs={{8,0},{16,8},{24,16},{9,1},{17,9},{25,17},{10,2},{18,10},{26,18},{... | collective-permute-start | bytes 786440 | tf_op jit(solution)/shard_map/ppermute | solution.py:12
  33.3 12.3 %collective-permute-start.5 = (bf16[128,512]{1,0:T(8,128)(2,1)S(1)}, bf16[128,512]{1,0:T(8,128)(2,1)S(1)}, u32[]{:S(2)}, u32[]{:S(2)}) collective-permute-start(bf16[128,512]{1,0:T(8,128)(2,1)S(1)} %get-tuple-element.16), channel_id=1, source_target_pairs={{2,0},{4,2},{6,4},{3,1},{5,3},{7,5},{10,8},{12,10},{14,12},{11,9},... | collective-permute-start | bytes 393224 | tf_op jit(solution)/shard_map/ppermute | solution.py:12
  34.6 11.0 %collective-permute-start.8 = (bf16[128,512]{1,0:T(8,128)(2,1)S(1)}, bf16[128,512]{1,0:T(8,128)(2,1)S(1)}, u32[]{:S(2)}, u32[]{:S(2)}) collective-permute-start(bf16[128,512]{1,0:T(8,128)(2,1)S(1)} %get-tuple-element.17), channel_id=1, source_target_pairs={{0,1},{2,3},{4,5},{6,7},{8,9},{10,11},{12,13},{14,15},{16,17},{18,... | collective-permute-start | bytes 393224 | tf_op jit(solution)/shard_map/ppermute | solution.py:12
  39.2 6.9 %collective-permute-start.7 = (bf16[128,512]{1,0:T(8,128)(2,1)S(1)}, bf16[128,512]{1,0:T(8,128)(2,1)S(1)}, u32[]{:S(2)}, u32[]{:S(2)}) collective-permute-start(bf16[128,512]{1,0:T(8,128)(2,1)S(1)} %get-tuple-element.18), channel_id=1, source_target_pairs={{1,0},{3,2},{5,4},{7,6},{9,8},{11,10},{13,12},{15,14},{17,16},{19,... | collective-permute-start | bytes 393224 | tf_op jit(solution)/shard_map/ppermute | solution.py:12
  40.5 7.5 %collective-permute-start.6 = (bf16[128,512]{1,0:T(8,128)(2,1)S(1)}, bf16[128,512]{1,0:T(8,128)(2,1)S(1)}, u32[]{:S(2)}, u32[]{:S(2)}) collective-permute-start(bf16[128,512]{1,0:T(8,128)(2,1)S(1)} %get-tuple-element.19), channel_id=1, source_target_pairs={{0,2},{2,4},{4,6},{1,3},{3,5},{5,7},{8,10},{10,12},{12,14},{9,11},... | collective-permute-start | bytes 393224 | tf_op jit(solution)/shard_map/ppermute | solution.py:12
  49.9 2.2 %copy-start.6 = (bf16[1,2,2,128,128]{4,3,2,1,0:T(8,128)(2,1)S(1)}, bf16[1,2,2,128,128]{4,3,2,1,0:T(8,128)(2,1)}, u32[]{:S(2)}) copy-start(bf16[1,2,2,128,128]{4,3,2,1,0:T(8,128)(2,1)} %get-tuple-element.25) | copy-start | bytes 393220
  50.8 6.3 %collective-permute-start.9 = (bf16[256,512]{1,0:T(8,128)(2,1)}, bf16[256,512]{1,0:T(8,128)(2,1)}, u32[]{:S(2)}, u32[]{:S(2)}) collective-permute-start(bf16[256,512]{1,0:T(8,128)(2,1)} %get-tuple-element.30), channel_id=1, source_target_pairs={{8,0},{16,8},{24,16},{9,1},{17,9},{25,17},{10,2},{18,10},{26,18},{... | collective-permute-start | bytes 786440 | tf_op jit(solution)/shard_map/ppermute | solution.py:12
  59.1 11.8 %copy-start.4 = (bf16[256,512]{1,0:T(8,128)(2,1)S(1)}, bf16[256,512]{1,0:T(8,128)(2,1)}, u32[]{:S(2)}) copy-start(bf16[256,512]{1,0:T(8,128)(2,1)} %copy-done.3) | copy-start | bytes 786436
  59.2 12.1 %collective-permute-start.10 = (bf16[128,512]{1,0:T(8,128)(2,1)S(1)}, bf16[128,512]{1,0:T(8,128)(2,1)S(1)}, u32[]{:S(2)}, u32[]{:S(2)}) collective-permute-start(bf16[128,512]{1,0:T(8,128)(2,1)S(1)} %get-tuple-element.12), channel_id=1, source_target_pairs={{2,0},{4,2},{6,4},{3,1},{5,3},{7,5},{10,8},{12,10},{14,12},{11,9},... | collective-permute-start | bytes 393224 | tf_op jit(solution)/shard_map/ppermute | solution.py:12
  60.6 10.6 %collective-permute-start.13 = (bf16[128,512]{1,0:T(8,128)(2,1)S(1)}, bf16[128,512]{1,0:T(8,128)(2,1)S(1)}, u32[]{:S(2)}, u32[]{:S(2)}) collective-permute-start(bf16[128,512]{1,0:T(8,128)(2,1)S(1)} %get-tuple-element.13), channel_id=1, source_target_pairs={{0,1},{2,3},{4,5},{6,7},{8,9},{10,11},{12,13},{14,15},{16,17},{18,... | collective-permute-start | bytes 393224 | tf_op jit(solution)/shard_map/ppermute | solution.py:12
  64.9 6.9 %collective-permute-start.12 = (bf16[128,512]{1,0:T(8,128)(2,1)S(1)}, bf16[128,512]{1,0:T(8,128)(2,1)S(1)}, u32[]{:S(2)}, u32[]{:S(2)}) collective-permute-start(bf16[128,512]{1,0:T(8,128)(2,1)S(1)} %get-tuple-element.14), channel_id=1, source_target_pairs={{1,0},{3,2},{5,4},{7,6},{9,8},{11,10},{13,12},{15,14},{17,16},{19,... | collective-permute-start | bytes 393224 | tf_op jit(solution)/shard_map/ppermute | solution.py:12
  66.2 7.2 %collective-permute-start.11 = (bf16[128,512]{1,0:T(8,128)(2,1)S(1)}, bf16[128,512]{1,0:T(8,128)(2,1)S(1)}, u32[]{:S(2)}, u32[]{:S(2)}) collective-permute-start(bf16[128,512]{1,0:T(8,128)(2,1)S(1)} %get-tuple-element.15), channel_id=1, source_target_pairs={{0,2},{2,4},{4,6},{1,3},{3,5},{5,7},{8,10},{10,12},{12,14},{9,11},... | collective-permute-start | bytes 393224 | tf_op jit(solution)/shard_map/ppermute | solution.py:12
  75.4 6.5 %collective-permute-start.14 = (bf16[256,512]{1,0:T(8,128)(2,1)S(1)}, bf16[256,512]{1,0:T(8,128)(2,1)S(1)}, u32[]{:S(2)}, u32[]{:S(2)}) collective-permute-start(bf16[256,512]{1,0:T(8,128)(2,1)S(1)} %get-tuple-element.32), channel_id=1, source_target_pairs={{8,0},{16,8},{24,16},{9,1},{17,9},{25,17},{10,2},{18,10},{26,18},{... | collective-permute-start | bytes 786440 | tf_op jit(solution)/shard_map/ppermute | solution.py:12
  83.1 11.9 %collective-permute-start.15 = (bf16[128,512]{1,0:T(8,128)(2,1)S(1)}, bf16[128,512]{1,0:T(8,128)(2,1)S(1)}, u32[]{:S(2)}, u32[]{:S(2)}) collective-permute-start(bf16[128,512]{1,0:T(8,128)(2,1)S(1)} %get-tuple-element.8), channel_id=1, source_target_pairs={{2,0},{4,2},{6,4},{3,1},{5,3},{7,5},{10,8},{12,10},{14,12},{11,9},... | collective-permute-start | bytes 393224 | tf_op jit(solution)/shard_map/ppermute | solution.py:12
  84.4 10.6 %collective-permute-start.18 = (bf16[128,512]{1,0:T(8,128)(2,1)S(1)}, bf16[128,512]{1,0:T(8,128)(2,1)S(1)}, u32[]{:S(2)}, u32[]{:S(2)}) collective-permute-start(bf16[128,512]{1,0:T(8,128)(2,1)S(1)} %get-tuple-element.9), channel_id=1, source_target_pairs={{0,1},{2,3},{4,5},{6,7},{8,9},{10,11},{12,13},{14,15},{16,17},{18,... | collective-permute-start | bytes 393224 | tf_op jit(solution)/shard_map/ppermute | solution.py:12
  88.7 6.9 %collective-permute-start.17 = (bf16[128,512]{1,0:T(8,128)(2,1)S(1)}, bf16[128,512]{1,0:T(8,128)(2,1)S(1)}, u32[]{:S(2)}, u32[]{:S(2)}) collective-permute-start(bf16[128,512]{1,0:T(8,128)(2,1)S(1)} %get-tuple-element.10), channel_id=1, source_target_pairs={{1,0},{3,2},{5,4},{7,6},{9,8},{11,10},{13,12},{15,14},{17,16},{19,... | collective-permute-start | bytes 393224 | tf_op jit(solution)/shard_map/ppermute | solution.py:12
  90.0 7.2 %collective-permute-start.16 = (bf16[128,512]{1,0:T(8,128)(2,1)S(1)}, bf16[128,512]{1,0:T(8,128)(2,1)S(1)}, u32[]{:S(2)}, u32[]{:S(2)}) collective-permute-start(bf16[128,512]{1,0:T(8,128)(2,1)S(1)} %get-tuple-element.11), channel_id=1, source_target_pairs={{0,2},{2,4},{4,6},{1,3},{3,5},{5,7},{8,10},{10,12},{12,14},{9,11},... | collective-permute-start | bytes 393224 | tf_op jit(solution)/shard_map/ppermute | solution.py:12
  98.3 6.6 %collective-permute-start.19 = (bf16[256,512]{1,0:T(8,128)(2,1)S(1)}, bf16[256,512]{1,0:T(8,128)(2,1)S(1)}, u32[]{:S(2)}, u32[]{:S(2)}) collective-permute-start(bf16[256,512]{1,0:T(8,128)(2,1)S(1)} %get-tuple-element.34), channel_id=1, source_target_pairs={{8,0},{16,8},{24,16},{9,1},{17,9},{25,17},{10,2},{18,10},{26,18},{... | collective-permute-start | bytes 786440 | tf_op jit(solution)/shard_map/ppermute | solution.py:12
  107.6 12.4 %collective-permute-start.20 = (bf16[128,512]{1,0:T(8,128)(2,1)S(1)}, bf16[128,512]{1,0:T(8,128)(2,1)S(1)}, u32[]{:S(2)}, u32[]{:S(2)}) collective-permute-start(bf16[128,512]{1,0:T(8,128)(2,1)S(1)} %get-tuple-element.4), channel_id=1, source_target_pairs={{2,0},{4,2},{6,4},{3,1},{5,3},{7,5},{10,8},{12,10},{14,12},{11,9},... | collective-permute-start | bytes 393224 | tf_op jit(solution)/shard_map/ppermute | solution.py:12
  108.9 11.1 %collective-permute-start.23 = (bf16[128,512]{1,0:T(8,128)(2,1)S(1)}, bf16[128,512]{1,0:T(8,128)(2,1)S(1)}, u32[]{:S(2)}, u32[]{:S(2)}) collective-permute-start(bf16[128,512]{1,0:T(8,128)(2,1)S(1)} %get-tuple-element.5), channel_id=1, source_target_pairs={{0,1},{2,3},{4,5},{6,7},{8,9},{10,11},{12,13},{14,15},{16,17},{18,... | collective-permute-start | bytes 393224 | tf_op jit(solution)/shard_map/ppermute | solution.py:12
  113.2 6.9 %collective-permute-start.22 = (bf16[128,512]{1,0:T(8,128)(2,1)S(1)}, bf16[128,512]{1,0:T(8,128)(2,1)S(1)}, u32[]{:S(2)}, u32[]{:S(2)}) collective-permute-start(bf16[128,512]{1,0:T(8,128)(2,1)S(1)} %get-tuple-element.6), channel_id=1, source_target_pairs={{1,0},{3,2},{5,4},{7,6},{9,8},{11,10},{13,12},{15,14},{17,16},{19,... | collective-permute-start | bytes 393224 | tf_op jit(solution)/shard_map/ppermute | solution.py:12
  114.5 8.6 %collective-permute-start.21 = (bf16[128,512]{1,0:T(8,128)(2,1)S(1)}, bf16[128,512]{1,0:T(8,128)(2,1)S(1)}, u32[]{:S(2)}, u32[]{:S(2)}) collective-permute-start(bf16[128,512]{1,0:T(8,128)(2,1)S(1)} %get-tuple-element.7), channel_id=1, source_target_pairs={{0,2},{2,4},{4,6},{1,3},{3,5},{5,7},{8,10},{10,12},{12,14},{9,11},... | collective-permute-start | bytes 393224 | tf_op jit(solution)/shard_map/ppermute | solution.py:12
  125.1 53.7 %copy-start.8 = (bf16[1,2,1,1,256,512]{5,4,1,3,2,0:T(8,128)(2,1)}, bf16[1,2,1,1,256,512]{5,4,1,3,2,0:T(8,128)(2,1)S(1)}, u32[]{:S(2)}) copy-start(bf16[1,2,1,1,256,512]{5,4,1,3,2,0:T(8,128)(2,1)S(1)} %bitcast_dynamic-update-slice_fusion) | copy-start | bytes 1572868
  (11 other events, 9.2 us)
Sparse Core Ops, SparseCore 0:
  107.0 70.2 reduce-scatter.1
where the time goes:
time: 187 us; the launch traced here: 186 us
  waiting for transfers between devices  77.6 us (41%)
  starting transfers between devices  64.1 us (34%)
  between operations  14.8 us (8%)
  matrix products  14.5 us (8%)
  local copies, waits for them, and re-layouts  10.2 us (5%)
  other arithmetic  4.61 us (2%)
    ppermute x24, starting transfers between devices, shifted(): lax.ppermute(value, axis, [(source, source + steps) for source in range(l...  64.1 us
    reduce_scatter x1, waiting for transfers between devices, per_device(): lax.psum_scatter(weight_total, ('tx', 'ty'), scatter_dimension=0, tiled=T...  52.2 us
    ppermute x24, waiting for transfers between devices, shifted(): lax.ppermute(value, axis, [(source, source + steps) for source in range(l...  25.4 us
    unnamed x37, local copies, waits for them, and re-layouts  6.36 us
    dot_general x5, matrix products, per_device(): jnp.dot(features, matrix, preferred_element_type=jnp.float32)  4.35 us
  transfers between devices with their start and end apart: 25, of which 13 were waited for; matrix products, arithmetic and copies ran while one was open for 3% of the time, Pallas kernels for 0%

commit v1 on v0

v1 whole, which is shorter than its diff:
```python
import math

import jax
import jax.numpy as jnp
from jax import lax
from jax.sharding import PartitionSpec as P

AXES = ("pipe", "tx", "ty")


def silu_slope(value):
    sigma = jax.nn.sigmoid(value)
    return sigma * (1.0 + value * (1.0 - sigma))


def swap_phases(count):
    phases = []
    for first in (0, 1):
        pairs = [(low, low + 1) for low in range(first, count - 1, 2)]
        if pairs:
            phases.append((first, pairs))
    return phases


def per_device(stored, cotangent, weight, local_edges, halo_edges, pattern, pick):
    sizes = tuple(lax.axis_size(name) for name in AXES)
    sections, rows, columns = sizes
    here, row, column = (lax.axis_index(name) for name in AXES)
    lower = sections // 2
    upper = sections - lower
    top = sections - 1

    def flat(section, x, y):
        return (section * rows + x) * columns + y

    def to_sections(value, moves):
        pairs = [
            (flat(source, x, y), flat(target, x, y))
            for source, target in moves
            for x in range(rows)
            for y in range(columns)
        ]
        return lax.ppermute(value, AXES, pairs)

    features = stored[0, :, 0, 0]
    matrix = weight[0]
    batches, nodes, width = features.shape
    blocks = local_edges.shape[3]
    block_size = local_edges.shape[5]
    block_mask = pattern[:, 0, 0].astype(jnp.bfloat16)
    local_masked = local_edges[:, 0, 0] * block_mask[:, :, :blocks, None, None]
    halo_masked = (
        halo_edges[:, 0, 0] * jnp.swapaxes(block_mask[:, :, blocks:], 1, 2)[:, :, :, None, None]
    )
    picks = pick[:, 0, 0]

    slope = silu_slope(
        jnp.einsum("mnd,de->mne", features, matrix, preferred_element_type=jnp.float32)
    ).astype(jnp.bfloat16)

    exchanges = []
    for axis, position, base, count in ((1, row, 0, rows), (2, column, 2, columns)):
        for first, couples in swap_phases(count):
            is_low = (position - first) % 2 == 0
            pairs = {}
            for lead in {0, top}:
                pairs[lead] = [
                    (
                        flat(lead, *((a, other) if axis == 1 else (other, a))),
                        flat(lead, *((b, other) if axis == 1 else (other, b))),
                    )
                    for low, high in couples
                    for a, b in ((low, high), (high, low))
                    for other in range(columns if axis == 1 else rows)
                ]
            edges = jnp.where(is_low, halo_masked[:, base + 1], halo_masked[:, base])
            target = jnp.where(is_low, picks[:, base], picks[:, base + 1])
            place = (target[:, None] == jnp.arange(blocks)[None]).astype(jnp.float32)
            exchanges.append((pairs, edges, place))

    def section_round(upstream, slope, matrix, lead):
        slope_grad = (upstream.astype(jnp.float32) * slope.astype(jnp.float32)).astype(jnp.bfloat16)
        message_grad = jnp.einsum(
            "mne,de->mnd", slope_grad, matrix, preferred_element_type=jnp.float32
        ).astype(jnp.bfloat16)
        grad_blocks = message_grad.reshape(batches, blocks, block_size, width)
        total = upstream.astype(jnp.float32).reshape(batches, blocks, block_size, width)
        arrivals = []
        for pairs, edges, place in exchanges:
            outward = jnp.einsum(
                "mbij,mbik->mjk", edges, grad_blocks, preferred_element_type=jnp.float32
            ).astype(jnp.bfloat16)
            arrivals.append((lax.ppermute(outward, AXES, pairs[lead]), place))
        total = total + jnp.einsum(
            "mbcij,mbik->mcjk", local_masked, grad_blocks, preferred_element_type=jnp.float32
        )
        for arrived, place in arrivals:
            total = total + place[:, :, None, None] * arrived.astype(jnp.float32)[:, None]
        return slope_grad, total.astype(jnp.bfloat16).reshape(batches, nodes, width)

    fetched = [(slope, matrix)]
    for step in range(1, upper):
        moves = [(top - step, top)] + ([(step, 0)] if step < lower else [])
        fetched.append((to_sections(slope, moves), to_sections(matrix, moves)))

    slope_grads, results = {}, {}
    upstream = cotangent[:, 0, 0]
    for section in reversed(range(sections)):
        lead = top if section >= lower else 0
        steps = top - section if section >= lower else section
        if section == lower - 1:
            upstream = to_sections(upstream, [(top, 0)])
        slope_grads[section], upstream = section_round(upstream, *fetched[steps], lead)
        results[section] = upstream

    def home(values):
        mine = values[top] if sections == 1 else jnp.where(here == top, values[top], values[0])
        for step in range(1, upper):
            moves = [(top, top - step)]
            sent = values[top - step]
            if step < lower:
                moves.append((0, step))
                sent = jnp.where(here == top, sent, values[step])
            got = to_sections(sent, moves)
            takes = here == top - step
            if step < lower:
                takes = takes | (here == step)
            mine = jnp.where(takes, got, mine)
        return mine

    own_grad = home(slope_grads)
    product = jnp.einsum("mnd,mne->de", features, own_grad, preferred_element_type=jnp.float32)
    tiles = rows * columns
    pieces = product.astype(jnp.bfloat16).reshape(tiles, width // tiles, width)
    pieces = lax.all_to_all(pieces, ("tx", "ty"), 0, 0, tiled=True)
    scale = 1.0 / math.sqrt(batches * nodes * tiles)
    summed = jnp.sum(pieces.astype(jnp.float32), axis=0) * scale
    return (summed[None], home(results)[None, :, None, None])


def solution(mesh):
    in_specs = (
        P("pipe", None, "tx", "ty", None, None),
        P(None, "tx", "ty", None, None),
        P("pipe", None, None),
        P(None, "tx", "ty", None, None, None, None),
        P(None, "tx", "ty", None, None, None, None),
        P(None, "tx", "ty", None, None),
        P(None, "tx", "ty", None),
    )
    out_specs = (P("pipe", ("tx", "ty"), None), P("pipe", None, "tx", "ty", None, None))
    return jax.shard_map(
        per_device, mesh=mesh, in_specs=in_specs, out_specs=out_specs, check_vma=False
    )
```

time: 187 us -> 96 us (0.51)
  waiting for transfers between devices: 77.6 us -> 32.4 us
  starting transfers between devices: 64.1 us -> 34.7 us
  between operations: 14.8 us -> 1.28 us
  local copies, waits for them, and re-layouts: 10.2 us -> 5.14 us
  other arithmetic: 4.61 us -> 7.61 us
    reduce_scatter x1 -> x0, waiting for transfers between devices: 52.2 us -> none  [per_device(): lax.psum_scatter(weight_total, ('tx', 'ty'), scatter_dimension=0, tiled=T...]
    ppermute x24 -> x17, starting transfers between devices: 64.1 us -> 30 us  [the longest x12 23.4 us: section_round(): arrivals.append((lax.ppermute(outward, AXES, pairs[lead]), place))]
    all_to_all x0 -> x1, starting transfers between devices: none -> 4.7 us  [per_device(): pieces = lax.all_to_all(pieces, ('tx', 'ty'), 0, 0, tiled=True)]
    convert_element_type x1 -> x17, other arithmetic: 0.07 us -> 4.3 us  [the longest x12 3.45 us: section_round(): arrived.astype(jnp.float32)[:, None]]
    ppermute x24 -> x17, waiting for transfers between devices: 25.4 us -> 29.3 us  [the longest x5 27 us: to_sections(): return lax.ppermute(value, AXES, pairs)]
    all_to_all x0 -> x1, waiting for transfers between devices: none -> 3.13 us  [per_device(): pieces = lax.all_to_all(pieces, ('tx', 'ty'), 0, 0, tiled=True)]
    dynamic_slice x6 -> x0, local copies, waits for them, and re-layouts: 2.72 us -> none  [take_entry(): return lax.dynamic_index_in_dim(array, index, 0, keepdims=False)]
    unnamed x37 -> x24, local copies, waits for them, and re-layouts: 6.36 us -> 4.94 us
  transfers between devices with their start and end apart: 25 -> 18, of which waited for: 13 -> 4; matrix products, arithmetic and copies ran while one was open for 3% -> 15% of each run, Pallas kernels for 0% -> 0%
where the time goes in v1:
time: 96 us; the launch traced here: 95 us
  starting transfers between devices  34.7 us (36%)
  waiting for transfers between devices  32.4 us (34%)
  matrix products  14 us (15%)
  other arithmetic  7.61 us (8%)
  local copies, waits for them, and re-layouts  5.14 us (5%)
  between operations  1.28 us (1%)
    ppermute x5, waiting for transfers between devices, to_sections(): return lax.ppermute(value, AXES, pairs)  27 us
    ppermute x12, starting transfers between devices, section_round(): arrivals.append((lax.ppermute(outward, AXES, pairs[lead]), place))  23.4 us
    ppermute x5, starting transfers between devices, to_sections(): return lax.ppermute(value, AXES, pairs)  6.51 us
    unnamed x24, local copies, waits for them, and re-layouts  4.94 us
    all_to_all x1, starting transfers between devices, per_device(): pieces = lax.all_to_all(pieces, ('tx', 'ty'), 0, 0, tiled=True)  4.7 us
    dot_general x12, matrix products, section_round(): jnp.einsum('mbij,mbik->mjk', edges, grad_blocks, preferred_element_type=j...  4.62 us
    convert_element_type x12, other arithmetic, section_round(): arrived.astype(jnp.float32)[:, None]  3.45 us
    dot_general x4, matrix products, section_round(): jnp.einsum('mbcij,mbik->mcjk', local_masked, grad_blocks, preferred_eleme...  3.33 us
  transfers between devices with their start and end apart: 18, of which 4 were waited for; matrix products, arithmetic and copies ran while one was open for 15% of the time, Pallas kernels for 0%

profile of v1, /device:TPU:0, one launch (start us, length us, event | category | flops | bytes accessed | tf_op | source)
XLA Modules:
  0.0 95.0 jit_solution(11530439870242546692)
XLA Ops:
  0.7 1.0 %copy-done = bf16[1,2,1,1,256,512]{5,4,3,2,1,0:T(8,128)(2,1)S(1)} copy-done((bf16[1,2,1,1,256,512]{5,4,3,2,1,0:T(8,128)(2,1)S(1)}, bf16[1,2,1,1,256,512]{5,4,3,2,1,0:T(8,128)(2,1)}, u32[]{:S(2)}) %copy-start) | copy-done | bytes 524312
  1.7 1.7 %multiply_convert_fusion = bf16[2,256,512]{2,1,0:T(8,128)(2,1)S(1)} fusion(bf16[1,512,512]{2,1,0:T(8,128)(2,1)} %param.9, bf16[1,2,1,1,256,512]{5,4,3,2,1,0:T(8,128)(2,1)S(1)} %copy-done), kind=kOutput, calls=%fused_computation.50 | convolution fusion | flops 270532608 | bytes 1572864 | tf_op jit(solution)/shard_map/mnd,de->mne/dot_general | solution.py:58
  3.4 1.3 %collective-permute-start.3 = (bf16[2,256,512]{2,1,0:T(8,128)(2,1)S(1)}, bf16[2,256,512]{2,1,0:T(8,128)(2,1)S(1)}, u32[]{:S(2)}, u32[]{:S(2)}) collective-permute-start(bf16[2,256,512]{2,1,0:T(8,128)(2,1)S(1)} %multiply_convert_fusion), channel_id=1, source_target_pairs={{16,24},{17,25},{18,26},{19,27},{20,28},{21,29},{22,30},{23,31},{8... | collective-permute-start | bytes 1572872 | tf_op jit(solution)/shard_map/ppermute | solution.py:43
  7.1 0.7 collective-permute-start.2
  9.7 1.3 %collective-permute-start.4 = (bf16[512,512]{1,0:T(8,128)(2,1)S(1)}, bf16[512,512]{1,0:T(8,128)(2,1)S(1)}, u32[]{:S(2)}, u32[]{:S(2)}) collective-permute-start(bf16[512,512]{1,0:T(8,128)(2,1)S(1)} %bitcast.256), channel_id=1, source_target_pairs={{16,24},{17,25},{18,26},{19,27},{20,28},{21,29},{22,30},{23,31},{8... | collective-permute-start | bytes 1572872 | tf_op jit(solution)/shard_map/ppermute | solution.py:43
  11.7 0.9 copy-done.1
  12.6 0.7 fusion.18
  15.6 0.7 collective-permute-start.6
  17.4 1.4 %add_convert_fusion.2 = bf16[2,2,128,512]{3,2,1,0:T(8,128)(2,1)} fusion(f32[2,128,512]{2,1,0:T(8,128)S(1)} %convert_element_type.220, f32[2,128,512]{2,1,0:T(8,128)S(1)} %convert_element_type.218, f32[2,128,512]{2,1,0:T(8,128)S(1)} %convert_element_type.216, f32[2,2]{1,0:T(2,128)S(1)} %get-tuple-element.14, f32[2,2]{1,0:T(2,128)S(1)} %get-tuple-element.15, ...), kind=kOutput, calls=%fused_computation.48 | convolution fusion | flops 136708096 | bytes 3407936 | tf_op jit(solution)/shard_map/mbcij,mbik->mcjk/dot_general | solution.py:94
  18.9 1.3 %collective-permute-start.8 = (bf16[2,256,512]{2,1,0:T(8,128)(2,1)}, bf16[2,256,512]{2,1,0:T(8,128)(2,1)S(1)}, u32[]{:S(2)}, u32[]{:S(2)}) collective-permute-start(bf16[2,256,512]{2,1,0:T(8,128)(2,1)} %bitcast.38), channel_id=1, source_target_pairs={{24,0},{25,1},{26,2},{27,3},{28,4},{29,5},{30,6},{31,7}} | collective-permute-start | bytes 1572872 | tf_op jit(solution)/shard_map/ppermute | solution.py:43
  20.2 26.8 %collective-permute-done.8 = bf16[2,256,512]{2,1,0:T(8,128)(2,1)S(1)} collective-permute-done((bf16[2,256,512]{2,1,0:T(8,128)(2,1)}, bf16[2,256,512]{2,1,0:T(8,128)(2,1)S(1)}, u32[]{:S(2)}, u32[]{:S(2)}) %collective-permute-start.8) | collective-permute-done | bytes 524320 | tf_op jit(solution)/shard_map/ppermute | solution.py:43
  47.0 1.5 %convolution_convert_fusion.1 = bf16[2,256,512]{2,1,0:T(8,128)(2,1)S(1)} fusion(bf16[512,512]{1,0:T(8,128)(2,1)} %copy-done.8, bf16[2,256,512]{2,1,0:T(8,128)(2,1)S(1)} %collective-permute-done.3, bf16[2,256,512]{2,1,0:T(8,128)(2,1)S(1)} %collective-permute-done.8), kind=kOutput, calls=%fused_computation.13 | convolution fusion | flops 269746176 | bytes 2097152 | tf_op jit(solution)/shard_map/mne,de->mnd/dot_general | solution.py:83
  49.3 3.4 %collective-permute-start.12 = (bf16[2,128,512]{2,1,0:T(8,128)(2,1)S(1)}, bf16[2,128,512]{2,1,0:T(8,128)(2,1)S(1)}, u32[]{:S(2)}, u32[]{:S(2)}) collective-permute-start(bf16[2,128,512]{2,1,0:T(8,128)(2,1)S(1)} %fusion.12), channel_id=1, source_target_pairs={{0,1},{2,3},{4,5},{6,7},{1,0},{3,2},{5,4},{7,6}} | collective-permute-start | bytes 786440 | tf_op jit(solution)/shard_map/ppermute | solution.py:93
  53.4 6.5 %collective-permute-start.10 = (bf16[2,128,512]{2,1,0:T(8,128)(2,1)S(1)}, bf16[2,128,512]{2,1,0:T(8,128)(2,1)S(1)}, u32[]{:S(2)}, u32[]{:S(2)}) collective-permute-start(bf16[2,128,512]{2,1,0:T(8,128)(2,1)S(1)} %fusion.10), channel_id=1, source_target_pairs={{0,2},{1,3},{2,0},{3,1},{4,6},{5,7},{6,4},{7,5}} | collective-permute-start | bytes 786440 | tf_op jit(solution)/shard_map/ppermute | solution.py:93
  60.1 1.3 %collective-permute-start.9 = (bf16[2,256,512]{2,1,0:T(8,128)(2,1)S(1)}, bf16[2,256,512]{2,1,0:T(8,128)(2,1)S(1)}, u32[]{:S(2)}, u32[]{:S(2)}) collective-permute-start(bf16[2,256,512]{2,1,0:T(8,128)(2,1)S(1)} %broadcast_select_fusion), channel_id=1, source_target_pairs={{24,16},{25,17},{26,18},{27,19},{28,20},{29,21},{30,22},{31,23},{0... | collective-permute-start | bytes 1572872 | tf_op jit(solution)/shard_map/ppermute | solution.py:43
  62.0 2.2 %collective-permute-done.10 = bf16[2,128,512]{2,1,0:T(8,128)(2,1)S(1)} collective-permute-done((bf16[2,128,512]{2,1,0:T(8,128)(2,1)S(1)}, bf16[2,128,512]{2,1,0:T(8,128)(2,1)S(1)}, u32[]{:S(2)}, u32[]{:S(2)}) %collective-permute-start.10) | collective-permute-done | bytes 262176 | tf_op jit(solution)/shard_map/ppermute | solution.py:93
  65.5 0.9 copy-done.3
  67.1 2.4 %collective-permute-start.16 = (bf16[2,128,512]{2,1,0:T(8,128)(2,1)S(1)}, bf16[2,128,512]{2,1,0:T(8,128)(2,1)}, u32[]{:S(2)}, u32[]{:S(2)}) collective-permute-start(bf16[2,128,512]{2,1,0:T(8,128)(2,1)S(1)} %fusion.15), channel_id=1, source_target_pairs={{0,1},{2,3},{4,5},{6,7},{1,0},{3,2},{5,4},{7,6}} | collective-permute-start | bytes 786440 | tf_op jit(solution)/shard_map/ppermute | solution.py:93
  69.5 1.0 %fusion.14 = bf16[2,128,512]{2,1,0:T(8,128)(2,1)} fusion(bf16[2,2,128,512]{3,2,1,0:T(8,128)(2,1)S(1)} %bitcast.239, bf16[2,1,2,128,128]{4,3,2,1,0:T(8,128)(2,1)S(1)} %get-tuple-element.11), kind=kOutput, calls=%fused_computation.39 | convolution fusion | flops 67239936 | bytes 917504 | tf_op jit(solution)/shard_map/mbij,mbik->mjk/dot_general | solution.py:90
  70.5 1.5 %collective-permute-start.15 = (bf16[2,128,512]{2,1,0:T(8,128)(2,1)}, bf16[2,128,512]{2,1,0:T(8,128)(2,1)}, u32[]{:S(2)}, u32[]{:S(2)}) collective-permute-start(bf16[2,128,512]{2,1,0:T(8,128)(2,1)} %fusion.14), channel_id=1, source_target_pairs={{2,4},{3,5},{4,2},{5,3}} | collective-permute-start | bytes 786440 | tf_op jit(solution)/shard_map/ppermute | solution.py:93
  72.0 1.0 %fusion.13 = bf16[2,128,512]{2,1,0:T(8,128)(2,1)} fusion(bf16[2,2,128,512]{3,2,1,0:T(8,128)(2,1)S(1)} %bitcast.240, bf16[2,1,2,128,128]{4,3,2,1,0:T(8,128)(2,1)S(1)} %get-tuple-element.9), kind=kOutput, calls=%fused_computation.38 | convolution fusion | flops 67239936 | bytes 917504 | tf_op jit(solution)/shard_map/mbij,mbik->mjk/dot_general | solution.py:90
  73.0 4.9 %collective-permute-start.14 = (bf16[2,128,512]{2,1,0:T(8,128)(2,1)}, bf16[2,128,512]{2,1,0:T(8,128)(2,1)}, u32[]{:S(2)}, u32[]{:S(2)}) collective-permute-start(bf16[2,128,512]{2,1,0:T(8,128)(2,1)} %fusion.13), channel_id=1, source_target_pairs={{0,2},{1,3},{2,0},{3,1},{4,6},{5,7},{6,4},{7,5}} | collective-permute-start | bytes 786440 | tf_op jit(solution)/shard_map/ppermute | solution.py:93
  77.9 1.4 %fusion.3 = bf16[512,512]{0,1:T(8,128)(2,1)} fusion(bf16[1,2,1,1,256,512]{5,4,3,2,1,0:T(8,128)(2,1)S(1)} %copy-done, bf16[2,256,512]{2,1,0:T(8,128)(2,1)S(1)} %collective-permute-done.9, bf16[2,256,512]{2,1,0:T(8,128)(2,1)S(1)} %fusion.17, pred[]{:T(512)S(6)} %eq.80, pred[]{:T(512)S(6)} %or.4, bf16[2,256,512]{2,1,0:T(8,128)(2,1)S(1)} %copy-done.7, ...), kind=kOutput, calls=%fused_computation.16 | convolution fusion | flops 270270464 | bytes 3145730 | tf_op jit(solution)/shard_map/mnd,mne->de/dot_general | solution.py:132
  79.3 4.7 %all-to-all-start = ((bf16[8,64,512]{2,1,0:T(8,128)(2,1)}), bf16[8,64,512]{2,1,0:T(8,128)(2,1)S(1)}, u32[]{:S(2)}, u32[]{:S(2)}) async-start(bf16[8,64,512]{2,1,0:T(8,128)(2,1)} %bitcast.257), calls=%async_computation | async-start | bytes 1048576 | tf_op jit(solution)/shard_map/all_to_all | solution.py:135
  84.0 1.1 %bitcast_select_fusion.1 = bf16[2,256,512]{2,1,0:T(8,128)(2,1)S(1)} fusion(bf16[2,2,128,512]{3,2,1,0:T(8,128)(2,1)S(1)} %add_convert_fusion.1, pred[]{:T(512)S(6)} %eq.80, bf16[2,2,128,512]{3,2,1,0:T(8,128)(2,1)} %add_convert_fusion.2), kind=kLoop, calls=%fused_computation.53 | loop fusion | flops 262144 | bytes 1572865 | tf_op jit(solution)/shard_map/jit(_where)/select_n | solution.py:123
  85.2 1.3 %collective-permute-start.13 = (bf16[2,256,512]{2,1,0:T(8,128)(2,1)S(1)}, bf16[2,256,512]{2,1,0:T(8,128)(2,1)S(1)}, u32[]{:S(2)}, u32[]{:S(2)}) collective-permute-start(bf16[2,256,512]{2,1,0:T(8,128)(2,1)S(1)} %bitcast_select_fusion.1), channel_id=1, source_target_pairs={{24,16},{25,17},{26,18},{27,19},{28,20},{29,21},{30,22},{31,23},{0... | collective-permute-start | bytes 1572872 | tf_op jit(solution)/shard_map/ppermute | solution.py:43
  86.5 1.0 %convert_element_type.244 = f32[2,128,512]{2,1,0:T(8,128)S(1)} convert(bf16[2,128,512]{2,1,0:T(8,128)(2,1)} %collective-permute-done.16) | non-fusion elementwise | flops 131072 | bytes 786432 | tf_op jit(solution)/shard_map/convert_element_type | solution.py:98
  87.5 1.0 %convert_element_type.242 = f32[2,128,512]{2,1,0:T(8,128)S(1)} convert(bf16[2,128,512]{2,1,0:T(8,128)(2,1)} %collective-permute-done.15) | non-fusion elementwise | flops 131072 | bytes 786432 | tf_op jit(solution)/shard_map/convert_element_type | solution.py:98
  88.5 1.0 %convert_element_type.240 = f32[2,128,512]{2,1,0:T(8,128)S(1)} convert(bf16[2,128,512]{2,1,0:T(8,128)(2,1)} %collective-permute-done.14) | non-fusion elementwise | flops 131072 | bytes 786432 | tf_op jit(solution)/shard_map/convert_element_type | solution.py:98
  89.5 0.7 fusion.20
  90.3 0.9 bitcast_select_fusion
  91.2 3.1 %all-to-all-done = bf16[8,64,512]{2,1,0:T(8,128)(2,1)S(1)} async-done(((bf16[8,64,512]{2,1,0:T(8,128)(2,1)}), bf16[8,64,512]{2,1,0:T(8,128)(2,1)S(1)}, u32[]{:S(2)}, u32[]{:S(2)}) %all-to-all-start) | async-done | bytes 524320 | tf_op jit(solution)/shard_map/all_to_all | solution.py:135
  (78 shorter events, 13.2 us)
Async XLA Ops:
  0.6 1.0 %copy-start = (bf16[1,2,1,1,256,512]{5,4,3,2,1,0:T(8,128)(2,1)S(1)}, bf16[1,2,1,1,256,512]{5,4,3,2,1,0:T(8,128)(2,1)}, u32[]{:S(2)}) copy-start(bf16[1,2,1,1,256,512]{5,4,3,2,1,0:T(8,128)(2,1)} %param.7) | copy-start | bytes 1572868
  0.6 5.0 %copy-start.2 = (bf16[1,512,512]{2,1,0:T(8,128)(2,1)S(1)}, bf16[1,512,512]{2,1,0:T(8,128)(2,1)}, u32[]{:S(2)}) copy-start(bf16[1,512,512]{2,1,0:T(8,128)(2,1)} %param.9) | copy-start | bytes 1572868
  0.7 4.9 %copy-start.4 = (bf16[2,1,1,256,512]{4,3,2,1,0:T(8,128)(2,1)S(1)}, bf16[2,1,1,256,512]{4,3,2,1,0:T(8,128)(2,1)}, u32[]{:S(2)}) copy-start(bf16[2,1,1,256,512]{4,3,2,1,0:T(8,128)(2,1)} %param.8) | copy-start | bytes 1572868
  3.4 2.7 %copy-start.6 = (bf16[2,256,512]{2,1,0:T(8,128)(2,1)}, bf16[2,256,512]{2,1,0:T(8,128)(2,1)S(1)}, u32[]{:S(2)}) copy-start(bf16[2,256,512]{2,1,0:T(8,128)(2,1)S(1)} %multiply_convert_fusion) | copy-start | bytes 1572868
  3.4 8.3 %collective-permute-start.3 = (bf16[2,256,512]{2,1,0:T(8,128)(2,1)S(1)}, bf16[2,256,512]{2,1,0:T(8,128)(2,1)S(1)}, u32[]{:S(2)}, u32[]{:S(2)}) collective-permute-start(bf16[2,256,512]{2,1,0:T(8,128)(2,1)S(1)} %multiply_convert_fusion), channel_id=1, source_target_pairs={{16,24},{17,25},{18,26},{19,27},{20,28},{21,29},{22,30},{23,31},{8... | collective-permute-start | bytes 1572872 | tf_op jit(solution)/shard_map/ppermute | solution.py:43
  4.7 0.7 copy-start.11
  5.6 1.0 %copy-start.9 = (bf16[2,1,1,4,2,128,128]{6,5,4,3,2,1,0:T(8,128)(2,1)S(1)}, bf16[2,1,1,4,2,128,128]{6,5,4,3,2,1,0:T(8,128)(2,1)}, u32[]{:S(2)}) copy-start(bf16[2,1,1,4,2,128,128]{6,5,4,3,2,1,0:T(8,128)(2,1)} %param.11) | copy-start | bytes 1572868
  7.1 4.4 %collective-permute-start.2 = (bf16[2,128,512]{2,1,0:T(8,128)(2,1)S(1)}, bf16[2,128,512]{2,1,0:T(8,128)(2,1)S(1)}, u32[]{:S(2)}, u32[]{:S(2)}) collective-permute-start(bf16[2,128,512]{2,1,0:T(8,128)(2,1)S(1)} %fusion.6), channel_id=1, source_target_pairs={{24,25},{26,27},{28,29},{30,31},{25,24},{27,26},{29,28},{31,30}} | collective-permute-start | bytes 786440 | tf_op jit(solution)/shard_map/ppermute | solution.py:93
  8.0 3.5 %collective-permute-start.1 = (bf16[2,128,512]{2,1,0:T(8,128)(2,1)S(1)}, bf16[2,128,512]{2,1,0:T(8,128)(2,1)S(1)}, u32[]{:S(2)}, u32[]{:S(2)}) collective-permute-start(bf16[2,128,512]{2,1,0:T(8,128)(2,1)S(1)} %fusion.5), channel_id=1, source_target_pairs={{26,28},{27,29},{28,26},{29,27}} | collective-permute-start | bytes 786440 | tf_op jit(solution)/shard_map/ppermute | solution.py:93
  9.0 2.7 %collective-permute-start = (bf16[2,128,512]{2,1,0:T(8,128)(2,1)S(1)}, bf16[2,128,512]{2,1,0:T(8,128)(2,1)S(1)}, u32[]{:S(2)}, u32[]{:S(2)}) collective-permute-start(bf16[2,128,512]{2,1,0:T(8,128)(2,1)S(1)} %fusion.4), channel_id=1, source_target_pairs={{24,26},{25,27},{26,24},{27,25},{28,30},{29,31},{30,28},{31,29}} | collective-permute-start | bytes 786440 | tf_op jit(solution)/shard_map/ppermute | solution.py:93
  9.7 1.3 %copy-start.10 = (s32[2,1,1,4]{3,2,1,0:T(1,128)S(1)}, s32[2,1,1,4]{3,2,1,0:T(1,128)}, u32[]{:S(2)}) copy-start(s32[2,1,1,4]{3,2,1,0:T(1,128)} %param.13) | copy-start | bytes 100
  9.7 3.8 %collective-permute-start.4 = (bf16[512,512]{1,0:T(8,128)(2,1)S(1)}, bf16[512,512]{1,0:T(8,128)(2,1)S(1)}, u32[]{:S(2)}, u32[]{:S(2)}) collective-permute-start(bf16[512,512]{1,0:T(8,128)(2,1)S(1)} %bitcast.256), channel_id=1, source_target_pairs={{16,24},{17,25},{18,26},{19,27},{20,28},{21,29},{22,30},{23,31},{8... | collective-permute-start | bytes 1572872 | tf_op jit(solution)/shard_map/ppermute | solution.py:43
  11.7 1.0 %copy-start.1 = (bf16[2,1,1,2,2,128,128]{6,5,4,3,2,1,0:T(8,128)(2,1)S(1)}, bf16[2,1,1,2,2,128,128]{6,5,4,3,2,1,0:T(8,128)(2,1)}, u32[]{:S(2)}) copy-start(bf16[2,1,1,2,2,128,128]{6,5,4,3,2,1,0:T(8,128)(2,1)} %param.10) | copy-start | bytes 786436
  13.5 0.8 copy-start.8
  14.9 2.3 %collective-permute-start.7 = (bf16[2,128,512]{2,1,0:T(8,128)(2,1)S(1)}, bf16[2,128,512]{2,1,0:T(8,128)(2,1)S(1)}, u32[]{:S(2)}, u32[]{:S(2)}) collective-permute-start(bf16[2,128,512]{2,1,0:T(8,128)(2,1)S(1)} %fusion.9), channel_id=1, source_target_pairs={{24,25},{26,27},{28,29},{30,31},{25,24},{27,26},{29,28},{31,30}} | collective-permute-start | bytes 786440 | tf_op jit(solution)/shard_map/ppermute | solution.py:93
  15.6 1.7 %collective-permute-start.6 = (bf16[2,128,512]{2,1,0:T(8,128)(2,1)S(1)}, bf16[2,128,512]{2,1,0:T(8,128)(2,1)S(1)}, u32[]{:S(2)}, u32[]{:S(2)}) collective-permute-start(bf16[2,128,512]{2,1,0:T(8,128)(2,1)S(1)} %fusion.8), channel_id=1, source_target_pairs={{26,28},{27,29},{28,26},{29,27}} | collective-permute-start | bytes 786440 | tf_op jit(solution)/shard_map/ppermute | solution.py:93
  16.5 0.8 collective-permute-start.5
  18.9 28.1 %collective-permute-start.8 = (bf16[2,256,512]{2,1,0:T(8,128)(2,1)}, bf16[2,256,512]{2,1,0:T(8,128)(2,1)S(1)}, u32[]{:S(2)}, u32[]{:S(2)}) collective-permute-start(bf16[2,256,512]{2,1,0:T(8,128)(2,1)} %bitcast.38), channel_id=1, source_target_pairs={{24,0},{25,1},{26,2},{27,3},{28,4},{29,5},{30,6},{31,7}} | collective-permute-start | bytes 1572872 | tf_op jit(solution)/shard_map/ppermute | solution.py:43
  49.3 12.6 %collective-permute-start.12 = (bf16[2,128,512]{2,1,0:T(8,128)(2,1)S(1)}, bf16[2,128,512]{2,1,0:T(8,128)(2,1)S(1)}, u32[]{:S(2)}, u32[]{:S(2)}) collective-permute-start(bf16[2,128,512]{2,1,0:T(8,128)(2,1)S(1)} %fusion.12), channel_id=1, source_target_pairs={{0,1},{2,3},{4,5},{6,7},{1,0},{3,2},{5,4},{7,6}} | collective-permute-start | bytes 786440 | tf_op jit(solution)/shard_map/ppermute | solution.py:93
  52.7 9.2 %collective-permute-start.11 = (bf16[2,128,512]{2,1,0:T(8,128)(2,1)S(1)}, bf16[2,128,512]{2,1,0:T(8,128)(2,1)S(1)}, u32[]{:S(2)}, u32[]{:S(2)}) collective-permute-start(bf16[2,128,512]{2,1,0:T(8,128)(2,1)S(1)} %fusion.11), channel_id=1, source_target_pairs={{2,4},{3,5},{4,2},{5,3}} | collective-permute-start | bytes 786440 | tf_op jit(solution)/shard_map/ppermute | solution.py:93
  53.4 10.8 %collective-permute-start.10 = (bf16[2,128,512]{2,1,0:T(8,128)(2,1)S(1)}, bf16[2,128,512]{2,1,0:T(8,128)(2,1)S(1)}, u32[]{:S(2)}, u32[]{:S(2)}) collective-permute-start(bf16[2,128,512]{2,1,0:T(8,128)(2,1)S(1)} %fusion.10), channel_id=1, source_target_pairs={{0,2},{1,3},{2,0},{3,1},{4,6},{5,7},{6,4},{7,5}} | collective-permute-start | bytes 786440 | tf_op jit(solution)/shard_map/ppermute | solution.py:93
  60.1 17.8 %collective-permute-start.9 = (bf16[2,256,512]{2,1,0:T(8,128)(2,1)S(1)}, bf16[2,256,512]{2,1,0:T(8,128)(2,1)S(1)}, u32[]{:S(2)}, u32[]{:S(2)}) collective-permute-start(bf16[2,256,512]{2,1,0:T(8,128)(2,1)S(1)} %broadcast_select_fusion), channel_id=1, source_target_pairs={{24,16},{25,17},{26,18},{27,19},{28,20},{29,21},{30,22},{31,23},{0... | collective-permute-start | bytes 1572872 | tf_op jit(solution)/shard_map/ppermute | solution.py:43
  64.3 1.0 %copy-start.7 = (bf16[2,256,512]{2,1,0:T(8,128)(2,1)S(1)}, bf16[2,256,512]{2,1,0:T(8,128)(2,1)}, u32[]{:S(2)}) copy-start(bf16[2,256,512]{2,1,0:T(8,128)(2,1)} %copy-done.6) | copy-start | bytes 1572868
  65.3 1.0 %copy-start.3 = (bf16[1,512,512]{2,1,0:T(8,128)(2,1)S(1)}, bf16[1,512,512]{2,1,0:T(8,128)(2,1)}, u32[]{:S(2)}) copy-start(bf16[1,512,512]{2,1,0:T(8,128)(2,1)} %param.9) | copy-start | bytes 1572868
  67.1 19.4 %collective-permute-start.16 = (bf16[2,128,512]{2,1,0:T(8,128)(2,1)S(1)}, bf16[2,128,512]{2,1,0:T(8,128)(2,1)}, u32[]{:S(2)}, u32[]{:S(2)}) collective-permute-start(bf16[2,128,512]{2,1,0:T(8,128)(2,1)S(1)} %fusion.15), channel_id=1, source_target_pairs={{0,1},{2,3},{4,5},{6,7},{1,0},{3,2},{5,4},{7,6}} | collective-permute-start | bytes 786440 | tf_op jit(solution)/shard_map/ppermute | solution.py:93
  70.5 7.4 %copy-start.5 = (bf16[2,1,1,256,512]{4,3,2,1,0:T(8,128)(2,1)S(1)}, bf16[2,1,1,256,512]{4,3,2,1,0:T(8,128)(2,1)}, u32[]{:S(2)}) copy-start(bf16[2,1,1,256,512]{4,3,2,1,0:T(8,128)(2,1)} %param.8) | copy-start | bytes 1572868
  70.5 17.0 %collective-permute-start.15 = (bf16[2,128,512]{2,1,0:T(8,128)(2,1)}, bf16[2,128,512]{2,1,0:T(8,128)(2,1)}, u32[]{:S(2)}, u32[]{:S(2)}) collective-permute-start(bf16[2,128,512]{2,1,0:T(8,128)(2,1)} %fusion.14), channel_id=1, source_target_pairs={{2,4},{3,5},{4,2},{5,3}} | collective-permute-start | bytes 786440 | tf_op jit(solution)/shard_map/ppermute | solution.py:93
  73.0 15.6 %collective-permute-start.14 = (bf16[2,128,512]{2,1,0:T(8,128)(2,1)}, bf16[2,128,512]{2,1,0:T(8,128)(2,1)}, u32[]{:S(2)}, u32[]{:S(2)}) collective-permute-start(bf16[2,128,512]{2,1,0:T(8,128)(2,1)} %fusion.13), channel_id=1, source_target_pairs={{0,2},{1,3},{2,0},{3,1},{4,6},{5,7},{6,4},{7,5}} | collective-permute-start | bytes 786440 | tf_op jit(solution)/shard_map/ppermute | solution.py:93
  79.3 15.0 %all-to-all-start = ((bf16[8,64,512]{2,1,0:T(8,128)(2,1)}), bf16[8,64,512]{2,1,0:T(8,128)(2,1)S(1)}, u32[]{:S(2)}, u32[]{:S(2)}) async-start(bf16[8,64,512]{2,1,0:T(8,128)(2,1)} %bitcast.257), calls=%async_computation | async-start | bytes 1048576 | tf_op jit(solution)/shard_map/all_to_all | solution.py:135
  85.2 5.1 %collective-permute-start.13 = (bf16[2,256,512]{2,1,0:T(8,128)(2,1)S(1)}, bf16[2,256,512]{2,1,0:T(8,128)(2,1)S(1)}, u32[]{:S(2)}, u32[]{:S(2)}) collective-permute-start(bf16[2,256,512]{2,1,0:T(8,128)(2,1)S(1)} %bitcast_select_fusion.1), channel_id=1, source_target_pairs={{24,16},{25,17},{26,18},{27,19},{28,20},{29,21},{30,22},{31,23},{0... | collective-permute-start | bytes 1572872 | tf_op jit(solution)/shard_map/ppermute | solution.py:43

commit v2 on v1

v2 whole, which is shorter than its diff:
```python
import functools
import math

import jax
import jax.numpy as jnp
from jax import lax
from jax.experimental import pallas as pl
from jax.experimental.pallas import tpu as pltpu
from jax.sharding import PartitionSpec as P

AXES = ("pipe", "tx", "ty")
F32, BF16 = jnp.float32, jnp.bfloat16
IN_VMEM = pl.BlockSpec(memory_space=pltpu.VMEM)
IN_SMEM = pl.BlockSpec(memory_space=pltpu.SMEM)


def silu_slope(value):
    sigma = jax.nn.sigmoid(value)
    return sigma * (1.0 + value * (1.0 - sigma))


def swap_phases(count):
    phases = []
    for first in (0, 1):
        pairs = [(low, low + 1) for low in range(first, count - 1, 2)]
        if pairs:
            phases.append((first, pairs))
    return phases


def side(phase):
    axis, base, first = phase
    return base, lax.rem(lax.axis_index(axis) + first, 2) == 0


def rows_dot(left, right):
    return lax.dot_general(left, right, (((1,), (0,)), ((), ())), preferred_element_type=F32)


def back_dot(left, right):
    return lax.dot_general(left, right, (((1,), (1,)), ((), ())), preferred_element_type=F32)


def send_blocks(grads, matrix, mixing_ref, message_ref, out_refs):
    batches, outgoing, nodes = mixing_ref.shape
    block = out_refs[0].shape[1]
    messages = back_dot(grads, matrix).astype(BF16)
    message_ref[...] = messages
    first = outgoing - block * len(out_refs)
    for batch in range(batches):
        mixed = rows_dot(
            mixing_ref[batch, first:, :], messages[batch * nodes : (batch + 1) * nodes]
        ).astype(BF16)
        for index, out_ref in enumerate(out_refs):
            out_ref[batch] = mixed[index * block : (index + 1) * block]


def first_kernel(
    phases, pattern_ref, features_ref, matrix_ref, given_ref, local_ref, halo_ref,
    layer_ref, mixing_ref, grad_ref, message_ref, *out_refs
):
    batches, blocks, _, block, _ = local_ref.shape
    pre_activation = rows_dot(features_ref[...], matrix_ref[...])
    slope = silu_slope(pre_activation).astype(BF16)
    layer_ref[0] = slope
    layer_ref[1] = matrix_ref[...]
    grads = (given_ref[...].astype(F32) * slope.astype(F32)).astype(BF16)
    grad_ref[...] = grads
    sides = [side(phase) for phase in phases]
    for batch in range(batches):
        for source in range(blocks):
            columns = slice(source * block, (source + 1) * block)
            for target in range(blocks):
                present = pattern_ref[batch, source, target].astype(F32)
                edges = local_ref[batch, source, target].astype(F32) * present
                mixing_ref[batch, target * block : (target + 1) * block, columns] = edges.T.astype(BF16)
            for index, (base, is_low) in enumerate(sides):
                slot = jnp.where(is_low, base + 1, base)
                present = pattern_ref[batch, source, blocks + slot].astype(F32)
                edges = halo_ref[batch, slot, source].astype(F32) * present
                start = (blocks + index) * block
                mixing_ref[batch, start : start + block, columns] = edges.T.astype(BF16)
    send_blocks(grads, matrix_ref[...], mixing_ref, message_ref, out_refs)


def inner_kernel(upstream_ref, message_ref, mixing_ref, total_ref):
    batches, _, nodes = mixing_ref.shape
    for batch in range(batches):
        rows = slice(batch * nodes, (batch + 1) * nodes)
        total_ref[rows] = upstream_ref[rows].astype(F32) + rows_dot(
            mixing_ref[batch, :nodes, :], message_ref[rows]
        )


def gathered(phases, pick_ref, total_ref, arrived_refs, batch, target):
    block = arrived_refs[0].shape[1]
    start = (batch * (total_ref.shape[0] // arrived_refs[0].shape[0])) + target * block
    value = total_ref[start : start + block]
    for phase, arrived_ref in zip(phases, arrived_refs):
        base, is_low = side(phase)
        slot = jnp.where(is_low, base, base + 1)
        here = (pick_ref[batch, slot] == target).astype(F32)
        value = value + arrived_ref[batch].astype(F32) * here
    return start, block, value.astype(BF16)


def close_blocks(phases, pick_ref, total_ref, arrived_refs, result_ref):
    batches, block, _ = arrived_refs[0].shape
    for batch in range(batches):
        for target in range(total_ref.shape[0] // batches // block):
            start, size, value = gathered(phases, pick_ref, total_ref, arrived_refs, batch, target)
            result_ref[start : start + size] = value


def close_kernel(phases, pick_ref, total_ref, *refs):
    close_blocks(phases, pick_ref, total_ref, refs[:-1], refs[-1])


def last_kernel(phases, top, pick_ref, total_ref, *refs):
    arrived_refs = refs[: len(phases)]
    top_ref, got_ref, result_ref = refs[len(phases) :]
    here = lax.axis_index("pipe")

    @pl.when(here == 0)
    def _():
        close_blocks(phases, pick_ref, total_ref, arrived_refs, result_ref)

    @pl.when(here == top)
    def _():
        result_ref[...] = top_ref[...]

    @pl.when((here != 0) & (here != top))
    def _():
        result_ref[...] = got_ref[...]


def step_kernel(layer_ref, mixing_ref, upstream_ref, grad_ref, message_ref, *out_refs):
    grads = (upstream_ref[...].astype(F32) * layer_ref[0].astype(F32)).astype(BF16)
    grad_ref[...] = grads
    send_blocks(grads, layer_ref[1], mixing_ref, message_ref, out_refs)


def close_step_kernel(phases, pick_ref, total_ref, *refs):
    count = len(phases)
    layer_ref, mixing_ref, result_ref, grad_ref, message_ref, *out_refs = refs[count:]
    close_blocks(phases, pick_ref, total_ref, refs[:count], result_ref)
    step_kernel(layer_ref, mixing_ref, result_ref, grad_ref, message_ref, *out_refs)


def weight_product(top, features_ref, grad_ref, top_ref, got_ref, product_ref):
    here = lax.axis_index("pipe")

    def product(ref):
        value = lax.dot_general(
            features_ref[...], ref[...], (((0,), (0,)), ((), ())), preferred_element_type=F32
        )
        product_ref[...] = value.astype(BF16)

    @pl.when(here == 0)
    def _():
        product(grad_ref)

    @pl.when(here == top)
    def _():
        product(top_ref)

    @pl.when((here != 0) & (here != top))
    def _():
        product(got_ref)


def bottom_kernel(phases, top, pick_ref, total_ref, *refs):
    count = len(phases)
    features_ref, top_ref, got_ref = refs[count : count + 3]
    result_ref, grad_ref, product_ref = refs[count + 5 : count + 8]
    close_step_kernel(
        phases, pick_ref, total_ref, *refs[:count], *refs[count + 3 : count + 7], *refs[count + 8 :]
    )
    weight_product(top, features_ref, grad_ref, top_ref, got_ref, product_ref)


def reduce_kernel(scale, pieces_ref, sum_ref):
    value = pieces_ref[0].astype(F32)
    for index in range(1, pieces_ref.shape[0]):
        value = value + pieces_ref[index].astype(F32)
    sum_ref[...] = value * scale


def after(value, token):
    return lax.optimization_barrier((value, token))


def call(body, inputs, outputs, flops, scalars=0, kind=pltpu.VMEM):
    size = sum(math.prod(shape) * jnp.dtype(dtype).itemsize for shape, dtype in outputs)
    size += sum(value.size * value.dtype.itemsize for value in inputs)
    return pl.pallas_call(
        body,
        out_shape=[kind(shape, dtype) for shape, dtype in outputs],
        in_specs=[IN_SMEM] * scalars + [IN_VMEM] * (len(inputs) - scalars),
        out_specs=[IN_VMEM] * len(outputs),
        compiler_params=pltpu.CompilerParams(vmem_limit_bytes=24 * 1024 * 1024),
        cost_estimate=pl.CostEstimate(flops=flops, bytes_accessed=size, transcendentals=0),
    )(*inputs)


def per_device(stored, cotangent, weight, local_edges, halo_edges, pattern, pick):
    sections, rows, columns = (lax.axis_size(name) for name in AXES)
    here = lax.axis_index("pipe")
    lower = sections // 2
    upper = sections - lower
    top = sections - 1

    def flat(section, x, y):
        return (section * rows + x) * columns + y

    def to_sections(value, moves):
        pairs = [
            (flat(source, x, y), flat(target, x, y))
            for source, target in moves
            for x in range(rows)
            for y in range(columns)
        ]
        return lax.ppermute(value, AXES, pairs)

    batches, nodes, width = stored.shape[1], stored.shape[4], stored.shape[5]
    blocks, block = local_edges.shape[3], local_edges.shape[5]
    total_rows = batches * nodes
    features = stored.reshape(total_rows, width)
    matrix = weight[0]
    picks = pick[:, 0, 0]

    phases, routes = [], []
    for axis, base, count in (("tx", 0, rows), ("ty", 2, columns)):
        for first, couples in swap_phases(count):
            phases.append((axis, base, first))
            route = {}
            for lead in {0, top}:
                route[lead] = [
                    (
                        flat(lead, *((a, other) if axis == "tx" else (other, a))),
                        flat(lead, *((b, other) if axis == "tx" else (other, b))),
                    )
                    for low, high in couples
                    for a, b in ((low, high), (high, low))
                    for other in range(columns if axis == "tx" else rows)
                ]
            routes.append(route)
    phases = tuple(phases)
    sent = [((batches, block, width), BF16)] * len(phases)
    whole = ((total_rows, width), BF16)
    mix_rows = (blocks + len(phases)) * block
    cost = 2 * total_rows * width * (width + len(phases) * block)

    def exchange(outs, lead):
        return [lax.ppermute(out, AXES, route[lead]) for out, route in zip(outs, routes)]

    def inner(upstream, message, mixing):
        return call(
            inner_kernel, [upstream, message, mixing], [((total_rows, width), F32)],
            2 * total_rows * width * nodes,
        )[0]

    given = cotangent.reshape(total_rows, width)
    layer, mixing, grad, message, *outs = call(
        functools.partial(first_kernel, phases),
        [pattern[:, 0, 0], features, matrix, given, local_edges[:, 0, 0], halo_edges[:, 0, 0]],
        [((2, total_rows, width), BF16), ((batches, mix_rows, nodes), BF16), whole, whole] + sent,
        cost + 2 * total_rows * width * width,
        1,
    )
    arrived = exchange(outs, top)
    total = inner(given, message, mixing)

    layer_sent, arrived[0] = after(layer, arrived[0])
    layers = [layer]
    for step in range(1, upper):
        moves = [(top - step, top)] + ([(step, 0)] if step < lower else [])
        layers.append(to_sections(layer_sent, moves))

    def fetch_home(values, arrived):
        got = None
        for step in range(1, upper):
            moves = [(top, top - step)]
            value = values[top - step]
            if step < lower:
                moves.append((0, step))
                value = jnp.where(here == top, value, values[step])
            value, arrived[0] = after(value, arrived[0])
            new = to_sections(value, moves)
            takes = here == top - step
            if step < lower:
                takes = takes | (here == step)
            got = new if step == 1 else jnp.where(takes, new, got)
        return got

    grads, results = {top: grad}, {}
    for section in reversed(range(top)):
        lead = top if section >= lower else 0
        steps = top - section if section >= lower else section
        layer_here = layers[steps]
        if section == lower - 1:
            upstream = call(
                functools.partial(close_kernel, phases), [picks, total, *arrived], [whole], 0, 1
            )[0]
            results[section + 1] = upstream
            upstream = to_sections(upstream, [(top, 0)])
            grad, message, *outs = call(
                step_kernel, [layer_here, mixing, upstream], [whole, whole] + sent, cost
            )
        elif section > 0:
            upstream, grad, message, *outs = call(
                functools.partial(close_step_kernel, phases),
                [picks, total, *arrived, layer_here, mixing],
                [whole, whole, whole] + sent, cost, 1,
            )
            results[section + 1] = upstream
        else:
            got = fetch_home(grads, arrived)
            upstream, grad, product, message, *outs = call(
                functools.partial(bottom_kernel, phases, top),
                [picks, total, *arrived, features, grads[top], got, layer_here, mixing],
                [whole, whole, ((width, width), BF16), whole] + sent,
                cost + 2 * total_rows * width * width, 1,
            )
            results[1] = upstream
        grads[section] = grad
        arrived = exchange(outs, lead)
        total = inner(upstream, message, mixing)

    tiles = rows * columns
    pieces = lax.all_to_all(
        product.reshape(tiles, width // tiles, width), ("tx", "ty"), 0, 0, tiled=True
    )
    got = fetch_home(results, arrived)
    result = call(
        functools.partial(last_kernel, phases, top),
        [picks, total, *arrived, results[top], got], [whole], 0, 1, jax.ShapeDtypeStruct,
    )[0]
    scale = 1.0 / math.sqrt(total_rows * tiles)
    summed = call(
        functools.partial(reduce_kernel, scale), [pieces], [((width // tiles, width), F32)], 0, 0,
        jax.ShapeDtypeStruct,
    )[0]
    return (summed[None], result.reshape(1, batches, 1, 1, nodes, width))


def solution(mesh):
    in_specs = (
        P("pipe", None, "tx", "ty", None, None),
        P(None, "tx", "ty", None, None),
        P("pipe", None, None),
        P(None, "tx", "ty", None, None, None, None),
        P(None, "tx", "ty", None, None, None, None),
        P(None, "tx", "ty", None, None),
        P(None, "tx", "ty", None),
    )
    out_specs = (P("pipe", ("tx", "ty"), None), P("pipe", None, "tx", "ty", None, None))
    return jax.shard_map(
        per_device, mesh=mesh, in_specs=in_specs, out_specs=out_specs, check_vma=False
    )
```

time: 96 us -> 107 us (1.11)
  waiting for transfers between devices: 32.4 us -> 53.9 us
  matrix products: 14 us -> 0 us
  Pallas kernels: 0 us -> 11.4 us
  other arithmetic: 7.61 us -> 0.11 us
  starting transfers between devices: 34.7 us -> 31.5 us
  local copies, waits for them, and re-layouts: 5.14 us -> 7.24 us
    ppermute x12, waiting for transfers between devices: 2.23 us -> 21.1 us  [exchange(): lax.ppermute(out, AXES, route[lead])]
    dot_general x22 -> x0, matrix products: 14 us -> none  [the longest x12 4.62 us: section_round(): jnp.einsum('mbij,mbik->mjk', edges, grad_blocks, preferred_element_type=j...]
    pallas_call x0 -> x11, Pallas kernels: none -> 11.4 us  [call(): pl.pallas_call(body, out_shape=[kind(shape, dtype) for shape, dtype in ou...]
    ppermute x5 -> x4, waiting for transfers between devices: 27 us -> 32.8 us  [to_sections(): return lax.ppermute(value, AXES, pairs)]
    convert_element_type x18 -> x0, other arithmetic: 4.3 us -> none  [the longest x12 3.45 us: section_round(): arrived.astype(jnp.float32)[:, None]]
    ppermute x12, starting transfers between devices: 23.4 us -> 19.6 us  [exchange(): lax.ppermute(out, AXES, route[lead])]
    all_to_all x1, waiting for transfers between devices: 3.13 us -> 0.01 us  [per_device(): lax.all_to_all(product.reshape(tiles, width // tiles, width), ('tx', 'ty'...]
    select_n x5 -> x2, other arithmetic: 2.48 us -> 0.11 us  [fetch_home(): value = jnp.where(here == top, value, values[step])]
  transfers between devices with their start and end apart: 18 -> 17, of which waited for: 4 -> 6; matrix products, arithmetic and copies ran while one was open for 15% -> 0% of each run, Pallas kernels for 0% -> 3%
where the time goes in v2:
time: 107 us; the launch traced here: 105 us
  waiting for transfers between devices  53.9 us (50%)
  starting transfers between devices  31.5 us (29%)
  Pallas kernels  11.4 us (11%)
  local copies, waits for them, and re-layouts  7.24 us (7%)
    ppermute x4, waiting for transfers between devices, to_sections(): return lax.ppermute(value, AXES, pairs)  32.8 us
    ppermute x12, waiting for transfers between devices, exchange(): lax.ppermute(out, AXES, route[lead])  21.1 us
    ppermute x12, starting transfers between devices, exchange(): lax.ppermute(out, AXES, route[lead])  19.6 us
    pallas_call x11, Pallas kernels, call(): pl.pallas_call(body, out_shape=[kind(shape, dtype) for shape, dtype in ou...  11.4 us
    unnamed x36, local copies, waits for them, and re-layouts  7.24 us
    all_to_all x1, starting transfers between devices, per_device(): lax.all_to_all(product.reshape(tiles, width // tiles, width), ('tx', 'ty'...  6.74 us
    ppermute x4, starting transfers between devices, to_sections(): return lax.ppermute(value, AXES, pairs)  5.21 us
  transfers between devices with their start and end apart: 17, of which 6 were waited for; matrix products, arithmetic and copies ran while one was open for 0% of the time, Pallas kernels for 3%

profile of v2, /device:TPU:0, one launch (start us, length us, event | category | flops | bytes accessed | tf_op | source)
XLA Modules:
  0.0 105.2 jit_solution(654931308179820856)
XLA Ops:
  1.3 1.0 copy-done.4
  2.4 1.0 copy-done.6
  3.4 1.0 copy-done.11
  4.4 1.0 copy-done.12
  5.5 0.9 copy-done.13
  6.4 1.8 %shard_map.86 = (bf16[2,512,512]{2,1,0:T(8,128)(2,1)S(1)}, bf16[2,640,256]{2,1,0:T(8,128)(2,1)S(1)}, bf16[512,512]{1,0:T(8,128)(2,1)S(1)}, bf16[512,512]{1,0:T(8...) custom-call(s32[2,2,6]{2,1,0:T(2,128)S(1)} %bitcast.23, ...), custom_call_target="tpu_custom_call" | custom-call | flops 738197504 | bytes 5898336 | tf_op jit(solution)/shard_map/pallas_call | solution.py:196
  8.2 0.7 collective-permute-start
  8.9 1.3 %collective-permute-start.3 = (bf16[2,512,512]{2,1,0:T(8,128)(2,1)S(1)}, bf16[2,512,512]{2,1,0:T(8,128)(2,1)S(1)}, u32[]{:S(2)}, u32[]{:S(2)}) collective-permute-start(bf16[2,512,512]{2,1,0:T(8,128)(2,1)S(1)} %get-tuple-element.39.refs_6_), channel_id=1, source_target_pairs={{16,24},{17,25},{18,26},{19,27},{20,28},{21,29},{22,30},{23,31},{8... | collective-permute-start | bytes 3145736 | tf_op jit(solution)/shard_map/ppermute | solution.py:223
  12.0 1.5 %collective-permute-done.3.refs_3_.layer_ref = bf16[2,512,512]{2,1,0:T(8,128)(2,1)S(1)} collective-permute-done((bf16[2,512,512]{2,1,0:T(8,128)(2,1)S(1)}, bf16[2,512,512]{2,1,0:T(8,128)(2,1)S(1)}, u32[]{:S(2)}, u32[]{:S(2)}) %collective-permute-start.3) | collective-permute-done | bytes 1048608 | tf_op jit(solution)/shard_map/ppermute | solution.py:223
  13.5 1.4 %shard_map.88 = (bf16[512,512]{1,0:T(8,128)(2,1)S(1)}, bf16[512,512]{1,0:T(8,128)(2,1)S(1)}, bf16[512,512]{1,0:T(8,128)(2,1)S(1)}, bf16[2,128,512]{2,1,0:T(8,128...) custom-call(s32[2,4]{1,0:T(2,128)S(1)} %bitcast.16, f32[512,512]{1,0:T(8,128)S(1)} %shard_map.87.total_ref, ...), custom_call_target="tpu_custom_call" | custom-call | flops 469762048 | bytes 5898272 | tf_op jit(solution)/shard_map/pallas_call | solution.py:196
  16.3 0.7 collective-permute-start.6
  17.3 0.9 shard_map.90
  18.2 1.3 %collective-permute-start.7 = (bf16[512,512]{1,0:T(8,128)(2,1)S(1)}, bf16[512,512]{1,0:T(8,128)(2,1)S(1)}, u32[]{:S(2)}, u32[]{:S(2)}) collective-permute-start(bf16[512,512]{1,0:T(8,128)(2,1)S(1)} %shard_map.90), channel_id=1, source_target_pairs={{24,0},{25,1},{26,2},{27,3},{28,4},{29,5},{30,6},{31,7}} | collective-permute-start | bytes 1572872 | tf_op jit(solution)/shard_map/ppermute | solution.py:223
  19.6 31.3 %collective-permute-done.7.upstream_ref = bf16[512,512]{1,0:T(8,128)(2,1)S(1)} collective-permute-done((bf16[512,512]{1,0:T(8,128)(2,1)S(1)}, bf16[512,512]{1,0:T(8,128)(2,1)S(1)}, u32[]{:S(2)}, u32[]{:S(2)}) %collective-permute-start.7) | collective-permute-done | bytes 524320 | tf_op jit(solution)/shard_map/ppermute | solution.py:223
  50.9 0.8 shard_map.91
  51.6 3.6 %collective-permute-start.8 = (bf16[2,128,512]{2,1,0:T(8,128)(2,1)S(1)}, bf16[2,128,512]{2,1,0:T(8,128)(2,1)S(1)}, u32[]{:S(2)}, u32[]{:S(2)}) collective-permute-start(bf16[2,128,512]{2,1,0:T(8,128)(2,1)S(1)} %get-tuple-element.48), channel_id=1, source_target_pairs={{0,2},{1,3},{2,0},{3,1},{4,6},{5,7},{6,4},{7,5}} | collective-permute-start | bytes 786440 | tf_op jit(solution)/shard_map/ppermute | solution.py:255
  55.3 4.6 %collective-permute-done.8.refs_0_ = bf16[2,128,512]{2,1,0:T(8,128)(2,1)S(1)} collective-permute-done((bf16[2,128,512]{2,1,0:T(8,128)(2,1)S(1)}, bf16[2,128,512]{2,1,0:T(8,128)(2,1)S(1)}, u32[]{:S(2)}, u32[]{:S(2)}) %collective-permute-start.8) | collective-permute-done | bytes 262176 | tf_op jit(solution)/shard_map/ppermute | solution.py:255
  59.9 1.3 %collective-permute-start.11 = (bf16[512,512]{1,0:T(8,128)(2,1)S(1)}, bf16[512,512]{1,0:T(8,128)(2,1)S(1)}, u32[]{:S(2)}, u32[]{:S(2)}) collective-permute-start(bf16[512,512]{1,0:T(8,128)(2,1)S(1)} %broadcast_select_fusion.1), channel_id=1, source_target_pairs={{24,16},{25,17},{26,18},{27,19},{28,20},{29,21},{30,22},{31,23},{0... | collective-permute-start | bytes 1572872 | tf_op jit(solution)/shard_map/ppermute | solution.py:223
  61.2 0.7 collective-permute-start.9
  61.9 3.4 %collective-permute-start.10 = (bf16[2,128,512]{2,1,0:T(8,128)(2,1)S(1)}, bf16[2,128,512]{2,1,0:T(8,128)(2,1)S(1)}, u32[]{:S(2)}, u32[]{:S(2)}) collective-permute-start(bf16[2,128,512]{2,1,0:T(8,128)(2,1)S(1)} %get-tuple-element.51), channel_id=1, source_target_pairs={{0,1},{2,3},{4,5},{6,7},{1,0},{3,2},{5,4},{7,6}} | collective-permute-start | bytes 786440 | tf_op jit(solution)/shard_map/ppermute | solution.py:255
  65.7 4.5 %collective-permute-done.10.refs_2_ = bf16[2,128,512]{2,1,0:T(8,128)(2,1)S(1)} collective-permute-done((bf16[2,128,512]{2,1,0:T(8,128)(2,1)S(1)}, bf16[2,128,512]{2,1,0:T(8,128)(2,1)S(1)}, u32[]{:S(2)}, u32[]{:S(2)}) %collective-permute-start.10) | collective-permute-done | bytes 262176 | tf_op jit(solution)/shard_map/ppermute | solution.py:255
  70.2 2.9 %shard_map.93 = (bf16[512,512]{1,0:T(8,128)(2,1)S(1)}, bf16[512,512]{1,0:T(8,128)(2,1)}, bf16[512,512]{1,0:T(8,128)(2,1)}, bf16[512,512]{1,0:T(8,128)(2,1)S(1)},...) custom-call(s32[2,4]{1,0:T(2,128)S(1)} %bitcast.18, ...), custom_call_target="tpu_custom_call" | custom-call | flops 738197504 | bytes 7995424 | tf_op jit(solution)/shard_map/pallas_call | solution.py:196
  73.1 0.7 copy-done.14
  73.8 0.7 copy-done.16
  74.5 6.7 %all-to-all-start = ((bf16[8,64,512]{2,1,0:T(8,128)(2,1)}), bf16[8,64,512]{2,1,0:T(8,128)(2,1)S(1)}, u32[]{:S(2)}, u32[]{:S(2)}) async-start(bf16[8,64,512]{2,1,0:T(8,128)(2,1)} %bitcast.7), calls=%async_computation | async-start | bytes 1048576 | tf_op jit(solution)/shard_map/all_to_all | solution.py:331
  81.2 3.9 %collective-permute-start.12 = (bf16[2,128,512]{2,1,0:T(8,128)(2,1)}, bf16[2,128,512]{2,1,0:T(8,128)(2,1)S(1)}, u32[]{:S(2)}, u32[]{:S(2)}) collective-permute-start(bf16[2,128,512]{2,1,0:T(8,128)(2,1)} %copy-done.16), channel_id=1, source_target_pairs={{0,2},{1,3},{2,0},{3,1},{4,6},{5,7},{6,4},{7,5}} | collective-permute-start | bytes 786440 | tf_op jit(solution)/shard_map/ppermute | solution.py:255
  85.2 7.3 %collective-permute-done.12.refs_0_ = bf16[2,128,512]{2,1,0:T(8,128)(2,1)S(1)} collective-permute-done((bf16[2,128,512]{2,1,0:T(8,128)(2,1)}, bf16[2,128,512]{2,1,0:T(8,128)(2,1)S(1)}, u32[]{:S(2)}, u32[]{:S(2)}) %collective-permute-start.12) | collective-permute-done | bytes 262176 | tf_op jit(solution)/shard_map/ppermute | solution.py:255
  92.5 1.3 %collective-permute-start.15 = (bf16[512,512]{1,0:T(8,128)(2,1)S(1)}, bf16[512,512]{1,0:T(8,128)(2,1)S(1)}, u32[]{:S(2)}, u32[]{:S(2)}) collective-permute-start(bf16[512,512]{1,0:T(8,128)(2,1)S(1)} %broadcast_select_fusion), channel_id=1, source_target_pairs={{24,16},{25,17},{26,18},{27,19},{28,20},{29,21},{30,22},{31,23},{0... | collective-permute-start | bytes 1572872 | tf_op jit(solution)/shard_map/ppermute | solution.py:223
  94.5 3.2 %collective-permute-start.14 = (bf16[2,128,512]{2,1,0:T(8,128)(2,1)S(1)}, bf16[2,128,512]{2,1,0:T(8,128)(2,1)S(1)}, u32[]{:S(2)}, u32[]{:S(2)}) collective-permute-start(bf16[2,128,512]{2,1,0:T(8,128)(2,1)S(1)} %get-tuple-element.60), channel_id=1, source_target_pairs={{0,1},{2,3},{4,5},{6,7},{1,0},{3,2},{5,4},{7,6}} | collective-permute-start | bytes 786440 | tf_op jit(solution)/shard_map/ppermute | solution.py:255
  98.0 4.7 %collective-permute-done.14.refs_2_ = bf16[2,128,512]{2,1,0:T(8,128)(2,1)S(1)} collective-permute-done((bf16[2,128,512]{2,1,0:T(8,128)(2,1)S(1)}, bf16[2,128,512]{2,1,0:T(8,128)(2,1)S(1)}, u32[]{:S(2)}, u32[]{:S(2)}) %collective-permute-start.14) | collective-permute-done | bytes 262176 | tf_op jit(solution)/shard_map/ppermute | solution.py:255
  102.8 1.7 %shard_map.96 = bf16[512,512]{1,0:T(8,128)(2,1)} custom-call(s32[2,4]{1,0:T(2,128)S(1)} %bitcast.19, f32[512,512]{1,0:T(8,128)S(1)} %shard_map.95.total_ref, bf16[2,128,512]{2,1,0:T(8,128)(2,1)S(1)} %collective-permute-done.12.refs_0_, bf16[2,128,512]{2,1,0:T(8,128)(2,1)S(1)} %collective-permute-done.13.refs_1_, ...), custom_call_target="tpu_custom_call" | custom-call | bytes 3407904 | tf_op jit(solution)/shard_map/pallas_call | solution.py:196
  104.5 0.7 shard_map.94
  (51 shorter events, 5.5 us)
Async XLA Ops:
  1.3 1.0 copy-start.4
  2.4 1.0 copy-start.6
  3.4 1.0 copy-start.11
  4.4 1.0 copy-start.12
  5.5 0.9 copy-start.13
  6.4 5.2 %copy-start.5 = (bf16[2,1,1,256,512]{4,3,2,1,0:T(8,128)(2,1)S(1)}, bf16[2,1,1,256,512]{4,3,2,1,0:T(8,128)(2,1)}, u32[]{:S(2)}) copy-start(bf16[2,1,1,256,512]{4,3,2,1,0:T(8,128)(2,1)} %param.8) | copy-start | bytes 1572868
  8.2 3.7 %copy-start = (bf16[2,512,512]{2,1,0:T(8,128)(2,1)}, bf16[2,512,512]{2,1,0:T(8,128)(2,1)S(1)}, u32[]{:S(2)}) copy-start(bf16[2,512,512]{2,1,0:T(8,128)(2,1)S(1)} %get-tuple-element.39.refs_6_) | copy-start | bytes 3145732
  8.2 3.7 %copy-start.8 = (bf16[512,512]{1,0:T(8,128)(2,1)}, bf16[512,512]{1,0:T(8,128)(2,1)S(1)}, u32[]{:S(2)}) copy-start(bf16[512,512]{1,0:T(8,128)(2,1)S(1)} %get-tuple-element.52.refs_4_) | copy-start | bytes 1572868
  8.2 0.7 collective-permute-start
  8.9 4.6 %collective-permute-start.3 = (bf16[2,512,512]{2,1,0:T(8,128)(2,1)S(1)}, bf16[2,512,512]{2,1,0:T(8,128)(2,1)S(1)}, u32[]{:S(2)}, u32[]{:S(2)}) collective-permute-start(bf16[2,512,512]{2,1,0:T(8,128)(2,1)S(1)} %get-tuple-element.39.refs_6_), channel_id=1, source_target_pairs={{16,24},{17,25},{18,26},{19,27},{20,28},{21,29},{22,30},{23,31},{8... | collective-permute-start | bytes 3145736 | tf_op jit(solution)/shard_map/ppermute | solution.py:223
  10.2 1.7 %collective-permute-start.1 = (bf16[2,128,512]{2,1,0:T(8,128)(2,1)S(1)}, bf16[2,128,512]{2,1,0:T(8,128)(2,1)S(1)}, u32[]{:S(2)}, u32[]{:S(2)}) collective-permute-start(bf16[2,128,512]{2,1,0:T(8,128)(2,1)S(1)} %get-tuple-element.37), channel_id=1, source_target_pairs={{26,28},{27,29},{28,26},{29,27}} | collective-permute-start | bytes 786440 | tf_op jit(solution)/shard_map/ppermute | solution.py:255
  10.9 1.0 collective-permute-start.2
  11.9 1.6 %copy-start.10 = (s32[2,1,1,4]{3,2,1,0:T(1,128)S(1)}, s32[2,1,1,4]{3,2,1,0:T(1,128)}, u32[]{:S(2)}) copy-start(s32[2,1,1,4]{3,2,1,0:T(1,128)} %param.13) | copy-start | bytes 100
  14.9 2.4 %copy-start.2 = (bf16[512,512]{1,0:T(8,128)(2,1)}, bf16[512,512]{1,0:T(8,128)(2,1)S(1)}, u32[]{:S(2)}) copy-start(bf16[512,512]{1,0:T(8,128)(2,1)S(1)} %get-tuple-element.46) | copy-start | bytes 1572868
  14.9 2.4 %collective-permute-start.4 = (bf16[2,128,512]{2,1,0:T(8,128)(2,1)S(1)}, bf16[2,128,512]{2,1,0:T(8,128)(2,1)S(1)}, u32[]{:S(2)}, u32[]{:S(2)}) collective-permute-start(bf16[2,128,512]{2,1,0:T(8,128)(2,1)S(1)} %get-tuple-element.42), channel_id=1, source_target_pairs={{24,26},{25,27},{26,24},{27,25},{28,30},{29,31},{30,28},{31,29}} | collective-permute-start | bytes 786440 | tf_op jit(solution)/shard_map/ppermute | solution.py:255
  15.6 1.7 %collective-permute-start.5 = (bf16[2,128,512]{2,1,0:T(8,128)(2,1)S(1)}, bf16[2,128,512]{2,1,0:T(8,128)(2,1)S(1)}, u32[]{:S(2)}, u32[]{:S(2)}) collective-permute-start(bf16[2,128,512]{2,1,0:T(8,128)(2,1)S(1)} %get-tuple-element.43), channel_id=1, source_target_pairs={{26,28},{27,29},{28,26},{29,27}} | collective-permute-start | bytes 786440 | tf_op jit(solution)/shard_map/ppermute | solution.py:255
  16.3 1.0 collective-permute-start.6
  18.2 32.6 %collective-permute-start.7 = (bf16[512,512]{1,0:T(8,128)(2,1)S(1)}, bf16[512,512]{1,0:T(8,128)(2,1)S(1)}, u32[]{:S(2)}, u32[]{:S(2)}) collective-permute-start(bf16[512,512]{1,0:T(8,128)(2,1)S(1)} %shard_map.90), channel_id=1, source_target_pairs={{24,0},{25,1},{26,2},{27,3},{28,4},{29,5},{30,6},{31,7}} | collective-permute-start | bytes 1572872 | tf_op jit(solution)/shard_map/ppermute | solution.py:223
  19.6 35.7 %copy-start.3 = (bf16[512,512]{1,0:T(8,128)(2,1)S(1)}, bf16[512,512]{1,0:T(8,128)(2,1)}, u32[]{:S(2)}) copy-start(bf16[512,512]{1,0:T(8,128)(2,1)} %copy-done.2) | copy-start | bytes 1572868
  51.6 8.3 %collective-permute-start.8 = (bf16[2,128,512]{2,1,0:T(8,128)(2,1)S(1)}, bf16[2,128,512]{2,1,0:T(8,128)(2,1)S(1)}, u32[]{:S(2)}, u32[]{:S(2)}) collective-permute-start(bf16[2,128,512]{2,1,0:T(8,128)(2,1)S(1)} %get-tuple-element.48), channel_id=1, source_target_pairs={{0,2},{1,3},{2,0},{3,1},{4,6},{5,7},{6,4},{7,5}} | collective-permute-start | bytes 786440 | tf_op jit(solution)/shard_map/ppermute | solution.py:255
  59.9 10.3 %collective-permute-start.11 = (bf16[512,512]{1,0:T(8,128)(2,1)S(1)}, bf16[512,512]{1,0:T(8,128)(2,1)S(1)}, u32[]{:S(2)}, u32[]{:S(2)}) collective-permute-start(bf16[512,512]{1,0:T(8,128)(2,1)S(1)} %broadcast_select_fusion.1), channel_id=1, source_target_pairs={{24,16},{25,17},{26,18},{27,19},{28,20},{29,21},{30,22},{31,23},{0... | collective-permute-start | bytes 1572872 | tf_op jit(solution)/shard_map/ppermute | solution.py:223
  61.2 4.5 %collective-permute-start.9 = (bf16[2,128,512]{2,1,0:T(8,128)(2,1)S(1)}, bf16[2,128,512]{2,1,0:T(8,128)(2,1)S(1)}, u32[]{:S(2)}, u32[]{:S(2)}) collective-permute-start(bf16[2,128,512]{2,1,0:T(8,128)(2,1)S(1)} %get-tuple-element.50), channel_id=1, source_target_pairs={{2,4},{3,5},{4,2},{5,3}} | collective-permute-start | bytes 786440 | tf_op jit(solution)/shard_map/ppermute | solution.py:255
  61.9 8.3 %collective-permute-start.10 = (bf16[2,128,512]{2,1,0:T(8,128)(2,1)S(1)}, bf16[2,128,512]{2,1,0:T(8,128)(2,1)S(1)}, u32[]{:S(2)}, u32[]{:S(2)}) collective-permute-start(bf16[2,128,512]{2,1,0:T(8,128)(2,1)S(1)} %get-tuple-element.51), channel_id=1, source_target_pairs={{0,1},{2,3},{4,5},{6,7},{1,0},{3,2},{5,4},{7,6}} | collective-permute-start | bytes 786440 | tf_op jit(solution)/shard_map/ppermute | solution.py:255
  65.3 4.8 %copy-start.1 = (bf16[2,512,512]{2,1,0:T(8,128)(2,1)S(1)}, bf16[2,512,512]{2,1,0:T(8,128)(2,1)}, u32[]{:S(2)}) copy-start(bf16[2,512,512]{2,1,0:T(8,128)(2,1)} %copy-done) | copy-start | bytes 3145732
  65.4 4.8 %copy-start.7 = (bf16[1,2,1,1,256,512]{5,4,3,2,1,0:T(8,128)(2,1)S(1)}, bf16[1,2,1,1,256,512]{5,4,3,2,1,0:T(8,128)(2,1)}, u32[]{:S(2)}) copy-start(bf16[1,2,1,1,256,512]{5,4,3,2,1,0:T(8,128)(2,1)} %param.7) | copy-start | bytes 1572868
  65.4 4.8 %copy-start.9 = (bf16[512,512]{1,0:T(8,128)(2,1)S(1)}, bf16[512,512]{1,0:T(8,128)(2,1)}, u32[]{:S(2)}) copy-start(bf16[512,512]{1,0:T(8,128)(2,1)} %copy-done.8) | copy-start | bytes 1572868
  74.5 30.0 %all-to-all-start = ((bf16[8,64,512]{2,1,0:T(8,128)(2,1)}), bf16[8,64,512]{2,1,0:T(8,128)(2,1)S(1)}, u32[]{:S(2)}, u32[]{:S(2)}) async-start(bf16[8,64,512]{2,1,0:T(8,128)(2,1)} %bitcast.7), calls=%async_computation | async-start | bytes 1048576 | tf_op jit(solution)/shard_map/all_to_all | solution.py:331
  81.2 11.3 %collective-permute-start.12 = (bf16[2,128,512]{2,1,0:T(8,128)(2,1)}, bf16[2,128,512]{2,1,0:T(8,128)(2,1)S(1)}, u32[]{:S(2)}, u32[]{:S(2)}) collective-permute-start(bf16[2,128,512]{2,1,0:T(8,128)(2,1)} %copy-done.16), channel_id=1, source_target_pairs={{0,2},{1,3},{2,0},{3,1},{4,6},{5,7},{6,4},{7,5}} | collective-permute-start | bytes 786440 | tf_op jit(solution)/shard_map/ppermute | solution.py:255
  85.1 8.7 %copy-start.15 = (bf16[2,128,512]{2,1,0:T(8,128)(2,1)S(1)}, bf16[2,128,512]{2,1,0:T(8,128)(2,1)}, u32[]{:S(2)}) copy-start(bf16[2,128,512]{2,1,0:T(8,128)(2,1)} %copy-done.14) | copy-start | bytes 786436
  92.5 10.3 %collective-permute-start.15 = (bf16[512,512]{1,0:T(8,128)(2,1)S(1)}, bf16[512,512]{1,0:T(8,128)(2,1)S(1)}, u32[]{:S(2)}, u32[]{:S(2)}) collective-permute-start(bf16[512,512]{1,0:T(8,128)(2,1)S(1)} %broadcast_select_fusion), channel_id=1, source_target_pairs={{24,16},{25,17},{26,18},{27,19},{28,20},{29,21},{30,22},{31,23},{0... | collective-permute-start | bytes 1572872 | tf_op jit(solution)/shard_map/ppermute | solution.py:223
  93.8 4.2 %collective-permute-start.13 = (bf16[2,128,512]{2,1,0:T(8,128)(2,1)S(1)}, bf16[2,128,512]{2,1,0:T(8,128)(2,1)S(1)}, u32[]{:S(2)}, u32[]{:S(2)}) collective-permute-start(bf16[2,128,512]{2,1,0:T(8,128)(2,1)S(1)} %copy-done.15), channel_id=1, source_target_pairs={{2,4},{3,5},{4,2},{5,3}} | collective-permute-start | bytes 786440 | tf_op jit(solution)/shard_map/ppermute | solution.py:255
  94.5 8.3 %collective-permute-start.14 = (bf16[2,128,512]{2,1,0:T(8,128)(2,1)S(1)}, bf16[2,128,512]{2,1,0:T(8,128)(2,1)S(1)}, u32[]{:S(2)}, u32[]{:S(2)}) collective-permute-start(bf16[2,128,512]{2,1,0:T(8,128)(2,1)S(1)} %get-tuple-element.60), channel_id=1, source_target_pairs={{0,1},{2,3},{4,5},{6,7},{1,0},{3,2},{5,4},{7,6}} | collective-permute-start | bytes 786440 | tf_op jit(solution)/shard_map/ppermute | solution.py:255
  (3 other events, 2.1 us)

commit v3 on v2

--- a/solution.py
+++ b/solution.py
@@ -11,7 +11,6 @@
 AXES = ("pipe", "tx", "ty")
 F32, BF16 = jnp.float32, jnp.bfloat16
 IN_VMEM = pl.BlockSpec(memory_space=pltpu.VMEM)
-IN_SMEM = pl.BlockSpec(memory_space=pltpu.SMEM)
 
 
 def silu_slope(value):
@@ -55,18 +54,31 @@
             out_ref[batch] = mixed[index * block : (index + 1) * block]
 
 
-def first_kernel(
-    phases, pattern_ref, features_ref, matrix_ref, given_ref, local_ref, halo_ref,
-    layer_ref, mixing_ref, grad_ref, message_ref, *out_refs
-):
+def first_kernel(phases, *refs):
+    sources, refs = refs[:7], refs[7:]
+    layer_ref, mixing_ref, mask_ref, grad_ref, message_ref = refs[:5]
+    out_refs = refs[5 : 5 + len(phases)]
+    held, sems = refs[5 + len(phases) : -1], refs[-1]
+    copies = [
+        pltpu.make_async_copy(source, target, sems.at[index])
+        for index, (source, target) in enumerate(zip(sources, held))
+    ]
+    for copy in copies:
+        copy.start()
+    features_ref, matrix_ref, given_ref, pattern_ref, pick_ref, local_ref, halo_ref = held
     batches, blocks, _, block, _ = local_ref.shape
+    sides = [side(phase) for phase in phases]
+    copies[0].wait()
+    copies[1].wait()
     pre_activation = rows_dot(features_ref[...], matrix_ref[...])
     slope = silu_slope(pre_activation).astype(BF16)
     layer_ref[0] = slope
     layer_ref[1] = matrix_ref[...]
+    copies[2].wait()
     grads = (given_ref[...].astype(F32) * slope.astype(F32)).astype(BF16)
     grad_ref[...] = grads
-    sides = [side(phase) for phase in phases]
+    for copy in copies[3:]:
+        copy.wait()
     for batch in range(batches):
         for source in range(blocks):
             columns = slice(source * block, (source + 1) * block)
@@ -80,6 +92,12 @@
                 edges = halo_ref[batch, slot, source].astype(F32) * present
                 start = (blocks + index) * block
                 mixing_ref[batch, start : start + block, columns] = edges.T.astype(BF16)
+        for index, (base, is_low) in enumerate(sides):
+            chosen = pick_ref[batch, jnp.where(is_low, base, base + 1)]
+            for target in range(blocks):
+                here = (chosen == target).astype(F32)
+                entry = (batch * blocks + target) * len(sides) + index
+                mask_ref[entry] = jnp.full(mask_ref.shape[1:], here, F32)
     send_blocks(grads, matrix_ref[...], mixing_ref, message_ref, out_refs)
 
 
@@ -92,38 +110,48 @@
         )
 
 
-def gathered(phases, pick_ref, total_ref, arrived_refs, batch, target):
-    block = arrived_refs[0].shape[1]
-    start = (batch * (total_ref.shape[0] // arrived_refs[0].shape[0])) + target * block
-    value = total_ref[start : start + block]
-    for phase, arrived_ref in zip(phases, arrived_refs):
-        base, is_low = side(phase)
-        slot = jnp.where(is_low, base, base + 1)
-        here = (pick_ref[batch, slot] == target).astype(F32)
-        value = value + arrived_ref[batch].astype(F32) * here
-    return start, block, value.astype(BF16)
-
-
-def close_blocks(phases, pick_ref, total_ref, arrived_refs, result_ref):
+def turn_kernel(features_ref, turned_ref):
+    turned_ref[...] = features_ref[...].T
+
+
+def choose_kernel(top, top_ref, other_ref, chosen_ref):
+    at_top = lax.axis_index("pipe") == top
+
+    @pl.when(at_top)
+    def _():
+        chosen_ref[...] = top_ref[...]
+
+    @pl.when(jnp.logical_not(at_top))
+    def _():
+        chosen_ref[...] = other_ref[...]
+
+
+def close_blocks(mask_ref, total_ref, arrived_refs, result_ref):
     batches, block, _ = arrived_refs[0].shape
+    count = len(arrived_refs)
     for batch in range(batches):
+        arrived = [ref[batch].astype(F32) for ref in arrived_refs]
         for target in range(total_ref.shape[0] // batches // block):
-            start, size, value = gathered(phases, pick_ref, total_ref, arrived_refs, batch, target)
-            result_ref[start : start + size] = value
-
-
-def close_kernel(phases, pick_ref, total_ref, *refs):
-    close_blocks(phases, pick_ref, total_ref, refs[:-1], refs[-1])
-
-
-def last_kernel(phases, top, pick_ref, total_ref, *refs):
-    arrived_refs = refs[: len(phases)]
-    top_ref, got_ref, result_ref = refs[len(phases) :]
+            order = batch * (total_ref.shape[0] // batches // block) + target
+            rows = slice(order * block, (order + 1) * block)
+            value = total_ref[rows]
+            for index in range(count):
+                value = value + arrived[index] * mask_ref[order * count + index]
+            result_ref[rows] = value.astype(BF16)
+
+
+def close_kernel(mask_ref, total_ref, *refs):
+    close_blocks(mask_ref, total_ref, refs[:-1], refs[-1])
+
+
+def last_kernel(top, mask_ref, total_ref, *refs):
+    arrived_refs = refs[:-3]
+    top_ref, got_ref, result_ref = refs[-3:]
     here = lax.axis_index("pipe")
 
     @pl.when(here == 0)
     def _():
-        close_blocks(phases, pick_ref, total_ref, arrived_refs, result_ref)
+        close_blocks(mask_ref, total_ref, arrived_refs, result_ref)
 
     @pl.when(here == top)
     def _():
@@ -140,21 +168,17 @@
     send_blocks(grads, layer_ref[1], mixing_ref, message_ref, out_refs)
 
 
-def close_step_kernel(phases, pick_ref, total_ref, *refs):
-    count = len(phases)
+def close_step_kernel(count, mask_ref, total_ref, *refs):
     layer_ref, mixing_ref, result_ref, grad_ref, message_ref, *out_refs = refs[count:]
-    close_blocks(phases, pick_ref, total_ref, refs[:count], result_ref)
+    close_blocks(mask_ref, total_ref, refs[:count], result_ref)
     step_kernel(layer_ref, mixing_ref, result_ref, grad_ref, message_ref, *out_refs)
 
 
-def weight_product(top, features_ref, grad_ref, top_ref, got_ref, product_ref):
+def weight_product(top, turned_ref, grad_ref, top_ref, got_ref, product_ref):
     here = lax.axis_index("pipe")
 
     def product(ref):
-        value = lax.dot_general(
-            features_ref[...], ref[...], (((0,), (0,)), ((), ())), preferred_element_type=F32
-        )
-        product_ref[...] = value.astype(BF16)
+        product_ref[...] = rows_dot(turned_ref[...], ref[...]).astype(BF16)
 
     @pl.when(here == 0)
     def _():
@@ -169,14 +193,17 @@
         product(got_ref)
 
 
-def bottom_kernel(phases, top, pick_ref, total_ref, *refs):
-    count = len(phases)
-    features_ref, top_ref, got_ref = refs[count : count + 3]
-    result_ref, grad_ref, product_ref = refs[count + 5 : count + 8]
+def bottom_kernel(count, top, mask_ref, total_ref, *refs):
+    turned_ref, top_ref, got_ref, layer_ref, mixing_ref = refs[count : count + 5]
+    result_ref, product_ref, next_ref = refs[count + 5 : count + 8]
+    out_refs = refs[count + 8 : -2]
+    grad_ref, message_ref = refs[-2:]
     close_step_kernel(
-        phases, pick_ref, total_ref, *refs[:count], *refs[count + 3 : count + 7], *refs[count + 8 :]
-    )
-    weight_product(top, features_ref, grad_ref, top_ref, got_ref, product_ref)
+        count, mask_ref, total_ref, *refs[:count], layer_ref, mixing_ref,
+        result_ref, grad_ref, message_ref, *out_refs
+    )
+    weight_product(top, turned_ref, grad_ref, top_ref, got_ref, product_ref)
+    inner_kernel(result_ref, message_ref, mixing_ref, next_ref)
 
 
 def reduce_kernel(scale, pieces_ref, sum_ref):
@@ -186,19 +213,16 @@
     sum_ref[...] = value * scale
 
 
-def after(value, token):
-    return lax.optimization_barrier((value, token))
-
-
-def call(body, inputs, outputs, flops, scalars=0, kind=pltpu.VMEM):
+def call(body, inputs, outputs, flops, kind=pltpu.VMEM, source=IN_VMEM, scratch=()):
     size = sum(math.prod(shape) * jnp.dtype(dtype).itemsize for shape, dtype in outputs)
     size += sum(value.size * value.dtype.itemsize for value in inputs)
     return pl.pallas_call(
         body,
         out_shape=[kind(shape, dtype) for shape, dtype in outputs],
-        in_specs=[IN_SMEM] * scalars + [IN_VMEM] * (len(inputs) - scalars),
+        in_specs=[source] * len(inputs),
         out_specs=[IN_VMEM] * len(outputs),
-        compiler_params=pltpu.CompilerParams(vmem_limit_bytes=24 * 1024 * 1024),
+        scratch_shapes=scratch,
+        compiler_params=pltpu.CompilerParams(vmem_limit_bytes=16 * 1024 * 1024),
         cost_estimate=pl.CostEstimate(flops=flops, bytes_accessed=size, transcendentals=0),
     )(*inputs)
 
@@ -261,31 +285,42 @@
         )[0]
 
     given = cotangent.reshape(total_rows, width)
-    layer, mixing, grad, message, *outs = call(
+    operands = [
+        features, matrix, given, pattern[:, 0, 0], picks, local_edges[:, 0, 0], halo_edges[:, 0, 0]
+    ]
+    layer, mixing, mask, grad, message, *outs = call(
         functools.partial(first_kernel, phases),
-        [pattern[:, 0, 0], features, matrix, given, local_edges[:, 0, 0], halo_edges[:, 0, 0]],
-        [((2, total_rows, width), BF16), ((batches, mix_rows, nodes), BF16), whole, whole] + sent,
+        [pltpu.with_memory_space_constraint(value, pltpu.HBM) for value in operands],
+        [
+            ((2, total_rows, width), BF16), ((batches, mix_rows, nodes), BF16),
+            ((batches * blocks * len(phases), 1, width), F32), whole, whole,
+        ] + sent,
         cost + 2 * total_rows * width * width,
-        1,
+        source=pl.BlockSpec(memory_space=pltpu.HBM),
+        scratch=[
+            (pltpu.VMEM if value.dtype == BF16 else pltpu.SMEM)(value.shape, value.dtype)
+            for value in operands
+        ] + [pltpu.SemaphoreType.DMA((len(operands),))],
     )
     arrived = exchange(outs, top)
     total = inner(given, message, mixing)
-
-    layer_sent, arrived[0] = after(layer, arrived[0])
+    turned = call(turn_kernel, [features], [((width, total_rows), BF16)], 0)[0]
+
     layers = [layer]
     for step in range(1, upper):
         moves = [(top - step, top)] + ([(step, 0)] if step < lower else [])
-        layers.append(to_sections(layer_sent, moves))
-
-    def fetch_home(values, arrived):
+        layers.append(to_sections(layer, moves))
+
+    def fetch_home(values):
         got = None
         for step in range(1, upper):
             moves = [(top, top - step)]
             value = values[top - step]
             if step < lower:
                 moves.append((0, step))
-                value = jnp.where(here == top, value, values[step])
-            value, arrived[0] = after(value, arrived[0])
+                value = call(
+                    functools.partial(choose_kernel, top), [value, values[step]], [whole], 0
+                )[0]
             new = to_sections(value, moves)
             takes = here == top - step
             if step < lower:
@@ -293,15 +328,14 @@
             got = new if step == 1 else jnp.where(takes, new, got)
         return got
 
+    count = len(phases)
     grads, results = {top: grad}, {}
     for section in reversed(range(top)):
         lead = top if section >= lower else 0
         steps = top - section if section >= lower else section
         layer_here = layers[steps]
         if section == lower - 1:
-            upstream = call(
-                functools.partial(close_kernel, phases), [picks, total, *arrived], [whole], 0, 1
-            )[0]
+            upstream = call(close_kernel, [mask, total, *arrived], [whole], 0)[0]
             results[section + 1] = upstream
             upstream = to_sections(upstream, [(top, 0)])
             grad, message, *outs = call(
@@ -309,36 +343,37 @@
             )
         elif section > 0:
             upstream, grad, message, *outs = call(
-                functools.partial(close_step_kernel, phases),
-                [picks, total, *arrived, layer_here, mixing],
-                [whole, whole, whole] + sent, cost, 1,
+                functools.partial(close_step_kernel, count),
+                [mask, total, *arrived, layer_here, mixing],
+                [whole, whole, whole] + sent, cost,
             )
             results[section + 1] = upstream
         else:
-            got = fetch_home(grads, arrived)
-            upstream, grad, product, message, *outs = call(
-                functools.partial(bottom_kernel, phases, top),
-                [picks, total, *arrived, features, grads[top], got, layer_here, mixing],
-                [whole, whole, ((width, width), BF16), whole] + sent,
-                cost + 2 * total_rows * width * width, 1,
+            upstream, product, total, *outs = call(
+                functools.partial(bottom_kernel, count, top),
+                [mask, total, *arrived, turned, grads[top], fetch_home(grads), layer_here, mixing],
+                [whole, ((width, width), BF16), ((total_rows, width), F32)] + sent,
+                cost + 2 * total_rows * width * (width + nodes),
+                scratch=[pltpu.VMEM(*whole), pltpu.VMEM(*whole)],
             )
             results[1] = upstream
-        grads[section] = grad
         arrived = exchange(outs, lead)
-        total = inner(upstream, message, mixing)
+        if section > 0:
+            grads[section] = grad
+            total = inner(upstream, message, mixing)
 
     tiles = rows * columns
     pieces = lax.all_to_all(
         product.reshape(tiles, width // tiles, width), ("tx", "ty"), 0, 0, tiled=True
     )
-    got = fetch_home(results, arrived)
     result = call(
-        functools.partial(last_kernel, phases, top),
-        [picks, total, *arrived, results[top], got], [whole], 0, 1, jax.ShapeDtypeStruct,
+        functools.partial(last_kernel, top),
+        [mask, total, *arrived, results[top], fetch_home(results)], [whole], 0,
+        jax.ShapeDtypeStruct,
     )[0]
     scale = 1.0 / math.sqrt(total_rows * tiles)
     summed = call(
-        functools.partial(reduce_kernel, scale), [pieces], [((width // tiles, width), F32)], 0, 0,
+        functools.partial(reduce_kernel, scale), [pieces], [((width // tiles, width), F32)], 0,
         jax.ShapeDtypeStruct,
     )[0]
     return (summed[None], result.reshape(1, batches, 1, 1, nodes, width))

time: 107 us -> 85.8 us (0.80)
  waiting for transfers between devices: 53.9 us -> 38.2 us
  local copies, waits for them, and re-layouts: 7.24 us -> 2.24 us
  Pallas kernels: 11.4 us -> 9.48 us
  starting transfers between devices: 31.5 us -> 33.2 us
    ppermute x12, waiting for transfers between devices: 21.1 us -> 9.23 us  [exchange(): lax.ppermute(out, AXES, route[lead])]
    unnamed x36 -> x14, local copies, waits for them, and re-layouts: 7.24 us -> 2.24 us
    ppermute x4, waiting for transfers between devices: 32.8 us -> 29 us  [to_sections(): return lax.ppermute(value, AXES, pairs)]
    pallas_call x11 -> x13, Pallas kernels: 11.4 us -> 9.48 us  [call(): pl.pallas_call(body, out_shape=[kind(shape, dtype) for shape, dtype in ou...]
    all_to_all x1, starting transfers between devices: 6.74 us -> 8.2 us  [per_device(): lax.all_to_all(product.reshape(tiles, width // tiles, width), ('tx', 'ty'...]
where the time goes in v3:
time: 85.8 us; the launch traced here: 84.2 us
  waiting for transfers between devices  38.2 us (45%)
  starting transfers between devices  33.2 us (39%)
  Pallas kernels  9.48 us (11%)
  local copies, waits for them, and re-layouts  2.24 us (3%)
  between operations  0.96 us (1%)
    ppermute x4, waiting for transfers between devices, to_sections(): return lax.ppermute(value, AXES, pairs)  29 us
    ppermute x12, starting transfers between devices, exchange(): lax.ppermute(out, AXES, route[lead])  19.6 us
    pallas_call x13, Pallas kernels, call(): pl.pallas_call(body, out_shape=[kind(shape, dtype) for shape, dtype in ou...  9.48 us
    ppermute x12, waiting for transfers between devices, exchange(): lax.ppermute(out, AXES, route[lead])  9.23 us
    all_to_all x1, starting transfers between devices, per_device(): lax.all_to_all(product.reshape(tiles, width // tiles, width), ('tx', 'ty'...  8.2 us
    ppermute x4, starting transfers between devices, to_sections(): return lax.ppermute(value, AXES, pairs)  5.49 us
    unnamed x14, local copies, waits for them, and re-layouts  2.24 us
  transfers between devices with their start and end apart: 17, of which 6 were waited for; matrix products, arithmetic and copies ran while one was open for 0% of the time, Pallas kernels for 3%

profile of v3, /device:TPU:0, one launch (start us, length us, event | category | flops | bytes accessed | tf_op | source)
XLA Modules:
  0.0 84.2 jit_solution(14781148151930669828)
XLA Ops:
  0.6 2.8 %shard_map.86 = (bf16[2,512,512]{2,1,0:T(8,128)(2,1)S(1)}, bf16[2,640,256]{2,1,0:T(8,128)(2,1)S(1)}, f32[12,1,512]{2,1,0:T(1,128)S(1)}, bf16[512,512]{1,0:T(8,12...) custom-call(bf16[512,512]{1,0:T(8,128)(2,1)} %bitcast.12, ...), custom_call_target="tpu_custom_call" | custom-call | flops 738197504 | bytes 5922944 | tf_op jit(solution)/shard_map/pallas_call | solution.py:219
  3.5 1.3 %collective-permute-start.3 = (bf16[2,512,512]{2,1,0:T(8,128)(2,1)S(1)}, bf16[2,512,512]{2,1,0:T(8,128)(2,1)S(1)}, u32[]{:S(2)}, u32[]{:S(2)}) collective-permute-start(bf16[2,512,512]{2,1,0:T(8,128)(2,1)S(1)} %get-tuple-element.33.refs_6_), channel_id=1, source_target_pairs={{16,24},{17,25},{18,26},{19,27},{20,28},{21,29},{22,30},{23,31},{8... | collective-permute-start | bytes 3145736 | tf_op jit(solution)/shard_map/ppermute | solution.py:247
  4.8 0.7 collective-permute-start
  5.4 0.7 collective-permute-start.1
  6.1 0.7 collective-permute-start.2
  7.2 0.9 %collective-permute-done.3.refs_3_.layer_ref = bf16[2,512,512]{2,1,0:T(8,128)(2,1)S(1)} collective-permute-done((bf16[2,512,512]{2,1,0:T(8,128)(2,1)S(1)}, bf16[2,512,512]{2,1,0:T(8,128)(2,1)S(1)}, u32[]{:S(2)}, u32[]{:S(2)}) %collective-permute-start.3) | collective-permute-done | bytes 1048608 | tf_op jit(solution)/shard_map/ppermute | solution.py:247
  8.0 0.9 %shard_map.88 = (bf16[512,512]{1,0:T(8,128)(2,1)S(1)}, bf16[512,512]{1,0:T(8,128)(2,1)S(1)}, bf16[512,512]{1,0:T(8,128)(2,1)S(1)}, bf16[2,128,512]{2,1,0:T(8,128...) custom-call(f32[12,1,512]{2,1,0:T(1,128)S(1)} %get-tuple-element.27.mask_ref, ...), custom_call_target="tpu_custom_call" | custom-call | flops 469762048 | bytes 5922816 | tf_op jit(solution)/shard_map/pallas_call | solution.py:219
  8.9 0.7 collective-permute-start.4
  9.6 0.7 collective-permute-start.5
  10.3 0.7 collective-permute-start.6
  11.3 0.4 shard_map.90.top_ref
  11.7 1.3 %collective-permute-start.7 = (bf16[512,512]{1,0:T(8,128)(2,1)S(1)}, bf16[512,512]{1,0:T(8,128)(2,1)S(1)}, u32[]{:S(2)}, u32[]{:S(2)}) collective-permute-start(bf16[512,512]{1,0:T(8,128)(2,1)S(1)} %shard_map.90.top_ref), channel_id=1, source_target_pairs={{24,0},{25,1},{26,2},{27,3},{28,4},{29,5},{30,6},{31,7}} | collective-permute-start | bytes 1572872 | tf_op jit(solution)/shard_map/ppermute | solution.py:247
  13.0 28.2 %collective-permute-done.7.upstream_ref = bf16[512,512]{1,0:T(8,128)(2,1)S(1)} collective-permute-done((bf16[512,512]{1,0:T(8,128)(2,1)S(1)}, bf16[512,512]{1,0:T(8,128)(2,1)S(1)}, u32[]{:S(2)}, u32[]{:S(2)}) %collective-permute-start.7) | collective-permute-done | bytes 524320 | tf_op jit(solution)/shard_map/ppermute | solution.py:247
  41.1 0.8 shard_map.91
  42.0 1.5 %collective-permute-start.11 = (bf16[512,512]{1,0:T(8,128)(2,1)S(1)}, bf16[512,512]{1,0:T(8,128)(2,1)S(1)}, u32[]{:S(2)}, u32[]{:S(2)}) collective-permute-start(bf16[512,512]{1,0:T(8,128)(2,1)S(1)} %shard_map.94), channel_id=1, source_target_pairs={{24,16},{25,17},{26,18},{27,19},{28,20},{29,21},{30,22},{31,23},{0... | collective-permute-start | bytes 1572872 | tf_op jit(solution)/shard_map/ppermute | solution.py:247
  43.4 3.4 %collective-permute-start.8 = (bf16[2,128,512]{2,1,0:T(8,128)(2,1)S(1)}, bf16[2,128,512]{2,1,0:T(8,128)(2,1)S(1)}, u32[]{:S(2)}, u32[]{:S(2)}) collective-permute-start(bf16[2,128,512]{2,1,0:T(8,128)(2,1)S(1)} %get-tuple-element.40), channel_id=1, source_target_pairs={{0,2},{1,3},{2,0},{3,1},{4,6},{5,7},{6,4},{7,5}} | collective-permute-start | bytes 786440 | tf_op jit(solution)/shard_map/ppermute | solution.py:279
  46.9 0.7 collective-permute-start.9
  47.6 3.4 %collective-permute-start.10 = (bf16[2,128,512]{2,1,0:T(8,128)(2,1)S(1)}, bf16[2,128,512]{2,1,0:T(8,128)(2,1)S(1)}, u32[]{:S(2)}, u32[]{:S(2)}) collective-permute-start(bf16[2,128,512]{2,1,0:T(8,128)(2,1)S(1)} %get-tuple-element.42), channel_id=1, source_target_pairs={{0,1},{2,3},{4,5},{6,7},{1,0},{3,2},{5,4},{7,6}} | collective-permute-start | bytes 786440 | tf_op jit(solution)/shard_map/ppermute | solution.py:279
  51.7 4.1 %collective-permute-done.10.refs_2_ = bf16[2,128,512]{2,1,0:T(8,128)(2,1)S(1)} collective-permute-done((bf16[2,128,512]{2,1,0:T(8,128)(2,1)S(1)}, bf16[2,128,512]{2,1,0:T(8,128)(2,1)S(1)}, u32[]{:S(2)}, u32[]{:S(2)}) %collective-permute-start.10) | collective-permute-done | bytes 262176 | tf_op jit(solution)/shard_map/ppermute | solution.py:279
  55.8 1.6 %shard_map.95 = (bf16[512,512]{1,0:T(8,128)(2,1)S(1)}, bf16[512,512]{1,0:T(8,128)(2,1)S(1)}, f32[512,512]{1,0:T(8,128)S(1)}, bf16[2,128,512]{2,1,0:T(8,128)(2,1)...) custom-call(f32[12,1,512]{2,1,0:T(1,128)S(1)} %get-tuple-element.27.mask_ref, ...), custom_call_target="tpu_custom_call" | custom-call | flops 872415232 | bytes 8019968 | tf_op jit(solution)/shard_map/pallas_call | solution.py:219
  57.5 0.7 copy-done.3
  58.2 0.7 copy-done.5
  58.9 0.8 copy-done.1
  59.7 8.2 %all-to-all-start = ((bf16[8,64,512]{2,1,0:T(8,128)(2,1)}), bf16[8,64,512]{2,1,0:T(8,128)(2,1)S(1)}, u32[]{:S(2)}, u32[]{:S(2)}) async-start(bf16[8,64,512]{2,1,0:T(8,128)(2,1)} %bitcast.14), calls=%async_computation | async-start | bytes 1048576 | tf_op jit(solution)/shard_map/all_to_all | solution.py:366
  68.0 1.5 %collective-permute-start.15 = (bf16[512,512]{1,0:T(8,128)(2,1)S(1)}, bf16[512,512]{1,0:T(8,128)(2,1)S(1)}, u32[]{:S(2)}, u32[]{:S(2)}) collective-permute-start(bf16[512,512]{1,0:T(8,128)(2,1)S(1)} %shard_map.97), channel_id=1, source_target_pairs={{24,16},{25,17},{26,18},{27,19},{28,20},{29,21},{30,22},{31,23},{0... | collective-permute-start | bytes 1572872 | tf_op jit(solution)/shard_map/ppermute | solution.py:247
  69.4 3.9 %collective-permute-start.12 = (bf16[2,128,512]{2,1,0:T(8,128)(2,1)S(1)}, bf16[2,128,512]{2,1,0:T(8,128)(2,1)S(1)}, u32[]{:S(2)}, u32[]{:S(2)}) collective-permute-start(bf16[2,128,512]{2,1,0:T(8,128)(2,1)S(1)} %copy-done.6), channel_id=1, source_target_pairs={{0,2},{1,3},{2,0},{3,1},{4,6},{5,7},{6,4},{7,5}} | collective-permute-start | bytes 786440 | tf_op jit(solution)/shard_map/ppermute | solution.py:279
  73.3 0.7 collective-permute-start.13
  74.0 3.4 %collective-permute-start.14 = (bf16[2,128,512]{2,1,0:T(8,128)(2,1)S(1)}, bf16[2,128,512]{2,1,0:T(8,128)(2,1)S(1)}, u32[]{:S(2)}, u32[]{:S(2)}) collective-permute-start(bf16[2,128,512]{2,1,0:T(8,128)(2,1)S(1)} %get-tuple-element.50), channel_id=1, source_target_pairs={{0,1},{2,3},{4,5},{6,7},{1,0},{3,2},{5,4},{7,6}} | collective-permute-start | bytes 786440 | tf_op jit(solution)/shard_map/ppermute | solution.py:279
  77.4 2.2 %collective-permute-done.12.refs_0_ = bf16[2,128,512]{2,1,0:T(8,128)(2,1)S(1)} collective-permute-done((bf16[2,128,512]{2,1,0:T(8,128)(2,1)S(1)}, bf16[2,128,512]{2,1,0:T(8,128)(2,1)S(1)}, u32[]{:S(2)}, u32[]{:S(2)}) %collective-permute-start.12) | collective-permute-done | bytes 262176 | tf_op jit(solution)/shard_map/ppermute | solution.py:279
  79.6 2.7 %collective-permute-done.14.refs_2_ = bf16[2,128,512]{2,1,0:T(8,128)(2,1)S(1)} collective-permute-done((bf16[2,128,512]{2,1,0:T(8,128)(2,1)S(1)}, bf16[2,128,512]{2,1,0:T(8,128)(2,1)S(1)}, u32[]{:S(2)}, u32[]{:S(2)}) %collective-permute-start.14) | collective-permute-done | bytes 262176 | tf_op jit(solution)/shard_map/ppermute | solution.py:279
  82.3 1.1 %shard_map.98 = bf16[512,512]{1,0:T(8,128)(2,1)} custom-call(f32[12,1,512]{2,1,0:T(1,128)S(1)} %get-tuple-element.27.mask_ref, f32[512,512]{1,0:T(8,128)S(1)} %get-tuple-element.47.total_ref, bf16[2,128,512]{2,1,0:T(8,128)(2,1)S(1)} %collective-permute-done.12.refs_0_, bf16[2,128,512]{2,1,0:T(8,128)(2,1)S(1)} %collective-permute-done.13.refs_1_, ...), custom_call_target="tpu_custom_call" | custom-call | bytes 3432448 | tf_op jit(solution)/shard_map/pallas_call | solution.py:219
  83.4 0.7 shard_map.96
  (29 shorter events, 1.4 us)
Async XLA Ops:
  0.6 6.2 %copy-start.2 = (bf16[2,1,1,256,512]{4,3,2,1,0:T(8,128)(2,1)S(1)}, bf16[2,1,1,256,512]{4,3,2,1,0:T(8,128)(2,1)}, u32[]{:S(2)}) copy-start(bf16[2,1,1,256,512]{4,3,2,1,0:T(8,128)(2,1)} %param.8) | copy-start | bytes 1572868
  3.5 4.6 %collective-permute-start.3 = (bf16[2,512,512]{2,1,0:T(8,128)(2,1)S(1)}, bf16[2,512,512]{2,1,0:T(8,128)(2,1)S(1)}, u32[]{:S(2)}, u32[]{:S(2)}) collective-permute-start(bf16[2,512,512]{2,1,0:T(8,128)(2,1)S(1)} %get-tuple-element.33.refs_6_), channel_id=1, source_target_pairs={{16,24},{17,25},{18,26},{19,27},{20,28},{21,29},{22,30},{23,31},{8... | collective-permute-start | bytes 3145736 | tf_op jit(solution)/shard_map/ppermute | solution.py:247
  4.8 2.4 %collective-permute-start = (bf16[2,128,512]{2,1,0:T(8,128)(2,1)S(1)}, bf16[2,128,512]{2,1,0:T(8,128)(2,1)S(1)}, u32[]{:S(2)}, u32[]{:S(2)}) collective-permute-start(bf16[2,128,512]{2,1,0:T(8,128)(2,1)S(1)} %get-tuple-element.30), channel_id=1, source_target_pairs={{24,26},{25,27},{26,24},{27,25},{28,30},{29,31},{30,28},{31,29}} | collective-permute-start | bytes 786440 | tf_op jit(solution)/shard_map/ppermute | solution.py:279
  5.4 1.7 %collective-permute-start.1 = (bf16[2,128,512]{2,1,0:T(8,128)(2,1)S(1)}, bf16[2,128,512]{2,1,0:T(8,128)(2,1)S(1)}, u32[]{:S(2)}, u32[]{:S(2)}) collective-permute-start(bf16[2,128,512]{2,1,0:T(8,128)(2,1)S(1)} %get-tuple-element.31), channel_id=1, source_target_pairs={{26,28},{27,29},{28,26},{29,27}} | collective-permute-start | bytes 786440 | tf_op jit(solution)/shard_map/ppermute | solution.py:279
  6.1 1.0 %collective-permute-start.2 = (bf16[2,128,512]{2,1,0:T(8,128)(2,1)S(1)}, bf16[2,128,512]{2,1,0:T(8,128)(2,1)S(1)}, u32[]{:S(2)}, u32[]{:S(2)}) collective-permute-start(bf16[2,128,512]{2,1,0:T(8,128)(2,1)S(1)} %get-tuple-element.32), channel_id=1, source_target_pairs={{24,25},{26,27},{28,29},{30,31},{25,24},{27,26},{29,28},{31,30}} | collective-permute-start | bytes 786440 | tf_op jit(solution)/shard_map/ppermute | solution.py:279
  8.9 2.4 %collective-permute-start.4 = (bf16[2,128,512]{2,1,0:T(8,128)(2,1)S(1)}, bf16[2,128,512]{2,1,0:T(8,128)(2,1)S(1)}, u32[]{:S(2)}, u32[]{:S(2)}) collective-permute-start(bf16[2,128,512]{2,1,0:T(8,128)(2,1)S(1)} %get-tuple-element.36), channel_id=1, source_target_pairs={{24,26},{25,27},{26,24},{27,25},{28,30},{29,31},{30,28},{31,29}} | collective-permute-start | bytes 786440 | tf_op jit(solution)/shard_map/ppermute | solution.py:279
  9.6 1.7 %collective-permute-start.5 = (bf16[2,128,512]{2,1,0:T(8,128)(2,1)S(1)}, bf16[2,128,512]{2,1,0:T(8,128)(2,1)S(1)}, u32[]{:S(2)}, u32[]{:S(2)}) collective-permute-start(bf16[2,128,512]{2,1,0:T(8,128)(2,1)S(1)} %get-tuple-element.37), channel_id=1, source_target_pairs={{26,28},{27,29},{28,26},{29,27}} | collective-permute-start | bytes 786440 | tf_op jit(solution)/shard_map/ppermute | solution.py:279
  10.3 1.0 %collective-permute-start.6 = (bf16[2,128,512]{2,1,0:T(8,128)(2,1)S(1)}, bf16[2,128,512]{2,1,0:T(8,128)(2,1)S(1)}, u32[]{:S(2)}, u32[]{:S(2)}) collective-permute-start(bf16[2,128,512]{2,1,0:T(8,128)(2,1)S(1)} %get-tuple-element.38), channel_id=1, source_target_pairs={{24,25},{26,27},{28,29},{30,31},{25,24},{27,26},{29,28},{31,30}} | collective-permute-start | bytes 786440 | tf_op jit(solution)/shard_map/ppermute | solution.py:279
  11.7 29.5 %collective-permute-start.7 = (bf16[512,512]{1,0:T(8,128)(2,1)S(1)}, bf16[512,512]{1,0:T(8,128)(2,1)S(1)}, u32[]{:S(2)}, u32[]{:S(2)}) collective-permute-start(bf16[512,512]{1,0:T(8,128)(2,1)S(1)} %shard_map.90.top_ref), channel_id=1, source_target_pairs={{24,0},{25,1},{26,2},{27,3},{28,4},{29,5},{30,6},{31,7}} | collective-permute-start | bytes 1572872 | tf_op jit(solution)/shard_map/ppermute | solution.py:247
  41.9 9.1 %copy-start = (bf16[1,2,1,1,256,512]{5,4,3,2,1,0:T(8,128)(2,1)S(1)}, bf16[1,2,1,1,256,512]{5,4,3,2,1,0:T(8,128)(2,1)}, u32[]{:S(2)}) copy-start(bf16[1,2,1,1,256,512]{5,4,3,2,1,0:T(8,128)(2,1)} %param.7) | copy-start | bytes 1572868
  42.0 13.9 %collective-permute-start.11 = (bf16[512,512]{1,0:T(8,128)(2,1)S(1)}, bf16[512,512]{1,0:T(8,128)(2,1)S(1)}, u32[]{:S(2)}, u32[]{:S(2)}) collective-permute-start(bf16[512,512]{1,0:T(8,128)(2,1)S(1)} %shard_map.94), channel_id=1, source_target_pairs={{24,16},{25,17},{26,18},{27,19},{28,20},{29,21},{30,22},{31,23},{0... | collective-permute-start | bytes 1572872 | tf_op jit(solution)/shard_map/ppermute | solution.py:247
  43.4 8.3 %collective-permute-start.8 = (bf16[2,128,512]{2,1,0:T(8,128)(2,1)S(1)}, bf16[2,128,512]{2,1,0:T(8,128)(2,1)S(1)}, u32[]{:S(2)}, u32[]{:S(2)}) collective-permute-start(bf16[2,128,512]{2,1,0:T(8,128)(2,1)S(1)} %get-tuple-element.40), channel_id=1, source_target_pairs={{0,2},{1,3},{2,0},{3,1},{4,6},{5,7},{6,4},{7,5}} | collective-permute-start | bytes 786440 | tf_op jit(solution)/shard_map/ppermute | solution.py:279
  46.9 4.8 %collective-permute-start.9 = (bf16[2,128,512]{2,1,0:T(8,128)(2,1)S(1)}, bf16[2,128,512]{2,1,0:T(8,128)(2,1)S(1)}, u32[]{:S(2)}, u32[]{:S(2)}) collective-permute-start(bf16[2,128,512]{2,1,0:T(8,128)(2,1)S(1)} %get-tuple-element.41), channel_id=1, source_target_pairs={{2,4},{3,5},{4,2},{5,3}} | collective-permute-start | bytes 786440 | tf_op jit(solution)/shard_map/ppermute | solution.py:279
  47.6 8.3 %collective-permute-start.10 = (bf16[2,128,512]{2,1,0:T(8,128)(2,1)S(1)}, bf16[2,128,512]{2,1,0:T(8,128)(2,1)S(1)}, u32[]{:S(2)}, u32[]{:S(2)}) collective-permute-start(bf16[2,128,512]{2,1,0:T(8,128)(2,1)S(1)} %get-tuple-element.42), channel_id=1, source_target_pairs={{0,1},{2,3},{4,5},{6,7},{1,0},{3,2},{5,4},{7,6}} | collective-permute-start | bytes 786440 | tf_op jit(solution)/shard_map/ppermute | solution.py:279
  57.5 0.7 copy-start.3
  58.2 0.7 copy-start.5
  58.9 0.8 copy-start.1
  59.7 23.7 %all-to-all-start = ((bf16[8,64,512]{2,1,0:T(8,128)(2,1)}), bf16[8,64,512]{2,1,0:T(8,128)(2,1)S(1)}, u32[]{:S(2)}, u32[]{:S(2)}) async-start(bf16[8,64,512]{2,1,0:T(8,128)(2,1)} %bitcast.14), calls=%async_computation | async-start | bytes 1048576 | tf_op jit(solution)/shard_map/all_to_all | solution.py:366
  67.9 1.5 %copy-start.6 = (bf16[2,128,512]{2,1,0:T(8,128)(2,1)S(1)}, bf16[2,128,512]{2,1,0:T(8,128)(2,1)}, u32[]{:S(2)}) copy-start(bf16[2,128,512]{2,1,0:T(8,128)(2,1)} %copy-done.5) | copy-start | bytes 786436
  67.9 5.5 %copy-start.4 = (bf16[2,128,512]{2,1,0:T(8,128)(2,1)S(1)}, bf16[2,128,512]{2,1,0:T(8,128)(2,1)}, u32[]{:S(2)}) copy-start(bf16[2,128,512]{2,1,0:T(8,128)(2,1)} %copy-done.3) | copy-start | bytes 786436
  68.0 14.3 %collective-permute-start.15 = (bf16[512,512]{1,0:T(8,128)(2,1)S(1)}, bf16[512,512]{1,0:T(8,128)(2,1)S(1)}, u32[]{:S(2)}, u32[]{:S(2)}) collective-permute-start(bf16[512,512]{1,0:T(8,128)(2,1)S(1)} %shard_map.97), channel_id=1, source_target_pairs={{24,16},{25,17},{26,18},{27,19},{28,20},{29,21},{30,22},{31,23},{0... | collective-permute-start | bytes 1572872 | tf_op jit(solution)/shard_map/ppermute | solution.py:247
  69.4 10.1 %collective-permute-start.12 = (bf16[2,128,512]{2,1,0:T(8,128)(2,1)S(1)}, bf16[2,128,512]{2,1,0:T(8,128)(2,1)S(1)}, u32[]{:S(2)}, u32[]{:S(2)}) collective-permute-start(bf16[2,128,512]{2,1,0:T(8,128)(2,1)S(1)} %copy-done.6), channel_id=1, source_target_pairs={{0,2},{1,3},{2,0},{3,1},{4,6},{5,7},{6,4},{7,5}} | collective-permute-start | bytes 786440 | tf_op jit(solution)/shard_map/ppermute | solution.py:279
  73.3 6.2 %collective-permute-start.13 = (bf16[2,128,512]{2,1,0:T(8,128)(2,1)S(1)}, bf16[2,128,512]{2,1,0:T(8,128)(2,1)S(1)}, u32[]{:S(2)}, u32[]{:S(2)}) collective-permute-start(bf16[2,128,512]{2,1,0:T(8,128)(2,1)S(1)} %copy-done.4), channel_id=1, source_target_pairs={{2,4},{3,5},{4,2},{5,3}} | collective-permute-start | bytes 786440 | tf_op jit(solution)/shard_map/ppermute | solution.py:279
  74.0 8.3 %collective-permute-start.14 = (bf16[2,128,512]{2,1,0:T(8,128)(2,1)S(1)}, bf16[2,128,512]{2,1,0:T(8,128)(2,1)S(1)}, u32[]{:S(2)}, u32[]{:S(2)}) collective-permute-start(bf16[2,128,512]{2,1,0:T(8,128)(2,1)S(1)} %get-tuple-element.50), channel_id=1, source_target_pairs={{0,1},{2,3},{4,5},{6,7},{1,0},{3,2},{5,4},{7,6}} | collective-permute-start | bytes 786440 | tf_op jit(solution)/shard_map/ppermute | solution.py:279

commit v4 on v3

--- a/solution.py
+++ b/solution.py
@@ -144,10 +144,14 @@
     close_blocks(mask_ref, total_ref, refs[:-1], refs[-1])
 
 
-def last_kernel(top, mask_ref, total_ref, *refs):
-    arrived_refs = refs[:-3]
-    top_ref, got_ref, result_ref = refs[-3:]
+def last_kernel(top, count, scale, mask_ref, total_ref, *refs):
+    arrived_refs = refs[:count]
+    top_ref, got_ref = refs[count : count + 2]
+    result_ref = refs[-1]
     here = lax.axis_index("pipe")
+    if scale is not None:
+        kept_ref, piece_ref, result_ref, sum_ref = refs[count + 2 :]
+        sum_ref[...] = (kept_ref[...] + piece_ref[...].astype(F32)) * scale
 
     @pl.when(here == 0)
     def _():
@@ -178,7 +182,7 @@
     here = lax.axis_index("pipe")
 
     def product(ref):
-        product_ref[...] = rows_dot(turned_ref[...], ref[...]).astype(BF16)
+        product_ref[...] = rows_dot(turned_ref[...], ref[...])
 
     @pl.when(here == 0)
     def _():
@@ -193,24 +197,40 @@
         product(got_ref)
 
 
-def bottom_kernel(count, top, mask_ref, total_ref, *refs):
+def split_halves(step, product_ref, sent_ref, kept_ref):
+    axis, distance, groups = step
+    size = kept_ref.shape[0] // groups
+    place = lax.rem(lax.axis_index(axis) // distance, 2)
+    for group in range(groups):
+        start = 2 * group * size
+        rows = slice(group * size, (group + 1) * size)
+        kept = pl.ds(pl.multiple_of(start + place * size, size), size)
+        sent = pl.ds(pl.multiple_of(start + (1 - place) * size, size), size)
+        kept_ref[rows] = product_ref[kept]
+        sent_ref[rows] = product_ref[sent].astype(BF16)
+
+
+def halve_kernel(step, kept_ref, got_ref, sent_ref, next_ref, sum_ref):
+    sum_ref[...] = kept_ref[...] + got_ref[...].astype(F32)
+    split_halves(step, sum_ref, sent_ref, next_ref)
+
+
+def bottom_kernel(count, top, step, mask_ref, total_ref, *refs):
     turned_ref, top_ref, got_ref, layer_ref, mixing_ref = refs[count : count + 5]
-    result_ref, product_ref, next_ref = refs[count + 5 : count + 8]
-    out_refs = refs[count + 8 : -2]
+    result_ref, next_ref = refs[count + 5 : count + 7]
+    out_refs = refs[count + 7 : 2 * count + 7]
     grad_ref, message_ref = refs[-2:]
     close_step_kernel(
         count, mask_ref, total_ref, *refs[:count], layer_ref, mixing_ref,
         result_ref, grad_ref, message_ref, *out_refs
     )
-    weight_product(top, turned_ref, grad_ref, top_ref, got_ref, product_ref)
+    if step is None:
+        weight_product(top, turned_ref, grad_ref, top_ref, got_ref, refs[2 * count + 7])
+    else:
+        sent_ref, kept_ref, product_ref = refs[2 * count + 7 : -2]
+        weight_product(top, turned_ref, grad_ref, top_ref, got_ref, product_ref)
+        split_halves(step, product_ref, sent_ref, kept_ref)
     inner_kernel(result_ref, message_ref, mixing_ref, next_ref)
-
-
-def reduce_kernel(scale, pieces_ref, sum_ref):
-    value = pieces_ref[0].astype(F32)
-    for index in range(1, pieces_ref.shape[0]):
-        value = value + pieces_ref[index].astype(F32)
-    sum_ref[...] = value * scale
 
 
 def call(body, inputs, outputs, flops, kind=pltpu.VMEM, source=IN_VMEM, scratch=()):
@@ -270,6 +290,19 @@
                 ]
             routes.append(route)
     phases = tuple(phases)
+    splits, left = [], rows * columns
+    if left & (left - 1) == 0 and width // left % 16 == 0:
+        for axis, count, other in (("ty", columns, rows), ("tx", rows, 1)):
+            distance = count // 2
+            while distance > 0:
+                pairs = [
+                    (flat(p, x, y), flat(p, x, y ^ distance) if axis == "ty" else flat(p, x ^ distance, y))
+                    for p in range(sections)
+                    for x in range(rows)
+                    for y in range(columns)
+                ]
+                splits.append(((axis, distance, other), pairs))
+                distance //= 2
     sent = [((batches, block, width), BF16)] * len(phases)
     whole = ((total_rows, width), BF16)
     mix_rows = (blocks + len(phases)) * block
@@ -349,33 +382,45 @@
             )
             results[section + 1] = upstream
         else:
-            upstream, product, total, *outs = call(
-                functools.partial(bottom_kernel, count, top),
+            product = ((width, width), F32)
+            halves = [((width // 2, width), BF16), ((width // 2, width), F32)] if splits else [product]
+            upstream, total, *outs = call(
+                functools.partial(bottom_kernel, count, top, splits[0][0] if splits else None),
                 [mask, total, *arrived, turned, grads[top], fetch_home(grads), layer_here, mixing],
-                [whole, ((width, width), BF16), ((total_rows, width), F32)] + sent,
+                [whole, ((total_rows, width), F32)] + sent + halves,
                 cost + 2 * total_rows * width * (width + nodes),
-                scratch=[pltpu.VMEM(*whole), pltpu.VMEM(*whole)],
+                scratch=[pltpu.VMEM(*product)] * len(splits[:1]) + [pltpu.VMEM(*whole)] * 2,
             )
+            outs, pieces = outs[:count], outs[count:]
             results[1] = upstream
         arrived = exchange(outs, lead)
         if section > 0:
             grads[section] = grad
             total = inner(upstream, message, mixing)
 
-    tiles = rows * columns
-    pieces = lax.all_to_all(
-        product.reshape(tiles, width // tiles, width), ("tx", "ty"), 0, 0, tiled=True
-    )
-    result = call(
-        functools.partial(last_kernel, top),
-        [mask, total, *arrived, results[top], fetch_home(results)], [whole], 0,
-        jax.ShapeDtypeStruct,
-    )[0]
-    scale = 1.0 / math.sqrt(total_rows * tiles)
-    summed = call(
-        functools.partial(reduce_kernel, scale), [pieces], [((width // tiles, width), F32)], 0,
-        jax.ShapeDtypeStruct,
-    )[0]
+    scale = 1.0 / math.sqrt(total_rows * rows * columns)
+    if splits:
+        parcel, kept = pieces
+        for (_, pairs), following in zip(splits, splits[1:]):
+            got = lax.ppermute(parcel, AXES, pairs)
+            half = (kept.shape[0] // 2, width)
+            parcel, kept = call(
+                functools.partial(halve_kernel, following[0]), [kept, got],
+                [(half, BF16), (half, F32)], 0, scratch=[pltpu.VMEM(kept.shape, F32)],
+            )
+        got = lax.ppermute(parcel, AXES, splits[-1][1])
+        result, summed = call(
+            functools.partial(last_kernel, top, count, scale),
+            [mask, total, *arrived, results[top], fetch_home(results), kept, got],
+            [whole, (kept.shape, F32)], 0, jax.ShapeDtypeStruct,
+        )
+    else:
+        summed = scale * lax.psum_scatter(pieces[0], ("tx", "ty"), scatter_dimension=0, tiled=True)
+        result = call(
+            functools.partial(last_kernel, top, count, None),
+            [mask, total, *arrived, results[top], fetch_home(results)], [whole], 0,
+            jax.ShapeDtypeStruct,
+        )[0]
     return (summed[None], result.reshape(1, batches, 1, 1, nodes, width))
 
 

time: 85.8 us -> 80.8 us (0.942); the launches traced: 84.2 us -> 80.4 us
  starting transfers between devices: 33.2 us -> 30.9 us
  local copies, waits for them, and re-layouts: 2.24 us -> 0.01 us
  waiting for transfers between devices: 38.2 us -> 39.5 us
    all_to_all x1 -> x0, starting transfers between devices: 8.2 us -> none  [per_device(): lax.all_to_all(product.reshape(tiles, width // tiles, width), ('tx', 'ty'...]
    ppermute x0 -> x3, starting transfers between devices: none -> 6.74 us  [the longest x2 4.35 us: per_device(): got = lax.ppermute(parcel, AXES, pairs)]
    ppermute x0 -> x3, waiting for transfers between devices: none -> 5.4 us  [the longest x2 3.16 us: per_device(): got = lax.ppermute(parcel, AXES, pairs)]
    ppermute x12, waiting for transfers between devices: 9.23 us -> 5.14 us  [exchange(): lax.ppermute(out, AXES, route[lead])]
    unnamed x14 -> x4, local copies, waits for them, and re-layouts: 2.24 us -> 0.01 us
    pallas_call x13 -> x14, Pallas kernels: 9.48 us -> 9.03 us  [call(): pl.pallas_call(body, out_shape=[kind(shape, dtype) for shape, dtype in ou...]
  transfers between devices with their start and end apart: 17 -> 19, of which waited for: 6 -> 6; matrix products, arithmetic and copies ran while one was open for 0% -> 0% of each run, Pallas kernels for 3% -> 2%
where the time goes in v4:
time: 80.8 us; the launch traced here: 80.4 us
  waiting for transfers between devices  39.5 us (49%)
  starting transfers between devices  30.9 us (38%)
  Pallas kernels  9.03 us (11%)
  between operations  0.94 us (1%)
    ppermute x4, waiting for transfers between devices, to_sections(): return lax.ppermute(value, AXES, pairs)  29 us
    ppermute x12, starting transfers between devices, exchange(): lax.ppermute(out, AXES, route[lead])  18.8 us
    pallas_call x14, Pallas kernels, call(): pl.pallas_call(body, out_shape=[kind(shape, dtype) for shape, dtype in ou...  9.03 us
    ppermute x4, starting transfers between devices, to_sections(): return lax.ppermute(value, AXES, pairs)  5.36 us
    ppermute x12, waiting for transfers between devices, exchange(): lax.ppermute(out, AXES, route[lead])  5.14 us
    ppermute x2, starting transfers between devices, per_device(): got = lax.ppermute(parcel, AXES, pairs)  4.35 us
    ppermute x2, waiting for transfers between devices, per_device(): got = lax.ppermute(parcel, AXES, pairs)  3.16 us
    ppermute x1, starting transfers between devices, per_device(): got = lax.ppermute(parcel, AXES, splits[-1][1])  2.39 us
  transfers between devices with their start and end apart: 19, of which 6 were waited for; matrix products, arithmetic and copies ran while one was open for 0% of the time, Pallas kernels for 2%

profile of v4, /device:TPU:0, one launch (start us, length us, event | category | flops | bytes accessed | tf_op | source)
XLA Modules:
  0.0 80.4 jit_solution(6759797303373181146)
XLA Ops:
  0.6 2.8 %shard_map.86 = (bf16[2,512,512]{2,1,0:T(8,128)(2,1)S(1)}, bf16[2,640,256]{2,1,0:T(8,128)(2,1)S(1)}, f32[12,1,512]{2,1,0:T(1,128)S(1)}, bf16[512,512]{1,0:T(8,12...) custom-call(bf16[512,512]{1,0:T(8,128)(2,1)} %bitcast.11, ...), custom_call_target="tpu_custom_call" | custom-call | flops 738197504 | bytes 5922944 | tf_op jit(solution)/shard_map/pallas_call | solution.py:239
  3.5 1.3 %collective-permute-start.3 = (bf16[2,512,512]{2,1,0:T(8,128)(2,1)S(1)}, bf16[2,512,512]{2,1,0:T(8,128)(2,1)S(1)}, u32[]{:S(2)}, u32[]{:S(2)}) collective-permute-start(bf16[2,512,512]{2,1,0:T(8,128)(2,1)S(1)} %get-tuple-element.40.refs_6_), channel_id=1, source_target_pairs={{16,24},{17,25},{18,26},{19,27},{20,28},{21,29},{22,30},{23,31},{8... | collective-permute-start | bytes 3145736 | tf_op jit(solution)/shard_map/ppermute | solution.py:267
  4.8 0.7 collective-permute-start
  5.4 0.7 collective-permute-start.1
  6.1 0.7 collective-permute-start.2
  6.8 0.3 shard_map.87.total_ref
  7.2 0.9 %collective-permute-done.3.refs_3_.layer_ref = bf16[2,512,512]{2,1,0:T(8,128)(2,1)S(1)} collective-permute-done((bf16[2,512,512]{2,1,0:T(8,128)(2,1)S(1)}, bf16[2,512,512]{2,1,0:T(8,128)(2,1)S(1)}, u32[]{:S(2)}, u32[]{:S(2)}) %collective-permute-start.3) | collective-permute-done | bytes 1048608 | tf_op jit(solution)/shard_map/ppermute | solution.py:267
  8.0 0.9 %shard_map.88 = (bf16[512,512]{1,0:T(8,128)(2,1)S(1)}, bf16[512,512]{1,0:T(8,128)(2,1)S(1)}, bf16[512,512]{1,0:T(8,128)(2,1)S(1)}, bf16[2,128,512]{2,1,0:T(8,128...) custom-call(f32[12,1,512]{2,1,0:T(1,128)S(1)} %get-tuple-element.34.mask_ref, ...), custom_call_target="tpu_custom_call" | custom-call | flops 469762048 | bytes 5922816 | tf_op jit(solution)/shard_map/pallas_call | solution.py:239
  8.9 0.7 collective-permute-start.4
  9.6 0.7 collective-permute-start.5
  10.3 0.7 collective-permute-start.6
  11.3 0.4 shard_map.90.top_ref
  11.7 1.3 %collective-permute-start.7 = (bf16[512,512]{1,0:T(8,128)(2,1)S(1)}, bf16[512,512]{1,0:T(8,128)(2,1)S(1)}, u32[]{:S(2)}, u32[]{:S(2)}) collective-permute-start(bf16[512,512]{1,0:T(8,128)(2,1)S(1)} %shard_map.90.top_ref), channel_id=1, source_target_pairs={{24,0},{25,1},{26,2},{27,3},{28,4},{29,5},{30,6},{31,7}} | collective-permute-start | bytes 1572872 | tf_op jit(solution)/shard_map/ppermute | solution.py:267
  13.0 28.1 %collective-permute-done.7.upstream_ref = bf16[512,512]{1,0:T(8,128)(2,1)S(1)} collective-permute-done((bf16[512,512]{1,0:T(8,128)(2,1)S(1)}, bf16[512,512]{1,0:T(8,128)(2,1)S(1)}, u32[]{:S(2)}, u32[]{:S(2)}) %collective-permute-start.7) | collective-permute-done | bytes 524320 | tf_op jit(solution)/shard_map/ppermute | solution.py:267
  41.1 0.8 shard_map.91
  41.9 1.5 %collective-permute-start.11 = (bf16[512,512]{1,0:T(8,128)(2,1)S(1)}, bf16[512,512]{1,0:T(8,128)(2,1)S(1)}, u32[]{:S(2)}, u32[]{:S(2)}) collective-permute-start(bf16[512,512]{1,0:T(8,128)(2,1)S(1)} %shard_map.94), channel_id=1, source_target_pairs={{24,16},{25,17},{26,18},{27,19},{28,20},{29,21},{30,22},{31,23},{0... | collective-permute-start | bytes 1572872 | tf_op jit(solution)/shard_map/ppermute | solution.py:267
  43.4 3.4 %collective-permute-start.8 = (bf16[2,128,512]{2,1,0:T(8,128)(2,1)S(1)}, bf16[2,128,512]{2,1,0:T(8,128)(2,1)S(1)}, u32[]{:S(2)}, u32[]{:S(2)}) collective-permute-start(bf16[2,128,512]{2,1,0:T(8,128)(2,1)S(1)} %get-tuple-element.47), channel_id=1, source_target_pairs={{0,2},{1,3},{2,0},{3,1},{4,6},{5,7},{6,4},{7,5}} | collective-permute-start | bytes 786440 | tf_op jit(solution)/shard_map/ppermute | solution.py:312
  46.9 0.7 collective-permute-start.9
  47.5 3.4 %collective-permute-start.10 = (bf16[2,128,512]{2,1,0:T(8,128)(2,1)S(1)}, bf16[2,128,512]{2,1,0:T(8,128)(2,1)S(1)}, u32[]{:S(2)}, u32[]{:S(2)}) collective-permute-start(bf16[2,128,512]{2,1,0:T(8,128)(2,1)S(1)} %get-tuple-element.49), channel_id=1, source_target_pairs={{0,1},{2,3},{4,5},{6,7},{1,0},{3,2},{5,4},{7,6}} | collective-permute-start | bytes 786440 | tf_op jit(solution)/shard_map/ppermute | solution.py:312
  51.2 0.3 shard_map.92.total_ref
  51.7 4.9 %collective-permute-done.10.refs_2_ = bf16[2,128,512]{2,1,0:T(8,128)(2,1)S(1)} collective-permute-done((bf16[2,128,512]{2,1,0:T(8,128)(2,1)S(1)}, bf16[2,128,512]{2,1,0:T(8,128)(2,1)S(1)}, u32[]{:S(2)}, u32[]{:S(2)}) %collective-permute-start.10) | collective-permute-done | bytes 262176 | tf_op jit(solution)/shard_map/ppermute | solution.py:312
  56.6 1.7 %shard_map.95 = (bf16[512,512]{1,0:T(8,128)(2,1)S(1)}, f32[512,512]{1,0:T(8,128)S(1)}, bf16[2,128,512]{2,1,0:T(8,128)(2,1)S(1)}, bf16[2,128,512]{2,1,0:T(8,128)(...) custom-call(f32[12,1,512]{2,1,0:T(1,128)S(1)} %get-tuple-element.34.mask_ref, ...), custom_call_target="tpu_custom_call" | custom-call | flops 872415232 | bytes 8282112 | tf_op jit(solution)/shard_map/pallas_call | solution.py:239
  58.3 1.3 %collective-permute-start.15 = (bf16[512,512]{1,0:T(8,128)(2,1)S(1)}, bf16[512,512]{1,0:T(8,128)(2,1)S(1)}, u32[]{:S(2)}, u32[]{:S(2)}) collective-permute-start(bf16[512,512]{1,0:T(8,128)(2,1)S(1)} %shard_map.96), channel_id=1, source_target_pairs={{24,16},{25,17},{26,18},{27,19},{28,20},{29,21},{30,22},{31,23},{0... | collective-permute-start | bytes 1572872 | tf_op jit(solution)/shard_map/ppermute | solution.py:267
  59.7 1.6 %collective-permute-start.16 = (bf16[256,512]{1,0:T(8,128)(2,1)S(1)}, bf16[256,512]{1,0:T(8,128)(2,1)S(1)}, u32[]{:S(2)}, u32[]{:S(2)}) collective-permute-start(bf16[256,512]{1,0:T(8,128)(2,1)S(1)} %get-tuple-element.59), channel_id=1, source_target_pairs={{0,1},{1,0},{2,3},{3,2},{4,5},{5,4},{6,7},{7,6},{8,9},{9,8},{10,11... | collective-permute-start | bytes 786440 | tf_op jit(solution)/shard_map/ppermute | solution.py:405
  61.3 4.1 %collective-permute-start.12 = (bf16[2,128,512]{2,1,0:T(8,128)(2,1)S(1)}, bf16[2,128,512]{2,1,0:T(8,128)(2,1)S(1)}, u32[]{:S(2)}, u32[]{:S(2)}) collective-permute-start(bf16[2,128,512]{2,1,0:T(8,128)(2,1)S(1)} %get-tuple-element.54), channel_id=1, source_target_pairs={{0,2},{1,3},{2,0},{3,1},{4,6},{5,7},{6,4},{7,5}} | collective-permute-start | bytes 786440 | tf_op jit(solution)/shard_map/ppermute | solution.py:312
  65.3 0.7 collective-permute-start.13
  66.0 2.4 %collective-permute-start.14 = (bf16[2,128,512]{2,1,0:T(8,128)(2,1)S(1)}, bf16[2,128,512]{2,1,0:T(8,128)(2,1)S(1)}, u32[]{:S(2)}, u32[]{:S(2)}) collective-permute-start(bf16[2,128,512]{2,1,0:T(8,128)(2,1)S(1)} %get-tuple-element.56), channel_id=1, source_target_pairs={{0,1},{2,3},{4,5},{6,7},{1,0},{3,2},{5,4},{7,6}} | collective-permute-start | bytes 786440 | tf_op jit(solution)/shard_map/ppermute | solution.py:312
  68.6 2.8 %collective-permute-start.17 = (bf16[128,512]{1,0:T(8,128)(2,1)S(1)}, bf16[128,512]{1,0:T(8,128)(2,1)S(1)}, u32[]{:S(2)}, u32[]{:S(2)}) collective-permute-start(bf16[128,512]{1,0:T(8,128)(2,1)S(1)} %get-tuple-element.61), channel_id=1, source_target_pairs={{0,4},{1,5},{2,6},{3,7},{4,0},{5,1},{6,2},{7,3},{8,12},{9,13},{10,... | collective-permute-start | bytes 393224 | tf_op jit(solution)/shard_map/ppermute | solution.py:405
  71.3 3.2 %collective-permute-done.17.got_ref = bf16[128,512]{1,0:T(8,128)(2,1)S(1)} collective-permute-done((bf16[128,512]{1,0:T(8,128)(2,1)S(1)}, bf16[128,512]{1,0:T(8,128)(2,1)S(1)}, u32[]{:S(2)}, u32[]{:S(2)}) %collective-permute-start.17) | collective-permute-done | bytes 131104 | tf_op jit(solution)/shard_map/ppermute | solution.py:405
  74.6 2.4 %collective-permute-start.18 = (bf16[64,512]{1,0:T(8,128)(2,1)S(1)}, bf16[64,512]{1,0:T(8,128)(2,1)S(1)}, u32[]{:S(2)}, u32[]{:S(2)}) collective-permute-start(bf16[64,512]{1,0:T(8,128)(2,1)S(1)} %get-tuple-element.63), channel_id=1, source_target_pairs={{0,2},{1,3},{2,0},{3,1},{4,6},{5,7},{6,4},{7,5},{8,10},{9,11},{10,... | collective-permute-start | bytes 196616 | tf_op jit(solution)/shard_map/ppermute | solution.py:411
  77.0 2.2 %collective-permute-done.18.refs_6_ = bf16[64,512]{1,0:T(8,128)(2,1)S(1)} collective-permute-done((bf16[64,512]{1,0:T(8,128)(2,1)S(1)}, bf16[64,512]{1,0:T(8,128)(2,1)S(1)}, u32[]{:S(2)}, u32[]{:S(2)}) %collective-permute-start.18) | collective-permute-done | bytes 65568 | tf_op jit(solution)/shard_map/ppermute | solution.py:411
  79.2 1.2 %shard_map.99 = (bf16[512,512]{1,0:T(8,128)(2,1)}, f32[64,512]{1,0:T(8,128)}) custom-call(f32[12,1,512]{2,1,0:T(1,128)S(1)} %get-tuple-element.34.mask_ref, f32[512,512]{1,0:T(8,128)S(1)} %get-tuple-element.53.total_ref, bf16[2,128,512]{2,1,0:T(8,128)(2,1)S(1)} %collective-permute-done.12.refs_0_, bf16[2,128,512]{2,1,0:T(8,128)(2,1)S(1)} %collective-permute-done.13.refs_1_, ...), custom_call_target="tpu_custom_call" | custom-call | bytes 3760128 | tf_op jit(solution)/shard_map/pallas_call | solution.py:239
  (24 shorter events, 1.0 us)
Async XLA Ops:
  0.6 6.2 %copy-start.1 = (bf16[2,1,1,256,512]{4,3,2,1,0:T(8,128)(2,1)S(1)}, bf16[2,1,1,256,512]{4,3,2,1,0:T(8,128)(2,1)}, u32[]{:S(2)}) copy-start(bf16[2,1,1,256,512]{4,3,2,1,0:T(8,128)(2,1)} %param.8) | copy-start | bytes 1572868
  3.5 4.6 %collective-permute-start.3 = (bf16[2,512,512]{2,1,0:T(8,128)(2,1)S(1)}, bf16[2,512,512]{2,1,0:T(8,128)(2,1)S(1)}, u32[]{:S(2)}, u32[]{:S(2)}) collective-permute-start(bf16[2,512,512]{2,1,0:T(8,128)(2,1)S(1)} %get-tuple-element.40.refs_6_), channel_id=1, source_target_pairs={{16,24},{17,25},{18,26},{19,27},{20,28},{21,29},{22,30},{23,31},{8... | collective-permute-start | bytes 3145736 | tf_op jit(solution)/shard_map/ppermute | solution.py:267
  4.8 2.4 %collective-permute-start = (bf16[2,128,512]{2,1,0:T(8,128)(2,1)S(1)}, bf16[2,128,512]{2,1,0:T(8,128)(2,1)S(1)}, u32[]{:S(2)}, u32[]{:S(2)}) collective-permute-start(bf16[2,128,512]{2,1,0:T(8,128)(2,1)S(1)} %get-tuple-element.37), channel_id=1, source_target_pairs={{24,26},{25,27},{26,24},{27,25},{28,30},{29,31},{30,28},{31,29}} | collective-permute-start | bytes 786440 | tf_op jit(solution)/shard_map/ppermute | solution.py:312
  5.4 1.7 %collective-permute-start.1 = (bf16[2,128,512]{2,1,0:T(8,128)(2,1)S(1)}, bf16[2,128,512]{2,1,0:T(8,128)(2,1)S(1)}, u32[]{:S(2)}, u32[]{:S(2)}) collective-permute-start(bf16[2,128,512]{2,1,0:T(8,128)(2,1)S(1)} %get-tuple-element.38), channel_id=1, source_target_pairs={{26,28},{27,29},{28,26},{29,27}} | collective-permute-start | bytes 786440 | tf_op jit(solution)/shard_map/ppermute | solution.py:312
  6.1 1.0 %collective-permute-start.2 = (bf16[2,128,512]{2,1,0:T(8,128)(2,1)S(1)}, bf16[2,128,512]{2,1,0:T(8,128)(2,1)S(1)}, u32[]{:S(2)}, u32[]{:S(2)}) collective-permute-start(bf16[2,128,512]{2,1,0:T(8,128)(2,1)S(1)} %get-tuple-element.39), channel_id=1, source_target_pairs={{24,25},{26,27},{28,29},{30,31},{25,24},{27,26},{29,28},{31,30}} | collective-permute-start | bytes 786440 | tf_op jit(solution)/shard_map/ppermute | solution.py:312
  8.9 2.4 %collective-permute-start.4 = (bf16[2,128,512]{2,1,0:T(8,128)(2,1)S(1)}, bf16[2,128,512]{2,1,0:T(8,128)(2,1)S(1)}, u32[]{:S(2)}, u32[]{:S(2)}) collective-permute-start(bf16[2,128,512]{2,1,0:T(8,128)(2,1)S(1)} %get-tuple-element.43), channel_id=1, source_target_pairs={{24,26},{25,27},{26,24},{27,25},{28,30},{29,31},{30,28},{31,29}} | collective-permute-start | bytes 786440 | tf_op jit(solution)/shard_map/ppermute | solution.py:312
  9.6 1.7 %collective-permute-start.5 = (bf16[2,128,512]{2,1,0:T(8,128)(2,1)S(1)}, bf16[2,128,512]{2,1,0:T(8,128)(2,1)S(1)}, u32[]{:S(2)}, u32[]{:S(2)}) collective-permute-start(bf16[2,128,512]{2,1,0:T(8,128)(2,1)S(1)} %get-tuple-element.44), channel_id=1, source_target_pairs={{26,28},{27,29},{28,26},{29,27}} | collective-permute-start | bytes 786440 | tf_op jit(solution)/shard_map/ppermute | solution.py:312
  10.3 1.0 %collective-permute-start.6 = (bf16[2,128,512]{2,1,0:T(8,128)(2,1)S(1)}, bf16[2,128,512]{2,1,0:T(8,128)(2,1)S(1)}, u32[]{:S(2)}, u32[]{:S(2)}) collective-permute-start(bf16[2,128,512]{2,1,0:T(8,128)(2,1)S(1)} %get-tuple-element.45), channel_id=1, source_target_pairs={{24,25},{26,27},{28,29},{30,31},{25,24},{27,26},{29,28},{31,30}} | collective-permute-start | bytes 786440 | tf_op jit(solution)/shard_map/ppermute | solution.py:312
  11.7 29.4 %collective-permute-start.7 = (bf16[512,512]{1,0:T(8,128)(2,1)S(1)}, bf16[512,512]{1,0:T(8,128)(2,1)S(1)}, u32[]{:S(2)}, u32[]{:S(2)}) collective-permute-start(bf16[512,512]{1,0:T(8,128)(2,1)S(1)} %shard_map.90.top_ref), channel_id=1, source_target_pairs={{24,0},{25,1},{26,2},{27,3},{28,4},{29,5},{30,6},{31,7}} | collective-permute-start | bytes 1572872 | tf_op jit(solution)/shard_map/ppermute | solution.py:267
  41.9 9.1 %copy-start = (bf16[1,2,1,1,256,512]{5,4,3,2,1,0:T(8,128)(2,1)S(1)}, bf16[1,2,1,1,256,512]{5,4,3,2,1,0:T(8,128)(2,1)}, u32[]{:S(2)}) copy-start(bf16[1,2,1,1,256,512]{5,4,3,2,1,0:T(8,128)(2,1)} %param.7) | copy-start | bytes 1572868
  41.9 14.7 %collective-permute-start.11 = (bf16[512,512]{1,0:T(8,128)(2,1)S(1)}, bf16[512,512]{1,0:T(8,128)(2,1)S(1)}, u32[]{:S(2)}, u32[]{:S(2)}) collective-permute-start(bf16[512,512]{1,0:T(8,128)(2,1)S(1)} %shard_map.94), channel_id=1, source_target_pairs={{24,16},{25,17},{26,18},{27,19},{28,20},{29,21},{30,22},{31,23},{0... | collective-permute-start | bytes 1572872 | tf_op jit(solution)/shard_map/ppermute | solution.py:267
  43.4 8.3 %collective-permute-start.8 = (bf16[2,128,512]{2,1,0:T(8,128)(2,1)S(1)}, bf16[2,128,512]{2,1,0:T(8,128)(2,1)S(1)}, u32[]{:S(2)}, u32[]{:S(2)}) collective-permute-start(bf16[2,128,512]{2,1,0:T(8,128)(2,1)S(1)} %get-tuple-element.47), channel_id=1, source_target_pairs={{0,2},{1,3},{2,0},{3,1},{4,6},{5,7},{6,4},{7,5}} | collective-permute-start | bytes 786440 | tf_op jit(solution)/shard_map/ppermute | solution.py:312
  46.9 4.8 %collective-permute-start.9 = (bf16[2,128,512]{2,1,0:T(8,128)(2,1)S(1)}, bf16[2,128,512]{2,1,0:T(8,128)(2,1)S(1)}, u32[]{:S(2)}, u32[]{:S(2)}) collective-permute-start(bf16[2,128,512]{2,1,0:T(8,128)(2,1)S(1)} %get-tuple-element.48), channel_id=1, source_target_pairs={{2,4},{3,5},{4,2},{5,3}} | collective-permute-start | bytes 786440 | tf_op jit(solution)/shard_map/ppermute | solution.py:312
  47.5 9.1 %collective-permute-start.10 = (bf16[2,128,512]{2,1,0:T(8,128)(2,1)S(1)}, bf16[2,128,512]{2,1,0:T(8,128)(2,1)S(1)}, u32[]{:S(2)}, u32[]{:S(2)}) collective-permute-start(bf16[2,128,512]{2,1,0:T(8,128)(2,1)S(1)} %get-tuple-element.49), channel_id=1, source_target_pairs={{0,1},{2,3},{4,5},{6,7},{1,0},{3,2},{5,4},{7,6}} | collective-permute-start | bytes 786440 | tf_op jit(solution)/shard_map/ppermute | solution.py:312
  58.3 20.8 %collective-permute-start.15 = (bf16[512,512]{1,0:T(8,128)(2,1)S(1)}, bf16[512,512]{1,0:T(8,128)(2,1)S(1)}, u32[]{:S(2)}, u32[]{:S(2)}) collective-permute-start(bf16[512,512]{1,0:T(8,128)(2,1)S(1)} %shard_map.96), channel_id=1, source_target_pairs={{24,16},{25,17},{26,18},{27,19},{28,20},{29,21},{30,22},{31,23},{0... | collective-permute-start | bytes 1572872 | tf_op jit(solution)/shard_map/ppermute | solution.py:267
  59.7 8.8 %collective-permute-start.16 = (bf16[256,512]{1,0:T(8,128)(2,1)S(1)}, bf16[256,512]{1,0:T(8,128)(2,1)S(1)}, u32[]{:S(2)}, u32[]{:S(2)}) collective-permute-start(bf16[256,512]{1,0:T(8,128)(2,1)S(1)} %get-tuple-element.59), channel_id=1, source_target_pairs={{0,1},{1,0},{2,3},{3,2},{4,5},{5,4},{6,7},{7,6},{8,9},{9,8},{10,11... | collective-permute-start | bytes 786440 | tf_op jit(solution)/shard_map/ppermute | solution.py:405
  61.3 15.7 %collective-permute-start.12 = (bf16[2,128,512]{2,1,0:T(8,128)(2,1)S(1)}, bf16[2,128,512]{2,1,0:T(8,128)(2,1)S(1)}, u32[]{:S(2)}, u32[]{:S(2)}) collective-permute-start(bf16[2,128,512]{2,1,0:T(8,128)(2,1)S(1)} %get-tuple-element.54), channel_id=1, source_target_pairs={{0,2},{1,3},{2,0},{3,1},{4,6},{5,7},{6,4},{7,5}} | collective-permute-start | bytes 786440 | tf_op jit(solution)/shard_map/ppermute | solution.py:312
  65.3 11.6 %collective-permute-start.13 = (bf16[2,128,512]{2,1,0:T(8,128)(2,1)S(1)}, bf16[2,128,512]{2,1,0:T(8,128)(2,1)S(1)}, u32[]{:S(2)}, u32[]{:S(2)}) collective-permute-start(bf16[2,128,512]{2,1,0:T(8,128)(2,1)S(1)} %get-tuple-element.55), channel_id=1, source_target_pairs={{2,4},{3,5},{4,2},{5,3}} | collective-permute-start | bytes 786440 | tf_op jit(solution)/shard_map/ppermute | solution.py:312
  66.0 10.9 %collective-permute-start.14 = (bf16[2,128,512]{2,1,0:T(8,128)(2,1)S(1)}, bf16[2,128,512]{2,1,0:T(8,128)(2,1)S(1)}, u32[]{:S(2)}, u32[]{:S(2)}) collective-permute-start(bf16[2,128,512]{2,1,0:T(8,128)(2,1)S(1)} %get-tuple-element.56), channel_id=1, source_target_pairs={{0,1},{2,3},{4,5},{6,7},{1,0},{3,2},{5,4},{7,6}} | collective-permute-start | bytes 786440 | tf_op jit(solution)/shard_map/ppermute | solution.py:312
  68.6 5.9 %collective-permute-start.17 = (bf16[128,512]{1,0:T(8,128)(2,1)S(1)}, bf16[128,512]{1,0:T(8,128)(2,1)S(1)}, u32[]{:S(2)}, u32[]{:S(2)}) collective-permute-start(bf16[128,512]{1,0:T(8,128)(2,1)S(1)} %get-tuple-element.61), channel_id=1, source_target_pairs={{0,4},{1,5},{2,6},{3,7},{4,0},{5,1},{6,2},{7,3},{8,12},{9,13},{10,... | collective-permute-start | bytes 393224 | tf_op jit(solution)/shard_map/ppermute | solution.py:405
  74.6 4.6 %collective-permute-start.18 = (bf16[64,512]{1,0:T(8,128)(2,1)S(1)}, bf16[64,512]{1,0:T(8,128)(2,1)S(1)}, u32[]{:S(2)}, u32[]{:S(2)}) collective-permute-start(bf16[64,512]{1,0:T(8,128)(2,1)S(1)} %get-tuple-element.63), channel_id=1, source_target_pairs={{0,2},{1,3},{2,0},{3,1},{4,6},{5,7},{6,4},{7,5},{8,10},{9,11},{10,... | collective-permute-start | bytes 196616 | tf_op jit(solution)/shard_map/ppermute | solution.py:411

commit v5 on v4

--- a/solution.py
+++ b/solution.py
@@ -27,9 +27,22 @@
     return phases
 
 
+def completed(pairs, devices):
+    pairs = list(pairs)
+    silent = set(range(devices)) - {source for source, _ in pairs}
+    unfed = set(range(devices)) - {target for _, target in pairs}
+    back = [(target, source) for source, target in pairs if target in silent and source in unfed]
+    pairs += back
+    silent -= {source for source, _ in back}
+    unfed -= {target for _, target in back}
+    return pairs + [(device, device) for device in sorted(silent & unfed)]
+
+
 def side(phase):
-    axis, base, first = phase
-    return base, lax.rem(lax.axis_index(axis) + first, 2) == 0
+    axis, base, first, count = phase
+    place = lax.axis_index(axis)
+    is_low = lax.rem(place + first, 2) == 0
+    return base, is_low, jnp.where(is_low, place < count - 1, place > 0)
 
 
 def rows_dot(left, right):
@@ -86,16 +99,16 @@
                 present = pattern_ref[batch, source, target].astype(F32)
                 edges = local_ref[batch, source, target].astype(F32) * present
                 mixing_ref[batch, target * block : (target + 1) * block, columns] = edges.T.astype(BF16)
-            for index, (base, is_low) in enumerate(sides):
+            for index, (base, is_low, _) in enumerate(sides):
                 slot = jnp.where(is_low, base + 1, base)
                 present = pattern_ref[batch, source, blocks + slot].astype(F32)
                 edges = halo_ref[batch, slot, source].astype(F32) * present
                 start = (blocks + index) * block
                 mixing_ref[batch, start : start + block, columns] = edges.T.astype(BF16)
-        for index, (base, is_low) in enumerate(sides):
+        for index, (base, is_low, paired) in enumerate(sides):
             chosen = pick_ref[batch, jnp.where(is_low, base, base + 1)]
             for target in range(blocks):
-                here = (chosen == target).astype(F32)
+                here = ((chosen == target) & paired).astype(F32)
                 entry = (batch * blocks + target) * len(sides) + index
                 mask_ref[entry] = jnp.full(mask_ref.shape[1:], here, F32)
     send_blocks(grads, matrix_ref[...], mixing_ref, message_ref, out_refs)
@@ -250,6 +263,7 @@
 def per_device(stored, cotangent, weight, local_edges, halo_edges, pattern, pick):
     sections, rows, columns = (lax.axis_size(name) for name in AXES)
     here = lax.axis_index("pipe")
+    devices = sections * rows * columns
     lower = sections // 2
     upper = sections - lower
     top = sections - 1
@@ -264,7 +278,7 @@
             for x in range(rows)
             for y in range(columns)
         ]
-        return lax.ppermute(value, AXES, pairs)
+        return lax.ppermute(value, AXES, completed(pairs, devices))
 
     batches, nodes, width = stored.shape[1], stored.shape[4], stored.shape[5]
     blocks, block = local_edges.shape[3], local_edges.shape[5]
@@ -276,10 +290,10 @@
     phases, routes = [], []
     for axis, base, count in (("tx", 0, rows), ("ty", 2, columns)):
         for first, couples in swap_phases(count):
-            phases.append((axis, base, first))
+            phases.append((axis, base, first, count))
             route = {}
             for lead in {0, top}:
-                route[lead] = [
+                route[lead] = completed([
                     (
                         flat(lead, *((a, other) if axis == "tx" else (other, a))),
                         flat(lead, *((b, other) if axis == "tx" else (other, b))),
@@ -287,7 +301,7 @@
                     for low, high in couples
                     for a, b in ((low, high), (high, low))
                     for other in range(columns if axis == "tx" else rows)
-                ]
+                ], devices)
             routes.append(route)
     phases = tuple(phases)
     splits, left = [], rows * columns

time: 80.8 us -> 82 us (1.015)
  starting transfers between devices: 30.9 us -> 48.9 us
  waiting for transfers between devices: 39.5 us -> 22.8 us
    ppermute x4, waiting for transfers between devices: 29 us -> 6.86 us  [to_sections(): return lax.ppermute(value, AXES, completed(pairs, devices))]
    ppermute x4, starting transfers between devices: 5.36 us -> 24.9 us  [to_sections(): return lax.ppermute(value, AXES, completed(pairs, devices))]
    ppermute x2, waiting for transfers between devices: 3.16 us -> 7.33 us  [per_device(): got = lax.ppermute(parcel, AXES, pairs)]
    ppermute x1, starting transfers between devices: 2.39 us -> 0.07 us  [per_device(): got = lax.ppermute(parcel, AXES, splits[-1][1])]
    ppermute x1, waiting for transfers between devices: 2.23 us -> 4.22 us  [per_device(): got = lax.ppermute(parcel, AXES, splits[-1][1])]
  transfers between devices with their start and end apart: 19 -> 19, of which waited for: 6 -> 5; matrix products, arithmetic and copies ran while one was open for 0% -> 0% of each run, Pallas kernels for 2% -> 2%
where the time goes in v5:
time: 82 us; the launch traced here: 81.7 us
  starting transfers between devices  48.9 us (60%)
  waiting for transfers between devices  22.8 us (28%)
  Pallas kernels  9.02 us (11%)
  between operations  0.97 us (1%)
    ppermute x4, starting transfers between devices, to_sections(): return lax.ppermute(value, AXES, completed(pairs, devices))  24.9 us
    ppermute x12, starting transfers between devices, exchange(): lax.ppermute(out, AXES, route[lead])  19.6 us
    pallas_call x14, Pallas kernels, call(): pl.pallas_call(body, out_shape=[kind(shape, dtype) for shape, dtype in ou...  9.02 us
    ppermute x2, waiting for transfers between devices, per_device(): got = lax.ppermute(parcel, AXES, pairs)  7.33 us
    ppermute x4, waiting for transfers between devices, to_sections(): return lax.ppermute(value, AXES, completed(pairs, devices))  6.86 us
    ppermute x2, starting transfers between devices, per_device(): got = lax.ppermute(parcel, AXES, pairs)  4.35 us
    ppermute x12, waiting for transfers between devices, exchange(): lax.ppermute(out, AXES, route[lead])  4.35 us
    ppermute x1, waiting for transfers between devices, per_device(): got = lax.ppermute(parcel, AXES, splits[-1][1])  4.22 us
  transfers between devices with their start and end apart: 19, of which 5 were waited for; matrix products, arithmetic and copies ran while one was open for 0% of the time, Pallas kernels for 2%

profile of v5, /device:TPU:0, one launch (start us, length us, event | category | flops | bytes accessed | tf_op | source)
XLA Modules:
  0.0 81.7 jit_solution(7171689079596183305)
XLA Ops:
  0.6 2.8 %shard_map.86 = (bf16[2,512,512]{2,1,0:T(8,128)(2,1)S(1)}, bf16[2,640,256]{2,1,0:T(8,128)(2,1)S(1)}, f32[12,1,512]{2,1,0:T(1,128)S(1)}, bf16[512,512]{1,0:T(8,12...) custom-call(bf16[512,512]{1,0:T(8,128)(2,1)} %bitcast.11, ...), custom_call_target="tpu_custom_call" | custom-call | flops 738197504 | bytes 5922944 | tf_op jit(solution)/shard_map/pallas_call | solution.py:252
  3.5 0.5 collective-permute-start.3
  4.0 0.7 collective-permute-start
  4.7 0.7 collective-permute-start.1
  5.3 0.7 collective-permute-start.2
  6.0 0.3 shard_map.87.total_ref
  6.4 0.9 %shard_map.88 = (bf16[512,512]{1,0:T(8,128)(2,1)S(1)}, bf16[512,512]{1,0:T(8,128)(2,1)S(1)}, bf16[512,512]{1,0:T(8,128)(2,1)S(1)}, bf16[2,128,512]{2,1,0:T(8,128...) custom-call(f32[12,1,512]{2,1,0:T(1,128)S(1)} %get-tuple-element.34.mask_ref, ...), custom_call_target="tpu_custom_call" | custom-call | flops 469762048 | bytes 5922816 | tf_op jit(solution)/shard_map/pallas_call | solution.py:252
  7.3 0.7 collective-permute-start.4
  8.0 0.7 collective-permute-start.5
  8.7 0.7 collective-permute-start.6
  9.3 0.3 shard_map.89.total_ref
  9.7 0.4 shard_map.90.top_ref
  10.0 24.3 %collective-permute-start.7 = (bf16[512,512]{1,0:T(8,128)(2,1)S(1)}, bf16[512,512]{1,0:T(8,128)(2,1)S(1)}, u32[]{:S(2)}, u32[]{:S(2)}) collective-permute-start(bf16[512,512]{1,0:T(8,128)(2,1)S(1)} %shard_map.90.top_ref), channel_id=1, source_target_pairs={{24,0},{25,1},{26,2},{27,3},{28,4},{29,5},{30,6},{31,7},{0,24},{1,... | collective-permute-start | bytes 1572872 | tf_op jit(solution)/shard_map/ppermute | solution.py:281
  34.3 6.8 %collective-permute-done.7.upstream_ref = bf16[512,512]{1,0:T(8,128)(2,1)S(1)} collective-permute-done((bf16[512,512]{1,0:T(8,128)(2,1)S(1)}, bf16[512,512]{1,0:T(8,128)(2,1)S(1)}, u32[]{:S(2)}, u32[]{:S(2)}) %collective-permute-start.7) | collective-permute-done | bytes 524320 | tf_op jit(solution)/shard_map/ppermute | solution.py:281
  41.2 0.8 shard_map.91
  42.1 3.4 %collective-permute-start.8 = (bf16[2,128,512]{2,1,0:T(8,128)(2,1)S(1)}, bf16[2,128,512]{2,1,0:T(8,128)(2,1)S(1)}, u32[]{:S(2)}, u32[]{:S(2)}) collective-permute-start(bf16[2,128,512]{2,1,0:T(8,128)(2,1)S(1)} %get-tuple-element.47), channel_id=1, source_target_pairs={{0,2},{1,3},{2,0},{3,1},{4,6},{5,7},{6,4},{7,5},{8,8},{9,9},{10,10... | collective-permute-start | bytes 786440 | tf_op jit(solution)/shard_map/ppermute | solution.py:326
  45.5 0.7 collective-permute-start.9
  46.2 3.4 %collective-permute-start.10 = (bf16[2,128,512]{2,1,0:T(8,128)(2,1)S(1)}, bf16[2,128,512]{2,1,0:T(8,128)(2,1)S(1)}, u32[]{:S(2)}, u32[]{:S(2)}) collective-permute-start(bf16[2,128,512]{2,1,0:T(8,128)(2,1)S(1)} %get-tuple-element.49), channel_id=1, source_target_pairs={{0,1},{2,3},{4,5},{6,7},{1,0},{3,2},{5,4},{7,6},{8,8},{9,9},{10,10... | collective-permute-start | bytes 786440 | tf_op jit(solution)/shard_map/ppermute | solution.py:326
  49.7 0.2 shard_map.93.refs_3_
  49.8 0.3 shard_map.92.total_ref
  50.2 0.2 collective-permute-done.8.refs_0_
  50.3 4.1 %collective-permute-done.10.refs_2_ = bf16[2,128,512]{2,1,0:T(8,128)(2,1)S(1)} collective-permute-done((bf16[2,128,512]{2,1,0:T(8,128)(2,1)S(1)}, bf16[2,128,512]{2,1,0:T(8,128)(2,1)S(1)}, u32[]{:S(2)}, u32[]{:S(2)}) %collective-permute-start.10) | collective-permute-done | bytes 262176 | tf_op jit(solution)/shard_map/ppermute | solution.py:326
  54.5 1.7 %shard_map.95 = (bf16[512,512]{1,0:T(8,128)(2,1)S(1)}, f32[512,512]{1,0:T(8,128)S(1)}, bf16[2,128,512]{2,1,0:T(8,128)(2,1)S(1)}, bf16[2,128,512]{2,1,0:T(8,128)(...) custom-call(f32[12,1,512]{2,1,0:T(1,128)S(1)} %get-tuple-element.34.mask_ref, ...), custom_call_target="tpu_custom_call" | custom-call | flops 872415232 | bytes 8282112 | tf_op jit(solution)/shard_map/pallas_call | solution.py:252
  56.3 1.6 %collective-permute-start.16 = (bf16[256,512]{1,0:T(8,128)(2,1)S(1)}, bf16[256,512]{1,0:T(8,128)(2,1)S(1)}, u32[]{:S(2)}, u32[]{:S(2)}) collective-permute-start(bf16[256,512]{1,0:T(8,128)(2,1)S(1)} %get-tuple-element.59), channel_id=1, source_target_pairs={{0,1},{1,0},{2,3},{3,2},{4,5},{5,4},{6,7},{7,6},{8,9},{9,8},{10,11... | collective-permute-start | bytes 786440 | tf_op jit(solution)/shard_map/ppermute | solution.py:419
  57.9 4.9 %collective-permute-start.12 = (bf16[2,128,512]{2,1,0:T(8,128)(2,1)S(1)}, bf16[2,128,512]{2,1,0:T(8,128)(2,1)S(1)}, u32[]{:S(2)}, u32[]{:S(2)}) collective-permute-start(bf16[2,128,512]{2,1,0:T(8,128)(2,1)S(1)} %get-tuple-element.54), channel_id=1, source_target_pairs={{0,2},{1,3},{2,0},{3,1},{4,6},{5,7},{6,4},{7,5},{8,8},{9,9},{10,10... | collective-permute-start | bytes 786440 | tf_op jit(solution)/shard_map/ppermute | solution.py:326
  62.8 0.7 collective-permute-start.13
  63.4 2.4 %collective-permute-start.14 = (bf16[2,128,512]{2,1,0:T(8,128)(2,1)S(1)}, bf16[2,128,512]{2,1,0:T(8,128)(2,1)S(1)}, u32[]{:S(2)}, u32[]{:S(2)}) collective-permute-start(bf16[2,128,512]{2,1,0:T(8,128)(2,1)S(1)} %get-tuple-element.56), channel_id=1, source_target_pairs={{0,1},{2,3},{4,5},{6,7},{1,0},{3,2},{5,4},{7,6},{8,8},{9,9},{10,10... | collective-permute-start | bytes 786440 | tf_op jit(solution)/shard_map/ppermute | solution.py:326
  65.9 0.1 shard_map.97
  66.0 2.8 %collective-permute-start.17 = (bf16[128,512]{1,0:T(8,128)(2,1)S(1)}, bf16[128,512]{1,0:T(8,128)(2,1)S(1)}, u32[]{:S(2)}, u32[]{:S(2)}) collective-permute-start(bf16[128,512]{1,0:T(8,128)(2,1)S(1)} %get-tuple-element.61), channel_id=1, source_target_pairs={{0,4},{1,5},{2,6},{3,7},{4,0},{5,1},{6,2},{7,3},{8,12},{9,13},{10,... | collective-permute-start | bytes 393224 | tf_op jit(solution)/shard_map/ppermute | solution.py:419
  68.8 7.3 %collective-permute-done.17.got_ref = bf16[128,512]{1,0:T(8,128)(2,1)S(1)} collective-permute-done((bf16[128,512]{1,0:T(8,128)(2,1)S(1)}, bf16[128,512]{1,0:T(8,128)(2,1)S(1)}, u32[]{:S(2)}, u32[]{:S(2)}) %collective-permute-start.17) | collective-permute-done | bytes 131104 | tf_op jit(solution)/shard_map/ppermute | solution.py:419
  76.2 4.2 %collective-permute-done.18.refs_6_ = bf16[64,512]{1,0:T(8,128)(2,1)S(1)} collective-permute-done((bf16[64,512]{1,0:T(8,128)(2,1)S(1)}, bf16[64,512]{1,0:T(8,128)(2,1)S(1)}, u32[]{:S(2)}, u32[]{:S(2)}) %collective-permute-start.18) | collective-permute-done | bytes 65568 | tf_op jit(solution)/shard_map/ppermute | solution.py:425
  80.5 1.2 %shard_map.99 = (bf16[512,512]{1,0:T(8,128)(2,1)}, f32[64,512]{1,0:T(8,128)}) custom-call(f32[12,1,512]{2,1,0:T(1,128)S(1)} %get-tuple-element.34.mask_ref, f32[512,512]{1,0:T(8,128)S(1)} %get-tuple-element.53.total_ref, bf16[2,128,512]{2,1,0:T(8,128)(2,1)S(1)} %collective-permute-done.12.refs_0_, bf16[2,128,512]{2,1,0:T(8,128)(2,1)S(1)} %collective-permute-done.13.refs_1_, ...), custom_call_target="tpu_custom_call" | custom-call | bytes 3760128 | tf_op jit(solution)/shard_map/pallas_call | solution.py:252
  (24 shorter events, 0.4 us)
Async XLA Ops:
  0.6 5.4 %copy-start.1 = (bf16[2,1,1,256,512]{4,3,2,1,0:T(8,128)(2,1)S(1)}, bf16[2,1,1,256,512]{4,3,2,1,0:T(8,128)(2,1)}, u32[]{:S(2)}) copy-start(bf16[2,1,1,256,512]{4,3,2,1,0:T(8,128)(2,1)} %param.8) | copy-start | bytes 1572868
  3.5 2.9 %collective-permute-start.3 = (bf16[2,512,512]{2,1,0:T(8,128)(2,1)S(1)}, bf16[2,512,512]{2,1,0:T(8,128)(2,1)S(1)}, u32[]{:S(2)}, u32[]{:S(2)}) collective-permute-start(bf16[2,512,512]{2,1,0:T(8,128)(2,1)S(1)} %get-tuple-element.40.refs_6_), channel_id=1, source_target_pairs={{16,24},{17,25},{18,26},{19,27},{20,28},{21,29},{22,30},{23,31},{8... | collective-permute-start | bytes 3145736 | tf_op jit(solution)/shard_map/ppermute | solution.py:281
  4.0 2.4 %collective-permute-start = (bf16[2,128,512]{2,1,0:T(8,128)(2,1)S(1)}, bf16[2,128,512]{2,1,0:T(8,128)(2,1)S(1)}, u32[]{:S(2)}, u32[]{:S(2)}) collective-permute-start(bf16[2,128,512]{2,1,0:T(8,128)(2,1)S(1)} %get-tuple-element.37), channel_id=1, source_target_pairs={{24,26},{25,27},{26,24},{27,25},{28,30},{29,31},{30,28},{31,29},{0... | collective-permute-start | bytes 786440 | tf_op jit(solution)/shard_map/ppermute | solution.py:326
  4.7 1.7 %collective-permute-start.1 = (bf16[2,128,512]{2,1,0:T(8,128)(2,1)S(1)}, bf16[2,128,512]{2,1,0:T(8,128)(2,1)S(1)}, u32[]{:S(2)}, u32[]{:S(2)}) collective-permute-start(bf16[2,128,512]{2,1,0:T(8,128)(2,1)S(1)} %get-tuple-element.38), channel_id=1, source_target_pairs={{26,28},{27,29},{28,26},{29,27},{0,0},{1,1},{2,2},{3,3},{4,4},{5,5... | collective-permute-start | bytes 786440 | tf_op jit(solution)/shard_map/ppermute | solution.py:326
  5.3 1.0 %collective-permute-start.2 = (bf16[2,128,512]{2,1,0:T(8,128)(2,1)S(1)}, bf16[2,128,512]{2,1,0:T(8,128)(2,1)S(1)}, u32[]{:S(2)}, u32[]{:S(2)}) collective-permute-start(bf16[2,128,512]{2,1,0:T(8,128)(2,1)S(1)} %get-tuple-element.39), channel_id=1, source_target_pairs={{24,25},{26,27},{28,29},{30,31},{25,24},{27,26},{29,28},{31,30},{0... | collective-permute-start | bytes 786440 | tf_op jit(solution)/shard_map/ppermute | solution.py:326
  7.3 2.4 %collective-permute-start.4 = (bf16[2,128,512]{2,1,0:T(8,128)(2,1)S(1)}, bf16[2,128,512]{2,1,0:T(8,128)(2,1)S(1)}, u32[]{:S(2)}, u32[]{:S(2)}) collective-permute-start(bf16[2,128,512]{2,1,0:T(8,128)(2,1)S(1)} %get-tuple-element.43), channel_id=1, source_target_pairs={{24,26},{25,27},{26,24},{27,25},{28,30},{29,31},{30,28},{31,29},{0... | collective-permute-start | bytes 786440 | tf_op jit(solution)/shard_map/ppermute | solution.py:326
  8.0 1.7 %collective-permute-start.5 = (bf16[2,128,512]{2,1,0:T(8,128)(2,1)S(1)}, bf16[2,128,512]{2,1,0:T(8,128)(2,1)S(1)}, u32[]{:S(2)}, u32[]{:S(2)}) collective-permute-start(bf16[2,128,512]{2,1,0:T(8,128)(2,1)S(1)} %get-tuple-element.44), channel_id=1, source_target_pairs={{26,28},{27,29},{28,26},{29,27},{0,0},{1,1},{2,2},{3,3},{4,4},{5,5... | collective-permute-start | bytes 786440 | tf_op jit(solution)/shard_map/ppermute | solution.py:326
  8.7 1.0 %collective-permute-start.6 = (bf16[2,128,512]{2,1,0:T(8,128)(2,1)S(1)}, bf16[2,128,512]{2,1,0:T(8,128)(2,1)S(1)}, u32[]{:S(2)}, u32[]{:S(2)}) collective-permute-start(bf16[2,128,512]{2,1,0:T(8,128)(2,1)S(1)} %get-tuple-element.45), channel_id=1, source_target_pairs={{24,25},{26,27},{28,29},{30,31},{25,24},{27,26},{29,28},{31,30},{0... | collective-permute-start | bytes 786440 | tf_op jit(solution)/shard_map/ppermute | solution.py:326
  10.0 31.1 %collective-permute-start.7 = (bf16[512,512]{1,0:T(8,128)(2,1)S(1)}, bf16[512,512]{1,0:T(8,128)(2,1)S(1)}, u32[]{:S(2)}, u32[]{:S(2)}) collective-permute-start(bf16[512,512]{1,0:T(8,128)(2,1)S(1)} %shard_map.90.top_ref), channel_id=1, source_target_pairs={{24,0},{25,1},{26,2},{27,3},{28,4},{29,5},{30,6},{31,7},{0,24},{1,... | collective-permute-start | bytes 1572872 | tf_op jit(solution)/shard_map/ppermute | solution.py:281
  41.9 7.7 %copy-start = (bf16[1,2,1,1,256,512]{5,4,3,2,1,0:T(8,128)(2,1)S(1)}, bf16[1,2,1,1,256,512]{5,4,3,2,1,0:T(8,128)(2,1)}, u32[]{:S(2)}) copy-start(bf16[1,2,1,1,256,512]{5,4,3,2,1,0:T(8,128)(2,1)} %param.7) | copy-start | bytes 1572868
  42.0 12.5 %collective-permute-start.11 = (bf16[512,512]{1,0:T(8,128)(2,1)S(1)}, bf16[512,512]{1,0:T(8,128)(2,1)S(1)}, u32[]{:S(2)}, u32[]{:S(2)}) collective-permute-start(bf16[512,512]{1,0:T(8,128)(2,1)S(1)} %shard_map.94), channel_id=1, source_target_pairs={{24,16},{25,17},{26,18},{27,19},{28,20},{29,21},{30,22},{31,23},{0... | collective-permute-start | bytes 1572872 | tf_op jit(solution)/shard_map/ppermute | solution.py:281
  42.1 8.3 %collective-permute-start.8 = (bf16[2,128,512]{2,1,0:T(8,128)(2,1)S(1)}, bf16[2,128,512]{2,1,0:T(8,128)(2,1)S(1)}, u32[]{:S(2)}, u32[]{:S(2)}) collective-permute-start(bf16[2,128,512]{2,1,0:T(8,128)(2,1)S(1)} %get-tuple-element.47), channel_id=1, source_target_pairs={{0,2},{1,3},{2,0},{3,1},{4,6},{5,7},{6,4},{7,5},{8,8},{9,9},{10,10... | collective-permute-start | bytes 786440 | tf_op jit(solution)/shard_map/ppermute | solution.py:326
  45.5 4.8 %collective-permute-start.9 = (bf16[2,128,512]{2,1,0:T(8,128)(2,1)S(1)}, bf16[2,128,512]{2,1,0:T(8,128)(2,1)S(1)}, u32[]{:S(2)}, u32[]{:S(2)}) collective-permute-start(bf16[2,128,512]{2,1,0:T(8,128)(2,1)S(1)} %get-tuple-element.48), channel_id=1, source_target_pairs={{2,4},{3,5},{4,2},{5,3},{0,0},{1,1},{6,6},{7,7},{8,8},{9,9},{10,10... | collective-permute-start | bytes 786440 | tf_op jit(solution)/shard_map/ppermute | solution.py:326
  46.2 8.3 %collective-permute-start.10 = (bf16[2,128,512]{2,1,0:T(8,128)(2,1)S(1)}, bf16[2,128,512]{2,1,0:T(8,128)(2,1)S(1)}, u32[]{:S(2)}, u32[]{:S(2)}) collective-permute-start(bf16[2,128,512]{2,1,0:T(8,128)(2,1)S(1)} %get-tuple-element.49), channel_id=1, source_target_pairs={{0,1},{2,3},{4,5},{6,7},{1,0},{3,2},{5,4},{7,6},{8,8},{9,9},{10,10... | collective-permute-start | bytes 786440 | tf_op jit(solution)/shard_map/ppermute | solution.py:326
  56.2 24.3 %collective-permute-start.15 = (bf16[512,512]{1,0:T(8,128)(2,1)S(1)}, bf16[512,512]{1,0:T(8,128)(2,1)S(1)}, u32[]{:S(2)}, u32[]{:S(2)}) collective-permute-start(bf16[512,512]{1,0:T(8,128)(2,1)S(1)} %shard_map.96), channel_id=1, source_target_pairs={{24,16},{25,17},{26,18},{27,19},{28,20},{29,21},{30,22},{31,23},{0... | collective-permute-start | bytes 1572872 | tf_op jit(solution)/shard_map/ppermute | solution.py:281
  56.3 9.6 %collective-permute-start.16 = (bf16[256,512]{1,0:T(8,128)(2,1)S(1)}, bf16[256,512]{1,0:T(8,128)(2,1)S(1)}, u32[]{:S(2)}, u32[]{:S(2)}) collective-permute-start(bf16[256,512]{1,0:T(8,128)(2,1)S(1)} %get-tuple-element.59), channel_id=1, source_target_pairs={{0,1},{1,0},{2,3},{3,2},{4,5},{5,4},{6,7},{7,6},{8,9},{9,8},{10,11... | collective-permute-start | bytes 786440 | tf_op jit(solution)/shard_map/ppermute | solution.py:419
  57.9 18.3 %collective-permute-start.12 = (bf16[2,128,512]{2,1,0:T(8,128)(2,1)S(1)}, bf16[2,128,512]{2,1,0:T(8,128)(2,1)S(1)}, u32[]{:S(2)}, u32[]{:S(2)}) collective-permute-start(bf16[2,128,512]{2,1,0:T(8,128)(2,1)S(1)} %get-tuple-element.54), channel_id=1, source_target_pairs={{0,2},{1,3},{2,0},{3,1},{4,6},{5,7},{6,4},{7,5},{8,8},{9,9},{10,10... | collective-permute-start | bytes 786440 | tf_op jit(solution)/shard_map/ppermute | solution.py:326
  62.8 13.5 %collective-permute-start.13 = (bf16[2,128,512]{2,1,0:T(8,128)(2,1)S(1)}, bf16[2,128,512]{2,1,0:T(8,128)(2,1)S(1)}, u32[]{:S(2)}, u32[]{:S(2)}) collective-permute-start(bf16[2,128,512]{2,1,0:T(8,128)(2,1)S(1)} %get-tuple-element.55), channel_id=1, source_target_pairs={{2,4},{3,5},{4,2},{5,3},{0,0},{1,1},{6,6},{7,7},{8,8},{9,9},{10,10... | collective-permute-start | bytes 786440 | tf_op jit(solution)/shard_map/ppermute | solution.py:326
  63.4 12.8 %collective-permute-start.14 = (bf16[2,128,512]{2,1,0:T(8,128)(2,1)S(1)}, bf16[2,128,512]{2,1,0:T(8,128)(2,1)S(1)}, u32[]{:S(2)}, u32[]{:S(2)}) collective-permute-start(bf16[2,128,512]{2,1,0:T(8,128)(2,1)S(1)} %get-tuple-element.56), channel_id=1, source_target_pairs={{0,1},{2,3},{4,5},{6,7},{1,0},{3,2},{5,4},{7,6},{8,8},{9,9},{10,10... | collective-permute-start | bytes 786440 | tf_op jit(solution)/shard_map/ppermute | solution.py:326
  66.0 10.1 %collective-permute-start.17 = (bf16[128,512]{1,0:T(8,128)(2,1)S(1)}, bf16[128,512]{1,0:T(8,128)(2,1)S(1)}, u32[]{:S(2)}, u32[]{:S(2)}) collective-permute-start(bf16[128,512]{1,0:T(8,128)(2,1)S(1)} %get-tuple-element.61), channel_id=1, source_target_pairs={{0,4},{1,5},{2,6},{3,7},{4,0},{5,1},{6,2},{7,3},{8,12},{9,13},{10,... | collective-permute-start | bytes 393224 | tf_op jit(solution)/shard_map/ppermute | solution.py:419
  76.1 4.3 %collective-permute-start.18 = (bf16[64,512]{1,0:T(8,128)(2,1)S(1)}, bf16[64,512]{1,0:T(8,128)(2,1)S(1)}, u32[]{:S(2)}, u32[]{:S(2)}) collective-permute-start(bf16[64,512]{1,0:T(8,128)(2,1)S(1)} %get-tuple-element.63), channel_id=1, source_target_pairs={{0,2},{1,3},{2,0},{3,1},{4,6},{5,7},{6,4},{7,5},{8,10},{9,11},{10,... | collective-permute-start | bytes 196616 | tf_op jit(solution)/shard_map/ppermute | solution.py:425

commit v6 on v5

--- a/solution.py
+++ b/solution.py
@@ -25,17 +25,6 @@
         if pairs:
             phases.append((first, pairs))
     return phases
-
-
-def completed(pairs, devices):
-    pairs = list(pairs)
-    silent = set(range(devices)) - {source for source, _ in pairs}
-    unfed = set(range(devices)) - {target for _, target in pairs}
-    back = [(target, source) for source, target in pairs if target in silent and source in unfed]
-    pairs += back
-    silent -= {source for source, _ in back}
-    unfed -= {target for _, target in back}
-    return pairs + [(device, device) for device in sorted(silent & unfed)]
 
 
 def side(phase):
@@ -263,7 +252,6 @@
 def per_device(stored, cotangent, weight, local_edges, halo_edges, pattern, pick):
     sections, rows, columns = (lax.axis_size(name) for name in AXES)
     here = lax.axis_index("pipe")
-    devices = sections * rows * columns
     lower = sections // 2
     upper = sections - lower
     top = sections - 1
@@ -271,14 +259,34 @@
     def flat(section, x, y):
         return (section * rows + x) * columns + y
 
-    def to_sections(value, moves):
+    def to_sections(value, moves, back=True):
+        if back:
+            moves = moves + [(target, source) for source, target in moves]
         pairs = [
             (flat(source, x, y), flat(target, x, y))
             for source, target in moves
             for x in range(rows)
             for y in range(columns)
         ]
-        return lax.ppermute(value, AXES, completed(pairs, devices))
+        return lax.ppermute(value, AXES, pairs)
+
+    def tile_swaps(axis, couples, lead):
+        partner = {}
+        for x in range(rows):
+            for y in range(columns):
+                if axis == "tx":
+                    spare = (x, y ^ 1) if columns % 2 == 0 else (x, y)
+                    near = [((a, y), (b, y)) for low, high in couples for a, b in ((low, high), (high, low)) if a == x]
+                else:
+                    spare = (x ^ 1, y) if rows % 2 == 0 else (x, y)
+                    near = [((x, a), (x, b)) for low, high in couples for a, b in ((low, high), (high, low)) if a == y]
+                partner[x, y] = near[0][1] if near else spare
+        others = [p for p in range(sections) if p != lead]
+        pairs = [(flat(lead, *tile), flat(lead, *other)) for tile, other in partner.items()]
+        for tile in partner:
+            for source, target in zip(others, others[1:] + others[:1]):
+                pairs.append((flat(source, *tile), flat(target, *tile)))
+        return pairs
 
     batches, nodes, width = stored.shape[1], stored.shape[4], stored.shape[5]
     blocks, block = local_edges.shape[3], local_edges.shape[5]
@@ -291,17 +299,7 @@
     for axis, base, count in (("tx", 0, rows), ("ty", 2, columns)):
         for first, couples in swap_phases(count):
             phases.append((axis, base, first, count))
-            route = {}
-            for lead in {0, top}:
-                route[lead] = completed([
-                    (
-                        flat(lead, *((a, other) if axis == "tx" else (other, a))),
-                        flat(lead, *((b, other) if axis == "tx" else (other, b))),
-                    )
-                    for low, high in couples
-                    for a, b in ((low, high), (high, low))
-                    for other in range(columns if axis == "tx" else rows)
-                ], devices)
+            route = {lead: tile_swaps(axis, couples, lead) for lead in {0, top}}
             routes.append(route)
     phases = tuple(phases)
     splits, left = [], rows * columns
@@ -384,7 +382,7 @@
         if section == lower - 1:
             upstream = call(close_kernel, [mask, total, *arrived], [whole], 0)[0]
             results[section + 1] = upstream
-            upstream = to_sections(upstream, [(top, 0)])
+            upstream = to_sections(upstream, [(top, 0)], False)
             grad, message, *outs = call(
                 step_kernel, [layer_here, mixing, upstream], [whole, whole] + sent, cost
             )

time: 82 us -> 77.7 us (0.948)
  starting transfers between devices: 48.9 us -> 20.1 us
  waiting for transfers between devices: 22.8 us -> 47.6 us
    ppermute x4, starting transfers between devices: 24.9 us -> 2.08 us  [to_sections(): return lax.ppermute(value, AXES, pairs)]
    ppermute x12, waiting for transfers between devices: 4.35 us -> 25.7 us  [exchange(): lax.ppermute(out, AXES, route[lead])]
    ppermute x12, starting transfers between devices: 19.6 us -> 12.7 us  [exchange(): lax.ppermute(out, AXES, route[lead])]
    ppermute x4, waiting for transfers between devices: 6.86 us -> 9.21 us  [to_sections(): return lax.ppermute(value, AXES, pairs)]
    ppermute x2, waiting for transfers between devices: 7.33 us -> 9 us  [per_device(): got = lax.ppermute(parcel, AXES, pairs)]
  transfers between devices with their start and end apart: 19 -> 19, of which waited for: 5 -> 13; matrix products, arithmetic and copies ran while one was open for 0% -> 0% of each run, Pallas kernels for 2% -> 2%
where the time goes in v6:
time: 77.7 us; the launch traced here: 77.5 us
  waiting for transfers between devices  47.6 us (61%)
  starting transfers between devices  20.1 us (26%)
  Pallas kernels  9.01 us (12%)
  between operations  0.78 us (1%)
    ppermute x12, waiting for transfers between devices, exchange(): lax.ppermute(out, AXES, route[lead])  25.7 us
    ppermute x12, starting transfers between devices, exchange(): lax.ppermute(out, AXES, route[lead])  12.7 us
    ppermute x4, waiting for transfers between devices, to_sections(): return lax.ppermute(value, AXES, pairs)  9.21 us
    pallas_call x14, Pallas kernels, call(): pl.pallas_call(body, out_shape=[kind(shape, dtype) for shape, dtype in ou...  9.01 us
    ppermute x2, waiting for transfers between devices, per_device(): got = lax.ppermute(parcel, AXES, pairs)  9 us
    ppermute x2, starting transfers between devices, per_device(): got = lax.ppermute(parcel, AXES, pairs)  4.74 us
    ppermute x1, waiting for transfers between devices, per_device(): got = lax.ppermute(parcel, AXES, splits[-1][1])  3.76 us
    ppermute x4, starting transfers between devices, to_sections(): return lax.ppermute(value, AXES, pairs)  2.08 us
  transfers between devices with their start and end apart: 19, of which 13 were waited for; matrix products, arithmetic and copies ran while one was open for 0% of the time, Pallas kernels for 2%

profile of v6, /device:TPU:0, one launch (start us, length us, event | category | flops | bytes accessed | tf_op | source)
XLA Modules:
  0.0 77.5 jit_solution(16839187904596125794)
XLA Ops:
  0.6 2.8 %shard_map.86 = (bf16[2,512,512]{2,1,0:T(8,128)(2,1)S(1)}, bf16[2,640,256]{2,1,0:T(8,128)(2,1)S(1)}, f32[12,1,512]{2,1,0:T(1,128)S(1)}, bf16[512,512]{1,0:T(8,12...) custom-call(bf16[512,512]{1,0:T(8,128)(2,1)} %bitcast.11, ...), custom_call_target="tpu_custom_call" | custom-call | flops 738197504 | bytes 5922944 | tf_op jit(solution)/shard_map/pallas_call | solution.py:241
  3.5 0.5 collective-permute-start.3
  4.1 2.6 %collective-permute-start.1 = (bf16[2,128,512]{2,1,0:T(8,128)(2,1)S(1)}, bf16[2,128,512]{2,1,0:T(8,128)(2,1)S(1)}, u32[]{:S(2)}, u32[]{:S(2)}) collective-permute-start(bf16[2,128,512]{2,1,0:T(8,128)(2,1)S(1)} %get-tuple-element.38), channel_id=1, source_target_pairs={{24,25},{25,24},{26,28},{27,29},{28,26},{29,27},{30,31},{31,30},{0... | collective-permute-start | bytes 786440 | tf_op jit(solution)/shard_map/ppermute | solution.py:324
  7.0 3.9 %collective-permute-done.refs_0_ = bf16[2,128,512]{2,1,0:T(8,128)(2,1)S(1)} collective-permute-done((bf16[2,128,512]{2,1,0:T(8,128)(2,1)S(1)}, bf16[2,128,512]{2,1,0:T(8,128)(2,1)S(1)}, u32[]{:S(2)}, u32[]{:S(2)}) %collective-permute-start) | collective-permute-done | bytes 262176 | tf_op jit(solution)/shard_map/ppermute | solution.py:324
  10.9 2.8 %collective-permute-done.1.refs_1_ = bf16[2,128,512]{2,1,0:T(8,128)(2,1)S(1)} collective-permute-done((bf16[2,128,512]{2,1,0:T(8,128)(2,1)S(1)}, bf16[2,128,512]{2,1,0:T(8,128)(2,1)S(1)}, u32[]{:S(2)}, u32[]{:S(2)}) %collective-permute-start.1) | collective-permute-done | bytes 262176 | tf_op jit(solution)/shard_map/ppermute | solution.py:324
  13.7 2.8 %collective-permute-done.2.refs_2_ = bf16[2,128,512]{2,1,0:T(8,128)(2,1)S(1)} collective-permute-done((bf16[2,128,512]{2,1,0:T(8,128)(2,1)S(1)}, bf16[2,128,512]{2,1,0:T(8,128)(2,1)S(1)}, u32[]{:S(2)}, u32[]{:S(2)}) %collective-permute-start.2) | collective-permute-done | bytes 262176 | tf_op jit(solution)/shard_map/ppermute | solution.py:324
  16.5 0.9 %shard_map.88 = (bf16[512,512]{1,0:T(8,128)(2,1)S(1)}, bf16[512,512]{1,0:T(8,128)(2,1)S(1)}, bf16[512,512]{1,0:T(8,128)(2,1)S(1)}, bf16[2,128,512]{2,1,0:T(8,128...) custom-call(f32[12,1,512]{2,1,0:T(1,128)S(1)} %get-tuple-element.34.mask_ref, ...), custom_call_target="tpu_custom_call" | custom-call | flops 469762048 | bytes 5922816 | tf_op jit(solution)/shard_map/pallas_call | solution.py:241
  17.5 1.5 %collective-permute-start.5 = (bf16[2,128,512]{2,1,0:T(8,128)(2,1)S(1)}, bf16[2,128,512]{2,1,0:T(8,128)(2,1)S(1)}, u32[]{:S(2)}, u32[]{:S(2)}) collective-permute-start(bf16[2,128,512]{2,1,0:T(8,128)(2,1)S(1)} %get-tuple-element.44), channel_id=1, source_target_pairs={{24,25},{25,24},{26,28},{27,29},{28,26},{29,27},{30,31},{31,30},{0... | collective-permute-start | bytes 786440 | tf_op jit(solution)/shard_map/ppermute | solution.py:324
  19.0 0.6 collective-permute-start.6
  19.9 3.9 %collective-permute-done.4.refs_0_ = bf16[2,128,512]{2,1,0:T(8,128)(2,1)S(1)} collective-permute-done((bf16[2,128,512]{2,1,0:T(8,128)(2,1)S(1)}, bf16[2,128,512]{2,1,0:T(8,128)(2,1)S(1)}, u32[]{:S(2)}, u32[]{:S(2)}) %collective-permute-start.4) | collective-permute-done | bytes 262176 | tf_op jit(solution)/shard_map/ppermute | solution.py:324
  23.9 2.8 %collective-permute-done.5.refs_1_ = bf16[2,128,512]{2,1,0:T(8,128)(2,1)S(1)} collective-permute-done((bf16[2,128,512]{2,1,0:T(8,128)(2,1)S(1)}, bf16[2,128,512]{2,1,0:T(8,128)(2,1)S(1)}, u32[]{:S(2)}, u32[]{:S(2)}) %collective-permute-start.5) | collective-permute-done | bytes 262176 | tf_op jit(solution)/shard_map/ppermute | solution.py:324
  26.7 2.8 %collective-permute-done.6.refs_2_ = bf16[2,128,512]{2,1,0:T(8,128)(2,1)S(1)} collective-permute-done((bf16[2,128,512]{2,1,0:T(8,128)(2,1)S(1)}, bf16[2,128,512]{2,1,0:T(8,128)(2,1)S(1)}, u32[]{:S(2)}, u32[]{:S(2)}) %collective-permute-start.6) | collective-permute-done | bytes 262176 | tf_op jit(solution)/shard_map/ppermute | solution.py:324
  29.8 1.3 %collective-permute-start.7 = (bf16[512,512]{1,0:T(8,128)(2,1)S(1)}, bf16[512,512]{1,0:T(8,128)(2,1)S(1)}, u32[]{:S(2)}, u32[]{:S(2)}) collective-permute-start(bf16[512,512]{1,0:T(8,128)(2,1)S(1)} %shard_map.90.top_ref), channel_id=1, source_target_pairs={{24,0},{25,1},{26,2},{27,3},{28,4},{29,5},{30,6},{31,7}} | collective-permute-start | bytes 1572872 | tf_op jit(solution)/shard_map/ppermute | solution.py:271
  31.1 9.2 %collective-permute-done.7.upstream_ref = bf16[512,512]{1,0:T(8,128)(2,1)S(1)} collective-permute-done((bf16[512,512]{1,0:T(8,128)(2,1)S(1)}, bf16[512,512]{1,0:T(8,128)(2,1)S(1)}, u32[]{:S(2)}, u32[]{:S(2)}) %collective-permute-start.7) | collective-permute-done | bytes 524320 | tf_op jit(solution)/shard_map/ppermute | solution.py:271
  40.3 0.8 shard_map.91
  41.2 2.2 %collective-permute-start.8 = (bf16[2,128,512]{2,1,0:T(8,128)(2,1)S(1)}, bf16[2,128,512]{2,1,0:T(8,128)(2,1)S(1)}, u32[]{:S(2)}, u32[]{:S(2)}) collective-permute-start(bf16[2,128,512]{2,1,0:T(8,128)(2,1)S(1)} %get-tuple-element.47), channel_id=1, source_target_pairs={{0,2},{1,3},{2,0},{3,1},{4,6},{5,7},{6,4},{7,5},{8,16},{16,24},{24... | collective-permute-start | bytes 786440 | tf_op jit(solution)/shard_map/ppermute | solution.py:324
  43.4 1.5 %collective-permute-start.9 = (bf16[2,128,512]{2,1,0:T(8,128)(2,1)S(1)}, bf16[2,128,512]{2,1,0:T(8,128)(2,1)S(1)}, u32[]{:S(2)}, u32[]{:S(2)}) collective-permute-start(bf16[2,128,512]{2,1,0:T(8,128)(2,1)S(1)} %get-tuple-element.48), channel_id=1, source_target_pairs={{0,1},{1,0},{2,4},{3,5},{4,2},{5,3},{6,7},{7,6},{8,16},{16,24},{24... | collective-permute-start | bytes 786440 | tf_op jit(solution)/shard_map/ppermute | solution.py:324
  44.9 0.5 collective-permute-start.10
  45.9 1.8 %collective-permute-done.8.refs_0_ = bf16[2,128,512]{2,1,0:T(8,128)(2,1)S(1)} collective-permute-done((bf16[2,128,512]{2,1,0:T(8,128)(2,1)S(1)}, bf16[2,128,512]{2,1,0:T(8,128)(2,1)S(1)}, u32[]{:S(2)}, u32[]{:S(2)}) %collective-permute-start.8) | collective-permute-done | bytes 262176 | tf_op jit(solution)/shard_map/ppermute | solution.py:324
  47.8 2.0 %collective-permute-done.9.refs_1_ = bf16[2,128,512]{2,1,0:T(8,128)(2,1)S(1)} collective-permute-done((bf16[2,128,512]{2,1,0:T(8,128)(2,1)S(1)}, bf16[2,128,512]{2,1,0:T(8,128)(2,1)S(1)}, u32[]{:S(2)}, u32[]{:S(2)}) %collective-permute-start.9) | collective-permute-done | bytes 262176 | tf_op jit(solution)/shard_map/ppermute | solution.py:324
  49.8 2.8 %collective-permute-done.10.refs_2_ = bf16[2,128,512]{2,1,0:T(8,128)(2,1)S(1)} collective-permute-done((bf16[2,128,512]{2,1,0:T(8,128)(2,1)S(1)}, bf16[2,128,512]{2,1,0:T(8,128)(2,1)S(1)}, u32[]{:S(2)}, u32[]{:S(2)}) %collective-permute-start.10) | collective-permute-done | bytes 262176 | tf_op jit(solution)/shard_map/ppermute | solution.py:324
  52.6 1.7 %shard_map.95 = (bf16[512,512]{1,0:T(8,128)(2,1)S(1)}, f32[512,512]{1,0:T(8,128)S(1)}, bf16[2,128,512]{2,1,0:T(8,128)(2,1)S(1)}, bf16[2,128,512]{2,1,0:T(8,128)(...) custom-call(f32[12,1,512]{2,1,0:T(1,128)S(1)} %get-tuple-element.34.mask_ref, ...), custom_call_target="tpu_custom_call" | custom-call | flops 872415232 | bytes 8282112 | tf_op jit(solution)/shard_map/pallas_call | solution.py:241
  54.5 1.9 %collective-permute-start.16 = (bf16[256,512]{1,0:T(8,128)(2,1)S(1)}, bf16[256,512]{1,0:T(8,128)(2,1)S(1)}, u32[]{:S(2)}, u32[]{:S(2)}) collective-permute-start(bf16[256,512]{1,0:T(8,128)(2,1)S(1)} %get-tuple-element.59), channel_id=1, source_target_pairs={{0,1},{1,0},{2,3},{3,2},{4,5},{5,4},{6,7},{7,6},{8,9},{9,8},{10,11... | collective-permute-start | bytes 786440 | tf_op jit(solution)/shard_map/ppermute | solution.py:417
  56.5 1.5 %collective-permute-start.12 = (bf16[2,128,512]{2,1,0:T(8,128)(2,1)S(1)}, bf16[2,128,512]{2,1,0:T(8,128)(2,1)S(1)}, u32[]{:S(2)}, u32[]{:S(2)}) collective-permute-start(bf16[2,128,512]{2,1,0:T(8,128)(2,1)S(1)} %get-tuple-element.54), channel_id=1, source_target_pairs={{0,2},{1,3},{2,0},{3,1},{4,6},{5,7},{6,4},{7,5},{8,16},{16,24},{24... | collective-permute-start | bytes 786440 | tf_op jit(solution)/shard_map/ppermute | solution.py:324
  58.0 0.5 collective-permute-start.13
  58.5 1.5 %collective-permute-start.14 = (bf16[2,128,512]{2,1,0:T(8,128)(2,1)S(1)}, bf16[2,128,512]{2,1,0:T(8,128)(2,1)S(1)}, u32[]{:S(2)}, u32[]{:S(2)}) collective-permute-start(bf16[2,128,512]{2,1,0:T(8,128)(2,1)S(1)} %get-tuple-element.56), channel_id=1, source_target_pairs={{0,1},{1,0},{2,3},{3,2},{4,5},{5,4},{6,7},{7,6},{8,16},{16,24},{24... | collective-permute-start | bytes 786440 | tf_op jit(solution)/shard_map/ppermute | solution.py:324
  60.0 3.1 %collective-permute-done.16.got_ref = bf16[256,512]{1,0:T(8,128)(2,1)S(1)} collective-permute-done((bf16[256,512]{1,0:T(8,128)(2,1)S(1)}, bf16[256,512]{1,0:T(8,128)(2,1)S(1)}, u32[]{:S(2)}, u32[]{:S(2)}) %collective-permute-start.16) | collective-permute-done | bytes 262176 | tf_op jit(solution)/shard_map/ppermute | solution.py:417
  63.2 2.8 %collective-permute-start.17 = (bf16[128,512]{1,0:T(8,128)(2,1)S(1)}, bf16[128,512]{1,0:T(8,128)(2,1)S(1)}, u32[]{:S(2)}, u32[]{:S(2)}) collective-permute-start(bf16[128,512]{1,0:T(8,128)(2,1)S(1)} %get-tuple-element.61), channel_id=1, source_target_pairs={{0,4},{1,5},{2,6},{3,7},{4,0},{5,1},{6,2},{7,3},{8,12},{9,13},{10,... | collective-permute-start | bytes 393224 | tf_op jit(solution)/shard_map/ppermute | solution.py:417
  66.0 5.9 %collective-permute-done.17.got_ref = bf16[128,512]{1,0:T(8,128)(2,1)S(1)} collective-permute-done((bf16[128,512]{1,0:T(8,128)(2,1)S(1)}, bf16[128,512]{1,0:T(8,128)(2,1)S(1)}, u32[]{:S(2)}, u32[]{:S(2)}) %collective-permute-start.17) | collective-permute-done | bytes 131104 | tf_op jit(solution)/shard_map/ppermute | solution.py:417
  72.0 0.6 collective-permute-start.18
  72.6 3.8 %collective-permute-done.18.refs_6_ = bf16[64,512]{1,0:T(8,128)(2,1)S(1)} collective-permute-done((bf16[64,512]{1,0:T(8,128)(2,1)S(1)}, bf16[64,512]{1,0:T(8,128)(2,1)S(1)}, u32[]{:S(2)}, u32[]{:S(2)}) %collective-permute-start.18) | collective-permute-done | bytes 65568 | tf_op jit(solution)/shard_map/ppermute | solution.py:423
  76.3 1.2 %shard_map.99 = (bf16[512,512]{1,0:T(8,128)(2,1)}, f32[64,512]{1,0:T(8,128)}) custom-call(f32[12,1,512]{2,1,0:T(1,128)S(1)} %get-tuple-element.34.mask_ref, f32[512,512]{1,0:T(8,128)S(1)} %get-tuple-element.53.total_ref, bf16[2,128,512]{2,1,0:T(8,128)(2,1)S(1)} %collective-permute-done.12.refs_0_, bf16[2,128,512]{2,1,0:T(8,128)(2,1)S(1)} %collective-permute-done.13.refs_1_, ...), custom_call_target="tpu_custom_call" | custom-call | bytes 3760128 | tf_op jit(solution)/shard_map/pallas_call | solution.py:241
  (24 shorter events, 2.2 us)
Async XLA Ops:
  0.6 6.1 %copy-start.1 = (bf16[2,1,1,256,512]{4,3,2,1,0:T(8,128)(2,1)S(1)}, bf16[2,1,1,256,512]{4,3,2,1,0:T(8,128)(2,1)}, u32[]{:S(2)}) copy-start(bf16[2,1,1,256,512]{4,3,2,1,0:T(8,128)(2,1)} %param.8) | copy-start | bytes 1572868
  3.5 13.0 %collective-permute-start.3 = (bf16[2,512,512]{2,1,0:T(8,128)(2,1)S(1)}, bf16[2,512,512]{2,1,0:T(8,128)(2,1)S(1)}, u32[]{:S(2)}, u32[]{:S(2)}) collective-permute-start(bf16[2,512,512]{2,1,0:T(8,128)(2,1)S(1)} %get-tuple-element.40.refs_6_), channel_id=1, source_target_pairs={{16,24},{17,25},{18,26},{19,27},{20,28},{21,29},{22,30},{23,31},{8... | collective-permute-start | bytes 3145736 | tf_op jit(solution)/shard_map/ppermute | solution.py:271
  4.0 6.9 %collective-permute-start = (bf16[2,128,512]{2,1,0:T(8,128)(2,1)S(1)}, bf16[2,128,512]{2,1,0:T(8,128)(2,1)S(1)}, u32[]{:S(2)}, u32[]{:S(2)}) collective-permute-start(bf16[2,128,512]{2,1,0:T(8,128)(2,1)S(1)} %get-tuple-element.37), channel_id=1, source_target_pairs={{24,26},{25,27},{26,24},{27,25},{28,30},{29,31},{30,28},{31,29},{0... | collective-permute-start | bytes 786440 | tf_op jit(solution)/shard_map/ppermute | solution.py:324
  4.1 9.6 %collective-permute-start.1 = (bf16[2,128,512]{2,1,0:T(8,128)(2,1)S(1)}, bf16[2,128,512]{2,1,0:T(8,128)(2,1)S(1)}, u32[]{:S(2)}, u32[]{:S(2)}) collective-permute-start(bf16[2,128,512]{2,1,0:T(8,128)(2,1)S(1)} %get-tuple-element.38), channel_id=1, source_target_pairs={{24,25},{25,24},{26,28},{27,29},{28,26},{29,27},{30,31},{31,30},{0... | collective-permute-start | bytes 786440 | tf_op jit(solution)/shard_map/ppermute | solution.py:324
  6.7 9.9 %collective-permute-start.2 = (bf16[2,128,512]{2,1,0:T(8,128)(2,1)S(1)}, bf16[2,128,512]{2,1,0:T(8,128)(2,1)S(1)}, u32[]{:S(2)}, u32[]{:S(2)}) collective-permute-start(bf16[2,128,512]{2,1,0:T(8,128)(2,1)S(1)} %get-tuple-element.39), channel_id=1, source_target_pairs={{24,25},{25,24},{26,27},{27,26},{28,29},{29,28},{30,31},{31,30},{0... | collective-permute-start | bytes 786440 | tf_op jit(solution)/shard_map/ppermute | solution.py:324
  17.4 6.4 %collective-permute-start.4 = (bf16[2,128,512]{2,1,0:T(8,128)(2,1)S(1)}, bf16[2,128,512]{2,1,0:T(8,128)(2,1)S(1)}, u32[]{:S(2)}, u32[]{:S(2)}) collective-permute-start(bf16[2,128,512]{2,1,0:T(8,128)(2,1)S(1)} %get-tuple-element.43), channel_id=1, source_target_pairs={{24,26},{25,27},{26,24},{27,25},{28,30},{29,31},{30,28},{31,29},{0... | collective-permute-start | bytes 786440 | tf_op jit(solution)/shard_map/ppermute | solution.py:324
  17.5 9.2 %collective-permute-start.5 = (bf16[2,128,512]{2,1,0:T(8,128)(2,1)S(1)}, bf16[2,128,512]{2,1,0:T(8,128)(2,1)S(1)}, u32[]{:S(2)}, u32[]{:S(2)}) collective-permute-start(bf16[2,128,512]{2,1,0:T(8,128)(2,1)S(1)} %get-tuple-element.44), channel_id=1, source_target_pairs={{24,25},{25,24},{26,28},{27,29},{28,26},{29,27},{30,31},{31,30},{0... | collective-permute-start | bytes 786440 | tf_op jit(solution)/shard_map/ppermute | solution.py:324
  19.0 10.4 %collective-permute-start.6 = (bf16[2,128,512]{2,1,0:T(8,128)(2,1)S(1)}, bf16[2,128,512]{2,1,0:T(8,128)(2,1)S(1)}, u32[]{:S(2)}, u32[]{:S(2)}) collective-permute-start(bf16[2,128,512]{2,1,0:T(8,128)(2,1)S(1)} %get-tuple-element.45), channel_id=1, source_target_pairs={{24,25},{25,24},{26,27},{27,26},{28,29},{29,28},{30,31},{31,30},{0... | collective-permute-start | bytes 786440 | tf_op jit(solution)/shard_map/ppermute | solution.py:324
  29.8 10.5 %collective-permute-start.7 = (bf16[512,512]{1,0:T(8,128)(2,1)S(1)}, bf16[512,512]{1,0:T(8,128)(2,1)S(1)}, u32[]{:S(2)}, u32[]{:S(2)}) collective-permute-start(bf16[512,512]{1,0:T(8,128)(2,1)S(1)} %shard_map.90.top_ref), channel_id=1, source_target_pairs={{24,0},{25,1},{26,2},{27,3},{28,4},{29,5},{30,6},{31,7}} | collective-permute-start | bytes 1572872 | tf_op jit(solution)/shard_map/ppermute | solution.py:271
  41.1 4.3 %copy-start = (bf16[1,2,1,1,256,512]{5,4,3,2,1,0:T(8,128)(2,1)S(1)}, bf16[1,2,1,1,256,512]{5,4,3,2,1,0:T(8,128)(2,1)}, u32[]{:S(2)}) copy-start(bf16[1,2,1,1,256,512]{5,4,3,2,1,0:T(8,128)(2,1)} %param.7) | copy-start | bytes 1572868
  41.2 11.4 %collective-permute-start.11 = (bf16[512,512]{1,0:T(8,128)(2,1)S(1)}, bf16[512,512]{1,0:T(8,128)(2,1)S(1)}, u32[]{:S(2)}, u32[]{:S(2)}) collective-permute-start(bf16[512,512]{1,0:T(8,128)(2,1)S(1)} %shard_map.94), channel_id=1, source_target_pairs={{24,16},{25,17},{26,18},{27,19},{28,20},{29,21},{30,22},{31,23},{0... | collective-permute-start | bytes 1572872 | tf_op jit(solution)/shard_map/ppermute | solution.py:271
  41.2 6.5 %collective-permute-start.8 = (bf16[2,128,512]{2,1,0:T(8,128)(2,1)S(1)}, bf16[2,128,512]{2,1,0:T(8,128)(2,1)S(1)}, u32[]{:S(2)}, u32[]{:S(2)}) collective-permute-start(bf16[2,128,512]{2,1,0:T(8,128)(2,1)S(1)} %get-tuple-element.47), channel_id=1, source_target_pairs={{0,2},{1,3},{2,0},{3,1},{4,6},{5,7},{6,4},{7,5},{8,16},{16,24},{24... | collective-permute-start | bytes 786440 | tf_op jit(solution)/shard_map/ppermute | solution.py:324
  43.4 6.4 %collective-permute-start.9 = (bf16[2,128,512]{2,1,0:T(8,128)(2,1)S(1)}, bf16[2,128,512]{2,1,0:T(8,128)(2,1)S(1)}, u32[]{:S(2)}, u32[]{:S(2)}) collective-permute-start(bf16[2,128,512]{2,1,0:T(8,128)(2,1)S(1)} %get-tuple-element.48), channel_id=1, source_target_pairs={{0,1},{1,0},{2,4},{3,5},{4,2},{5,3},{6,7},{7,6},{8,16},{16,24},{24... | collective-permute-start | bytes 786440 | tf_op jit(solution)/shard_map/ppermute | solution.py:324
  44.9 7.7 %collective-permute-start.10 = (bf16[2,128,512]{2,1,0:T(8,128)(2,1)S(1)}, bf16[2,128,512]{2,1,0:T(8,128)(2,1)S(1)}, u32[]{:S(2)}, u32[]{:S(2)}) collective-permute-start(bf16[2,128,512]{2,1,0:T(8,128)(2,1)S(1)} %get-tuple-element.49), channel_id=1, source_target_pairs={{0,1},{1,0},{2,3},{3,2},{4,5},{5,4},{6,7},{7,6},{8,16},{16,24},{24... | collective-permute-start | bytes 786440 | tf_op jit(solution)/shard_map/ppermute | solution.py:324
  54.3 22.0 %collective-permute-start.15 = (bf16[512,512]{1,0:T(8,128)(2,1)S(1)}, bf16[512,512]{1,0:T(8,128)(2,1)S(1)}, u32[]{:S(2)}, u32[]{:S(2)}) collective-permute-start(bf16[512,512]{1,0:T(8,128)(2,1)S(1)} %shard_map.96), channel_id=1, source_target_pairs={{24,16},{25,17},{26,18},{27,19},{28,20},{29,21},{30,22},{31,23},{0... | collective-permute-start | bytes 1572872 | tf_op jit(solution)/shard_map/ppermute | solution.py:271
  54.5 8.6 %collective-permute-start.16 = (bf16[256,512]{1,0:T(8,128)(2,1)S(1)}, bf16[256,512]{1,0:T(8,128)(2,1)S(1)}, u32[]{:S(2)}, u32[]{:S(2)}) collective-permute-start(bf16[256,512]{1,0:T(8,128)(2,1)S(1)} %get-tuple-element.59), channel_id=1, source_target_pairs={{0,1},{1,0},{2,3},{3,2},{4,5},{5,4},{6,7},{7,6},{8,9},{9,8},{10,11... | collective-permute-start | bytes 786440 | tf_op jit(solution)/shard_map/ppermute | solution.py:417
  56.5 16.1 %collective-permute-start.12 = (bf16[2,128,512]{2,1,0:T(8,128)(2,1)S(1)}, bf16[2,128,512]{2,1,0:T(8,128)(2,1)S(1)}, u32[]{:S(2)}, u32[]{:S(2)}) collective-permute-start(bf16[2,128,512]{2,1,0:T(8,128)(2,1)S(1)} %get-tuple-element.54), channel_id=1, source_target_pairs={{0,2},{1,3},{2,0},{3,1},{4,6},{5,7},{6,4},{7,5},{8,16},{16,24},{24... | collective-permute-start | bytes 786440 | tf_op jit(solution)/shard_map/ppermute | solution.py:324
  58.0 14.5 %collective-permute-start.13 = (bf16[2,128,512]{2,1,0:T(8,128)(2,1)S(1)}, bf16[2,128,512]{2,1,0:T(8,128)(2,1)S(1)}, u32[]{:S(2)}, u32[]{:S(2)}) collective-permute-start(bf16[2,128,512]{2,1,0:T(8,128)(2,1)S(1)} %get-tuple-element.55), channel_id=1, source_target_pairs={{0,1},{1,0},{2,4},{3,5},{4,2},{5,3},{6,7},{7,6},{8,16},{16,24},{24... | collective-permute-start | bytes 786440 | tf_op jit(solution)/shard_map/ppermute | solution.py:324
  58.5 14.0 %collective-permute-start.14 = (bf16[2,128,512]{2,1,0:T(8,128)(2,1)S(1)}, bf16[2,128,512]{2,1,0:T(8,128)(2,1)S(1)}, u32[]{:S(2)}, u32[]{:S(2)}) collective-permute-start(bf16[2,128,512]{2,1,0:T(8,128)(2,1)S(1)} %get-tuple-element.56), channel_id=1, source_target_pairs={{0,1},{1,0},{2,3},{3,2},{4,5},{5,4},{6,7},{7,6},{8,16},{16,24},{24... | collective-permute-start | bytes 786440 | tf_op jit(solution)/shard_map/ppermute | solution.py:324
  63.2 8.7 %collective-permute-start.17 = (bf16[128,512]{1,0:T(8,128)(2,1)S(1)}, bf16[128,512]{1,0:T(8,128)(2,1)S(1)}, u32[]{:S(2)}, u32[]{:S(2)}) collective-permute-start(bf16[128,512]{1,0:T(8,128)(2,1)S(1)} %get-tuple-element.61), channel_id=1, source_target_pairs={{0,4},{1,5},{2,6},{3,7},{4,0},{5,1},{6,2},{7,3},{8,12},{9,13},{10,... | collective-permute-start | bytes 393224 | tf_op jit(solution)/shard_map/ppermute | solution.py:417
  72.0 4.3 %collective-permute-start.18 = (bf16[64,512]{1,0:T(8,128)(2,1)S(1)}, bf16[64,512]{1,0:T(8,128)(2,1)S(1)}, u32[]{:S(2)}, u32[]{:S(2)}) collective-permute-start(bf16[64,512]{1,0:T(8,128)(2,1)S(1)} %get-tuple-element.63), channel_id=1, source_target_pairs={{0,2},{1,3},{2,0},{3,1},{4,6},{5,7},{6,4},{7,5},{8,10},{9,11},{10,... | collective-permute-start | bytes 196616 | tf_op jit(solution)/shard_map/ppermute | solution.py:423

commit v7 on v6

--- a/solution.py
+++ b/solution.py
@@ -259,9 +259,11 @@
     def flat(section, x, y):
         return (section * rows + x) * columns + y
 
-    def to_sections(value, moves, back=True):
+    def to_sections(value, moves, back=True, crossed=False):
         if back:
-            moves = moves + [(target, source) for source, target in moves]
+            returns = [source for source, _ in moves]
+            returns = returns[::-1] if crossed else returns
+            moves = moves + [(target, source) for (_, target), source in zip(moves, returns)]
         pairs = [
             (flat(source, x, y), flat(target, x, y))
             for source, target in moves
@@ -270,23 +272,45 @@
         ]
         return lax.ppermute(value, AXES, pairs)
 
-    def tile_swaps(axis, couples, lead):
-        partner = {}
-        for x in range(rows):
-            for y in range(columns):
-                if axis == "tx":
-                    spare = (x, y ^ 1) if columns % 2 == 0 else (x, y)
-                    near = [((a, y), (b, y)) for low, high in couples for a, b in ((low, high), (high, low)) if a == x]
-                else:
-                    spare = (x ^ 1, y) if rows % 2 == 0 else (x, y)
-                    near = [((x, a), (x, b)) for low, high in couples for a, b in ((low, high), (high, low)) if a == y]
-                partner[x, y] = near[0][1] if near else spare
+    def beside(axis):
+        def other(x, y):
+            if axis == "tx":
+                return (x ^ 1, y) if rows % 2 == 0 else (x, y)
+            return (x, y ^ 1) if columns % 2 == 0 else (x, y)
+
+        return other
+
+    def tile_swaps(axis, first, couples, lead):
+        places = {}
+        for low, high in couples:
+            places[low], places[high] = high, low
+        across = beside("ty" if axis == "tx" else "tx")
+
+        def swapped(x, y):
+            if axis == "tx":
+                return (places[x], y) if x in places else across(x, y)
+            return (x, places[y]) if y in places else across(x, y)
+
+        def same(x, y):
+            return (x, y)
+
         others = [p for p in range(sections) if p != lead]
-        pairs = [(flat(lead, *tile), flat(lead, *other)) for tile, other in partner.items()]
-        for tile in partner:
-            for source, target in zip(others, others[1:] + others[:1]):
-                pairs.append((flat(source, *tile), flat(target, *tile)))
-        return pairs
+        moves = [(lead, lead, swapped)]
+        if sections == 4:
+            buddy, inner, outer = lead ^ 1, 3 - (lead ^ 1), 3 - lead
+            if axis == "tx":
+                moves += [(buddy, inner, same), (inner, buddy, same)]
+                moves += [(outer, outer, beside("tx") if first else across)]
+            else:
+                moves += [(inner, outer, same), (outer, inner, same), (buddy, buddy, across)]
+        else:
+            moves += [(p, q, same) for p, q in zip(others, others[1:] + others[:1])]
+        return [
+            (flat(source, x, y), flat(target, *place(x, y)))
+            for source, target, place in moves
+            for x in range(rows)
+            for y in range(columns)
+        ]
 
     batches, nodes, width = stored.shape[1], stored.shape[4], stored.shape[5]
     blocks, block = local_edges.shape[3], local_edges.shape[5]
@@ -299,7 +323,7 @@
     for axis, base, count in (("tx", 0, rows), ("ty", 2, columns)):
         for first, couples in swap_phases(count):
             phases.append((axis, base, first, count))
-            route = {lead: tile_swaps(axis, couples, lead) for lead in {0, top}}
+            route = {lead: tile_swaps(axis, first, couples, lead) for lead in {0, top}}
             routes.append(route)
     phases = tuple(phases)
     splits, left = [], rows * columns
@@ -356,7 +380,7 @@
         moves = [(top - step, top)] + ([(step, 0)] if step < lower else [])
         layers.append(to_sections(layer, moves))
 
-    def fetch_home(values):
+    def fetch_home(values, crossed=False):
         got = None
         for step in range(1, upper):
             moves = [(top, top - step)]
@@ -366,7 +390,7 @@
                 value = call(
                     functools.partial(choose_kernel, top), [value, values[step]], [whole], 0
                 )[0]
-            new = to_sections(value, moves)
+            new = to_sections(value, moves, crossed=crossed)
             takes = here == top - step
             if step < lower:
                 takes = takes | (here == step)
@@ -423,14 +447,14 @@
         got = lax.ppermute(parcel, AXES, splits[-1][1])
         result, summed = call(
             functools.partial(last_kernel, top, count, scale),
-            [mask, total, *arrived, results[top], fetch_home(results), kept, got],
+            [mask, total, *arrived, results[top], fetch_home(results, True), kept, got],
             [whole, (kept.shape, F32)], 0, jax.ShapeDtypeStruct,
         )
     else:
         summed = scale * lax.psum_scatter(pieces[0], ("tx", "ty"), scatter_dimension=0, tiled=True)
         result = call(
             functools.partial(last_kernel, top, count, None),
-            [mask, total, *arrived, results[top], fetch_home(results)], [whole], 0,
+            [mask, total, *arrived, results[top], fetch_home(results, True)], [whole], 0,
             jax.ShapeDtypeStruct,
         )[0]
     return (summed[None], result.reshape(1, batches, 1, 1, nodes, width))

time: 77.7 us -> 68 us (0.88)
  waiting for transfers between devices: 47.6 us -> 41.7 us
  starting transfers between devices: 20.1 us -> 16.3 us
    ppermute x12, waiting for transfers between devices: 25.7 us -> 14.8 us  [exchange(): lax.ppermute(out, AXES, route[lead])]
    ppermute x4, waiting for transfers between devices: 9.21 us -> 11.7 us  [to_sections(): return lax.ppermute(value, AXES, pairs)]
    ppermute x2, starting transfers between devices: 4.74 us -> 2.54 us  [per_device(): got = lax.ppermute(parcel, AXES, pairs)]
    ppermute x2, waiting for transfers between devices: 9 us -> 11 us  [per_device(): got = lax.ppermute(parcel, AXES, pairs)]
    ppermute x12, starting transfers between devices: 12.7 us -> 11.8 us  [exchange(): lax.ppermute(out, AXES, route[lead])]
  transfers between devices with their start and end apart: 19 -> 19, of which waited for: 13 -> 10; matrix products, arithmetic and copies ran while one was open for 0% -> 0% of each run, Pallas kernels for 2% -> 2%
where the time goes in v7:
time: 68 us; the launch traced here: 67.9 us
  waiting for transfers between devices  41.7 us (61%)
  starting transfers between devices  16.3 us (24%)
  Pallas kernels  9.01 us (13%)
  between operations  0.8 us (1%)
    ppermute x12, waiting for transfers between devices, exchange(): lax.ppermute(out, AXES, route[lead])  14.8 us
    ppermute x12, starting transfers between devices, exchange(): lax.ppermute(out, AXES, route[lead])  11.8 us
    ppermute x4, waiting for transfers between devices, to_sections(): return lax.ppermute(value, AXES, pairs)  11.7 us
    ppermute x2, waiting for transfers between devices, per_device(): got = lax.ppermute(parcel, AXES, pairs)  11 us
    pallas_call x14, Pallas kernels, call(): pl.pallas_call(body, out_shape=[kind(shape, dtype) for shape, dtype in ou...  9.01 us
    ppermute x1, waiting for transfers between devices, per_device(): got = lax.ppermute(parcel, AXES, splits[-1][1])  4.22 us
    ppermute x2, starting transfers between devices, per_device(): got = lax.ppermute(parcel, AXES, pairs)  2.54 us
    ppermute x4, starting transfers between devices, to_sections(): return lax.ppermute(value, AXES, pairs)  1.9 us
  transfers between devices with their start and end apart: 19, of which 10 were waited for; matrix products, arithmetic and copies ran while one was open for 0% of the time, Pallas kernels for 2%

profile of v7, /device:TPU:0, one launch (start us, length us, event | category | flops | bytes accessed | tf_op | source)
XLA Modules:
  0.0 67.9 jit_solution(18018629620122905420)
XLA Ops:
  0.6 2.8 %shard_map.86 = (bf16[2,512,512]{2,1,0:T(8,128)(2,1)S(1)}, bf16[2,640,256]{2,1,0:T(8,128)(2,1)S(1)}, f32[12,1,512]{2,1,0:T(1,128)S(1)}, bf16[512,512]{1,0:T(8,12...) custom-call(bf16[512,512]{1,0:T(8,128)(2,1)} %bitcast.11, ...), custom_call_target="tpu_custom_call" | custom-call | flops 738197504 | bytes 5922944 | tf_op jit(solution)/shard_map/pallas_call | solution.py:241
  3.5 0.5 collective-permute-start.3
  4.0 2.6 %collective-permute-start = (bf16[2,128,512]{2,1,0:T(8,128)(2,1)S(1)}, bf16[2,128,512]{2,1,0:T(8,128)(2,1)S(1)}, u32[]{:S(2)}, u32[]{:S(2)}) collective-permute-start(bf16[2,128,512]{2,1,0:T(8,128)(2,1)S(1)} %get-tuple-element.37), channel_id=1, source_target_pairs={{24,26},{25,27},{26,24},{27,25},{28,30},{29,31},{30,28},{31,29},{1... | collective-permute-start | bytes 786440 | tf_op jit(solution)/shard_map/ppermute | solution.py:348
  6.6 1.6 %collective-permute-start.1 = (bf16[2,128,512]{2,1,0:T(8,128)(2,1)S(1)}, bf16[2,128,512]{2,1,0:T(8,128)(2,1)S(1)}, u32[]{:S(2)}, u32[]{:S(2)}) collective-permute-start(bf16[2,128,512]{2,1,0:T(8,128)(2,1)S(1)} %get-tuple-element.38), channel_id=1, source_target_pairs={{24,25},{25,24},{26,28},{27,29},{28,26},{29,27},{30,31},{31,30},{1... | collective-permute-start | bytes 786440 | tf_op jit(solution)/shard_map/ppermute | solution.py:348
  8.2 0.3 shard_map.87.total_ref
  8.5 2.5 %collective-permute-done.refs_0_ = bf16[2,128,512]{2,1,0:T(8,128)(2,1)S(1)} collective-permute-done((bf16[2,128,512]{2,1,0:T(8,128)(2,1)S(1)}, bf16[2,128,512]{2,1,0:T(8,128)(2,1)S(1)}, u32[]{:S(2)}, u32[]{:S(2)}) %collective-permute-start) | collective-permute-done | bytes 262176 | tf_op jit(solution)/shard_map/ppermute | solution.py:348
  10.9 2.0 %collective-permute-done.1.refs_1_ = bf16[2,128,512]{2,1,0:T(8,128)(2,1)S(1)} collective-permute-done((bf16[2,128,512]{2,1,0:T(8,128)(2,1)S(1)}, bf16[2,128,512]{2,1,0:T(8,128)(2,1)S(1)}, u32[]{:S(2)}, u32[]{:S(2)}) %collective-permute-start.1) | collective-permute-done | bytes 262176 | tf_op jit(solution)/shard_map/ppermute | solution.py:348
  13.0 0.9 %shard_map.88 = (bf16[512,512]{1,0:T(8,128)(2,1)S(1)}, bf16[512,512]{1,0:T(8,128)(2,1)S(1)}, bf16[512,512]{1,0:T(8,128)(2,1)S(1)}, bf16[2,128,512]{2,1,0:T(8,128...) custom-call(f32[12,1,512]{2,1,0:T(1,128)S(1)} %get-tuple-element.34.mask_ref, ...), custom_call_target="tpu_custom_call" | custom-call | flops 469762048 | bytes 5922816 | tf_op jit(solution)/shard_map/pallas_call | solution.py:241
  14.0 2.0 %collective-permute-start.5 = (bf16[2,128,512]{2,1,0:T(8,128)(2,1)S(1)}, bf16[2,128,512]{2,1,0:T(8,128)(2,1)S(1)}, u32[]{:S(2)}, u32[]{:S(2)}) collective-permute-start(bf16[2,128,512]{2,1,0:T(8,128)(2,1)S(1)} %get-tuple-element.44), channel_id=1, source_target_pairs={{24,25},{25,24},{26,28},{27,29},{28,26},{29,27},{30,31},{31,30},{1... | collective-permute-start | bytes 786440 | tf_op jit(solution)/shard_map/ppermute | solution.py:348
  16.0 0.3 collective-permute-start.6
  16.4 0.3 shard_map.89.total_ref
  16.7 3.6 %collective-permute-done.4.refs_0_ = bf16[2,128,512]{2,1,0:T(8,128)(2,1)S(1)} collective-permute-done((bf16[2,128,512]{2,1,0:T(8,128)(2,1)S(1)}, bf16[2,128,512]{2,1,0:T(8,128)(2,1)S(1)}, u32[]{:S(2)}, u32[]{:S(2)}) %collective-permute-start.4) | collective-permute-done | bytes 262176 | tf_op jit(solution)/shard_map/ppermute | solution.py:348
  20.4 0.4 shard_map.90.top_ref
  20.7 1.3 %collective-permute-start.7 = (bf16[512,512]{1,0:T(8,128)(2,1)S(1)}, bf16[512,512]{1,0:T(8,128)(2,1)S(1)}, u32[]{:S(2)}, u32[]{:S(2)}) collective-permute-start(bf16[512,512]{1,0:T(8,128)(2,1)S(1)} %shard_map.90.top_ref), channel_id=1, source_target_pairs={{24,0},{25,1},{26,2},{27,3},{28,4},{29,5},{30,6},{31,7}} | collective-permute-start | bytes 1572872 | tf_op jit(solution)/shard_map/ppermute | solution.py:273
  22.0 11.7 %collective-permute-done.7.upstream_ref = bf16[512,512]{1,0:T(8,128)(2,1)S(1)} collective-permute-done((bf16[512,512]{1,0:T(8,128)(2,1)S(1)}, bf16[512,512]{1,0:T(8,128)(2,1)S(1)}, u32[]{:S(2)}, u32[]{:S(2)}) %collective-permute-start.7) | collective-permute-done | bytes 524320 | tf_op jit(solution)/shard_map/ppermute | solution.py:273
  33.7 0.8 %shard_map.91 = (bf16[512,512]{1,0:T(8,128)(2,1)S(1)}, bf16[512,512]{1,0:T(8,128)(2,1)S(1)}, bf16[2,128,512]{2,1,0:T(8,128)(2,1)S(1)}, bf16[2,128,512]{2,1,0:T(8,128)(2,1)S(1)}, bf16[2,128,512]{2,1,0:T(8,128)(2,1)S(1)}) custom-call(bf16[2,512,512]{2,1,0:T(8,128)(2,1)S(1)} %collective-permute-done.3.refs_3_.layer_ref, ...), custom_call_target="tpu_custom_call" | custom-call | flops 469762048 | bytes 4063232 | tf_op jit(solution)/shard_map/pallas_call | solution.py:241
  34.6 0.4 collective-permute-start.8
  35.1 1.5 %collective-permute-start.9 = (bf16[2,128,512]{2,1,0:T(8,128)(2,1)S(1)}, bf16[2,128,512]{2,1,0:T(8,128)(2,1)S(1)}, u32[]{:S(2)}, u32[]{:S(2)}) collective-permute-start(bf16[2,128,512]{2,1,0:T(8,128)(2,1)S(1)} %get-tuple-element.48), channel_id=1, source_target_pairs={{0,1},{1,0},{2,4},{3,5},{4,2},{5,3},{6,7},{7,6},{8,16},{9,17},{10,... | collective-permute-start | bytes 786440 | tf_op jit(solution)/shard_map/ppermute | solution.py:348
  36.6 0.5 collective-permute-start.10
  37.3 0.3 shard_map.92.total_ref
  37.6 5.0 %collective-permute-done.8.refs_0_ = bf16[2,128,512]{2,1,0:T(8,128)(2,1)S(1)} collective-permute-done((bf16[2,128,512]{2,1,0:T(8,128)(2,1)S(1)}, bf16[2,128,512]{2,1,0:T(8,128)(2,1)S(1)}, u32[]{:S(2)}, u32[]{:S(2)}) %collective-permute-start.8) | collective-permute-done | bytes 262176 | tf_op jit(solution)/shard_map/ppermute | solution.py:348
  42.6 1.6 %collective-permute-done.10.refs_2_ = bf16[2,128,512]{2,1,0:T(8,128)(2,1)S(1)} collective-permute-done((bf16[2,128,512]{2,1,0:T(8,128)(2,1)S(1)}, bf16[2,128,512]{2,1,0:T(8,128)(2,1)S(1)}, u32[]{:S(2)}, u32[]{:S(2)}) %collective-permute-start.10) | collective-permute-done | bytes 262176 | tf_op jit(solution)/shard_map/ppermute | solution.py:348
  44.3 1.7 %shard_map.95 = (bf16[512,512]{1,0:T(8,128)(2,1)S(1)}, f32[512,512]{1,0:T(8,128)S(1)}, bf16[2,128,512]{2,1,0:T(8,128)(2,1)S(1)}, bf16[2,128,512]{2,1,0:T(8,128)(...) custom-call(f32[12,1,512]{2,1,0:T(1,128)S(1)} %get-tuple-element.34.mask_ref, ...), custom_call_target="tpu_custom_call" | custom-call | flops 872415232 | bytes 8282112 | tf_op jit(solution)/shard_map/pallas_call | solution.py:241
  46.0 1.6 %collective-permute-start.16 = (bf16[256,512]{1,0:T(8,128)(2,1)S(1)}, bf16[256,512]{1,0:T(8,128)(2,1)S(1)}, u32[]{:S(2)}, u32[]{:S(2)}) collective-permute-start(bf16[256,512]{1,0:T(8,128)(2,1)S(1)} %get-tuple-element.59), channel_id=1, source_target_pairs={{0,1},{1,0},{2,3},{3,2},{4,5},{5,4},{6,7},{7,6},{8,9},{9,8},{10,11... | collective-permute-start | bytes 786440 | tf_op jit(solution)/shard_map/ppermute | solution.py:441
  47.6 0.6 collective-permute-start.12
  48.2 0.5 collective-permute-start.13
  48.7 1.5 %collective-permute-start.14 = (bf16[2,128,512]{2,1,0:T(8,128)(2,1)S(1)}, bf16[2,128,512]{2,1,0:T(8,128)(2,1)S(1)}, u32[]{:S(2)}, u32[]{:S(2)}) collective-permute-start(bf16[2,128,512]{2,1,0:T(8,128)(2,1)S(1)} %get-tuple-element.56), channel_id=1, source_target_pairs={{0,1},{1,0},{2,3},{3,2},{4,5},{5,4},{6,7},{7,6},{16,24},{17,25},{1... | collective-permute-start | bytes 786440 | tf_op jit(solution)/shard_map/ppermute | solution.py:348
  50.2 3.8 %collective-permute-done.16.got_ref = bf16[256,512]{1,0:T(8,128)(2,1)S(1)} collective-permute-done((bf16[256,512]{1,0:T(8,128)(2,1)S(1)}, bf16[256,512]{1,0:T(8,128)(2,1)S(1)}, u32[]{:S(2)}, u32[]{:S(2)}) %collective-permute-start.16) | collective-permute-done | bytes 262176 | tf_op jit(solution)/shard_map/ppermute | solution.py:441
  54.2 1.0 %collective-permute-start.17 = (bf16[128,512]{1,0:T(8,128)(2,1)S(1)}, bf16[128,512]{1,0:T(8,128)(2,1)S(1)}, u32[]{:S(2)}, u32[]{:S(2)}) collective-permute-start(bf16[128,512]{1,0:T(8,128)(2,1)S(1)} %get-tuple-element.61), channel_id=1, source_target_pairs={{0,4},{1,5},{2,6},{3,7},{4,0},{5,1},{6,2},{7,3},{8,12},{9,13},{10,... | collective-permute-start | bytes 393224 | tf_op jit(solution)/shard_map/ppermute | solution.py:441
  55.2 7.1 %collective-permute-done.17.got_ref = bf16[128,512]{1,0:T(8,128)(2,1)S(1)} collective-permute-done((bf16[128,512]{1,0:T(8,128)(2,1)S(1)}, bf16[128,512]{1,0:T(8,128)(2,1)S(1)}, u32[]{:S(2)}, u32[]{:S(2)}) %collective-permute-start.17) | collective-permute-done | bytes 131104 | tf_op jit(solution)/shard_map/ppermute | solution.py:441
  62.4 4.2 %collective-permute-done.18.refs_6_ = bf16[64,512]{1,0:T(8,128)(2,1)S(1)} collective-permute-done((bf16[64,512]{1,0:T(8,128)(2,1)S(1)}, bf16[64,512]{1,0:T(8,128)(2,1)S(1)}, u32[]{:S(2)}, u32[]{:S(2)}) %collective-permute-start.18) | collective-permute-done | bytes 65568 | tf_op jit(solution)/shard_map/ppermute | solution.py:447
  66.7 1.2 %shard_map.99 = (bf16[512,512]{1,0:T(8,128)(2,1)}, f32[64,512]{1,0:T(8,128)}) custom-call(f32[12,1,512]{2,1,0:T(1,128)S(1)} %get-tuple-element.34.mask_ref, f32[512,512]{1,0:T(8,128)S(1)} %get-tuple-element.53.total_ref, bf16[2,128,512]{2,1,0:T(8,128)(2,1)S(1)} %collective-permute-done.12.refs_0_, bf16[2,128,512]{2,1,0:T(8,128)(2,1)S(1)} %collective-permute-done.13.refs_1_, ...), custom_call_target="tpu_custom_call" | custom-call | bytes 3760128 | tf_op jit(solution)/shard_map/pallas_call | solution.py:241
  (24 shorter events, 0.9 us)
Async XLA Ops:
  0.6 7.5 %copy-start.1 = (bf16[2,1,1,256,512]{4,3,2,1,0:T(8,128)(2,1)S(1)}, bf16[2,1,1,256,512]{4,3,2,1,0:T(8,128)(2,1)}, u32[]{:S(2)}) copy-start(bf16[2,1,1,256,512]{4,3,2,1,0:T(8,128)(2,1)} %param.8) | copy-start | bytes 1572868
  3.5 9.5 %collective-permute-start.3 = (bf16[2,512,512]{2,1,0:T(8,128)(2,1)S(1)}, bf16[2,512,512]{2,1,0:T(8,128)(2,1)S(1)}, u32[]{:S(2)}, u32[]{:S(2)}) collective-permute-start(bf16[2,512,512]{2,1,0:T(8,128)(2,1)S(1)} %get-tuple-element.40.refs_6_), channel_id=1, source_target_pairs={{16,24},{17,25},{18,26},{19,27},{20,28},{21,29},{22,30},{23,31},{8... | collective-permute-start | bytes 3145736 | tf_op jit(solution)/shard_map/ppermute | solution.py:273
  4.0 6.9 %collective-permute-start = (bf16[2,128,512]{2,1,0:T(8,128)(2,1)S(1)}, bf16[2,128,512]{2,1,0:T(8,128)(2,1)S(1)}, u32[]{:S(2)}, u32[]{:S(2)}) collective-permute-start(bf16[2,128,512]{2,1,0:T(8,128)(2,1)S(1)} %get-tuple-element.37), channel_id=1, source_target_pairs={{24,26},{25,27},{26,24},{27,25},{28,30},{29,31},{30,28},{31,29},{1... | collective-permute-start | bytes 786440 | tf_op jit(solution)/shard_map/ppermute | solution.py:348
  6.6 6.4 %collective-permute-start.1 = (bf16[2,128,512]{2,1,0:T(8,128)(2,1)S(1)}, bf16[2,128,512]{2,1,0:T(8,128)(2,1)S(1)}, u32[]{:S(2)}, u32[]{:S(2)}) collective-permute-start(bf16[2,128,512]{2,1,0:T(8,128)(2,1)S(1)} %get-tuple-element.38), channel_id=1, source_target_pairs={{24,25},{25,24},{26,28},{27,29},{28,26},{29,27},{30,31},{31,30},{1... | collective-permute-start | bytes 786440 | tf_op jit(solution)/shard_map/ppermute | solution.py:348
  8.2 4.8 %collective-permute-start.2 = (bf16[2,128,512]{2,1,0:T(8,128)(2,1)S(1)}, bf16[2,128,512]{2,1,0:T(8,128)(2,1)S(1)}, u32[]{:S(2)}, u32[]{:S(2)}) collective-permute-start(bf16[2,128,512]{2,1,0:T(8,128)(2,1)S(1)} %get-tuple-element.39), channel_id=1, source_target_pairs={{24,25},{25,24},{26,27},{27,26},{28,29},{29,28},{30,31},{31,30},{8... | collective-permute-start | bytes 786440 | tf_op jit(solution)/shard_map/ppermute | solution.py:348
  13.9 6.4 %collective-permute-start.4 = (bf16[2,128,512]{2,1,0:T(8,128)(2,1)S(1)}, bf16[2,128,512]{2,1,0:T(8,128)(2,1)S(1)}, u32[]{:S(2)}, u32[]{:S(2)}) collective-permute-start(bf16[2,128,512]{2,1,0:T(8,128)(2,1)S(1)} %get-tuple-element.43), channel_id=1, source_target_pairs={{24,26},{25,27},{26,24},{27,25},{28,30},{29,31},{30,28},{31,29},{1... | collective-permute-start | bytes 786440 | tf_op jit(solution)/shard_map/ppermute | solution.py:348
  14.0 6.4 %collective-permute-start.5 = (bf16[2,128,512]{2,1,0:T(8,128)(2,1)S(1)}, bf16[2,128,512]{2,1,0:T(8,128)(2,1)S(1)}, u32[]{:S(2)}, u32[]{:S(2)}) collective-permute-start(bf16[2,128,512]{2,1,0:T(8,128)(2,1)S(1)} %get-tuple-element.44), channel_id=1, source_target_pairs={{24,25},{25,24},{26,28},{27,29},{28,26},{29,27},{30,31},{31,30},{1... | collective-permute-start | bytes 786440 | tf_op jit(solution)/shard_map/ppermute | solution.py:348
  16.0 4.4 %collective-permute-start.6 = (bf16[2,128,512]{2,1,0:T(8,128)(2,1)S(1)}, bf16[2,128,512]{2,1,0:T(8,128)(2,1)S(1)}, u32[]{:S(2)}, u32[]{:S(2)}) collective-permute-start(bf16[2,128,512]{2,1,0:T(8,128)(2,1)S(1)} %get-tuple-element.45), channel_id=1, source_target_pairs={{24,25},{25,24},{26,27},{27,26},{28,29},{29,28},{30,31},{31,30},{8... | collective-permute-start | bytes 786440 | tf_op jit(solution)/shard_map/ppermute | solution.py:348
  20.7 13.0 %collective-permute-start.7 = (bf16[512,512]{1,0:T(8,128)(2,1)S(1)}, bf16[512,512]{1,0:T(8,128)(2,1)S(1)}, u32[]{:S(2)}, u32[]{:S(2)}) collective-permute-start(bf16[512,512]{1,0:T(8,128)(2,1)S(1)} %shard_map.90.top_ref), channel_id=1, source_target_pairs={{24,0},{25,1},{26,2},{27,3},{28,4},{29,5},{30,6},{31,7}} | collective-permute-start | bytes 1572872 | tf_op jit(solution)/shard_map/ppermute | solution.py:273
  34.5 2.6 %copy-start = (bf16[1,2,1,1,256,512]{5,4,3,2,1,0:T(8,128)(2,1)S(1)}, bf16[1,2,1,1,256,512]{5,4,3,2,1,0:T(8,128)(2,1)}, u32[]{:S(2)}) copy-start(bf16[1,2,1,1,256,512]{5,4,3,2,1,0:T(8,128)(2,1)} %param.7) | copy-start | bytes 1572868
  34.5 9.7 %collective-permute-start.11 = (bf16[512,512]{1,0:T(8,128)(2,1)S(1)}, bf16[512,512]{1,0:T(8,128)(2,1)S(1)}, u32[]{:S(2)}, u32[]{:S(2)}) collective-permute-start(bf16[512,512]{1,0:T(8,128)(2,1)S(1)} %shard_map.94), channel_id=1, source_target_pairs={{24,16},{25,17},{26,18},{27,19},{28,20},{29,21},{30,22},{31,23},{0... | collective-permute-start | bytes 1572872 | tf_op jit(solution)/shard_map/ppermute | solution.py:273
  34.6 8.0 %collective-permute-start.8 = (bf16[2,128,512]{2,1,0:T(8,128)(2,1)S(1)}, bf16[2,128,512]{2,1,0:T(8,128)(2,1)S(1)}, u32[]{:S(2)}, u32[]{:S(2)}) collective-permute-start(bf16[2,128,512]{2,1,0:T(8,128)(2,1)S(1)} %get-tuple-element.47), channel_id=1, source_target_pairs={{0,2},{1,3},{2,0},{3,1},{4,6},{5,7},{6,4},{7,5},{8,16},{9,17},{10,... | collective-permute-start | bytes 786440 | tf_op jit(solution)/shard_map/ppermute | solution.py:348
  35.1 7.6 %collective-permute-start.9 = (bf16[2,128,512]{2,1,0:T(8,128)(2,1)S(1)}, bf16[2,128,512]{2,1,0:T(8,128)(2,1)S(1)}, u32[]{:S(2)}, u32[]{:S(2)}) collective-permute-start(bf16[2,128,512]{2,1,0:T(8,128)(2,1)S(1)} %get-tuple-element.48), channel_id=1, source_target_pairs={{0,1},{1,0},{2,4},{3,5},{4,2},{5,3},{6,7},{7,6},{8,16},{9,17},{10,... | collective-permute-start | bytes 786440 | tf_op jit(solution)/shard_map/ppermute | solution.py:348
  36.6 7.7 %collective-permute-start.10 = (bf16[2,128,512]{2,1,0:T(8,128)(2,1)S(1)}, bf16[2,128,512]{2,1,0:T(8,128)(2,1)S(1)}, u32[]{:S(2)}, u32[]{:S(2)}) collective-permute-start(bf16[2,128,512]{2,1,0:T(8,128)(2,1)S(1)} %get-tuple-element.49), channel_id=1, source_target_pairs={{0,1},{1,0},{2,3},{3,2},{4,5},{5,4},{6,7},{7,6},{16,24},{17,25},{1... | collective-permute-start | bytes 786440 | tf_op jit(solution)/shard_map/ppermute | solution.py:348
  46.0 20.7 %collective-permute-start.15 = (bf16[512,512]{1,0:T(8,128)(2,1)S(1)}, bf16[512,512]{1,0:T(8,128)(2,1)S(1)}, u32[]{:S(2)}, u32[]{:S(2)}) collective-permute-start(bf16[512,512]{1,0:T(8,128)(2,1)S(1)} %shard_map.96), channel_id=1, source_target_pairs={{24,16},{25,17},{26,18},{27,19},{28,20},{29,21},{30,22},{31,23},{0... | collective-permute-start | bytes 1572872 | tf_op jit(solution)/shard_map/ppermute | solution.py:273
  46.0 8.1 %collective-permute-start.16 = (bf16[256,512]{1,0:T(8,128)(2,1)S(1)}, bf16[256,512]{1,0:T(8,128)(2,1)S(1)}, u32[]{:S(2)}, u32[]{:S(2)}) collective-permute-start(bf16[256,512]{1,0:T(8,128)(2,1)S(1)} %get-tuple-element.59), channel_id=1, source_target_pairs={{0,1},{1,0},{2,3},{3,2},{4,5},{5,4},{6,7},{7,6},{8,9},{9,8},{10,11... | collective-permute-start | bytes 786440 | tf_op jit(solution)/shard_map/ppermute | solution.py:441
  47.6 14.8 %collective-permute-start.12 = (bf16[2,128,512]{2,1,0:T(8,128)(2,1)S(1)}, bf16[2,128,512]{2,1,0:T(8,128)(2,1)S(1)}, u32[]{:S(2)}, u32[]{:S(2)}) collective-permute-start(bf16[2,128,512]{2,1,0:T(8,128)(2,1)S(1)} %get-tuple-element.54), channel_id=1, source_target_pairs={{0,2},{1,3},{2,0},{3,1},{4,6},{5,7},{6,4},{7,5},{8,16},{9,17},{10,... | collective-permute-start | bytes 786440 | tf_op jit(solution)/shard_map/ppermute | solution.py:348
  48.2 14.2 %collective-permute-start.13 = (bf16[2,128,512]{2,1,0:T(8,128)(2,1)S(1)}, bf16[2,128,512]{2,1,0:T(8,128)(2,1)S(1)}, u32[]{:S(2)}, u32[]{:S(2)}) collective-permute-start(bf16[2,128,512]{2,1,0:T(8,128)(2,1)S(1)} %get-tuple-element.55), channel_id=1, source_target_pairs={{0,1},{1,0},{2,4},{3,5},{4,2},{5,3},{6,7},{7,6},{8,16},{9,17},{10,... | collective-permute-start | bytes 786440 | tf_op jit(solution)/shard_map/ppermute | solution.py:348
  48.7 13.7 %collective-permute-start.14 = (bf16[2,128,512]{2,1,0:T(8,128)(2,1)S(1)}, bf16[2,128,512]{2,1,0:T(8,128)(2,1)S(1)}, u32[]{:S(2)}, u32[]{:S(2)}) collective-permute-start(bf16[2,128,512]{2,1,0:T(8,128)(2,1)S(1)} %get-tuple-element.56), channel_id=1, source_target_pairs={{0,1},{1,0},{2,3},{3,2},{4,5},{5,4},{6,7},{7,6},{16,24},{17,25},{1... | collective-permute-start | bytes 786440 | tf_op jit(solution)/shard_map/ppermute | solution.py:348
  54.2 8.1 %collective-permute-start.17 = (bf16[128,512]{1,0:T(8,128)(2,1)S(1)}, bf16[128,512]{1,0:T(8,128)(2,1)S(1)}, u32[]{:S(2)}, u32[]{:S(2)}) collective-permute-start(bf16[128,512]{1,0:T(8,128)(2,1)S(1)} %get-tuple-element.61), channel_id=1, source_target_pairs={{0,4},{1,5},{2,6},{3,7},{4,0},{5,1},{6,2},{7,3},{8,12},{9,13},{10,... | collective-permute-start | bytes 393224 | tf_op jit(solution)/shard_map/ppermute | solution.py:441
  62.3 4.3 %collective-permute-start.18 = (bf16[64,512]{1,0:T(8,128)(2,1)S(1)}, bf16[64,512]{1,0:T(8,128)(2,1)S(1)}, u32[]{:S(2)}, u32[]{:S(2)}) collective-permute-start(bf16[64,512]{1,0:T(8,128)(2,1)S(1)} %get-tuple-element.63), channel_id=1, source_target_pairs={{0,2},{1,3},{2,0},{3,1},{4,6},{5,7},{6,4},{7,5},{8,10},{9,11},{10,... | collective-permute-start | bytes 196616 | tf_op jit(solution)/shard_map/ppermute | solution.py:447

commit v8 on v7

--- a/solution.py
+++ b/solution.py
@@ -199,17 +199,30 @@
         product(got_ref)
 
 
-def split_halves(step, product_ref, sent_ref, kept_ref):
-    axis, distance, groups = step
-    size = kept_ref.shape[0] // groups
-    place = lax.rem(lax.axis_index(axis) // distance, 2)
-    for group in range(groups):
-        start = 2 * group * size
-        rows = slice(group * size, (group + 1) * size)
-        kept = pl.ds(pl.multiple_of(start + place * size, size), size)
-        sent = pl.ds(pl.multiple_of(start + (1 - place) * size, size), size)
-        kept_ref[rows] = product_ref[kept]
-        sent_ref[rows] = product_ref[sent].astype(BF16)
+def split_halves(steps, product_ref, sent_ref, kept_ref):
+    def split(axis, distance, groups):
+        size = kept_ref.shape[0] // groups
+        place = lax.rem(lax.axis_index(axis) // distance, 2)
+        for group in range(groups):
+            start = 2 * group * size
+            rows = slice(group * size, (group + 1) * size)
+            kept = pl.ds(pl.multiple_of(start + place * size, size), size)
+            sent = pl.ds(pl.multiple_of(start + (1 - place) * size, size), size)
+            kept_ref[rows] = product_ref[kept]
+            sent_ref[rows] = product_ref[sent].astype(BF16)
+
+    if steps[0] == steps[1]:
+        split(*steps[0])
+    else:
+        odd = lax.rem(lax.axis_index("pipe"), 2) == 1
+
+        @pl.when(odd)
+        def _():
+            split(*steps[1])
+
+        @pl.when(jnp.logical_not(odd))
+        def _():
+            split(*steps[0])
 
 
 def halve_kernel(step, kept_ref, got_ref, sent_ref, next_ref, sum_ref):
@@ -328,17 +341,27 @@
     phases = tuple(phases)
     splits, left = [], rows * columns
     if left & (left - 1) == 0 and width // left % 16 == 0:
-        for axis, count, other in (("ty", columns, rows), ("tx", rows, 1)):
-            distance = count // 2
-            while distance > 0:
-                pairs = [
+        along = {"tx": [], "ty": []}
+        for axis, count in (("tx", rows), ("ty", columns)):
+            while 1 << len(along[axis]) < count:
+                along[axis].append((axis, 1 << len(along[axis])))
+        orders = [
+            along["ty"][::-1] + along["tx"], along["tx"][:1] + along["ty"][::-1] + along["tx"][1:]
+        ]
+        levels = [along["tx"][::-1] + along["ty"][::-1] for _ in orders]
+        for index in range(len(orders[0])):
+            steps, pairs = [], []
+            for order, level in zip(orders, levels):
+                steps.append((*order[index], 1 << level.index(order[index])))
+                level.remove(order[index])
+            for p in range(sections):
+                axis, distance, _ = steps[p % 2]
+                pairs += [
                     (flat(p, x, y), flat(p, x, y ^ distance) if axis == "ty" else flat(p, x ^ distance, y))
-                    for p in range(sections)
                     for x in range(rows)
                     for y in range(columns)
                 ]
-                splits.append(((axis, distance, other), pairs))
-                distance //= 2
+            splits.append((tuple(steps), pairs))
     sent = [((batches, block, width), BF16)] * len(phases)
     whole = ((total_rows, width), BF16)
     mix_rows = (blocks + len(phases)) * block

time: 68 us -> 65.7 us (0.966)
  waiting for transfers between devices: 41.7 us -> 38.2 us
  starting transfers between devices: 16.3 us -> 17.6 us
    ppermute x2, waiting for transfers between devices: 11 us -> 7.24 us  [per_device(): got = lax.ppermute(parcel, AXES, pairs)]
    ppermute x1, starting transfers between devices: 0.07 us -> 1.58 us  [per_device(): got = lax.ppermute(parcel, AXES, splits[-1][1])]
where the time goes in v8:
time: 65.7 us; the launch traced here: 65.6 us
  waiting for transfers between devices  38.2 us (58%)
  starting transfers between devices  17.6 us (27%)
  Pallas kernels  9.01 us (14%)
  between operations  0.78 us (1%)
    ppermute x12, waiting for transfers between devices, exchange(): lax.ppermute(out, AXES, route[lead])  14.8 us
    ppermute x12, starting transfers between devices, exchange(): lax.ppermute(out, AXES, route[lead])  11.8 us
    ppermute x4, waiting for transfers between devices, to_sections(): return lax.ppermute(value, AXES, pairs)  11.7 us
    pallas_call x14, Pallas kernels, call(): pl.pallas_call(body, out_shape=[kind(shape, dtype) for shape, dtype in ou...  9.01 us
    ppermute x2, waiting for transfers between devices, per_device(): got = lax.ppermute(parcel, AXES, pairs)  7.24 us
    ppermute x1, waiting for transfers between devices, per_device(): got = lax.ppermute(parcel, AXES, splits[-1][1])  4.43 us
    ppermute x2, starting transfers between devices, per_device(): got = lax.ppermute(parcel, AXES, pairs)  2.28 us
    ppermute x4, starting transfers between devices, to_sections(): return lax.ppermute(value, AXES, pairs)  1.9 us
  transfers between devices with their start and end apart: 19, of which 10 were waited for; matrix products, arithmetic and copies ran while one was open for 0% of the time, Pallas kernels for 2%

profile of v8, /device:TPU:0, one launch (start us, length us, event | category | flops | bytes accessed | tf_op | source)
XLA Modules:
  0.0 65.6 jit_solution(14210012483835358628)
XLA Ops:
  0.6 2.8 %shard_map.86 = (bf16[2,512,512]{2,1,0:T(8,128)(2,1)S(1)}, bf16[2,640,256]{2,1,0:T(8,128)(2,1)S(1)}, f32[12,1,512]{2,1,0:T(1,128)S(1)}, bf16[512,512]{1,0:T(8,12...) custom-call(bf16[512,512]{1,0:T(8,128)(2,1)} %bitcast.11, ...), custom_call_target="tpu_custom_call" | custom-call | flops 738197504 | bytes 5922944 | tf_op jit(solution)/shard_map/pallas_call | solution.py:254
  3.5 0.5 collective-permute-start.3
  4.0 2.6 %collective-permute-start = (bf16[2,128,512]{2,1,0:T(8,128)(2,1)S(1)}, bf16[2,128,512]{2,1,0:T(8,128)(2,1)S(1)}, u32[]{:S(2)}, u32[]{:S(2)}) collective-permute-start(bf16[2,128,512]{2,1,0:T(8,128)(2,1)S(1)} %get-tuple-element.37), channel_id=1, source_target_pairs={{24,26},{25,27},{26,24},{27,25},{28,30},{29,31},{30,28},{31,29},{1... | collective-permute-start | bytes 786440 | tf_op jit(solution)/shard_map/ppermute | solution.py:371
  6.6 1.6 %collective-permute-start.1 = (bf16[2,128,512]{2,1,0:T(8,128)(2,1)S(1)}, bf16[2,128,512]{2,1,0:T(8,128)(2,1)S(1)}, u32[]{:S(2)}, u32[]{:S(2)}) collective-permute-start(bf16[2,128,512]{2,1,0:T(8,128)(2,1)S(1)} %get-tuple-element.38), channel_id=1, source_target_pairs={{24,25},{25,24},{26,28},{27,29},{28,26},{29,27},{30,31},{31,30},{1... | collective-permute-start | bytes 786440 | tf_op jit(solution)/shard_map/ppermute | solution.py:371
  8.2 0.3 shard_map.87.total_ref
  8.5 2.5 %collective-permute-done.refs_0_ = bf16[2,128,512]{2,1,0:T(8,128)(2,1)S(1)} collective-permute-done((bf16[2,128,512]{2,1,0:T(8,128)(2,1)S(1)}, bf16[2,128,512]{2,1,0:T(8,128)(2,1)S(1)}, u32[]{:S(2)}, u32[]{:S(2)}) %collective-permute-start) | collective-permute-done | bytes 262176 | tf_op jit(solution)/shard_map/ppermute | solution.py:371
  10.9 2.0 %collective-permute-done.1.refs_1_ = bf16[2,128,512]{2,1,0:T(8,128)(2,1)S(1)} collective-permute-done((bf16[2,128,512]{2,1,0:T(8,128)(2,1)S(1)}, bf16[2,128,512]{2,1,0:T(8,128)(2,1)S(1)}, u32[]{:S(2)}, u32[]{:S(2)}) %collective-permute-start.1) | collective-permute-done | bytes 262176 | tf_op jit(solution)/shard_map/ppermute | solution.py:371
  13.0 0.9 %shard_map.88 = (bf16[512,512]{1,0:T(8,128)(2,1)S(1)}, bf16[512,512]{1,0:T(8,128)(2,1)S(1)}, bf16[512,512]{1,0:T(8,128)(2,1)S(1)}, bf16[2,128,512]{2,1,0:T(8,128...) custom-call(f32[12,1,512]{2,1,0:T(1,128)S(1)} %get-tuple-element.34.mask_ref, ...), custom_call_target="tpu_custom_call" | custom-call | flops 469762048 | bytes 5922816 | tf_op jit(solution)/shard_map/pallas_call | solution.py:254
  14.0 2.0 %collective-permute-start.5 = (bf16[2,128,512]{2,1,0:T(8,128)(2,1)S(1)}, bf16[2,128,512]{2,1,0:T(8,128)(2,1)S(1)}, u32[]{:S(2)}, u32[]{:S(2)}) collective-permute-start(bf16[2,128,512]{2,1,0:T(8,128)(2,1)S(1)} %get-tuple-element.44), channel_id=1, source_target_pairs={{24,25},{25,24},{26,28},{27,29},{28,26},{29,27},{30,31},{31,30},{1... | collective-permute-start | bytes 786440 | tf_op jit(solution)/shard_map/ppermute | solution.py:371
  16.0 0.3 collective-permute-start.6
  16.7 3.6 %collective-permute-done.4.refs_0_ = bf16[2,128,512]{2,1,0:T(8,128)(2,1)S(1)} collective-permute-done((bf16[2,128,512]{2,1,0:T(8,128)(2,1)S(1)}, bf16[2,128,512]{2,1,0:T(8,128)(2,1)S(1)}, u32[]{:S(2)}, u32[]{:S(2)}) %collective-permute-start.4) | collective-permute-done | bytes 262176 | tf_op jit(solution)/shard_map/ppermute | solution.py:371
  20.4 0.4 shard_map.90.top_ref
  20.7 1.3 %collective-permute-start.7 = (bf16[512,512]{1,0:T(8,128)(2,1)S(1)}, bf16[512,512]{1,0:T(8,128)(2,1)S(1)}, u32[]{:S(2)}, u32[]{:S(2)}) collective-permute-start(bf16[512,512]{1,0:T(8,128)(2,1)S(1)} %shard_map.90.top_ref), channel_id=1, source_target_pairs={{24,0},{25,1},{26,2},{27,3},{28,4},{29,5},{30,6},{31,7}} | collective-permute-start | bytes 1572872 | tf_op jit(solution)/shard_map/ppermute | solution.py:286
  22.0 11.7 %collective-permute-done.7.upstream_ref = bf16[512,512]{1,0:T(8,128)(2,1)S(1)} collective-permute-done((bf16[512,512]{1,0:T(8,128)(2,1)S(1)}, bf16[512,512]{1,0:T(8,128)(2,1)S(1)}, u32[]{:S(2)}, u32[]{:S(2)}) %collective-permute-start.7) | collective-permute-done | bytes 524320 | tf_op jit(solution)/shard_map/ppermute | solution.py:286
  33.7 0.8 %shard_map.91 = (bf16[512,512]{1,0:T(8,128)(2,1)S(1)}, bf16[512,512]{1,0:T(8,128)(2,1)S(1)}, bf16[2,128,512]{2,1,0:T(8,128)(2,1)S(1)}, bf16[2,128,512]{2,1,0:T(8,128)(2,1)S(1)}, bf16[2,128,512]{2,1,0:T(8,128)(2,1)S(1)}) custom-call(bf16[2,512,512]{2,1,0:T(8,128)(2,1)S(1)} %collective-permute-done.3.refs_3_.layer_ref, ...), custom_call_target="tpu_custom_call" | custom-call | flops 469762048 | bytes 4063232 | tf_op jit(solution)/shard_map/pallas_call | solution.py:254
  34.6 0.4 collective-permute-start.8
  35.1 1.5 %collective-permute-start.9 = (bf16[2,128,512]{2,1,0:T(8,128)(2,1)S(1)}, bf16[2,128,512]{2,1,0:T(8,128)(2,1)S(1)}, u32[]{:S(2)}, u32[]{:S(2)}) collective-permute-start(bf16[2,128,512]{2,1,0:T(8,128)(2,1)S(1)} %get-tuple-element.48), channel_id=1, source_target_pairs={{0,1},{1,0},{2,4},{3,5},{4,2},{5,3},{6,7},{7,6},{8,16},{9,17},{10,... | collective-permute-start | bytes 786440 | tf_op jit(solution)/shard_map/ppermute | solution.py:371
  36.6 0.5 collective-permute-start.10
  37.3 0.3 shard_map.92.total_ref
  37.6 5.0 %collective-permute-done.8.refs_0_ = bf16[2,128,512]{2,1,0:T(8,128)(2,1)S(1)} collective-permute-done((bf16[2,128,512]{2,1,0:T(8,128)(2,1)S(1)}, bf16[2,128,512]{2,1,0:T(8,128)(2,1)S(1)}, u32[]{:S(2)}, u32[]{:S(2)}) %collective-permute-start.8) | collective-permute-done | bytes 262176 | tf_op jit(solution)/shard_map/ppermute | solution.py:371
  42.6 1.6 %collective-permute-done.10.refs_2_ = bf16[2,128,512]{2,1,0:T(8,128)(2,1)S(1)} collective-permute-done((bf16[2,128,512]{2,1,0:T(8,128)(2,1)S(1)}, bf16[2,128,512]{2,1,0:T(8,128)(2,1)S(1)}, u32[]{:S(2)}, u32[]{:S(2)}) %collective-permute-start.10) | collective-permute-done | bytes 262176 | tf_op jit(solution)/shard_map/ppermute | solution.py:371
  44.3 1.7 %shard_map.95 = (bf16[512,512]{1,0:T(8,128)(2,1)S(1)}, f32[512,512]{1,0:T(8,128)S(1)}, bf16[2,128,512]{2,1,0:T(8,128)(2,1)S(1)}, bf16[2,128,512]{2,1,0:T(8,128)(...) custom-call(f32[12,1,512]{2,1,0:T(1,128)S(1)} %get-tuple-element.34.mask_ref, ...), custom_call_target="tpu_custom_call" | custom-call | flops 872415232 | bytes 8282112 | tf_op jit(solution)/shard_map/pallas_call | solution.py:254
  46.0 1.6 %collective-permute-start.16 = (bf16[256,512]{1,0:T(8,128)(2,1)S(1)}, bf16[256,512]{1,0:T(8,128)(2,1)S(1)}, u32[]{:S(2)}, u32[]{:S(2)}) collective-permute-start(bf16[256,512]{1,0:T(8,128)(2,1)S(1)} %get-tuple-element.59), channel_id=1, source_target_pairs={{0,1},{1,0},{2,3},{3,2},{4,5},{5,4},{6,7},{7,6},{8,10},{9,11},{10,... | collective-permute-start | bytes 786440 | tf_op jit(solution)/shard_map/ppermute | solution.py:464
  47.6 0.6 collective-permute-start.12
  48.2 0.5 collective-permute-start.13
  48.8 1.5 %collective-permute-start.14 = (bf16[2,128,512]{2,1,0:T(8,128)(2,1)S(1)}, bf16[2,128,512]{2,1,0:T(8,128)(2,1)S(1)}, u32[]{:S(2)}, u32[]{:S(2)}) collective-permute-start(bf16[2,128,512]{2,1,0:T(8,128)(2,1)S(1)} %get-tuple-element.56), channel_id=1, source_target_pairs={{0,1},{1,0},{2,3},{3,2},{4,5},{5,4},{6,7},{7,6},{16,24},{17,25},{1... | collective-permute-start | bytes 786440 | tf_op jit(solution)/shard_map/ppermute | solution.py:371
  50.3 2.2 %collective-permute-done.16.got_ref = bf16[256,512]{1,0:T(8,128)(2,1)S(1)} collective-permute-done((bf16[256,512]{1,0:T(8,128)(2,1)S(1)}, bf16[256,512]{1,0:T(8,128)(2,1)S(1)}, u32[]{:S(2)}, u32[]{:S(2)}) %collective-permute-start.16) | collective-permute-done | bytes 262176 | tf_op jit(solution)/shard_map/ppermute | solution.py:464
  52.6 0.7 %collective-permute-start.17 = (bf16[128,512]{1,0:T(8,128)(2,1)S(1)}, bf16[128,512]{1,0:T(8,128)(2,1)S(1)}, u32[]{:S(2)}, u32[]{:S(2)}) collective-permute-start(bf16[128,512]{1,0:T(8,128)(2,1)S(1)} %get-tuple-element.61), channel_id=1, source_target_pairs={{0,2},{1,3},{2,0},{3,1},{4,6},{5,7},{6,4},{7,5},{8,9},{9,8},{10,11... | collective-permute-start | bytes 393224 | tf_op jit(solution)/shard_map/ppermute | solution.py:464
  53.3 5.0 %collective-permute-done.17.got_ref = bf16[128,512]{1,0:T(8,128)(2,1)S(1)} collective-permute-done((bf16[128,512]{1,0:T(8,128)(2,1)S(1)}, bf16[128,512]{1,0:T(8,128)(2,1)S(1)}, u32[]{:S(2)}, u32[]{:S(2)}) %collective-permute-start.17) | collective-permute-done | bytes 131104 | tf_op jit(solution)/shard_map/ppermute | solution.py:464
  58.4 1.6 %collective-permute-start.18 = (bf16[64,512]{1,0:T(8,128)(2,1)S(1)}, bf16[64,512]{1,0:T(8,128)(2,1)S(1)}, u32[]{:S(2)}, u32[]{:S(2)}) collective-permute-start(bf16[64,512]{1,0:T(8,128)(2,1)S(1)} %get-tuple-element.63), channel_id=1, source_target_pairs={{0,4},{1,5},{2,6},{3,7},{4,0},{5,1},{6,2},{7,3},{8,12},{9,13},{10,... | collective-permute-start | bytes 196616 | tf_op jit(solution)/shard_map/ppermute | solution.py:470
  60.0 4.4 %collective-permute-done.18.refs_6_ = bf16[64,512]{1,0:T(8,128)(2,1)S(1)} collective-permute-done((bf16[64,512]{1,0:T(8,128)(2,1)S(1)}, bf16[64,512]{1,0:T(8,128)(2,1)S(1)}, u32[]{:S(2)}, u32[]{:S(2)}) %collective-permute-start.18) | collective-permute-done | bytes 65568 | tf_op jit(solution)/shard_map/ppermute | solution.py:470
  64.4 1.2 %shard_map.99 = (bf16[512,512]{1,0:T(8,128)(2,1)}, f32[64,512]{1,0:T(8,128)}) custom-call(f32[12,1,512]{2,1,0:T(1,128)S(1)} %get-tuple-element.34.mask_ref, f32[512,512]{1,0:T(8,128)S(1)} %get-tuple-element.53.total_ref, bf16[2,128,512]{2,1,0:T(8,128)(2,1)S(1)} %collective-permute-done.12.refs_0_, bf16[2,128,512]{2,1,0:T(8,128)(2,1)S(1)} %collective-permute-done.13.refs_1_, ...), custom_call_target="tpu_custom_call" | custom-call | bytes 3760128 | tf_op jit(solution)/shard_map/pallas_call | solution.py:254
  (24 shorter events, 1.1 us)
Async XLA Ops:
  0.6 7.5 %copy-start.1 = (bf16[2,1,1,256,512]{4,3,2,1,0:T(8,128)(2,1)S(1)}, bf16[2,1,1,256,512]{4,3,2,1,0:T(8,128)(2,1)}, u32[]{:S(2)}) copy-start(bf16[2,1,1,256,512]{4,3,2,1,0:T(8,128)(2,1)} %param.8) | copy-start | bytes 1572868
  3.5 9.5 %collective-permute-start.3 = (bf16[2,512,512]{2,1,0:T(8,128)(2,1)S(1)}, bf16[2,512,512]{2,1,0:T(8,128)(2,1)S(1)}, u32[]{:S(2)}, u32[]{:S(2)}) collective-permute-start(bf16[2,512,512]{2,1,0:T(8,128)(2,1)S(1)} %get-tuple-element.40.refs_6_), channel_id=1, source_target_pairs={{16,24},{17,25},{18,26},{19,27},{20,28},{21,29},{22,30},{23,31},{8... | collective-permute-start | bytes 3145736 | tf_op jit(solution)/shard_map/ppermute | solution.py:286
  4.0 6.9 %collective-permute-start = (bf16[2,128,512]{2,1,0:T(8,128)(2,1)S(1)}, bf16[2,128,512]{2,1,0:T(8,128)(2,1)S(1)}, u32[]{:S(2)}, u32[]{:S(2)}) collective-permute-start(bf16[2,128,512]{2,1,0:T(8,128)(2,1)S(1)} %get-tuple-element.37), channel_id=1, source_target_pairs={{24,26},{25,27},{26,24},{27,25},{28,30},{29,31},{30,28},{31,29},{1... | collective-permute-start | bytes 786440 | tf_op jit(solution)/shard_map/ppermute | solution.py:371
  6.6 6.4 %collective-permute-start.1 = (bf16[2,128,512]{2,1,0:T(8,128)(2,1)S(1)}, bf16[2,128,512]{2,1,0:T(8,128)(2,1)S(1)}, u32[]{:S(2)}, u32[]{:S(2)}) collective-permute-start(bf16[2,128,512]{2,1,0:T(8,128)(2,1)S(1)} %get-tuple-element.38), channel_id=1, source_target_pairs={{24,25},{25,24},{26,28},{27,29},{28,26},{29,27},{30,31},{31,30},{1... | collective-permute-start | bytes 786440 | tf_op jit(solution)/shard_map/ppermute | solution.py:371
  8.2 4.8 %collective-permute-start.2 = (bf16[2,128,512]{2,1,0:T(8,128)(2,1)S(1)}, bf16[2,128,512]{2,1,0:T(8,128)(2,1)S(1)}, u32[]{:S(2)}, u32[]{:S(2)}) collective-permute-start(bf16[2,128,512]{2,1,0:T(8,128)(2,1)S(1)} %get-tuple-element.39), channel_id=1, source_target_pairs={{24,25},{25,24},{26,27},{27,26},{28,29},{29,28},{30,31},{31,30},{8... | collective-permute-start | bytes 786440 | tf_op jit(solution)/shard_map/ppermute | solution.py:371
  13.9 6.4 %collective-permute-start.4 = (bf16[2,128,512]{2,1,0:T(8,128)(2,1)S(1)}, bf16[2,128,512]{2,1,0:T(8,128)(2,1)S(1)}, u32[]{:S(2)}, u32[]{:S(2)}) collective-permute-start(bf16[2,128,512]{2,1,0:T(8,128)(2,1)S(1)} %get-tuple-element.43), channel_id=1, source_target_pairs={{24,26},{25,27},{26,24},{27,25},{28,30},{29,31},{30,28},{31,29},{1... | collective-permute-start | bytes 786440 | tf_op jit(solution)/shard_map/ppermute | solution.py:371
  14.0 6.4 %collective-permute-start.5 = (bf16[2,128,512]{2,1,0:T(8,128)(2,1)S(1)}, bf16[2,128,512]{2,1,0:T(8,128)(2,1)S(1)}, u32[]{:S(2)}, u32[]{:S(2)}) collective-permute-start(bf16[2,128,512]{2,1,0:T(8,128)(2,1)S(1)} %get-tuple-element.44), channel_id=1, source_target_pairs={{24,25},{25,24},{26,28},{27,29},{28,26},{29,27},{30,31},{31,30},{1... | collective-permute-start | bytes 786440 | tf_op jit(solution)/shard_map/ppermute | solution.py:371
  16.0 4.4 %collective-permute-start.6 = (bf16[2,128,512]{2,1,0:T(8,128)(2,1)S(1)}, bf16[2,128,512]{2,1,0:T(8,128)(2,1)S(1)}, u32[]{:S(2)}, u32[]{:S(2)}) collective-permute-start(bf16[2,128,512]{2,1,0:T(8,128)(2,1)S(1)} %get-tuple-element.45), channel_id=1, source_target_pairs={{24,25},{25,24},{26,27},{27,26},{28,29},{29,28},{30,31},{31,30},{8... | collective-permute-start | bytes 786440 | tf_op jit(solution)/shard_map/ppermute | solution.py:371
  20.7 13.0 %collective-permute-start.7 = (bf16[512,512]{1,0:T(8,128)(2,1)S(1)}, bf16[512,512]{1,0:T(8,128)(2,1)S(1)}, u32[]{:S(2)}, u32[]{:S(2)}) collective-permute-start(bf16[512,512]{1,0:T(8,128)(2,1)S(1)} %shard_map.90.top_ref), channel_id=1, source_target_pairs={{24,0},{25,1},{26,2},{27,3},{28,4},{29,5},{30,6},{31,7}} | collective-permute-start | bytes 1572872 | tf_op jit(solution)/shard_map/ppermute | solution.py:286
  34.5 2.6 %copy-start = (bf16[1,2,1,1,256,512]{5,4,3,2,1,0:T(8,128)(2,1)S(1)}, bf16[1,2,1,1,256,512]{5,4,3,2,1,0:T(8,128)(2,1)}, u32[]{:S(2)}) copy-start(bf16[1,2,1,1,256,512]{5,4,3,2,1,0:T(8,128)(2,1)} %param.7) | copy-start | bytes 1572868
  34.5 9.7 %collective-permute-start.11 = (bf16[512,512]{1,0:T(8,128)(2,1)S(1)}, bf16[512,512]{1,0:T(8,128)(2,1)S(1)}, u32[]{:S(2)}, u32[]{:S(2)}) collective-permute-start(bf16[512,512]{1,0:T(8,128)(2,1)S(1)} %shard_map.94), channel_id=1, source_target_pairs={{24,16},{25,17},{26,18},{27,19},{28,20},{29,21},{30,22},{31,23},{0... | collective-permute-start | bytes 1572872 | tf_op jit(solution)/shard_map/ppermute | solution.py:286
  34.6 8.0 %collective-permute-start.8 = (bf16[2,128,512]{2,1,0:T(8,128)(2,1)S(1)}, bf16[2,128,512]{2,1,0:T(8,128)(2,1)S(1)}, u32[]{:S(2)}, u32[]{:S(2)}) collective-permute-start(bf16[2,128,512]{2,1,0:T(8,128)(2,1)S(1)} %get-tuple-element.47), channel_id=1, source_target_pairs={{0,2},{1,3},{2,0},{3,1},{4,6},{5,7},{6,4},{7,5},{8,16},{9,17},{10,... | collective-permute-start | bytes 786440 | tf_op jit(solution)/shard_map/ppermute | solution.py:371
  35.1 7.6 %collective-permute-start.9 = (bf16[2,128,512]{2,1,0:T(8,128)(2,1)S(1)}, bf16[2,128,512]{2,1,0:T(8,128)(2,1)S(1)}, u32[]{:S(2)}, u32[]{:S(2)}) collective-permute-start(bf16[2,128,512]{2,1,0:T(8,128)(2,1)S(1)} %get-tuple-element.48), channel_id=1, source_target_pairs={{0,1},{1,0},{2,4},{3,5},{4,2},{5,3},{6,7},{7,6},{8,16},{9,17},{10,... | collective-permute-start | bytes 786440 | tf_op jit(solution)/shard_map/ppermute | solution.py:371
  36.6 7.7 %collective-permute-start.10 = (bf16[2,128,512]{2,1,0:T(8,128)(2,1)S(1)}, bf16[2,128,512]{2,1,0:T(8,128)(2,1)S(1)}, u32[]{:S(2)}, u32[]{:S(2)}) collective-permute-start(bf16[2,128,512]{2,1,0:T(8,128)(2,1)S(1)} %get-tuple-element.49), channel_id=1, source_target_pairs={{0,1},{1,0},{2,3},{3,2},{4,5},{5,4},{6,7},{7,6},{16,24},{17,25},{1... | collective-permute-start | bytes 786440 | tf_op jit(solution)/shard_map/ppermute | solution.py:371
  46.0 18.4 %collective-permute-start.15 = (bf16[512,512]{1,0:T(8,128)(2,1)S(1)}, bf16[512,512]{1,0:T(8,128)(2,1)S(1)}, u32[]{:S(2)}, u32[]{:S(2)}) collective-permute-start(bf16[512,512]{1,0:T(8,128)(2,1)S(1)} %shard_map.96), channel_id=1, source_target_pairs={{24,16},{25,17},{26,18},{27,19},{28,20},{29,21},{30,22},{31,23},{0... | collective-permute-start | bytes 1572872 | tf_op jit(solution)/shard_map/ppermute | solution.py:286
  46.0 6.4 %collective-permute-start.16 = (bf16[256,512]{1,0:T(8,128)(2,1)S(1)}, bf16[256,512]{1,0:T(8,128)(2,1)S(1)}, u32[]{:S(2)}, u32[]{:S(2)}) collective-permute-start(bf16[256,512]{1,0:T(8,128)(2,1)S(1)} %get-tuple-element.59), channel_id=1, source_target_pairs={{0,1},{1,0},{2,3},{3,2},{4,5},{5,4},{6,7},{7,6},{8,10},{9,11},{10,... | collective-permute-start | bytes 786440 | tf_op jit(solution)/shard_map/ppermute | solution.py:464
  47.6 12.3 %collective-permute-start.12 = (bf16[2,128,512]{2,1,0:T(8,128)(2,1)S(1)}, bf16[2,128,512]{2,1,0:T(8,128)(2,1)S(1)}, u32[]{:S(2)}, u32[]{:S(2)}) collective-permute-start(bf16[2,128,512]{2,1,0:T(8,128)(2,1)S(1)} %get-tuple-element.54), channel_id=1, source_target_pairs={{0,2},{1,3},{2,0},{3,1},{4,6},{5,7},{6,4},{7,5},{8,16},{9,17},{10,... | collective-permute-start | bytes 786440 | tf_op jit(solution)/shard_map/ppermute | solution.py:371
  48.2 11.7 %collective-permute-start.13 = (bf16[2,128,512]{2,1,0:T(8,128)(2,1)S(1)}, bf16[2,128,512]{2,1,0:T(8,128)(2,1)S(1)}, u32[]{:S(2)}, u32[]{:S(2)}) collective-permute-start(bf16[2,128,512]{2,1,0:T(8,128)(2,1)S(1)} %get-tuple-element.55), channel_id=1, source_target_pairs={{0,1},{1,0},{2,4},{3,5},{4,2},{5,3},{6,7},{7,6},{8,16},{9,17},{10,... | collective-permute-start | bytes 786440 | tf_op jit(solution)/shard_map/ppermute | solution.py:371
  48.8 11.2 %collective-permute-start.14 = (bf16[2,128,512]{2,1,0:T(8,128)(2,1)S(1)}, bf16[2,128,512]{2,1,0:T(8,128)(2,1)S(1)}, u32[]{:S(2)}, u32[]{:S(2)}) collective-permute-start(bf16[2,128,512]{2,1,0:T(8,128)(2,1)S(1)} %get-tuple-element.56), channel_id=1, source_target_pairs={{0,1},{1,0},{2,3},{3,2},{4,5},{5,4},{6,7},{7,6},{16,24},{17,25},{1... | collective-permute-start | bytes 786440 | tf_op jit(solution)/shard_map/ppermute | solution.py:371
  52.6 5.8 %collective-permute-start.17 = (bf16[128,512]{1,0:T(8,128)(2,1)S(1)}, bf16[128,512]{1,0:T(8,128)(2,1)S(1)}, u32[]{:S(2)}, u32[]{:S(2)}) collective-permute-start(bf16[128,512]{1,0:T(8,128)(2,1)S(1)} %get-tuple-element.61), channel_id=1, source_target_pairs={{0,2},{1,3},{2,0},{3,1},{4,6},{5,7},{6,4},{7,5},{8,9},{9,8},{10,11... | collective-permute-start | bytes 393224 | tf_op jit(solution)/shard_map/ppermute | solution.py:464
  58.4 6.0 %collective-permute-start.18 = (bf16[64,512]{1,0:T(8,128)(2,1)S(1)}, bf16[64,512]{1,0:T(8,128)(2,1)S(1)}, u32[]{:S(2)}, u32[]{:S(2)}) collective-permute-start(bf16[64,512]{1,0:T(8,128)(2,1)S(1)} %get-tuple-element.63), channel_id=1, source_target_pairs={{0,4},{1,5},{2,6},{3,7},{4,0},{5,1},{6,2},{7,3},{8,12},{9,13},{10,... | collective-permute-start | bytes 196616 | tf_op jit(solution)/shard_map/ppermute | solution.py:470

commit v9 on v8

--- a/solution.py
+++ b/solution.py
@@ -272,11 +272,9 @@
     def flat(section, x, y):
         return (section * rows + x) * columns + y
 
-    def to_sections(value, moves, back=True, crossed=False):
+    def to_sections(value, moves, back=True):
         if back:
-            returns = [source for source, _ in moves]
-            returns = returns[::-1] if crossed else returns
-            moves = moves + [(target, source) for (_, target), source in zip(moves, returns)]
+            moves = moves + [(target, source) for source, target in moves]
         pairs = [
             (flat(source, x, y), flat(target, x, y))
             for source, target in moves
@@ -285,45 +283,34 @@
         ]
         return lax.ppermute(value, AXES, pairs)
 
-    def beside(axis):
-        def other(x, y):
-            if axis == "tx":
-                return (x ^ 1, y) if rows % 2 == 0 else (x, y)
-            return (x, y ^ 1) if columns % 2 == 0 else (x, y)
-
-        return other
-
-    def tile_swaps(axis, first, couples, lead):
+    def tile_swaps(axis, couples, lead):
         places = {}
         for low, high in couples:
             places[low], places[high] = high, low
-        across = beside("ty" if axis == "tx" else "tx")
-
-        def swapped(x, y):
-            if axis == "tx":
-                return (places[x], y) if x in places else across(x, y)
-            return (x, places[y]) if y in places else across(x, y)
-
-        def same(x, y):
-            return (x, y)
-
         others = [p for p in range(sections) if p != lead]
-        moves = [(lead, lead, swapped)]
-        if sections == 4:
-            buddy, inner, outer = lead ^ 1, 3 - (lead ^ 1), 3 - lead
-            if axis == "tx":
-                moves += [(buddy, inner, same), (inner, buddy, same)]
-                moves += [(outer, outer, beside("tx") if first else across)]
-            else:
-                moves += [(inner, outer, same), (outer, inner, same), (buddy, buddy, across)]
-        else:
-            moves += [(p, q, same) for p, q in zip(others, others[1:] + others[:1])]
-        return [
-            (flat(source, x, y), flat(target, *place(x, y)))
-            for source, target, place in moves
-            for x in range(rows)
-            for y in range(columns)
-        ]
+        buddy, inner, outer = lead ^ 1, 3 - (lead ^ 1), 3 - lead
+        pairs = []
+        for x in range(rows):
+            for y in range(columns):
+                place = x if axis == "tx" else y
+                paired = place in places
+                facing = places.get(place, place)
+                near = (facing, y) if axis == "tx" else (x, facing)
+                aside = (x, y ^ 1) if axis == "tx" else (x ^ 1, y)
+                if aside[0] >= rows or aside[1] >= columns:
+                    aside = (x, y)
+                moves = {}
+                if paired or sections != 4:
+                    moves[lead] = (lead, near)
+                if sections != 4:
+                    moves.update((p, (q, (x, y))) for p, q in zip(others, others[1:] + others[:1]))
+                elif paired:
+                    moves.update({buddy: (inner, (x, y)), inner: (buddy, (x, y)), outer: (outer, aside)})
+                else:
+                    for p, q in ((lead, buddy), (inner, outer)):
+                        moves.update({p: (q, (x, y)), q: (p, (x, y))})
+                pairs += [(flat(p, x, y), flat(q, *tile)) for p, (q, tile) in moves.items()]
+        return pairs
 
     batches, nodes, width = stored.shape[1], stored.shape[4], stored.shape[5]
     blocks, block = local_edges.shape[3], local_edges.shape[5]
@@ -336,7 +323,7 @@
     for axis, base, count in (("tx", 0, rows), ("ty", 2, columns)):
         for first, couples in swap_phases(count):
             phases.append((axis, base, first, count))
-            route = {lead: tile_swaps(axis, first, couples, lead) for lead in {0, top}}
+            route = {lead: tile_swaps(axis, couples, lead) for lead in {0, top}}
             routes.append(route)
     phases = tuple(phases)
     splits, left = [], rows * columns
@@ -403,7 +390,7 @@
         moves = [(top - step, top)] + ([(step, 0)] if step < lower else [])
         layers.append(to_sections(layer, moves))
 
-    def fetch_home(values, crossed=False):
+    def fetch_home(values):
         got = None
         for step in range(1, upper):
             moves = [(top, top - step)]
@@ -413,7 +400,7 @@
                 value = call(
                     functools.partial(choose_kernel, top), [value, values[step]], [whole], 0
                 )[0]
-            new = to_sections(value, moves, crossed=crossed)
+            new = to_sections(value, moves)
             takes = here == top - step
             if step < lower:
                 takes = takes | (here == step)
@@ -470,14 +457,14 @@
         got = lax.ppermute(parcel, AXES, splits[-1][1])
         result, summed = call(
             functools.partial(last_kernel, top, count, scale),
-            [mask, total, *arrived, results[top], fetch_home(results, True), kept, got],
+            [mask, total, *arrived, results[top], fetch_home(results), kept, got],
             [whole, (kept.shape, F32)], 0, jax.ShapeDtypeStruct,
         )
     else:
         summed = scale * lax.psum_scatter(pieces[0], ("tx", "ty"), scatter_dimension=0, tiled=True)
         result = call(
             functools.partial(last_kernel, top, count, None),
-            [mask, total, *arrived, results[top], fetch_home(results, True)], [whole], 0,
+            [mask, total, *arrived, results[top], fetch_home(results)], [whole], 0,
             jax.ShapeDtypeStruct,
         )[0]
     return (summed[None], result.reshape(1, batches, 1, 1, nodes, width))

time: 65.7 us -> 68.3 us (1.040)
  starting transfers between devices: 17.6 us -> 30.9 us
  waiting for transfers between devices: 38.2 us -> 27.4 us
    ppermute x12, starting transfers between devices: 11.8 us -> 19.8 us  [exchange(): lax.ppermute(out, AXES, route[lead])]
    ppermute x2, waiting for transfers between devices: 7.24 us -> 2.95 us  [per_device(): got = lax.ppermute(parcel, AXES, pairs)]
    ppermute x2, starting transfers between devices: 2.28 us -> 5.93 us  [per_device(): got = lax.ppermute(parcel, AXES, pairs)]
    ppermute x4, waiting for transfers between devices: 11.7 us -> 9.21 us  [to_sections(): return lax.ppermute(value, AXES, pairs)]
    ppermute x12, waiting for transfers between devices: 14.8 us -> 12.5 us  [exchange(): lax.ppermute(out, AXES, route[lead])]
    ppermute x1, waiting for transfers between devices: 4.43 us -> 2.81 us  [per_device(): got = lax.ppermute(parcel, AXES, splits[-1][1])]
    ppermute x1, starting transfers between devices: 1.58 us -> 3.09 us  [per_device(): got = lax.ppermute(parcel, AXES, splits[-1][1])]
  transfers between devices with their start and end apart: 19 -> 19, of which waited for: 10 -> 9; matrix products, arithmetic and copies ran while one was open for 0% -> 0% of each run, Pallas kernels for 2% -> 2%
where the time goes in v9:
time: 68.3 us; the launch traced here: 68.1 us
  starting transfers between devices  30.9 us (45%)
  waiting for transfers between devices  27.4 us (40%)
  Pallas kernels  9.03 us (13%)
  between operations  0.77 us (1%)
    ppermute x12, starting transfers between devices, exchange(): lax.ppermute(out, AXES, route[lead])  19.8 us
    ppermute x12, waiting for transfers between devices, exchange(): lax.ppermute(out, AXES, route[lead])  12.5 us
    ppermute x4, waiting for transfers between devices, to_sections(): return lax.ppermute(value, AXES, pairs)  9.21 us
    pallas_call x14, Pallas kernels, call(): pl.pallas_call(body, out_shape=[kind(shape, dtype) for shape, dtype in ou...  9.03 us
    ppermute x2, starting transfers between devices, per_device(): got = lax.ppermute(parcel, AXES, pairs)  5.93 us
    ppermute x1, starting transfers between devices, per_device(): got = lax.ppermute(parcel, AXES, splits[-1][1])  3.09 us
    ppermute x2, waiting for transfers between devices, per_device(): got = lax.ppermute(parcel, AXES, pairs)  2.95 us
    ppermute x1, waiting for transfers between devices, per_device(): got = lax.ppermute(parcel, AXES, splits[-1][1])  2.81 us
  transfers between devices with their start and end apart: 19, of which 9 were waited for; matrix products, arithmetic and copies ran while one was open for 0% of the time, Pallas kernels for 2%

profile of v9, /device:TPU:0, one launch (start us, length us, event | category | flops | bytes accessed | tf_op | source)
XLA Modules:
  0.0 68.1 jit_solution(5002368083856751277)
XLA Ops:
  0.6 2.8 %shard_map.86 = (bf16[2,512,512]{2,1,0:T(8,128)(2,1)S(1)}, bf16[2,640,256]{2,1,0:T(8,128)(2,1)S(1)}, f32[12,1,512]{2,1,0:T(1,128)S(1)}, bf16[512,512]{1,0:T(8,12...) custom-call(bf16[512,512]{1,0:T(8,128)(2,1)} %bitcast.11, ...), custom_call_target="tpu_custom_call" | custom-call | flops 738197504 | bytes 5922944 | tf_op jit(solution)/shard_map/pallas_call | solution.py:254
  3.5 0.5 collective-permute-start.3
  4.0 2.6 %collective-permute-start = (bf16[2,128,512]{2,1,0:T(8,128)(2,1)S(1)}, bf16[2,128,512]{2,1,0:T(8,128)(2,1)S(1)}, u32[]{:S(2)}, u32[]{:S(2)}) collective-permute-start(bf16[2,128,512]{2,1,0:T(8,128)(2,1)S(1)} %get-tuple-element.37), channel_id=1, source_target_pairs={{24,26},{16,8},{8,16},{0,1},{25,27},{17,9},{9,17},{1,0},{26,24},{1... | collective-permute-start | bytes 786440 | tf_op jit(solution)/shard_map/ppermute | solution.py:358
  6.7 2.0 %collective-permute-start.2 = (bf16[2,128,512]{2,1,0:T(8,128)(2,1)S(1)}, bf16[2,128,512]{2,1,0:T(8,128)(2,1)S(1)}, u32[]{:S(2)}, u32[]{:S(2)}) collective-permute-start(bf16[2,128,512]{2,1,0:T(8,128)(2,1)S(1)} %get-tuple-element.39), channel_id=1, source_target_pairs={{24,25},{16,8},{8,16},{0,2},{25,24},{17,9},{9,17},{1,3},{26,27},{1... | collective-permute-start | bytes 786440 | tf_op jit(solution)/shard_map/ppermute | solution.py:358
  8.7 0.3 shard_map.87.total_ref
  9.0 2.0 %collective-permute-done.refs_0_ = bf16[2,128,512]{2,1,0:T(8,128)(2,1)S(1)} collective-permute-done((bf16[2,128,512]{2,1,0:T(8,128)(2,1)S(1)}, bf16[2,128,512]{2,1,0:T(8,128)(2,1)S(1)}, u32[]{:S(2)}, u32[]{:S(2)}) %collective-permute-start) | collective-permute-done | bytes 262176 | tf_op jit(solution)/shard_map/ppermute | solution.py:358
  10.9 2.1 %collective-permute-done.2.refs_2_ = bf16[2,128,512]{2,1,0:T(8,128)(2,1)S(1)} collective-permute-done((bf16[2,128,512]{2,1,0:T(8,128)(2,1)S(1)}, bf16[2,128,512]{2,1,0:T(8,128)(2,1)S(1)}, u32[]{:S(2)}, u32[]{:S(2)}) %collective-permute-start.2) | collective-permute-done | bytes 262176 | tf_op jit(solution)/shard_map/ppermute | solution.py:358
  13.0 0.9 %shard_map.88 = (bf16[512,512]{1,0:T(8,128)(2,1)S(1)}, bf16[512,512]{1,0:T(8,128)(2,1)S(1)}, bf16[512,512]{1,0:T(8,128)(2,1)S(1)}, bf16[2,128,512]{2,1,0:T(8,128...) custom-call(f32[12,1,512]{2,1,0:T(1,128)S(1)} %get-tuple-element.34.mask_ref, ...), custom_call_target="tpu_custom_call" | custom-call | flops 469762048 | bytes 5922816 | tf_op jit(solution)/shard_map/pallas_call | solution.py:254
  14.0 1.6 %collective-permute-start.4 = (bf16[2,128,512]{2,1,0:T(8,128)(2,1)S(1)}, bf16[2,128,512]{2,1,0:T(8,128)(2,1)S(1)}, u32[]{:S(2)}, u32[]{:S(2)}) collective-permute-start(bf16[2,128,512]{2,1,0:T(8,128)(2,1)S(1)} %get-tuple-element.43), channel_id=1, source_target_pairs={{24,26},{16,8},{8,16},{0,1},{25,27},{17,9},{9,17},{1,0},{26,24},{1... | collective-permute-start | bytes 786440 | tf_op jit(solution)/shard_map/ppermute | solution.py:358
  15.5 0.7 %collective-permute-start.5 = (bf16[2,128,512]{2,1,0:T(8,128)(2,1)S(1)}, bf16[2,128,512]{2,1,0:T(8,128)(2,1)S(1)}, u32[]{:S(2)}, u32[]{:S(2)}) collective-permute-start(bf16[2,128,512]{2,1,0:T(8,128)(2,1)S(1)} %get-tuple-element.44), channel_id=1, source_target_pairs={{24,16},{16,24},{8,0},{0,8},{25,17},{17,25},{9,1},{1,9},{26,28},{1... | collective-permute-start | bytes 786440 | tf_op jit(solution)/shard_map/ppermute | solution.py:358
  16.2 2.6 %collective-permute-start.6 = (bf16[2,128,512]{2,1,0:T(8,128)(2,1)S(1)}, bf16[2,128,512]{2,1,0:T(8,128)(2,1)S(1)}, u32[]{:S(2)}, u32[]{:S(2)}) collective-permute-start(bf16[2,128,512]{2,1,0:T(8,128)(2,1)S(1)} %get-tuple-element.45), channel_id=1, source_target_pairs={{24,25},{16,8},{8,16},{0,2},{25,24},{17,9},{9,17},{1,3},{26,27},{1... | collective-permute-start | bytes 786440 | tf_op jit(solution)/shard_map/ppermute | solution.py:358
  18.8 0.3 shard_map.89.total_ref
  19.1 1.3 %collective-permute-done.4.refs_0_ = bf16[2,128,512]{2,1,0:T(8,128)(2,1)S(1)} collective-permute-done((bf16[2,128,512]{2,1,0:T(8,128)(2,1)S(1)}, bf16[2,128,512]{2,1,0:T(8,128)(2,1)S(1)}, u32[]{:S(2)}, u32[]{:S(2)}) %collective-permute-start.4) | collective-permute-done | bytes 262176 | tf_op jit(solution)/shard_map/ppermute | solution.py:358
  20.4 2.8 %collective-permute-done.6.refs_2_ = bf16[2,128,512]{2,1,0:T(8,128)(2,1)S(1)} collective-permute-done((bf16[2,128,512]{2,1,0:T(8,128)(2,1)S(1)}, bf16[2,128,512]{2,1,0:T(8,128)(2,1)S(1)}, u32[]{:S(2)}, u32[]{:S(2)}) %collective-permute-start.6) | collective-permute-done | bytes 262176 | tf_op jit(solution)/shard_map/ppermute | solution.py:358
  23.2 0.4 shard_map.90.top_ref
  23.5 1.3 %collective-permute-start.7 = (bf16[512,512]{1,0:T(8,128)(2,1)S(1)}, bf16[512,512]{1,0:T(8,128)(2,1)S(1)}, u32[]{:S(2)}, u32[]{:S(2)}) collective-permute-start(bf16[512,512]{1,0:T(8,128)(2,1)S(1)} %shard_map.90.top_ref), channel_id=1, source_target_pairs={{24,0},{25,1},{26,2},{27,3},{28,4},{29,5},{30,6},{31,7}} | collective-permute-start | bytes 1572872 | tf_op jit(solution)/shard_map/ppermute | solution.py:284
  24.8 9.2 %collective-permute-done.7.upstream_ref = bf16[512,512]{1,0:T(8,128)(2,1)S(1)} collective-permute-done((bf16[512,512]{1,0:T(8,128)(2,1)S(1)}, bf16[512,512]{1,0:T(8,128)(2,1)S(1)}, u32[]{:S(2)}, u32[]{:S(2)}) %collective-permute-start.7) | collective-permute-done | bytes 524320 | tf_op jit(solution)/shard_map/ppermute | solution.py:284
  34.0 0.7 %shard_map.91 = (bf16[512,512]{1,0:T(8,128)(2,1)S(1)}, bf16[512,512]{1,0:T(8,128)(2,1)S(1)}, bf16[2,128,512]{2,1,0:T(8,128)(2,1)S(1)}, bf16[2,128,512]{2,1,0:T(8,128)(2,1)S(1)}, bf16[2,128,512]{2,1,0:T(8,128)(2,1)S(1)}) custom-call(bf16[2,512,512]{2,1,0:T(8,128)(2,1)S(1)} %collective-permute-done.3.refs_3_.layer_ref, ...), custom_call_target="tpu_custom_call" | custom-call | flops 469762048 | bytes 4063232 | tf_op jit(solution)/shard_map/pallas_call | solution.py:254
  34.9 2.9 %collective-permute-start.8 = (bf16[2,128,512]{2,1,0:T(8,128)(2,1)S(1)}, bf16[2,128,512]{2,1,0:T(8,128)(2,1)S(1)}, u32[]{:S(2)}, u32[]{:S(2)}) collective-permute-start(bf16[2,128,512]{2,1,0:T(8,128)(2,1)S(1)} %get-tuple-element.47), channel_id=1, source_target_pairs={{0,2},{8,16},{16,8},{24,25},{1,3},{9,17},{17,9},{25,24},{2,0},{10,... | collective-permute-start | bytes 786440 | tf_op jit(solution)/shard_map/ppermute | solution.py:358
  37.8 1.5 %collective-permute-start.10 = (bf16[2,128,512]{2,1,0:T(8,128)(2,1)S(1)}, bf16[2,128,512]{2,1,0:T(8,128)(2,1)S(1)}, u32[]{:S(2)}, u32[]{:S(2)}) collective-permute-start(bf16[2,128,512]{2,1,0:T(8,128)(2,1)S(1)} %get-tuple-element.49), channel_id=1, source_target_pairs={{0,1},{8,16},{16,8},{24,26},{1,0},{9,17},{17,9},{25,27},{2,3},{10,... | collective-permute-start | bytes 786440 | tf_op jit(solution)/shard_map/ppermute | solution.py:358
  39.5 0.3 shard_map.92.total_ref
  39.8 2.3 %collective-permute-done.8.refs_0_ = bf16[2,128,512]{2,1,0:T(8,128)(2,1)S(1)} collective-permute-done((bf16[2,128,512]{2,1,0:T(8,128)(2,1)S(1)}, bf16[2,128,512]{2,1,0:T(8,128)(2,1)S(1)}, u32[]{:S(2)}, u32[]{:S(2)}) %collective-permute-start.8) | collective-permute-done | bytes 262176 | tf_op jit(solution)/shard_map/ppermute | solution.py:358
  42.2 2.0 %collective-permute-done.10.refs_2_ = bf16[2,128,512]{2,1,0:T(8,128)(2,1)S(1)} collective-permute-done((bf16[2,128,512]{2,1,0:T(8,128)(2,1)S(1)}, bf16[2,128,512]{2,1,0:T(8,128)(2,1)S(1)}, u32[]{:S(2)}, u32[]{:S(2)}) %collective-permute-start.10) | collective-permute-done | bytes 262176 | tf_op jit(solution)/shard_map/ppermute | solution.py:358
  44.2 1.7 %shard_map.95 = (bf16[512,512]{1,0:T(8,128)(2,1)S(1)}, f32[512,512]{1,0:T(8,128)S(1)}, bf16[2,128,512]{2,1,0:T(8,128)(2,1)S(1)}, bf16[2,128,512]{2,1,0:T(8,128)(...) custom-call(f32[12,1,512]{2,1,0:T(1,128)S(1)} %get-tuple-element.34.mask_ref, ...), custom_call_target="tpu_custom_call" | custom-call | flops 872415232 | bytes 8282112 | tf_op jit(solution)/shard_map/pallas_call | solution.py:254
  46.1 1.5 %collective-permute-start.16 = (bf16[256,512]{1,0:T(8,128)(2,1)S(1)}, bf16[256,512]{1,0:T(8,128)(2,1)S(1)}, u32[]{:S(2)}, u32[]{:S(2)}) collective-permute-start(bf16[256,512]{1,0:T(8,128)(2,1)S(1)} %get-tuple-element.59), channel_id=1, source_target_pairs={{0,1},{1,0},{2,3},{3,2},{4,5},{5,4},{6,7},{7,6},{8,10},{9,11},{10,... | collective-permute-start | bytes 786440 | tf_op jit(solution)/shard_map/ppermute | solution.py:451
  47.7 5.3 %collective-permute-start.12 = (bf16[2,128,512]{2,1,0:T(8,128)(2,1)S(1)}, bf16[2,128,512]{2,1,0:T(8,128)(2,1)S(1)}, u32[]{:S(2)}, u32[]{:S(2)}) collective-permute-start(bf16[2,128,512]{2,1,0:T(8,128)(2,1)S(1)} %get-tuple-element.54), channel_id=1, source_target_pairs={{0,2},{8,16},{16,8},{24,25},{1,3},{9,17},{17,9},{25,24},{2,0},{10,... | collective-permute-start | bytes 786440 | tf_op jit(solution)/shard_map/ppermute | solution.py:358
  53.0 0.5 collective-permute-start.14
  53.6 4.4 %collective-permute-start.17 = (bf16[128,512]{1,0:T(8,128)(2,1)S(1)}, bf16[128,512]{1,0:T(8,128)(2,1)S(1)}, u32[]{:S(2)}, u32[]{:S(2)}) collective-permute-start(bf16[128,512]{1,0:T(8,128)(2,1)S(1)} %get-tuple-element.61), channel_id=1, source_target_pairs={{0,2},{1,3},{2,0},{3,1},{4,6},{5,7},{6,4},{7,5},{8,9},{9,8},{10,11... | collective-permute-start | bytes 393224 | tf_op jit(solution)/shard_map/ppermute | solution.py:451
  58.0 2.9 %collective-permute-done.17.got_ref = bf16[128,512]{1,0:T(8,128)(2,1)S(1)} collective-permute-done((bf16[128,512]{1,0:T(8,128)(2,1)S(1)}, bf16[128,512]{1,0:T(8,128)(2,1)S(1)}, u32[]{:S(2)}, u32[]{:S(2)}) %collective-permute-start.17) | collective-permute-done | bytes 131104 | tf_op jit(solution)/shard_map/ppermute | solution.py:451
  61.0 3.1 %collective-permute-start.18 = (bf16[64,512]{1,0:T(8,128)(2,1)S(1)}, bf16[64,512]{1,0:T(8,128)(2,1)S(1)}, u32[]{:S(2)}, u32[]{:S(2)}) collective-permute-start(bf16[64,512]{1,0:T(8,128)(2,1)S(1)} %get-tuple-element.63), channel_id=1, source_target_pairs={{0,4},{1,5},{2,6},{3,7},{4,0},{5,1},{6,2},{7,3},{8,12},{9,13},{10,... | collective-permute-start | bytes 196616 | tf_op jit(solution)/shard_map/ppermute | solution.py:457
  64.1 2.8 %collective-permute-done.18.refs_6_ = bf16[64,512]{1,0:T(8,128)(2,1)S(1)} collective-permute-done((bf16[64,512]{1,0:T(8,128)(2,1)S(1)}, bf16[64,512]{1,0:T(8,128)(2,1)S(1)}, u32[]{:S(2)}, u32[]{:S(2)}) %collective-permute-start.18) | collective-permute-done | bytes 65568 | tf_op jit(solution)/shard_map/ppermute | solution.py:457
  66.9 1.2 %shard_map.99 = (bf16[512,512]{1,0:T(8,128)(2,1)}, f32[64,512]{1,0:T(8,128)}) custom-call(f32[12,1,512]{2,1,0:T(1,128)S(1)} %get-tuple-element.34.mask_ref, f32[512,512]{1,0:T(8,128)S(1)} %get-tuple-element.53.total_ref, bf16[2,128,512]{2,1,0:T(8,128)(2,1)S(1)} %collective-permute-done.12.refs_0_, bf16[2,128,512]{2,1,0:T(8,128)(2,1)S(1)} %collective-permute-done.13.refs_1_, ...), custom_call_target="tpu_custom_call" | custom-call | bytes 3760128 | tf_op jit(solution)/shard_map/pallas_call | solution.py:254
  (24 shorter events, 0.8 us)
Async XLA Ops:
  0.6 8.0 %copy-start.1 = (bf16[2,1,1,256,512]{4,3,2,1,0:T(8,128)(2,1)S(1)}, bf16[2,1,1,256,512]{4,3,2,1,0:T(8,128)(2,1)}, u32[]{:S(2)}) copy-start(bf16[2,1,1,256,512]{4,3,2,1,0:T(8,128)(2,1)} %param.8) | copy-start | bytes 1572868
  3.5 9.6 %collective-permute-start.3 = (bf16[2,512,512]{2,1,0:T(8,128)(2,1)S(1)}, bf16[2,512,512]{2,1,0:T(8,128)(2,1)S(1)}, u32[]{:S(2)}, u32[]{:S(2)}) collective-permute-start(bf16[2,512,512]{2,1,0:T(8,128)(2,1)S(1)} %get-tuple-element.40.refs_6_), channel_id=1, source_target_pairs={{16,24},{17,25},{18,26},{19,27},{20,28},{21,29},{22,30},{23,31},{8... | collective-permute-start | bytes 3145736 | tf_op jit(solution)/shard_map/ppermute | solution.py:284
  4.0 6.9 %collective-permute-start = (bf16[2,128,512]{2,1,0:T(8,128)(2,1)S(1)}, bf16[2,128,512]{2,1,0:T(8,128)(2,1)S(1)}, u32[]{:S(2)}, u32[]{:S(2)}) collective-permute-start(bf16[2,128,512]{2,1,0:T(8,128)(2,1)S(1)} %get-tuple-element.37), channel_id=1, source_target_pairs={{24,26},{16,8},{8,16},{0,1},{25,27},{17,9},{9,17},{1,0},{26,24},{1... | collective-permute-start | bytes 786440 | tf_op jit(solution)/shard_map/ppermute | solution.py:358
  6.6 4.4 %collective-permute-start.1 = (bf16[2,128,512]{2,1,0:T(8,128)(2,1)S(1)}, bf16[2,128,512]{2,1,0:T(8,128)(2,1)S(1)}, u32[]{:S(2)}, u32[]{:S(2)}) collective-permute-start(bf16[2,128,512]{2,1,0:T(8,128)(2,1)S(1)} %get-tuple-element.38), channel_id=1, source_target_pairs={{24,16},{16,24},{8,0},{0,8},{25,17},{17,25},{9,1},{1,9},{26,28},{1... | collective-permute-start | bytes 786440 | tf_op jit(solution)/shard_map/ppermute | solution.py:358
  6.7 6.4 %collective-permute-start.2 = (bf16[2,128,512]{2,1,0:T(8,128)(2,1)S(1)}, bf16[2,128,512]{2,1,0:T(8,128)(2,1)S(1)}, u32[]{:S(2)}, u32[]{:S(2)}) collective-permute-start(bf16[2,128,512]{2,1,0:T(8,128)(2,1)S(1)} %get-tuple-element.39), channel_id=1, source_target_pairs={{24,25},{16,8},{8,16},{0,2},{25,24},{17,9},{9,17},{1,3},{26,27},{1... | collective-permute-start | bytes 786440 | tf_op jit(solution)/shard_map/ppermute | solution.py:358
  14.0 6.4 %collective-permute-start.4 = (bf16[2,128,512]{2,1,0:T(8,128)(2,1)S(1)}, bf16[2,128,512]{2,1,0:T(8,128)(2,1)S(1)}, u32[]{:S(2)}, u32[]{:S(2)}) collective-permute-start(bf16[2,128,512]{2,1,0:T(8,128)(2,1)S(1)} %get-tuple-element.43), channel_id=1, source_target_pairs={{24,26},{16,8},{8,16},{0,1},{25,27},{17,9},{9,17},{1,0},{26,24},{1... | collective-permute-start | bytes 786440 | tf_op jit(solution)/shard_map/ppermute | solution.py:358
  15.5 4.9 %collective-permute-start.5 = (bf16[2,128,512]{2,1,0:T(8,128)(2,1)S(1)}, bf16[2,128,512]{2,1,0:T(8,128)(2,1)S(1)}, u32[]{:S(2)}, u32[]{:S(2)}) collective-permute-start(bf16[2,128,512]{2,1,0:T(8,128)(2,1)S(1)} %get-tuple-element.44), channel_id=1, source_target_pairs={{24,16},{16,24},{8,0},{0,8},{25,17},{17,25},{9,1},{1,9},{26,28},{1... | collective-permute-start | bytes 786440 | tf_op jit(solution)/shard_map/ppermute | solution.py:358
  16.2 6.9 %collective-permute-start.6 = (bf16[2,128,512]{2,1,0:T(8,128)(2,1)S(1)}, bf16[2,128,512]{2,1,0:T(8,128)(2,1)S(1)}, u32[]{:S(2)}, u32[]{:S(2)}) collective-permute-start(bf16[2,128,512]{2,1,0:T(8,128)(2,1)S(1)} %get-tuple-element.45), channel_id=1, source_target_pairs={{24,25},{16,8},{8,16},{0,2},{25,24},{17,9},{9,17},{1,3},{26,27},{1... | collective-permute-start | bytes 786440 | tf_op jit(solution)/shard_map/ppermute | solution.py:358
  23.5 10.5 %collective-permute-start.7 = (bf16[512,512]{1,0:T(8,128)(2,1)S(1)}, bf16[512,512]{1,0:T(8,128)(2,1)S(1)}, u32[]{:S(2)}, u32[]{:S(2)}) collective-permute-start(bf16[512,512]{1,0:T(8,128)(2,1)S(1)} %shard_map.90.top_ref), channel_id=1, source_target_pairs={{24,0},{25,1},{26,2},{27,3},{28,4},{29,5},{30,6},{31,7}} | collective-permute-start | bytes 1572872 | tf_op jit(solution)/shard_map/ppermute | solution.py:284
  34.8 4.6 %copy-start = (bf16[1,2,1,1,256,512]{5,4,3,2,1,0:T(8,128)(2,1)S(1)}, bf16[1,2,1,1,256,512]{5,4,3,2,1,0:T(8,128)(2,1)}, u32[]{:S(2)}) copy-start(bf16[1,2,1,1,256,512]{5,4,3,2,1,0:T(8,128)(2,1)} %param.7) | copy-start | bytes 1572868
  34.9 9.3 %collective-permute-start.11 = (bf16[512,512]{1,0:T(8,128)(2,1)S(1)}, bf16[512,512]{1,0:T(8,128)(2,1)S(1)}, u32[]{:S(2)}, u32[]{:S(2)}) collective-permute-start(bf16[512,512]{1,0:T(8,128)(2,1)S(1)} %shard_map.94), channel_id=1, source_target_pairs={{24,16},{25,17},{26,18},{27,19},{28,20},{29,21},{30,22},{31,23},{0... | collective-permute-start | bytes 1572872 | tf_op jit(solution)/shard_map/ppermute | solution.py:284
  34.9 7.2 %collective-permute-start.8 = (bf16[2,128,512]{2,1,0:T(8,128)(2,1)S(1)}, bf16[2,128,512]{2,1,0:T(8,128)(2,1)S(1)}, u32[]{:S(2)}, u32[]{:S(2)}) collective-permute-start(bf16[2,128,512]{2,1,0:T(8,128)(2,1)S(1)} %get-tuple-element.47), channel_id=1, source_target_pairs={{0,2},{8,16},{16,8},{24,25},{1,3},{9,17},{17,9},{25,24},{2,0},{10,... | collective-permute-start | bytes 786440 | tf_op jit(solution)/shard_map/ppermute | solution.py:358
  37.8 4.4 %collective-permute-start.9 = (bf16[2,128,512]{2,1,0:T(8,128)(2,1)S(1)}, bf16[2,128,512]{2,1,0:T(8,128)(2,1)S(1)}, u32[]{:S(2)}, u32[]{:S(2)}) collective-permute-start(bf16[2,128,512]{2,1,0:T(8,128)(2,1)S(1)} %get-tuple-element.48), channel_id=1, source_target_pairs={{0,8},{8,0},{16,24},{24,16},{1,9},{9,1},{17,25},{25,17},{2,4},{10,... | collective-permute-start | bytes 786440 | tf_op jit(solution)/shard_map/ppermute | solution.py:358
  37.8 6.4 %collective-permute-start.10 = (bf16[2,128,512]{2,1,0:T(8,128)(2,1)S(1)}, bf16[2,128,512]{2,1,0:T(8,128)(2,1)S(1)}, u32[]{:S(2)}, u32[]{:S(2)}) collective-permute-start(bf16[2,128,512]{2,1,0:T(8,128)(2,1)S(1)} %get-tuple-element.49), channel_id=1, source_target_pairs={{0,1},{8,16},{16,8},{24,26},{1,0},{9,17},{17,9},{25,27},{2,3},{10,... | collective-permute-start | bytes 786440 | tf_op jit(solution)/shard_map/ppermute | solution.py:358
  45.9 21.0 %collective-permute-start.15 = (bf16[512,512]{1,0:T(8,128)(2,1)S(1)}, bf16[512,512]{1,0:T(8,128)(2,1)S(1)}, u32[]{:S(2)}, u32[]{:S(2)}) collective-permute-start(bf16[512,512]{1,0:T(8,128)(2,1)S(1)} %shard_map.96), channel_id=1, source_target_pairs={{24,16},{25,17},{26,18},{27,19},{28,20},{29,21},{30,22},{31,23},{0... | collective-permute-start | bytes 1572872 | tf_op jit(solution)/shard_map/ppermute | solution.py:284
  46.1 7.4 %collective-permute-start.16 = (bf16[256,512]{1,0:T(8,128)(2,1)S(1)}, bf16[256,512]{1,0:T(8,128)(2,1)S(1)}, u32[]{:S(2)}, u32[]{:S(2)}) collective-permute-start(bf16[256,512]{1,0:T(8,128)(2,1)S(1)} %get-tuple-element.59), channel_id=1, source_target_pairs={{0,1},{1,0},{2,3},{3,2},{4,5},{5,4},{6,7},{7,6},{8,10},{9,11},{10,... | collective-permute-start | bytes 786440 | tf_op jit(solution)/shard_map/ppermute | solution.py:451
  47.7 16.5 %collective-permute-start.12 = (bf16[2,128,512]{2,1,0:T(8,128)(2,1)S(1)}, bf16[2,128,512]{2,1,0:T(8,128)(2,1)S(1)}, u32[]{:S(2)}, u32[]{:S(2)}) collective-permute-start(bf16[2,128,512]{2,1,0:T(8,128)(2,1)S(1)} %get-tuple-element.54), channel_id=1, source_target_pairs={{0,2},{8,16},{16,8},{24,25},{1,3},{9,17},{17,9},{25,24},{2,0},{10,... | collective-permute-start | bytes 786440 | tf_op jit(solution)/shard_map/ppermute | solution.py:358
  53.0 11.1 %collective-permute-start.13 = (bf16[2,128,512]{2,1,0:T(8,128)(2,1)S(1)}, bf16[2,128,512]{2,1,0:T(8,128)(2,1)S(1)}, u32[]{:S(2)}, u32[]{:S(2)}) collective-permute-start(bf16[2,128,512]{2,1,0:T(8,128)(2,1)S(1)} %get-tuple-element.55), channel_id=1, source_target_pairs={{0,8},{8,0},{16,24},{24,16},{1,9},{9,1},{17,25},{25,17},{2,4},{10,... | collective-permute-start | bytes 786440 | tf_op jit(solution)/shard_map/ppermute | solution.py:358
  53.0 11.1 %collective-permute-start.14 = (bf16[2,128,512]{2,1,0:T(8,128)(2,1)S(1)}, bf16[2,128,512]{2,1,0:T(8,128)(2,1)S(1)}, u32[]{:S(2)}, u32[]{:S(2)}) collective-permute-start(bf16[2,128,512]{2,1,0:T(8,128)(2,1)S(1)} %get-tuple-element.56), channel_id=1, source_target_pairs={{0,1},{8,16},{16,8},{24,26},{1,0},{9,17},{17,9},{25,27},{2,3},{10,... | collective-permute-start | bytes 786440 | tf_op jit(solution)/shard_map/ppermute | solution.py:358
  53.6 7.4 %collective-permute-start.17 = (bf16[128,512]{1,0:T(8,128)(2,1)S(1)}, bf16[128,512]{1,0:T(8,128)(2,1)S(1)}, u32[]{:S(2)}, u32[]{:S(2)}) collective-permute-start(bf16[128,512]{1,0:T(8,128)(2,1)S(1)} %get-tuple-element.61), channel_id=1, source_target_pairs={{0,2},{1,3},{2,0},{3,1},{4,6},{5,7},{6,4},{7,5},{8,9},{9,8},{10,11... | collective-permute-start | bytes 393224 | tf_op jit(solution)/shard_map/ppermute | solution.py:451
  61.0 5.9 %collective-permute-start.18 = (bf16[64,512]{1,0:T(8,128)(2,1)S(1)}, bf16[64,512]{1,0:T(8,128)(2,1)S(1)}, u32[]{:S(2)}, u32[]{:S(2)}) collective-permute-start(bf16[64,512]{1,0:T(8,128)(2,1)S(1)} %get-tuple-element.63), channel_id=1, source_target_pairs={{0,4},{1,5},{2,6},{3,7},{4,0},{5,1},{6,2},{7,3},{8,12},{9,13},{10,... | collective-permute-start | bytes 196616 | tf_op jit(solution)/shard_map/ppermute | solution.py:457

commit v10 on v9

--- a/solution.py
+++ b/solution.py
@@ -283,7 +283,7 @@
         ]
         return lax.ppermute(value, AXES, pairs)
 
-    def tile_swaps(axis, couples, lead):
+    def tile_swaps(axis, first, couples, lead):
         places = {}
         for low, high in couples:
             places[low], places[high] = high, low
@@ -296,16 +296,16 @@
                 paired = place in places
                 facing = places.get(place, place)
                 near = (facing, y) if axis == "tx" else (x, facing)
-                aside = (x, y ^ 1) if axis == "tx" else (x ^ 1, y)
-                if aside[0] >= rows or aside[1] >= columns:
-                    aside = (x, y)
+                aside = (x, y ^ 1) if columns % 2 == 0 else (x, y)
                 moves = {}
                 if paired or sections != 4:
                     moves[lead] = (lead, near)
                 if sections != 4:
                     moves.update((p, (q, (x, y))) for p, q in zip(others, others[1:] + others[:1]))
+                elif paired and axis == "tx" and first == 0 and aside != (x, y):
+                    moves.update({buddy: (buddy, aside), inner: (outer, (x, y)), outer: (inner, (x, y))})
                 elif paired:
-                    moves.update({buddy: (inner, (x, y)), inner: (buddy, (x, y)), outer: (outer, aside)})
+                    moves.update({buddy: (inner, (x, y)), inner: (buddy, (x, y)), outer: (outer, near)})
                 else:
                     for p, q in ((lead, buddy), (inner, outer)):
                         moves.update({p: (q, (x, y)), q: (p, (x, y))})
@@ -323,7 +323,7 @@
     for axis, base, count in (("tx", 0, rows), ("ty", 2, columns)):
         for first, couples in swap_phases(count):
             phases.append((axis, base, first, count))
-            route = {lead: tile_swaps(axis, couples, lead) for lead in {0, top}}
+            route = {lead: tile_swaps(axis, first, couples, lead) for lead in {0, top}}
             routes.append(route)
     phases = tuple(phases)
     splits, left = [], rows * columns

time: 68.3 us -> 67 us (0.981)
  starting transfers between devices: 30.9 us -> 24.1 us
  waiting for transfers between devices: 27.4 us -> 32.8 us
    ppermute x12, starting transfers between devices: 19.8 us -> 14.5 us  [exchange(): lax.ppermute(out, AXES, route[lead])]
    ppermute x2, waiting for transfers between devices: 2.95 us -> 5.52 us  [per_device(): got = lax.ppermute(parcel, AXES, pairs)]
    ppermute x4, waiting for transfers between devices: 9.21 us -> 11.2 us  [to_sections(): return lax.ppermute(value, AXES, pairs)]
    ppermute x2, starting transfers between devices: 5.93 us -> 4.41 us  [per_device(): got = lax.ppermute(parcel, AXES, pairs)]
    ppermute x12, waiting for transfers between devices: 12.5 us -> 13.9 us  [exchange(): lax.ppermute(out, AXES, route[lead])]
  transfers between devices with their start and end apart: 19 -> 19, of which waited for: 9 -> 8; matrix products, arithmetic and copies ran while one was open for 0% -> 0% of each run, Pallas kernels for 2% -> 2%
where the time goes in v10:
time: 67 us; the launch traced here: 66.8 us
  waiting for transfers between devices  32.8 us (49%)
  starting transfers between devices  24.1 us (36%)
  Pallas kernels  9.01 us (13%)
  between operations  0.8 us (1%)
    ppermute x12, starting transfers between devices, exchange(): lax.ppermute(out, AXES, route[lead])  14.5 us
    ppermute x12, waiting for transfers between devices, exchange(): lax.ppermute(out, AXES, route[lead])  13.9 us
    ppermute x4, waiting for transfers between devices, to_sections(): return lax.ppermute(value, AXES, pairs)  11.2 us
    pallas_call x14, Pallas kernels, call(): pl.pallas_call(body, out_shape=[kind(shape, dtype) for shape, dtype in ou...  9.01 us
    ppermute x2, waiting for transfers between devices, per_device(): got = lax.ppermute(parcel, AXES, pairs)  5.52 us
    ppermute x2, starting transfers between devices, per_device(): got = lax.ppermute(parcel, AXES, pairs)  4.41 us
    ppermute x1, starting transfers between devices, per_device(): got = lax.ppermute(parcel, AXES, splits[-1][1])  3.12 us
    ppermute x1, waiting for transfers between devices, per_device(): got = lax.ppermute(parcel, AXES, splits[-1][1])  2.23 us
  transfers between devices with their start and end apart: 19, of which 8 were waited for; matrix products, arithmetic and copies ran while one was open for 0% of the time, Pallas kernels for 2%

profile of v10, /device:TPU:0, one launch (start us, length us, event | category | flops | bytes accessed | tf_op | source)
XLA Modules:
  0.0 66.8 jit_solution(12134807567489770815)
XLA Ops:
  0.6 2.8 %shard_map.86 = (bf16[2,512,512]{2,1,0:T(8,128)(2,1)S(1)}, bf16[2,640,256]{2,1,0:T(8,128)(2,1)S(1)}, f32[12,1,512]{2,1,0:T(1,128)S(1)}, bf16[512,512]{1,0:T(8,12...) custom-call(bf16[512,512]{1,0:T(8,128)(2,1)} %bitcast.11, ...), custom_call_target="tpu_custom_call" | custom-call | flops 738197504 | bytes 5922944 | tf_op jit(solution)/shard_map/pallas_call | solution.py:254
  3.5 0.5 collective-permute-start.3
  4.1 0.4 collective-permute-start.1
  4.5 2.6 %collective-permute-start.2 = (bf16[2,128,512]{2,1,0:T(8,128)(2,1)S(1)}, bf16[2,128,512]{2,1,0:T(8,128)(2,1)S(1)}, u32[]{:S(2)}, u32[]{:S(2)}) collective-permute-start(bf16[2,128,512]{2,1,0:T(8,128)(2,1)S(1)} %get-tuple-element.39), channel_id=1, source_target_pairs={{24,25},{16,8},{8,16},{0,1},{25,24},{17,9},{9,17},{1,0},{26,27},{1... | collective-permute-start | bytes 786440 | tf_op jit(solution)/shard_map/ppermute | solution.py:358
  7.1 0.3 shard_map.87.total_ref
  7.4 4.0 %collective-permute-done.2.refs_2_ = bf16[2,128,512]{2,1,0:T(8,128)(2,1)S(1)} collective-permute-done((bf16[2,128,512]{2,1,0:T(8,128)(2,1)S(1)}, bf16[2,128,512]{2,1,0:T(8,128)(2,1)S(1)}, u32[]{:S(2)}, u32[]{:S(2)}) %collective-permute-start.2) | collective-permute-done | bytes 262176 | tf_op jit(solution)/shard_map/ppermute | solution.py:358
  11.4 0.9 %shard_map.88 = (bf16[512,512]{1,0:T(8,128)(2,1)S(1)}, bf16[512,512]{1,0:T(8,128)(2,1)S(1)}, bf16[512,512]{1,0:T(8,128)(2,1)S(1)}, bf16[2,128,512]{2,1,0:T(8,128...) custom-call(f32[12,1,512]{2,1,0:T(1,128)S(1)} %get-tuple-element.34.mask_ref, ...), custom_call_target="tpu_custom_call" | custom-call | flops 469762048 | bytes 5922816 | tf_op jit(solution)/shard_map/pallas_call | solution.py:254
  12.4 1.1 %collective-permute-start.4 = (bf16[2,128,512]{2,1,0:T(8,128)(2,1)S(1)}, bf16[2,128,512]{2,1,0:T(8,128)(2,1)S(1)}, u32[]{:S(2)}, u32[]{:S(2)}) collective-permute-start(bf16[2,128,512]{2,1,0:T(8,128)(2,1)S(1)} %get-tuple-element.43), channel_id=1, source_target_pairs={{24,26},{16,17},{8,0},{0,8},{25,27},{17,16},{9,1},{1,9},{26,24},{1... | collective-permute-start | bytes 786440 | tf_op jit(solution)/shard_map/ppermute | solution.py:358
  13.5 1.5 %collective-permute-start.6 = (bf16[2,128,512]{2,1,0:T(8,128)(2,1)S(1)}, bf16[2,128,512]{2,1,0:T(8,128)(2,1)S(1)}, u32[]{:S(2)}, u32[]{:S(2)}) collective-permute-start(bf16[2,128,512]{2,1,0:T(8,128)(2,1)S(1)} %get-tuple-element.45), channel_id=1, source_target_pairs={{24,25},{16,8},{8,16},{0,1},{25,24},{17,9},{9,17},{1,0},{26,27},{1... | collective-permute-start | bytes 786440 | tf_op jit(solution)/shard_map/ppermute | solution.py:358
  15.0 0.3 shard_map.89.total_ref
  15.3 4.5 %collective-permute-done.6.refs_2_ = bf16[2,128,512]{2,1,0:T(8,128)(2,1)S(1)} collective-permute-done((bf16[2,128,512]{2,1,0:T(8,128)(2,1)S(1)}, bf16[2,128,512]{2,1,0:T(8,128)(2,1)S(1)}, u32[]{:S(2)}, u32[]{:S(2)}) %collective-permute-start.6) | collective-permute-done | bytes 262176 | tf_op jit(solution)/shard_map/ppermute | solution.py:358
  19.9 0.4 shard_map.90.top_ref
  20.2 1.3 %collective-permute-start.7 = (bf16[512,512]{1,0:T(8,128)(2,1)S(1)}, bf16[512,512]{1,0:T(8,128)(2,1)S(1)}, u32[]{:S(2)}, u32[]{:S(2)}) collective-permute-start(bf16[512,512]{1,0:T(8,128)(2,1)S(1)} %shard_map.90.top_ref), channel_id=1, source_target_pairs={{24,0},{25,1},{26,2},{27,3},{28,4},{29,5},{30,6},{31,7}} | collective-permute-start | bytes 1572872 | tf_op jit(solution)/shard_map/ppermute | solution.py:284
  21.5 11.2 %collective-permute-done.7.upstream_ref = bf16[512,512]{1,0:T(8,128)(2,1)S(1)} collective-permute-done((bf16[512,512]{1,0:T(8,128)(2,1)S(1)}, bf16[512,512]{1,0:T(8,128)(2,1)S(1)}, u32[]{:S(2)}, u32[]{:S(2)}) %collective-permute-start.7) | collective-permute-done | bytes 524320 | tf_op jit(solution)/shard_map/ppermute | solution.py:284
  32.7 0.8 %shard_map.91 = (bf16[512,512]{1,0:T(8,128)(2,1)S(1)}, bf16[512,512]{1,0:T(8,128)(2,1)S(1)}, bf16[2,128,512]{2,1,0:T(8,128)(2,1)S(1)}, bf16[2,128,512]{2,1,0:T(8,128)(2,1)S(1)}, bf16[2,128,512]{2,1,0:T(8,128)(2,1)S(1)}) custom-call(bf16[2,512,512]{2,1,0:T(8,128)(2,1)S(1)} %collective-permute-done.3.refs_3_.layer_ref, ...), custom_call_target="tpu_custom_call" | custom-call | flops 469762048 | bytes 4063232 | tf_op jit(solution)/shard_map/pallas_call | solution.py:254
  33.7 3.9 %collective-permute-start.8 = (bf16[2,128,512]{2,1,0:T(8,128)(2,1)S(1)}, bf16[2,128,512]{2,1,0:T(8,128)(2,1)S(1)}, u32[]{:S(2)}, u32[]{:S(2)}) collective-permute-start(bf16[2,128,512]{2,1,0:T(8,128)(2,1)S(1)} %get-tuple-element.47), channel_id=1, source_target_pairs={{0,2},{8,9},{16,24},{24,16},{1,3},{9,8},{17,25},{25,17},{2,0},{10,... | collective-permute-start | bytes 786440 | tf_op jit(solution)/shard_map/ppermute | solution.py:358
  37.5 0.6 collective-permute-start.10
  38.1 0.2 shard_map.93.refs_3_
  38.3 0.3 shard_map.92.total_ref
  38.6 3.3 %collective-permute-done.8.refs_0_ = bf16[2,128,512]{2,1,0:T(8,128)(2,1)S(1)} collective-permute-done((bf16[2,128,512]{2,1,0:T(8,128)(2,1)S(1)}, bf16[2,128,512]{2,1,0:T(8,128)(2,1)S(1)}, u32[]{:S(2)}, u32[]{:S(2)}) %collective-permute-start.8) | collective-permute-done | bytes 262176 | tf_op jit(solution)/shard_map/ppermute | solution.py:358
  41.9 2.0 %collective-permute-done.10.refs_2_ = bf16[2,128,512]{2,1,0:T(8,128)(2,1)S(1)} collective-permute-done((bf16[2,128,512]{2,1,0:T(8,128)(2,1)S(1)}, bf16[2,128,512]{2,1,0:T(8,128)(2,1)S(1)}, u32[]{:S(2)}, u32[]{:S(2)}) %collective-permute-start.10) | collective-permute-done | bytes 262176 | tf_op jit(solution)/shard_map/ppermute | solution.py:358
  43.9 1.7 %shard_map.95 = (bf16[512,512]{1,0:T(8,128)(2,1)S(1)}, f32[512,512]{1,0:T(8,128)S(1)}, bf16[2,128,512]{2,1,0:T(8,128)(2,1)S(1)}, bf16[2,128,512]{2,1,0:T(8,128)(...) custom-call(f32[12,1,512]{2,1,0:T(1,128)S(1)} %get-tuple-element.34.mask_ref, ...), custom_call_target="tpu_custom_call" | custom-call | flops 872415232 | bytes 8282112 | tf_op jit(solution)/shard_map/pallas_call | solution.py:254
  45.7 0.2 collective-permute-start.15
  45.9 0.6 collective-permute-start.16
  46.4 3.7 %collective-permute-start.12 = (bf16[2,128,512]{2,1,0:T(8,128)(2,1)S(1)}, bf16[2,128,512]{2,1,0:T(8,128)(2,1)S(1)}, u32[]{:S(2)}, u32[]{:S(2)}) collective-permute-start(bf16[2,128,512]{2,1,0:T(8,128)(2,1)S(1)} %get-tuple-element.54), channel_id=1, source_target_pairs={{0,2},{8,9},{16,24},{24,16},{1,3},{9,8},{17,25},{25,17},{2,0},{10,... | collective-permute-start | bytes 786440 | tf_op jit(solution)/shard_map/ppermute | solution.py:358
  50.2 0.6 collective-permute-start.14
  50.7 2.6 %collective-permute-done.16.got_ref = bf16[256,512]{1,0:T(8,128)(2,1)S(1)} collective-permute-done((bf16[256,512]{1,0:T(8,128)(2,1)S(1)}, bf16[256,512]{1,0:T(8,128)(2,1)S(1)}, u32[]{:S(2)}, u32[]{:S(2)}) %collective-permute-start.16) | collective-permute-done | bytes 262176 | tf_op jit(solution)/shard_map/ppermute | solution.py:451
  53.4 3.8 %collective-permute-start.17 = (bf16[128,512]{1,0:T(8,128)(2,1)S(1)}, bf16[128,512]{1,0:T(8,128)(2,1)S(1)}, u32[]{:S(2)}, u32[]{:S(2)}) collective-permute-start(bf16[128,512]{1,0:T(8,128)(2,1)S(1)} %get-tuple-element.61), channel_id=1, source_target_pairs={{0,2},{1,3},{2,0},{3,1},{4,6},{5,7},{6,4},{7,5},{8,9},{9,8},{10,11... | collective-permute-start | bytes 393224 | tf_op jit(solution)/shard_map/ppermute | solution.py:451
  57.2 2.9 %collective-permute-done.17.got_ref = bf16[128,512]{1,0:T(8,128)(2,1)S(1)} collective-permute-done((bf16[128,512]{1,0:T(8,128)(2,1)S(1)}, bf16[128,512]{1,0:T(8,128)(2,1)S(1)}, u32[]{:S(2)}, u32[]{:S(2)}) %collective-permute-start.17) | collective-permute-done | bytes 131104 | tf_op jit(solution)/shard_map/ppermute | solution.py:451
  60.2 3.1 %collective-permute-start.18 = (bf16[64,512]{1,0:T(8,128)(2,1)S(1)}, bf16[64,512]{1,0:T(8,128)(2,1)S(1)}, u32[]{:S(2)}, u32[]{:S(2)}) collective-permute-start(bf16[64,512]{1,0:T(8,128)(2,1)S(1)} %get-tuple-element.63), channel_id=1, source_target_pairs={{0,4},{1,5},{2,6},{3,7},{4,0},{5,1},{6,2},{7,3},{8,12},{9,13},{10,... | collective-permute-start | bytes 196616 | tf_op jit(solution)/shard_map/ppermute | solution.py:457
  63.4 2.2 %collective-permute-done.18.refs_6_ = bf16[64,512]{1,0:T(8,128)(2,1)S(1)} collective-permute-done((bf16[64,512]{1,0:T(8,128)(2,1)S(1)}, bf16[64,512]{1,0:T(8,128)(2,1)S(1)}, u32[]{:S(2)}, u32[]{:S(2)}) %collective-permute-start.18) | collective-permute-done | bytes 65568 | tf_op jit(solution)/shard_map/ppermute | solution.py:457
  65.6 1.2 %shard_map.99 = (bf16[512,512]{1,0:T(8,128)(2,1)}, f32[64,512]{1,0:T(8,128)}) custom-call(f32[12,1,512]{2,1,0:T(1,128)S(1)} %get-tuple-element.34.mask_ref, f32[512,512]{1,0:T(8,128)S(1)} %get-tuple-element.53.total_ref, bf16[2,128,512]{2,1,0:T(8,128)(2,1)S(1)} %collective-permute-done.12.refs_0_, bf16[2,128,512]{2,1,0:T(8,128)(2,1)S(1)} %collective-permute-done.13.refs_1_, ...), custom_call_target="tpu_custom_call" | custom-call | bytes 3760128 | tf_op jit(solution)/shard_map/pallas_call | solution.py:254
  (24 shorter events, 0.5 us)
Async XLA Ops:
  0.6 6.5 %copy-start.1 = (bf16[2,1,1,256,512]{4,3,2,1,0:T(8,128)(2,1)S(1)}, bf16[2,1,1,256,512]{4,3,2,1,0:T(8,128)(2,1)}, u32[]{:S(2)}) copy-start(bf16[2,1,1,256,512]{4,3,2,1,0:T(8,128)(2,1)} %param.8) | copy-start | bytes 1572868
  3.5 8.0 %collective-permute-start.3 = (bf16[2,512,512]{2,1,0:T(8,128)(2,1)S(1)}, bf16[2,512,512]{2,1,0:T(8,128)(2,1)S(1)}, u32[]{:S(2)}, u32[]{:S(2)}) collective-permute-start(bf16[2,512,512]{2,1,0:T(8,128)(2,1)S(1)} %get-tuple-element.40.refs_6_), channel_id=1, source_target_pairs={{16,24},{17,25},{18,26},{19,27},{20,28},{21,29},{22,30},{23,31},{8... | collective-permute-start | bytes 3145736 | tf_op jit(solution)/shard_map/ppermute | solution.py:284
  4.0 3.4 %collective-permute-start = (bf16[2,128,512]{2,1,0:T(8,128)(2,1)S(1)}, bf16[2,128,512]{2,1,0:T(8,128)(2,1)S(1)}, u32[]{:S(2)}, u32[]{:S(2)}) collective-permute-start(bf16[2,128,512]{2,1,0:T(8,128)(2,1)S(1)} %get-tuple-element.37), channel_id=1, source_target_pairs={{24,26},{16,17},{8,0},{0,8},{25,27},{17,16},{9,1},{1,9},{26,24},{1... | collective-permute-start | bytes 786440 | tf_op jit(solution)/shard_map/ppermute | solution.py:358
  4.1 3.3 %collective-permute-start.1 = (bf16[2,128,512]{2,1,0:T(8,128)(2,1)S(1)}, bf16[2,128,512]{2,1,0:T(8,128)(2,1)S(1)}, u32[]{:S(2)}, u32[]{:S(2)}) collective-permute-start(bf16[2,128,512]{2,1,0:T(8,128)(2,1)S(1)} %get-tuple-element.38), channel_id=1, source_target_pairs={{24,16},{16,24},{8,0},{0,8},{25,17},{17,25},{9,1},{1,9},{26,28},{1... | collective-permute-start | bytes 786440 | tf_op jit(solution)/shard_map/ppermute | solution.py:358
  4.5 6.9 %collective-permute-start.2 = (bf16[2,128,512]{2,1,0:T(8,128)(2,1)S(1)}, bf16[2,128,512]{2,1,0:T(8,128)(2,1)S(1)}, u32[]{:S(2)}, u32[]{:S(2)}) collective-permute-start(bf16[2,128,512]{2,1,0:T(8,128)(2,1)S(1)} %get-tuple-element.39), channel_id=1, source_target_pairs={{24,25},{16,8},{8,16},{0,1},{25,24},{17,9},{9,17},{1,0},{26,27},{1... | collective-permute-start | bytes 786440 | tf_op jit(solution)/shard_map/ppermute | solution.py:358
  12.4 3.0 %collective-permute-start.4 = (bf16[2,128,512]{2,1,0:T(8,128)(2,1)S(1)}, bf16[2,128,512]{2,1,0:T(8,128)(2,1)S(1)}, u32[]{:S(2)}, u32[]{:S(2)}) collective-permute-start(bf16[2,128,512]{2,1,0:T(8,128)(2,1)S(1)} %get-tuple-element.43), channel_id=1, source_target_pairs={{24,26},{16,17},{8,0},{0,8},{25,27},{17,16},{9,1},{1,9},{26,24},{1... | collective-permute-start | bytes 786440 | tf_op jit(solution)/shard_map/ppermute | solution.py:358
  13.4 1.9 %collective-permute-start.5 = (bf16[2,128,512]{2,1,0:T(8,128)(2,1)S(1)}, bf16[2,128,512]{2,1,0:T(8,128)(2,1)S(1)}, u32[]{:S(2)}, u32[]{:S(2)}) collective-permute-start(bf16[2,128,512]{2,1,0:T(8,128)(2,1)S(1)} %get-tuple-element.44), channel_id=1, source_target_pairs={{24,16},{16,24},{8,0},{0,8},{25,17},{17,25},{9,1},{1,9},{26,28},{1... | collective-permute-start | bytes 786440 | tf_op jit(solution)/shard_map/ppermute | solution.py:358
  13.5 6.4 %collective-permute-start.6 = (bf16[2,128,512]{2,1,0:T(8,128)(2,1)S(1)}, bf16[2,128,512]{2,1,0:T(8,128)(2,1)S(1)}, u32[]{:S(2)}, u32[]{:S(2)}) collective-permute-start(bf16[2,128,512]{2,1,0:T(8,128)(2,1)S(1)} %get-tuple-element.45), channel_id=1, source_target_pairs={{24,25},{16,8},{8,16},{0,1},{25,24},{17,9},{9,17},{1,0},{26,27},{1... | collective-permute-start | bytes 786440 | tf_op jit(solution)/shard_map/ppermute | solution.py:358
  20.2 12.5 %collective-permute-start.7 = (bf16[512,512]{1,0:T(8,128)(2,1)S(1)}, bf16[512,512]{1,0:T(8,128)(2,1)S(1)}, u32[]{:S(2)}, u32[]{:S(2)}) collective-permute-start(bf16[512,512]{1,0:T(8,128)(2,1)S(1)} %shard_map.90.top_ref), channel_id=1, source_target_pairs={{24,0},{25,1},{26,2},{27,3},{28,4},{29,5},{30,6},{31,7}} | collective-permute-start | bytes 1572872 | tf_op jit(solution)/shard_map/ppermute | solution.py:284
  33.5 4.6 %copy-start = (bf16[1,2,1,1,256,512]{5,4,3,2,1,0:T(8,128)(2,1)S(1)}, bf16[1,2,1,1,256,512]{5,4,3,2,1,0:T(8,128)(2,1)}, u32[]{:S(2)}) copy-start(bf16[1,2,1,1,256,512]{5,4,3,2,1,0:T(8,128)(2,1)} %param.7) | copy-start | bytes 1572868
  33.6 10.3 %collective-permute-start.11 = (bf16[512,512]{1,0:T(8,128)(2,1)S(1)}, bf16[512,512]{1,0:T(8,128)(2,1)S(1)}, u32[]{:S(2)}, u32[]{:S(2)}) collective-permute-start(bf16[512,512]{1,0:T(8,128)(2,1)S(1)} %shard_map.94), channel_id=1, source_target_pairs={{24,16},{25,17},{26,18},{27,19},{28,20},{29,21},{30,22},{31,23},{0... | collective-permute-start | bytes 1572872 | tf_op jit(solution)/shard_map/ppermute | solution.py:284
  33.7 8.2 %collective-permute-start.8 = (bf16[2,128,512]{2,1,0:T(8,128)(2,1)S(1)}, bf16[2,128,512]{2,1,0:T(8,128)(2,1)S(1)}, u32[]{:S(2)}, u32[]{:S(2)}) collective-permute-start(bf16[2,128,512]{2,1,0:T(8,128)(2,1)S(1)} %get-tuple-element.47), channel_id=1, source_target_pairs={{0,2},{8,9},{16,24},{24,16},{1,3},{9,8},{17,25},{25,17},{2,0},{10,... | collective-permute-start | bytes 786440 | tf_op jit(solution)/shard_map/ppermute | solution.py:358
  37.5 4.4 %collective-permute-start.9 = (bf16[2,128,512]{2,1,0:T(8,128)(2,1)S(1)}, bf16[2,128,512]{2,1,0:T(8,128)(2,1)S(1)}, u32[]{:S(2)}, u32[]{:S(2)}) collective-permute-start(bf16[2,128,512]{2,1,0:T(8,128)(2,1)S(1)} %get-tuple-element.48), channel_id=1, source_target_pairs={{0,8},{8,0},{16,24},{24,16},{1,9},{9,1},{17,25},{25,17},{2,4},{10,... | collective-permute-start | bytes 786440 | tf_op jit(solution)/shard_map/ppermute | solution.py:358
  37.5 6.4 %collective-permute-start.10 = (bf16[2,128,512]{2,1,0:T(8,128)(2,1)S(1)}, bf16[2,128,512]{2,1,0:T(8,128)(2,1)S(1)}, u32[]{:S(2)}, u32[]{:S(2)}) collective-permute-start(bf16[2,128,512]{2,1,0:T(8,128)(2,1)S(1)} %get-tuple-element.49), channel_id=1, source_target_pairs={{0,1},{8,16},{16,8},{24,25},{1,0},{9,17},{17,9},{25,24},{2,3},{10,... | collective-permute-start | bytes 786440 | tf_op jit(solution)/shard_map/ppermute | solution.py:358
  45.7 19.9 %collective-permute-start.15 = (bf16[512,512]{1,0:T(8,128)(2,1)S(1)}, bf16[512,512]{1,0:T(8,128)(2,1)S(1)}, u32[]{:S(2)}, u32[]{:S(2)}) collective-permute-start(bf16[512,512]{1,0:T(8,128)(2,1)S(1)} %shard_map.96), channel_id=1, source_target_pairs={{24,16},{25,17},{26,18},{27,19},{28,20},{29,21},{30,22},{31,23},{0... | collective-permute-start | bytes 1572872 | tf_op jit(solution)/shard_map/ppermute | solution.py:284
  45.9 7.4 %collective-permute-start.16 = (bf16[256,512]{1,0:T(8,128)(2,1)S(1)}, bf16[256,512]{1,0:T(8,128)(2,1)S(1)}, u32[]{:S(2)}, u32[]{:S(2)}) collective-permute-start(bf16[256,512]{1,0:T(8,128)(2,1)S(1)} %get-tuple-element.59), channel_id=1, source_target_pairs={{0,1},{1,0},{2,3},{3,2},{4,5},{5,4},{6,7},{7,6},{8,10},{9,11},{10,... | collective-permute-start | bytes 786440 | tf_op jit(solution)/shard_map/ppermute | solution.py:451
  46.4 16.9 %collective-permute-start.12 = (bf16[2,128,512]{2,1,0:T(8,128)(2,1)S(1)}, bf16[2,128,512]{2,1,0:T(8,128)(2,1)S(1)}, u32[]{:S(2)}, u32[]{:S(2)}) collective-permute-start(bf16[2,128,512]{2,1,0:T(8,128)(2,1)S(1)} %get-tuple-element.54), channel_id=1, source_target_pairs={{0,2},{8,9},{16,24},{24,16},{1,3},{9,8},{17,25},{25,17},{2,0},{10,... | collective-permute-start | bytes 786440 | tf_op jit(solution)/shard_map/ppermute | solution.py:358
  50.2 13.2 %collective-permute-start.13 = (bf16[2,128,512]{2,1,0:T(8,128)(2,1)S(1)}, bf16[2,128,512]{2,1,0:T(8,128)(2,1)S(1)}, u32[]{:S(2)}, u32[]{:S(2)}) collective-permute-start(bf16[2,128,512]{2,1,0:T(8,128)(2,1)S(1)} %get-tuple-element.55), channel_id=1, source_target_pairs={{0,8},{8,0},{16,24},{24,16},{1,9},{9,1},{17,25},{25,17},{2,4},{10,... | collective-permute-start | bytes 786440 | tf_op jit(solution)/shard_map/ppermute | solution.py:358
  50.2 13.2 %collective-permute-start.14 = (bf16[2,128,512]{2,1,0:T(8,128)(2,1)S(1)}, bf16[2,128,512]{2,1,0:T(8,128)(2,1)S(1)}, u32[]{:S(2)}, u32[]{:S(2)}) collective-permute-start(bf16[2,128,512]{2,1,0:T(8,128)(2,1)S(1)} %get-tuple-element.56), channel_id=1, source_target_pairs={{0,1},{8,16},{16,8},{24,25},{1,0},{9,17},{17,9},{25,24},{2,3},{10,... | collective-permute-start | bytes 786440 | tf_op jit(solution)/shard_map/ppermute | solution.py:358
  53.4 6.8 %collective-permute-start.17 = (bf16[128,512]{1,0:T(8,128)(2,1)S(1)}, bf16[128,512]{1,0:T(8,128)(2,1)S(1)}, u32[]{:S(2)}, u32[]{:S(2)}) collective-permute-start(bf16[128,512]{1,0:T(8,128)(2,1)S(1)} %get-tuple-element.61), channel_id=1, source_target_pairs={{0,2},{1,3},{2,0},{3,1},{4,6},{5,7},{6,4},{7,5},{8,9},{9,8},{10,11... | collective-permute-start | bytes 393224 | tf_op jit(solution)/shard_map/ppermute | solution.py:451
  60.2 5.4 %collective-permute-start.18 = (bf16[64,512]{1,0:T(8,128)(2,1)S(1)}, bf16[64,512]{1,0:T(8,128)(2,1)S(1)}, u32[]{:S(2)}, u32[]{:S(2)}) collective-permute-start(bf16[64,512]{1,0:T(8,128)(2,1)S(1)} %get-tuple-element.63), channel_id=1, source_target_pairs={{0,4},{1,5},{2,6},{3,7},{4,0},{5,1},{6,2},{7,3},{8,12},{9,13},{10,... | collective-permute-start | bytes 196616 | tf_op jit(solution)/shard_map/ppermute | solution.py:457

commit v11 on v10

--- a/solution.py
+++ b/solution.py
@@ -283,7 +283,7 @@
         ]
         return lax.ppermute(value, AXES, pairs)
 
-    def tile_swaps(axis, first, couples, lead):
+    def tile_swaps(axis, first, couples, lead, spread):
         places = {}
         for low, high in couples:
             places[low], places[high] = high, low
@@ -302,7 +302,7 @@
                     moves[lead] = (lead, near)
                 if sections != 4:
                     moves.update((p, (q, (x, y))) for p, q in zip(others, others[1:] + others[:1]))
-                elif paired and axis == "tx" and first == 0 and aside != (x, y):
+                elif paired and spread and axis == "tx" and first == 0 and aside != (x, y):
                     moves.update({buddy: (buddy, aside), inner: (outer, (x, y)), outer: (inner, (x, y))})
                 elif paired:
                     moves.update({buddy: (inner, (x, y)), inner: (buddy, (x, y)), outer: (outer, near)})
@@ -323,7 +323,12 @@
     for axis, base, count in (("tx", 0, rows), ("ty", 2, columns)):
         for first, couples in swap_phases(count):
             phases.append((axis, base, first, count))
-            route = {lead: tile_swaps(axis, first, couples, lead) for lead in {0, top}}
+            route = {
+                section: tile_swaps(
+                    axis, first, couples, top if section >= lower else 0, 0 < section < lower
+                )
+                for section in range(sections)
+            }
             routes.append(route)
     phases = tuple(phases)
     splits, left = [], rows * columns
@@ -354,8 +359,8 @@
     mix_rows = (blocks + len(phases)) * block
     cost = 2 * total_rows * width * (width + len(phases) * block)
 
-    def exchange(outs, lead):
-        return [lax.ppermute(out, AXES, route[lead]) for out, route in zip(outs, routes)]
+    def exchange(outs, section):
+        return [lax.ppermute(out, AXES, route[section]) for out, route in zip(outs, routes)]
 
     def inner(upstream, message, mixing):
         return call(
@@ -410,7 +415,6 @@
     count = len(phases)
     grads, results = {top: grad}, {}
     for section in reversed(range(top)):
-        lead = top if section >= lower else 0
         steps = top - section if section >= lower else section
         layer_here = layers[steps]
         if section == lower - 1:
@@ -439,7 +443,7 @@
             )
             outs, pieces = outs[:count], outs[count:]
             results[1] = upstream
-        arrived = exchange(outs, lead)
+        arrived = exchange(outs, section)
         if section > 0:
             grads[section] = grad
             total = inner(upstream, message, mixing)

time: 67 us -> 67.4 us (level)
  starting transfers between devices: 24.1 us -> 27.6 us
  waiting for transfers between devices: 32.8 us -> 29.8 us
    ppermute x12, starting transfers between devices: 14.5 us -> 17.1 us  [exchange(): lax.ppermute(out, AXES, route[section])]
    ppermute x2, waiting for transfers between devices: 5.52 us -> 3.48 us  [per_device(): got = lax.ppermute(parcel, AXES, pairs)]
    ppermute x4, waiting for transfers between devices: 11.2 us -> 9.21 us  [to_sections(): return lax.ppermute(value, AXES, pairs)]
    ppermute x1, waiting for transfers between devices: 2.23 us -> 3.64 us  [per_device(): got = lax.ppermute(parcel, AXES, splits[-1][1])]
    ppermute x2, starting transfers between devices: 4.41 us -> 5.42 us  [per_device(): got = lax.ppermute(parcel, AXES, pairs)]
  transfers between devices with their start and end apart: 19 -> 19, of which waited for: 8 -> 10; matrix products, arithmetic and copies ran while one was open for 0% -> 0% of each run, Pallas kernels for 2% -> 2%
where the time goes in v11:
time: 67.4 us; the launch traced here: 67.2 us
  waiting for transfers between devices  29.8 us (44%)
  starting transfers between devices  27.6 us (41%)
  Pallas kernels  9.03 us (13%)
  between operations  0.77 us (1%)
    ppermute x12, starting transfers between devices, exchange(): lax.ppermute(out, AXES, route[section])  17.1 us
    ppermute x12, waiting for transfers between devices, exchange(): lax.ppermute(out, AXES, route[section])  13.5 us
    ppermute x4, waiting for transfers between devices, to_sections(): return lax.ppermute(value, AXES, pairs)  9.21 us
    pallas_call x14, Pallas kernels, call(): pl.pallas_call(body, out_shape=[kind(shape, dtype) for shape, dtype in ou...  9.03 us
    ppermute x2, starting transfers between devices, per_device(): got = lax.ppermute(parcel, AXES, pairs)  5.42 us
    ppermute x1, waiting for transfers between devices, per_device(): got = lax.ppermute(parcel, AXES, splits[-1][1])  3.64 us
    ppermute x2, waiting for transfers between devices, per_device(): got = lax.ppermute(parcel, AXES, pairs)  3.48 us
    ppermute x1, starting transfers between devices, per_device(): got = lax.ppermute(parcel, AXES, splits[-1][1])  3.08 us
  transfers between devices with their start and end apart: 19, of which 10 were waited for; matrix products, arithmetic and copies ran while one was open for 0% of the time, Pallas kernels for 2%

profile of v11, /device:TPU:0, one launch (start us, length us, event | category | flops | bytes accessed | tf_op | source)
XLA Modules:
  0.0 67.2 jit_solution(1187235952133652248)
XLA Ops:
  0.6 2.8 %shard_map.86 = (bf16[2,512,512]{2,1,0:T(8,128)(2,1)S(1)}, bf16[2,640,256]{2,1,0:T(8,128)(2,1)S(1)}, f32[12,1,512]{2,1,0:T(1,128)S(1)}, bf16[512,512]{1,0:T(8,12...) custom-call(bf16[512,512]{1,0:T(8,128)(2,1)} %bitcast.11, ...), custom_call_target="tpu_custom_call" | custom-call | flops 738197504 | bytes 5922944 | tf_op jit(solution)/shard_map/pallas_call | solution.py:254
  3.5 0.5 collective-permute-start.3
  4.0 2.7 %collective-permute-start = (bf16[2,128,512]{2,1,0:T(8,128)(2,1)S(1)}, bf16[2,128,512]{2,1,0:T(8,128)(2,1)S(1)}, u32[]{:S(2)}, u32[]{:S(2)}) collective-permute-start(bf16[2,128,512]{2,1,0:T(8,128)(2,1)S(1)} %get-tuple-element.37), channel_id=1, source_target_pairs={{24,26},{16,8},{8,16},{0,2},{25,27},{17,9},{9,17},{1,3},{26,24},{1... | collective-permute-start | bytes 786440 | tf_op jit(solution)/shard_map/ppermute | solution.py:363
  6.7 1.5 %collective-permute-start.2 = (bf16[2,128,512]{2,1,0:T(8,128)(2,1)S(1)}, bf16[2,128,512]{2,1,0:T(8,128)(2,1)S(1)}, u32[]{:S(2)}, u32[]{:S(2)}) collective-permute-start(bf16[2,128,512]{2,1,0:T(8,128)(2,1)S(1)} %get-tuple-element.39), channel_id=1, source_target_pairs={{24,25},{16,8},{8,16},{0,1},{25,24},{17,9},{9,17},{1,0},{26,27},{1... | collective-permute-start | bytes 786440 | tf_op jit(solution)/shard_map/ppermute | solution.py:363
  8.2 0.3 shard_map.87.total_ref
  8.5 2.5 %collective-permute-done.refs_0_ = bf16[2,128,512]{2,1,0:T(8,128)(2,1)S(1)} collective-permute-done((bf16[2,128,512]{2,1,0:T(8,128)(2,1)S(1)}, bf16[2,128,512]{2,1,0:T(8,128)(2,1)S(1)}, u32[]{:S(2)}, u32[]{:S(2)}) %collective-permute-start) | collective-permute-done | bytes 262176 | tf_op jit(solution)/shard_map/ppermute | solution.py:363
  11.0 2.0 %collective-permute-done.2.refs_2_ = bf16[2,128,512]{2,1,0:T(8,128)(2,1)S(1)} collective-permute-done((bf16[2,128,512]{2,1,0:T(8,128)(2,1)S(1)}, bf16[2,128,512]{2,1,0:T(8,128)(2,1)S(1)}, u32[]{:S(2)}, u32[]{:S(2)}) %collective-permute-start.2) | collective-permute-done | bytes 262176 | tf_op jit(solution)/shard_map/ppermute | solution.py:363
  13.0 0.9 %shard_map.88 = (bf16[512,512]{1,0:T(8,128)(2,1)S(1)}, bf16[512,512]{1,0:T(8,128)(2,1)S(1)}, bf16[512,512]{1,0:T(8,128)(2,1)S(1)}, bf16[2,128,512]{2,1,0:T(8,128...) custom-call(f32[12,1,512]{2,1,0:T(1,128)S(1)} %get-tuple-element.34.mask_ref, ...), custom_call_target="tpu_custom_call" | custom-call | flops 469762048 | bytes 5922816 | tf_op jit(solution)/shard_map/pallas_call | solution.py:254
  14.0 3.2 %collective-permute-start.4 = (bf16[2,128,512]{2,1,0:T(8,128)(2,1)S(1)}, bf16[2,128,512]{2,1,0:T(8,128)(2,1)S(1)}, u32[]{:S(2)}, u32[]{:S(2)}) collective-permute-start(bf16[2,128,512]{2,1,0:T(8,128)(2,1)S(1)} %get-tuple-element.43), channel_id=1, source_target_pairs={{24,26},{16,8},{8,16},{0,2},{25,27},{17,9},{9,17},{1,3},{26,24},{1... | collective-permute-start | bytes 786440 | tf_op jit(solution)/shard_map/ppermute | solution.py:363
  17.2 1.5 %collective-permute-start.6 = (bf16[2,128,512]{2,1,0:T(8,128)(2,1)S(1)}, bf16[2,128,512]{2,1,0:T(8,128)(2,1)S(1)}, u32[]{:S(2)}, u32[]{:S(2)}) collective-permute-start(bf16[2,128,512]{2,1,0:T(8,128)(2,1)S(1)} %get-tuple-element.45), channel_id=1, source_target_pairs={{24,25},{16,8},{8,16},{0,1},{25,24},{17,9},{9,17},{1,0},{26,27},{1... | collective-permute-start | bytes 786440 | tf_op jit(solution)/shard_map/ppermute | solution.py:363
  18.7 0.3 shard_map.89.total_ref
  19.0 2.5 %collective-permute-done.4.refs_0_ = bf16[2,128,512]{2,1,0:T(8,128)(2,1)S(1)} collective-permute-done((bf16[2,128,512]{2,1,0:T(8,128)(2,1)S(1)}, bf16[2,128,512]{2,1,0:T(8,128)(2,1)S(1)}, u32[]{:S(2)}, u32[]{:S(2)}) %collective-permute-start.4) | collective-permute-done | bytes 262176 | tf_op jit(solution)/shard_map/ppermute | solution.py:363
  21.5 2.0 %collective-permute-done.6.refs_2_ = bf16[2,128,512]{2,1,0:T(8,128)(2,1)S(1)} collective-permute-done((bf16[2,128,512]{2,1,0:T(8,128)(2,1)S(1)}, bf16[2,128,512]{2,1,0:T(8,128)(2,1)S(1)}, u32[]{:S(2)}, u32[]{:S(2)}) %collective-permute-start.6) | collective-permute-done | bytes 262176 | tf_op jit(solution)/shard_map/ppermute | solution.py:363
  23.5 0.4 shard_map.90.top_ref
  23.9 1.3 %collective-permute-start.7 = (bf16[512,512]{1,0:T(8,128)(2,1)S(1)}, bf16[512,512]{1,0:T(8,128)(2,1)S(1)}, u32[]{:S(2)}, u32[]{:S(2)}) collective-permute-start(bf16[512,512]{1,0:T(8,128)(2,1)S(1)} %shard_map.90.top_ref), channel_id=1, source_target_pairs={{24,0},{25,1},{26,2},{27,3},{28,4},{29,5},{30,6},{31,7}} | collective-permute-start | bytes 1572872 | tf_op jit(solution)/shard_map/ppermute | solution.py:284
  25.2 9.2 %collective-permute-done.7.upstream_ref = bf16[512,512]{1,0:T(8,128)(2,1)S(1)} collective-permute-done((bf16[512,512]{1,0:T(8,128)(2,1)S(1)}, bf16[512,512]{1,0:T(8,128)(2,1)S(1)}, u32[]{:S(2)}, u32[]{:S(2)}) %collective-permute-start.7) | collective-permute-done | bytes 524320 | tf_op jit(solution)/shard_map/ppermute | solution.py:284
  34.4 0.8 %shard_map.91 = (bf16[512,512]{1,0:T(8,128)(2,1)S(1)}, bf16[512,512]{1,0:T(8,128)(2,1)S(1)}, bf16[2,128,512]{2,1,0:T(8,128)(2,1)S(1)}, bf16[2,128,512]{2,1,0:T(8,128)(2,1)S(1)}, bf16[2,128,512]{2,1,0:T(8,128)(2,1)S(1)}) custom-call(bf16[2,512,512]{2,1,0:T(8,128)(2,1)S(1)} %collective-permute-done.3.refs_3_.layer_ref, ...), custom_call_target="tpu_custom_call" | custom-call | flops 469762048 | bytes 4063232 | tf_op jit(solution)/shard_map/pallas_call | solution.py:254
  35.3 2.3 %collective-permute-start.8 = (bf16[2,128,512]{2,1,0:T(8,128)(2,1)S(1)}, bf16[2,128,512]{2,1,0:T(8,128)(2,1)S(1)}, u32[]{:S(2)}, u32[]{:S(2)}) collective-permute-start(bf16[2,128,512]{2,1,0:T(8,128)(2,1)S(1)} %get-tuple-element.47), channel_id=1, source_target_pairs={{0,2},{8,9},{16,24},{24,16},{1,3},{9,8},{17,25},{25,17},{2,0},{10,... | collective-permute-start | bytes 786440 | tf_op jit(solution)/shard_map/ppermute | solution.py:363
  37.6 1.5 %collective-permute-start.10 = (bf16[2,128,512]{2,1,0:T(8,128)(2,1)S(1)}, bf16[2,128,512]{2,1,0:T(8,128)(2,1)S(1)}, u32[]{:S(2)}, u32[]{:S(2)}) collective-permute-start(bf16[2,128,512]{2,1,0:T(8,128)(2,1)S(1)} %get-tuple-element.49), channel_id=1, source_target_pairs={{0,1},{8,16},{16,8},{24,25},{1,0},{9,17},{17,9},{25,24},{2,3},{10,... | collective-permute-start | bytes 786440 | tf_op jit(solution)/shard_map/ppermute | solution.py:363
  39.4 0.3 shard_map.92.total_ref
  39.7 2.3 %collective-permute-done.8.refs_0_ = bf16[2,128,512]{2,1,0:T(8,128)(2,1)S(1)} collective-permute-done((bf16[2,128,512]{2,1,0:T(8,128)(2,1)S(1)}, bf16[2,128,512]{2,1,0:T(8,128)(2,1)S(1)}, u32[]{:S(2)}, u32[]{:S(2)}) %collective-permute-start.8) | collective-permute-done | bytes 262176 | tf_op jit(solution)/shard_map/ppermute | solution.py:363
  42.0 2.0 %collective-permute-done.10.refs_2_ = bf16[2,128,512]{2,1,0:T(8,128)(2,1)S(1)} collective-permute-done((bf16[2,128,512]{2,1,0:T(8,128)(2,1)S(1)}, bf16[2,128,512]{2,1,0:T(8,128)(2,1)S(1)}, u32[]{:S(2)}, u32[]{:S(2)}) %collective-permute-start.10) | collective-permute-done | bytes 262176 | tf_op jit(solution)/shard_map/ppermute | solution.py:363
  44.0 1.7 %shard_map.95 = (bf16[512,512]{1,0:T(8,128)(2,1)S(1)}, f32[512,512]{1,0:T(8,128)S(1)}, bf16[2,128,512]{2,1,0:T(8,128)(2,1)S(1)}, bf16[2,128,512]{2,1,0:T(8,128)(...) custom-call(f32[12,1,512]{2,1,0:T(1,128)S(1)} %get-tuple-element.34.mask_ref, ...), custom_call_target="tpu_custom_call" | custom-call | flops 872415232 | bytes 8282112 | tf_op jit(solution)/shard_map/pallas_call | solution.py:254
  46.0 1.5 %collective-permute-start.16 = (bf16[256,512]{1,0:T(8,128)(2,1)S(1)}, bf16[256,512]{1,0:T(8,128)(2,1)S(1)}, u32[]{:S(2)}, u32[]{:S(2)}) collective-permute-start(bf16[256,512]{1,0:T(8,128)(2,1)S(1)} %get-tuple-element.59), channel_id=1, source_target_pairs={{0,1},{1,0},{2,3},{3,2},{4,5},{5,4},{6,7},{7,6},{8,10},{9,11},{10,... | collective-permute-start | bytes 786440 | tf_op jit(solution)/shard_map/ppermute | solution.py:455
  47.5 2.8 %collective-permute-start.12 = (bf16[2,128,512]{2,1,0:T(8,128)(2,1)S(1)}, bf16[2,128,512]{2,1,0:T(8,128)(2,1)S(1)}, u32[]{:S(2)}, u32[]{:S(2)}) collective-permute-start(bf16[2,128,512]{2,1,0:T(8,128)(2,1)S(1)} %get-tuple-element.54), channel_id=1, source_target_pairs={{0,2},{8,16},{16,8},{24,26},{1,3},{9,17},{17,9},{25,27},{2,0},{10,... | collective-permute-start | bytes 786440 | tf_op jit(solution)/shard_map/ppermute | solution.py:363
  50.3 1.5 %collective-permute-start.14 = (bf16[2,128,512]{2,1,0:T(8,128)(2,1)S(1)}, bf16[2,128,512]{2,1,0:T(8,128)(2,1)S(1)}, u32[]{:S(2)}, u32[]{:S(2)}) collective-permute-start(bf16[2,128,512]{2,1,0:T(8,128)(2,1)S(1)} %get-tuple-element.56), channel_id=1, source_target_pairs={{0,1},{8,16},{16,8},{24,25},{1,0},{9,17},{17,9},{25,24},{2,3},{10,... | collective-permute-start | bytes 786440 | tf_op jit(solution)/shard_map/ppermute | solution.py:363
  51.8 0.5 collective-permute-done.16.got_ref
  52.4 3.9 %collective-permute-start.17 = (bf16[128,512]{1,0:T(8,128)(2,1)S(1)}, bf16[128,512]{1,0:T(8,128)(2,1)S(1)}, u32[]{:S(2)}, u32[]{:S(2)}) collective-permute-start(bf16[128,512]{1,0:T(8,128)(2,1)S(1)} %get-tuple-element.61), channel_id=1, source_target_pairs={{0,2},{1,3},{2,0},{3,1},{4,6},{5,7},{6,4},{7,5},{8,9},{9,8},{10,11... | collective-permute-start | bytes 393224 | tf_op jit(solution)/shard_map/ppermute | solution.py:455
  56.3 2.9 %collective-permute-done.17.got_ref = bf16[128,512]{1,0:T(8,128)(2,1)S(1)} collective-permute-done((bf16[128,512]{1,0:T(8,128)(2,1)S(1)}, bf16[128,512]{1,0:T(8,128)(2,1)S(1)}, u32[]{:S(2)}, u32[]{:S(2)}) %collective-permute-start.17) | collective-permute-done | bytes 131104 | tf_op jit(solution)/shard_map/ppermute | solution.py:455
  59.3 3.1 %collective-permute-start.18 = (bf16[64,512]{1,0:T(8,128)(2,1)S(1)}, bf16[64,512]{1,0:T(8,128)(2,1)S(1)}, u32[]{:S(2)}, u32[]{:S(2)}) collective-permute-start(bf16[64,512]{1,0:T(8,128)(2,1)S(1)} %get-tuple-element.63), channel_id=1, source_target_pairs={{0,4},{1,5},{2,6},{3,7},{4,0},{5,1},{6,2},{7,3},{8,12},{9,13},{10,... | collective-permute-start | bytes 196616 | tf_op jit(solution)/shard_map/ppermute | solution.py:461
  62.4 3.6 %collective-permute-done.18.refs_6_ = bf16[64,512]{1,0:T(8,128)(2,1)S(1)} collective-permute-done((bf16[64,512]{1,0:T(8,128)(2,1)S(1)}, bf16[64,512]{1,0:T(8,128)(2,1)S(1)}, u32[]{:S(2)}, u32[]{:S(2)}) %collective-permute-start.18) | collective-permute-done | bytes 65568 | tf_op jit(solution)/shard_map/ppermute | solution.py:461
  66.0 1.2 %shard_map.99 = (bf16[512,512]{1,0:T(8,128)(2,1)}, f32[64,512]{1,0:T(8,128)}) custom-call(f32[12,1,512]{2,1,0:T(1,128)S(1)} %get-tuple-element.34.mask_ref, f32[512,512]{1,0:T(8,128)S(1)} %get-tuple-element.53.total_ref, bf16[2,128,512]{2,1,0:T(8,128)(2,1)S(1)} %collective-permute-done.12.refs_0_, bf16[2,128,512]{2,1,0:T(8,128)(2,1)S(1)} %collective-permute-done.13.refs_1_, ...), custom_call_target="tpu_custom_call" | custom-call | bytes 3760128 | tf_op jit(solution)/shard_map/pallas_call | solution.py:254
  (24 shorter events, 0.7 us)
Async XLA Ops:
  0.6 7.6 %copy-start.1 = (bf16[2,1,1,256,512]{4,3,2,1,0:T(8,128)(2,1)S(1)}, bf16[2,1,1,256,512]{4,3,2,1,0:T(8,128)(2,1)}, u32[]{:S(2)}) copy-start(bf16[2,1,1,256,512]{4,3,2,1,0:T(8,128)(2,1)} %param.8) | copy-start | bytes 1572868
  3.5 9.6 %collective-permute-start.3 = (bf16[2,512,512]{2,1,0:T(8,128)(2,1)S(1)}, bf16[2,512,512]{2,1,0:T(8,128)(2,1)S(1)}, u32[]{:S(2)}, u32[]{:S(2)}) collective-permute-start(bf16[2,512,512]{2,1,0:T(8,128)(2,1)S(1)} %get-tuple-element.40.refs_6_), channel_id=1, source_target_pairs={{16,24},{17,25},{18,26},{19,27},{20,28},{21,29},{22,30},{23,31},{8... | collective-permute-start | bytes 3145736 | tf_op jit(solution)/shard_map/ppermute | solution.py:284
  4.0 7.0 %collective-permute-start = (bf16[2,128,512]{2,1,0:T(8,128)(2,1)S(1)}, bf16[2,128,512]{2,1,0:T(8,128)(2,1)S(1)}, u32[]{:S(2)}, u32[]{:S(2)}) collective-permute-start(bf16[2,128,512]{2,1,0:T(8,128)(2,1)S(1)} %get-tuple-element.37), channel_id=1, source_target_pairs={{24,26},{16,8},{8,16},{0,2},{25,27},{17,9},{9,17},{1,3},{26,24},{1... | collective-permute-start | bytes 786440 | tf_op jit(solution)/shard_map/ppermute | solution.py:363
  6.6 4.4 %collective-permute-start.1 = (bf16[2,128,512]{2,1,0:T(8,128)(2,1)S(1)}, bf16[2,128,512]{2,1,0:T(8,128)(2,1)S(1)}, u32[]{:S(2)}, u32[]{:S(2)}) collective-permute-start(bf16[2,128,512]{2,1,0:T(8,128)(2,1)S(1)} %get-tuple-element.38), channel_id=1, source_target_pairs={{24,16},{16,24},{8,0},{0,8},{25,17},{17,25},{9,1},{1,9},{26,28},{1... | collective-permute-start | bytes 786440 | tf_op jit(solution)/shard_map/ppermute | solution.py:363
  6.7 6.4 %collective-permute-start.2 = (bf16[2,128,512]{2,1,0:T(8,128)(2,1)S(1)}, bf16[2,128,512]{2,1,0:T(8,128)(2,1)S(1)}, u32[]{:S(2)}, u32[]{:S(2)}) collective-permute-start(bf16[2,128,512]{2,1,0:T(8,128)(2,1)S(1)} %get-tuple-element.39), channel_id=1, source_target_pairs={{24,25},{16,8},{8,16},{0,1},{25,24},{17,9},{9,17},{1,0},{26,27},{1... | collective-permute-start | bytes 786440 | tf_op jit(solution)/shard_map/ppermute | solution.py:363
  14.0 7.5 %collective-permute-start.4 = (bf16[2,128,512]{2,1,0:T(8,128)(2,1)S(1)}, bf16[2,128,512]{2,1,0:T(8,128)(2,1)S(1)}, u32[]{:S(2)}, u32[]{:S(2)}) collective-permute-start(bf16[2,128,512]{2,1,0:T(8,128)(2,1)S(1)} %get-tuple-element.43), channel_id=1, source_target_pairs={{24,26},{16,8},{8,16},{0,2},{25,27},{17,9},{9,17},{1,3},{26,24},{1... | collective-permute-start | bytes 786440 | tf_op jit(solution)/shard_map/ppermute | solution.py:363
  17.2 4.4 %collective-permute-start.5 = (bf16[2,128,512]{2,1,0:T(8,128)(2,1)S(1)}, bf16[2,128,512]{2,1,0:T(8,128)(2,1)S(1)}, u32[]{:S(2)}, u32[]{:S(2)}) collective-permute-start(bf16[2,128,512]{2,1,0:T(8,128)(2,1)S(1)} %get-tuple-element.44), channel_id=1, source_target_pairs={{24,16},{16,24},{8,0},{0,8},{25,17},{17,25},{9,1},{1,9},{26,28},{1... | collective-permute-start | bytes 786440 | tf_op jit(solution)/shard_map/ppermute | solution.py:363
  17.2 6.4 %collective-permute-start.6 = (bf16[2,128,512]{2,1,0:T(8,128)(2,1)S(1)}, bf16[2,128,512]{2,1,0:T(8,128)(2,1)S(1)}, u32[]{:S(2)}, u32[]{:S(2)}) collective-permute-start(bf16[2,128,512]{2,1,0:T(8,128)(2,1)S(1)} %get-tuple-element.45), channel_id=1, source_target_pairs={{24,25},{16,8},{8,16},{0,1},{25,24},{17,9},{9,17},{1,0},{26,27},{1... | collective-permute-start | bytes 786440 | tf_op jit(solution)/shard_map/ppermute | solution.py:363
  23.9 10.5 %collective-permute-start.7 = (bf16[512,512]{1,0:T(8,128)(2,1)S(1)}, bf16[512,512]{1,0:T(8,128)(2,1)S(1)}, u32[]{:S(2)}, u32[]{:S(2)}) collective-permute-start(bf16[512,512]{1,0:T(8,128)(2,1)S(1)} %shard_map.90.top_ref), channel_id=1, source_target_pairs={{24,0},{25,1},{26,2},{27,3},{28,4},{29,5},{30,6},{31,7}} | collective-permute-start | bytes 1572872 | tf_op jit(solution)/shard_map/ppermute | solution.py:284
  35.1 4.0 %copy-start = (bf16[1,2,1,1,256,512]{5,4,3,2,1,0:T(8,128)(2,1)S(1)}, bf16[1,2,1,1,256,512]{5,4,3,2,1,0:T(8,128)(2,1)}, u32[]{:S(2)}) copy-start(bf16[1,2,1,1,256,512]{5,4,3,2,1,0:T(8,128)(2,1)} %param.7) | copy-start | bytes 1572868
  35.2 8.8 %collective-permute-start.11 = (bf16[512,512]{1,0:T(8,128)(2,1)S(1)}, bf16[512,512]{1,0:T(8,128)(2,1)S(1)}, u32[]{:S(2)}, u32[]{:S(2)}) collective-permute-start(bf16[512,512]{1,0:T(8,128)(2,1)S(1)} %shard_map.94), channel_id=1, source_target_pairs={{24,16},{25,17},{26,18},{27,19},{28,20},{29,21},{30,22},{31,23},{0... | collective-permute-start | bytes 1572872 | tf_op jit(solution)/shard_map/ppermute | solution.py:284
  35.3 6.7 %collective-permute-start.8 = (bf16[2,128,512]{2,1,0:T(8,128)(2,1)S(1)}, bf16[2,128,512]{2,1,0:T(8,128)(2,1)S(1)}, u32[]{:S(2)}, u32[]{:S(2)}) collective-permute-start(bf16[2,128,512]{2,1,0:T(8,128)(2,1)S(1)} %get-tuple-element.47), channel_id=1, source_target_pairs={{0,2},{8,9},{16,24},{24,16},{1,3},{9,8},{17,25},{25,17},{2,0},{10,... | collective-permute-start | bytes 786440 | tf_op jit(solution)/shard_map/ppermute | solution.py:363
  37.6 4.4 %collective-permute-start.9 = (bf16[2,128,512]{2,1,0:T(8,128)(2,1)S(1)}, bf16[2,128,512]{2,1,0:T(8,128)(2,1)S(1)}, u32[]{:S(2)}, u32[]{:S(2)}) collective-permute-start(bf16[2,128,512]{2,1,0:T(8,128)(2,1)S(1)} %get-tuple-element.48), channel_id=1, source_target_pairs={{0,8},{8,0},{16,24},{24,16},{1,9},{9,1},{17,25},{25,17},{2,4},{10,... | collective-permute-start | bytes 786440 | tf_op jit(solution)/shard_map/ppermute | solution.py:363
  37.6 6.4 %collective-permute-start.10 = (bf16[2,128,512]{2,1,0:T(8,128)(2,1)S(1)}, bf16[2,128,512]{2,1,0:T(8,128)(2,1)S(1)}, u32[]{:S(2)}, u32[]{:S(2)}) collective-permute-start(bf16[2,128,512]{2,1,0:T(8,128)(2,1)S(1)} %get-tuple-element.49), channel_id=1, source_target_pairs={{0,1},{8,16},{16,8},{24,25},{1,0},{9,17},{17,9},{25,24},{2,3},{10,... | collective-permute-start | bytes 786440 | tf_op jit(solution)/shard_map/ppermute | solution.py:363
  45.8 20.3 %collective-permute-start.15 = (bf16[512,512]{1,0:T(8,128)(2,1)S(1)}, bf16[512,512]{1,0:T(8,128)(2,1)S(1)}, u32[]{:S(2)}, u32[]{:S(2)}) collective-permute-start(bf16[512,512]{1,0:T(8,128)(2,1)S(1)} %shard_map.96), channel_id=1, source_target_pairs={{24,16},{25,17},{26,18},{27,19},{28,20},{29,21},{30,22},{31,23},{0... | collective-permute-start | bytes 1572872 | tf_op jit(solution)/shard_map/ppermute | solution.py:284
  46.0 6.4 %collective-permute-start.16 = (bf16[256,512]{1,0:T(8,128)(2,1)S(1)}, bf16[256,512]{1,0:T(8,128)(2,1)S(1)}, u32[]{:S(2)}, u32[]{:S(2)}) collective-permute-start(bf16[256,512]{1,0:T(8,128)(2,1)S(1)} %get-tuple-element.59), channel_id=1, source_target_pairs={{0,1},{1,0},{2,3},{3,2},{4,5},{5,4},{6,7},{7,6},{8,10},{9,11},{10,... | collective-permute-start | bytes 786440 | tf_op jit(solution)/shard_map/ppermute | solution.py:455
  47.5 14.9 %collective-permute-start.12 = (bf16[2,128,512]{2,1,0:T(8,128)(2,1)S(1)}, bf16[2,128,512]{2,1,0:T(8,128)(2,1)S(1)}, u32[]{:S(2)}, u32[]{:S(2)}) collective-permute-start(bf16[2,128,512]{2,1,0:T(8,128)(2,1)S(1)} %get-tuple-element.54), channel_id=1, source_target_pairs={{0,2},{8,16},{16,8},{24,26},{1,3},{9,17},{17,9},{25,27},{2,0},{10,... | collective-permute-start | bytes 786440 | tf_op jit(solution)/shard_map/ppermute | solution.py:363
  50.3 12.1 %collective-permute-start.13 = (bf16[2,128,512]{2,1,0:T(8,128)(2,1)S(1)}, bf16[2,128,512]{2,1,0:T(8,128)(2,1)S(1)}, u32[]{:S(2)}, u32[]{:S(2)}) collective-permute-start(bf16[2,128,512]{2,1,0:T(8,128)(2,1)S(1)} %get-tuple-element.55), channel_id=1, source_target_pairs={{0,8},{8,0},{16,24},{24,16},{1,9},{9,1},{17,25},{25,17},{2,4},{10,... | collective-permute-start | bytes 786440 | tf_op jit(solution)/shard_map/ppermute | solution.py:363
  50.3 12.1 %collective-permute-start.14 = (bf16[2,128,512]{2,1,0:T(8,128)(2,1)S(1)}, bf16[2,128,512]{2,1,0:T(8,128)(2,1)S(1)}, u32[]{:S(2)}, u32[]{:S(2)}) collective-permute-start(bf16[2,128,512]{2,1,0:T(8,128)(2,1)S(1)} %get-tuple-element.56), channel_id=1, source_target_pairs={{0,1},{8,16},{16,8},{24,25},{1,0},{9,17},{17,9},{25,24},{2,3},{10,... | collective-permute-start | bytes 786440 | tf_op jit(solution)/shard_map/ppermute | solution.py:363
  52.4 6.8 %collective-permute-start.17 = (bf16[128,512]{1,0:T(8,128)(2,1)S(1)}, bf16[128,512]{1,0:T(8,128)(2,1)S(1)}, u32[]{:S(2)}, u32[]{:S(2)}) collective-permute-start(bf16[128,512]{1,0:T(8,128)(2,1)S(1)} %get-tuple-element.61), channel_id=1, source_target_pairs={{0,2},{1,3},{2,0},{3,1},{4,6},{5,7},{6,4},{7,5},{8,9},{9,8},{10,11... | collective-permute-start | bytes 393224 | tf_op jit(solution)/shard_map/ppermute | solution.py:455
  59.3 6.7 %collective-permute-start.18 = (bf16[64,512]{1,0:T(8,128)(2,1)S(1)}, bf16[64,512]{1,0:T(8,128)(2,1)S(1)}, u32[]{:S(2)}, u32[]{:S(2)}) collective-permute-start(bf16[64,512]{1,0:T(8,128)(2,1)S(1)} %get-tuple-element.63), channel_id=1, source_target_pairs={{0,4},{1,5},{2,6},{3,7},{4,0},{5,1},{6,2},{7,3},{8,12},{9,13},{10,... | collective-permute-start | bytes 196616 | tf_op jit(solution)/shard_map/ppermute | solution.py:461

commit v12 on v11

--- a/solution.py
+++ b/solution.py
@@ -296,7 +296,9 @@
                 paired = place in places
                 facing = places.get(place, place)
                 near = (facing, y) if axis == "tx" else (x, facing)
-                aside = (x, y ^ 1) if columns % 2 == 0 else (x, y)
+                aside = (x, y ^ 1) if axis == "tx" else (x ^ 1, y)
+                if aside[0] >= rows or aside[1] >= columns:
+                    aside = (x, y)
                 moves = {}
                 if paired or sections != 4:
                     moves[lead] = (lead, near)
@@ -307,8 +309,8 @@
                 elif paired:
                     moves.update({buddy: (inner, (x, y)), inner: (buddy, (x, y)), outer: (outer, near)})
                 else:
-                    for p, q in ((lead, buddy), (inner, outer)):
-                        moves.update({p: (q, (x, y)), q: (p, (x, y))})
+                    moves.update({lead: (buddy, (x, y)), buddy: (lead, (x, y))})
+                    moves.update({inner: (inner, aside), outer: (outer, aside)})
                 pairs += [(flat(p, x, y), flat(q, *tile)) for p, (q, tile) in moves.items()]
         return pairs
 
@@ -442,6 +444,9 @@
                 scratch=[pltpu.VMEM(*product)] * len(splits[:1]) + [pltpu.VMEM(*whole)] * 2,
             )
             outs, pieces = outs[:count], outs[count:]
+            if splits:
+                halved = lax.ppermute(pieces[0], AXES, splits[0][1])
+                outs[-1], halved = lax.optimization_barrier((outs[-1], halved))
             results[1] = upstream
         arrived = exchange(outs, section)
         if section > 0:
@@ -452,13 +457,13 @@
     if splits:
         parcel, kept = pieces
         for (_, pairs), following in zip(splits, splits[1:]):
-            got = lax.ppermute(parcel, AXES, pairs)
+            got = halved if parcel is pieces[0] else lax.ppermute(parcel, AXES, pairs)
             half = (kept.shape[0] // 2, width)
             parcel, kept = call(
                 functools.partial(halve_kernel, following[0]), [kept, got],
                 [(half, BF16), (half, F32)], 0, scratch=[pltpu.VMEM(kept.shape, F32)],
             )
-        got = lax.ppermute(parcel, AXES, splits[-1][1])
+        got = halved if parcel is pieces[0] else lax.ppermute(parcel, AXES, splits[-1][1])
         result, summed = call(
             functools.partial(last_kernel, top, count, scale),
             [mask, total, *arrived, results[top], fetch_home(results), kept, got],

time: 67.4 us -> 70.3 us (1.043)
  waiting for transfers between devices: 29.8 us -> 38.6 us
  starting transfers between devices: 27.6 us -> 21.5 us
    ppermute x12, waiting for transfers between devices: 13.5 us -> 20.6 us  [exchange(): lax.ppermute(out, AXES, route[section])]
    ppermute x12, starting transfers between devices: 17.1 us -> 12.4 us  [exchange(): lax.ppermute(out, AXES, route[section])]
    ppermute x3, starting transfers between devices: 8.5 us -> 5.67 us  [the longest x1 2.32 us: per_device(): got = halved if parcel is pieces[0] else lax.ppermute(parcel, AXES, pairs)]
    ppermute x3, waiting for transfers between devices: 7.11 us -> 8.81 us  [the longest x1 3.45 us: per_device(): lax.ppermute(parcel, AXES, splits[-1][1])]
    ppermute x4, starting transfers between devices: 2.07 us -> 3.43 us  [to_sections(): return lax.ppermute(value, AXES, pairs)]
  transfers between devices with their start and end apart: 19 -> 19, of which waited for: 10 -> 12; matrix products, arithmetic and copies ran while one was open for 0% -> 0% of each run, Pallas kernels for 2% -> 2%
where the time goes in v12:
time: 70.3 us; the launch traced here: 69.9 us
  waiting for transfers between devices  38.6 us (55%)
  starting transfers between devices  21.5 us (31%)
  Pallas kernels  9.04 us (13%)
  between operations  0.77 us (1%)
    ppermute x12, waiting for transfers between devices, exchange(): lax.ppermute(out, AXES, route[section])  20.6 us
    ppermute x12, starting transfers between devices, exchange(): lax.ppermute(out, AXES, route[section])  12.4 us
    ppermute x4, waiting for transfers between devices, to_sections(): return lax.ppermute(value, AXES, pairs)  9.21 us
    pallas_call x14, Pallas kernels, call(): pl.pallas_call(body, out_shape=[kind(shape, dtype) for shape, dtype in ou...  9.04 us
    ppermute x1, waiting for transfers between devices, per_device(): lax.ppermute(parcel, AXES, splits[-1][1])  3.45 us
    ppermute x4, starting transfers between devices, to_sections(): return lax.ppermute(value, AXES, pairs)  3.43 us
    ppermute x1, waiting for transfers between devices, per_device(): got = halved if parcel is pieces[0] else lax.ppermute(parcel, AXES, pairs)  2.95 us
    ppermute x1, waiting for transfers between devices, per_device(): halved = lax.ppermute(pieces[0], AXES, splits[0][1])  2.42 us
  transfers between devices with their start and end apart: 19, of which 12 were waited for; matrix products, arithmetic and copies ran while one was open for 0% of the time, Pallas kernels for 2%

profile of v12, /device:TPU:0, one launch (start us, length us, event | category | flops | bytes accessed | tf_op | source)
XLA Modules:
  0.0 69.9 jit_solution(2214841210074555449)
XLA Ops:
  0.6 2.8 %shard_map.86 = (bf16[2,512,512]{2,1,0:T(8,128)(2,1)S(1)}, bf16[2,640,256]{2,1,0:T(8,128)(2,1)S(1)}, f32[12,1,512]{2,1,0:T(1,128)S(1)}, bf16[512,512]{1,0:T(8,12...) custom-call(bf16[512,512]{1,0:T(8,128)(2,1)} %bitcast.11, ...), custom_call_target="tpu_custom_call" | custom-call | flops 738197504 | bytes 5922944 | tf_op jit(solution)/shard_map/pallas_call | solution.py:254
  3.5 0.5 collective-permute-start.3
  4.0 2.7 %collective-permute-start = (bf16[2,128,512]{2,1,0:T(8,128)(2,1)S(1)}, bf16[2,128,512]{2,1,0:T(8,128)(2,1)S(1)}, u32[]{:S(2)}, u32[]{:S(2)}) collective-permute-start(bf16[2,128,512]{2,1,0:T(8,128)(2,1)S(1)} %get-tuple-element.39), channel_id=1, source_target_pairs={{24,26},{16,8},{8,16},{0,2},{25,27},{17,9},{9,17},{1,3},{26,24},{1... | collective-permute-start | bytes 786440 | tf_op jit(solution)/shard_map/ppermute | solution.py:365
  6.6 1.5 %collective-permute-start.1 = (bf16[2,128,512]{2,1,0:T(8,128)(2,1)S(1)}, bf16[2,128,512]{2,1,0:T(8,128)(2,1)S(1)}, u32[]{:S(2)}, u32[]{:S(2)}) collective-permute-start(bf16[2,128,512]{2,1,0:T(8,128)(2,1)S(1)} %get-tuple-element.40), channel_id=1, source_target_pairs={{24,16},{16,24},{8,9},{0,1},{25,17},{17,25},{9,8},{1,0},{26,28},{1... | collective-permute-start | bytes 786440 | tf_op jit(solution)/shard_map/ppermute | solution.py:365
  8.2 0.5 collective-permute-start.2
  9.0 2.0 %collective-permute-done.refs_0_ = bf16[2,128,512]{2,1,0:T(8,128)(2,1)S(1)} collective-permute-done((bf16[2,128,512]{2,1,0:T(8,128)(2,1)S(1)}, bf16[2,128,512]{2,1,0:T(8,128)(2,1)S(1)}, u32[]{:S(2)}, u32[]{:S(2)}) %collective-permute-start) | collective-permute-done | bytes 262176 | tf_op jit(solution)/shard_map/ppermute | solution.py:365
  11.0 3.9 %collective-permute-done.1.refs_1_ = bf16[2,128,512]{2,1,0:T(8,128)(2,1)S(1)} collective-permute-done((bf16[2,128,512]{2,1,0:T(8,128)(2,1)S(1)}, bf16[2,128,512]{2,1,0:T(8,128)(2,1)S(1)}, u32[]{:S(2)}, u32[]{:S(2)}) %collective-permute-start.1) | collective-permute-done | bytes 262176 | tf_op jit(solution)/shard_map/ppermute | solution.py:365
  14.9 2.8 %collective-permute-done.2.refs_2_ = bf16[2,128,512]{2,1,0:T(8,128)(2,1)S(1)} collective-permute-done((bf16[2,128,512]{2,1,0:T(8,128)(2,1)S(1)}, bf16[2,128,512]{2,1,0:T(8,128)(2,1)S(1)}, u32[]{:S(2)}, u32[]{:S(2)}) %collective-permute-start.2) | collective-permute-done | bytes 262176 | tf_op jit(solution)/shard_map/ppermute | solution.py:365
  17.7 0.9 %shard_map.88 = (bf16[512,512]{1,0:T(8,128)(2,1)S(1)}, bf16[512,512]{1,0:T(8,128)(2,1)S(1)}, bf16[512,512]{1,0:T(8,128)(2,1)S(1)}, bf16[2,128,512]{2,1,0:T(8,128...) custom-call(f32[12,1,512]{2,1,0:T(1,128)S(1)} %get-tuple-element.36.mask_ref, ...), custom_call_target="tpu_custom_call" | custom-call | flops 469762048 | bytes 5922816 | tf_op jit(solution)/shard_map/pallas_call | solution.py:254
  18.7 1.6 %collective-permute-start.5 = (bf16[2,128,512]{2,1,0:T(8,128)(2,1)S(1)}, bf16[2,128,512]{2,1,0:T(8,128)(2,1)S(1)}, u32[]{:S(2)}, u32[]{:S(2)}) collective-permute-start(bf16[2,128,512]{2,1,0:T(8,128)(2,1)S(1)} %get-tuple-element.46), channel_id=1, source_target_pairs={{24,16},{16,24},{8,9},{0,1},{25,17},{17,25},{9,8},{1,0},{26,28},{1... | collective-permute-start | bytes 786440 | tf_op jit(solution)/shard_map/ppermute | solution.py:365
  20.3 0.5 collective-permute-start.6
  21.1 4.0 %collective-permute-done.4.refs_0_ = bf16[2,128,512]{2,1,0:T(8,128)(2,1)S(1)} collective-permute-done((bf16[2,128,512]{2,1,0:T(8,128)(2,1)S(1)}, bf16[2,128,512]{2,1,0:T(8,128)(2,1)S(1)}, u32[]{:S(2)}, u32[]{:S(2)}) %collective-permute-start.4) | collective-permute-done | bytes 262176 | tf_op jit(solution)/shard_map/ppermute | solution.py:365
  25.1 2.8 %collective-permute-done.6.refs_2_ = bf16[2,128,512]{2,1,0:T(8,128)(2,1)S(1)} collective-permute-done((bf16[2,128,512]{2,1,0:T(8,128)(2,1)S(1)}, bf16[2,128,512]{2,1,0:T(8,128)(2,1)S(1)}, u32[]{:S(2)}, u32[]{:S(2)}) %collective-permute-start.6) | collective-permute-done | bytes 262176 | tf_op jit(solution)/shard_map/ppermute | solution.py:365
  27.9 0.4 shard_map.90.top_ref
  28.3 1.3 %collective-permute-start.7 = (bf16[512,512]{1,0:T(8,128)(2,1)S(1)}, bf16[512,512]{1,0:T(8,128)(2,1)S(1)}, u32[]{:S(2)}, u32[]{:S(2)}) collective-permute-start(bf16[512,512]{1,0:T(8,128)(2,1)S(1)} %shard_map.90.top_ref), channel_id=1, source_target_pairs={{24,0},{25,1},{26,2},{27,3},{28,4},{29,5},{30,6},{31,7}} | collective-permute-start | bytes 1572872 | tf_op jit(solution)/shard_map/ppermute | solution.py:284
  29.6 9.2 %collective-permute-done.7.upstream_ref = bf16[512,512]{1,0:T(8,128)(2,1)S(1)} collective-permute-done((bf16[512,512]{1,0:T(8,128)(2,1)S(1)}, bf16[512,512]{1,0:T(8,128)(2,1)S(1)}, u32[]{:S(2)}, u32[]{:S(2)}) %collective-permute-start.7) | collective-permute-done | bytes 524320 | tf_op jit(solution)/shard_map/ppermute | solution.py:284
  38.8 0.8 %shard_map.91 = (bf16[512,512]{1,0:T(8,128)(2,1)S(1)}, bf16[512,512]{1,0:T(8,128)(2,1)S(1)}, bf16[2,128,512]{2,1,0:T(8,128)(2,1)S(1)}, bf16[2,128,512]{2,1,0:T(8,128)(2,1)S(1)}, bf16[2,128,512]{2,1,0:T(8,128)(2,1)S(1)}) custom-call(bf16[2,512,512]{2,1,0:T(8,128)(2,1)S(1)} %collective-permute-done.3.refs_3_.layer_ref, ...), custom_call_target="tpu_custom_call" | custom-call | flops 469762048 | bytes 4063232 | tf_op jit(solution)/shard_map/pallas_call | solution.py:254
  39.7 1.7 %collective-permute-start.8 = (bf16[2,128,512]{2,1,0:T(8,128)(2,1)S(1)}, bf16[2,128,512]{2,1,0:T(8,128)(2,1)S(1)}, u32[]{:S(2)}, u32[]{:S(2)}) collective-permute-start(bf16[2,128,512]{2,1,0:T(8,128)(2,1)S(1)} %get-tuple-element.49), channel_id=1, source_target_pairs={{0,2},{8,9},{16,24},{24,16},{1,3},{9,8},{17,25},{25,17},{2,0},{10,... | collective-permute-start | bytes 786440 | tf_op jit(solution)/shard_map/ppermute | solution.py:365
  41.4 1.5 %collective-permute-start.10 = (bf16[2,128,512]{2,1,0:T(8,128)(2,1)S(1)}, bf16[2,128,512]{2,1,0:T(8,128)(2,1)S(1)}, u32[]{:S(2)}, u32[]{:S(2)}) collective-permute-start(bf16[2,128,512]{2,1,0:T(8,128)(2,1)S(1)} %get-tuple-element.51), channel_id=1, source_target_pairs={{0,1},{8,16},{16,8},{24,25},{1,0},{9,17},{17,9},{25,24},{2,3},{10,... | collective-permute-start | bytes 786440 | tf_op jit(solution)/shard_map/ppermute | solution.py:365
  43.4 2.7 %collective-permute-done.8.refs_0_ = bf16[2,128,512]{2,1,0:T(8,128)(2,1)S(1)} collective-permute-done((bf16[2,128,512]{2,1,0:T(8,128)(2,1)S(1)}, bf16[2,128,512]{2,1,0:T(8,128)(2,1)S(1)}, u32[]{:S(2)}, u32[]{:S(2)}) %collective-permute-start.8) | collective-permute-done | bytes 262176 | tf_op jit(solution)/shard_map/ppermute | solution.py:365
  46.1 2.3 %collective-permute-done.10.refs_2_ = bf16[2,128,512]{2,1,0:T(8,128)(2,1)S(1)} collective-permute-done((bf16[2,128,512]{2,1,0:T(8,128)(2,1)S(1)}, bf16[2,128,512]{2,1,0:T(8,128)(2,1)S(1)}, u32[]{:S(2)}, u32[]{:S(2)}) %collective-permute-start.10) | collective-permute-done | bytes 262176 | tf_op jit(solution)/shard_map/ppermute | solution.py:365
  48.4 1.7 %shard_map.95 = (bf16[512,512]{1,0:T(8,128)(2,1)S(1)}, f32[512,512]{1,0:T(8,128)S(1)}, bf16[2,128,512]{2,1,0:T(8,128)(2,1)S(1)}, bf16[2,128,512]{2,1,0:T(8,128)(...) custom-call(f32[12,1,512]{2,1,0:T(1,128)S(1)} %get-tuple-element.36.mask_ref, ...), custom_call_target="tpu_custom_call" | custom-call | flops 872415232 | bytes 8282112 | tf_op jit(solution)/shard_map/pallas_call | solution.py:254
  50.1 1.6 %collective-permute-start.14 = (bf16[256,512]{1,0:T(8,128)(2,1)S(1)}, bf16[256,512]{1,0:T(8,128)(2,1)S(1)}, u32[]{:S(2)}, u32[]{:S(2)}) collective-permute-start(bf16[256,512]{1,0:T(8,128)(2,1)S(1)} %get-tuple-element.59), channel_id=1, source_target_pairs={{0,1},{1,0},{2,3},{3,2},{4,5},{5,4},{6,7},{7,6},{8,10},{9,11},{10,... | collective-permute-start | bytes 786440 | tf_op jit(solution)/shard_map/ppermute | solution.py:448
  51.7 1.6 %collective-permute-start.16 = (bf16[512,512]{1,0:T(8,128)(2,1)S(1)}, bf16[512,512]{1,0:T(8,128)(2,1)S(1)}, u32[]{:S(2)}, u32[]{:S(2)}) collective-permute-start(bf16[512,512]{1,0:T(8,128)(2,1)S(1)} %shard_map.96), channel_id=1, source_target_pairs={{24,16},{25,17},{26,18},{27,19},{28,20},{29,21},{30,22},{31,23},{0... | collective-permute-start | bytes 1572872 | tf_op jit(solution)/shard_map/ppermute | solution.py:284
  53.3 0.8 %collective-permute-start.12 = (bf16[2,128,512]{2,1,0:T(8,128)(2,1)S(1)}, bf16[2,128,512]{2,1,0:T(8,128)(2,1)S(1)}, u32[]{:S(2)}, u32[]{:S(2)}) collective-permute-start(bf16[2,128,512]{2,1,0:T(8,128)(2,1)S(1)} %get-tuple-element.56), channel_id=1, source_target_pairs={{0,2},{8,16},{16,8},{24,26},{1,3},{9,17},{17,9},{25,27},{2,0},{10,... | collective-permute-start | bytes 786440 | tf_op jit(solution)/shard_map/ppermute | solution.py:365
  54.1 2.4 %collective-permute-done.14.got_ref = bf16[256,512]{1,0:T(8,128)(2,1)S(1)} collective-permute-done((bf16[256,512]{1,0:T(8,128)(2,1)S(1)}, bf16[256,512]{1,0:T(8,128)(2,1)S(1)}, u32[]{:S(2)}, u32[]{:S(2)}) %collective-permute-start.14) | collective-permute-done | bytes 262176 | tf_op jit(solution)/shard_map/ppermute | solution.py:448
  56.6 1.5 %collective-permute-start.15 = (bf16[2,128,512]{2,1,0:T(8,128)(2,1)S(1)}, bf16[2,128,512]{2,1,0:T(8,128)(2,1)S(1)}, u32[]{:S(2)}, u32[]{:S(2)}) collective-permute-start(bf16[2,128,512]{2,1,0:T(8,128)(2,1)S(1)} %get-tuple-element.60), channel_id=1, source_target_pairs={{0,1},{8,16},{16,8},{24,25},{1,0},{9,17},{17,9},{25,24},{2,3},{10,... | collective-permute-start | bytes 786440 | tf_op jit(solution)/shard_map/ppermute | solution.py:365
  58.2 2.3 %collective-permute-start.17 = (bf16[128,512]{1,0:T(8,128)(2,1)S(1)}, bf16[128,512]{1,0:T(8,128)(2,1)S(1)}, u32[]{:S(2)}, u32[]{:S(2)}) collective-permute-start(bf16[128,512]{1,0:T(8,128)(2,1)S(1)} %get-tuple-element.65), channel_id=1, source_target_pairs={{0,2},{1,3},{2,0},{3,1},{4,6},{5,7},{6,4},{7,5},{8,9},{9,8},{10,11... | collective-permute-start | bytes 393224 | tf_op jit(solution)/shard_map/ppermute | solution.py:460
  60.5 2.9 %collective-permute-done.17.got_ref = bf16[128,512]{1,0:T(8,128)(2,1)S(1)} collective-permute-done((bf16[128,512]{1,0:T(8,128)(2,1)S(1)}, bf16[128,512]{1,0:T(8,128)(2,1)S(1)}, u32[]{:S(2)}, u32[]{:S(2)}) %collective-permute-start.17) | collective-permute-done | bytes 131104 | tf_op jit(solution)/shard_map/ppermute | solution.py:460
  63.5 1.8 %collective-permute-start.18 = (bf16[64,512]{1,0:T(8,128)(2,1)S(1)}, bf16[64,512]{1,0:T(8,128)(2,1)S(1)}, u32[]{:S(2)}, u32[]{:S(2)}) collective-permute-start(bf16[64,512]{1,0:T(8,128)(2,1)S(1)} %get-tuple-element.67), channel_id=1, source_target_pairs={{0,4},{1,5},{2,6},{3,7},{4,0},{5,1},{6,2},{7,3},{8,12},{9,13},{10,... | collective-permute-start | bytes 196616 | tf_op jit(solution)/shard_map/ppermute | solution.py:466
  65.3 3.5 %collective-permute-done.18.refs_6_ = bf16[64,512]{1,0:T(8,128)(2,1)S(1)} collective-permute-done((bf16[64,512]{1,0:T(8,128)(2,1)S(1)}, bf16[64,512]{1,0:T(8,128)(2,1)S(1)}, u32[]{:S(2)}, u32[]{:S(2)}) %collective-permute-start.18) | collective-permute-done | bytes 65568 | tf_op jit(solution)/shard_map/ppermute | solution.py:466
  68.7 1.2 %shard_map.99 = (bf16[512,512]{1,0:T(8,128)(2,1)}, f32[64,512]{1,0:T(8,128)}) custom-call(f32[12,1,512]{2,1,0:T(1,128)S(1)} %get-tuple-element.36.mask_ref, f32[512,512]{1,0:T(8,128)S(1)} %get-tuple-element.55.total_ref, bf16[2,128,512]{2,1,0:T(8,128)(2,1)S(1)} %collective-permute-done.12.refs_0_, bf16[2,128,512]{2,1,0:T(8,128)(2,1)S(1)} %collective-permute-done.13.refs_1_, ...), custom_call_target="tpu_custom_call" | custom-call | bytes 3760128 | tf_op jit(solution)/shard_map/pallas_call | solution.py:254
  (24 shorter events, 1.6 us)
Async XLA Ops:
  0.6 8.0 %copy-start.1 = (bf16[2,1,1,256,512]{4,3,2,1,0:T(8,128)(2,1)S(1)}, bf16[2,1,1,256,512]{4,3,2,1,0:T(8,128)(2,1)}, u32[]{:S(2)}) copy-start(bf16[2,1,1,256,512]{4,3,2,1,0:T(8,128)(2,1)} %param.8) | copy-start | bytes 1572868
  3.5 14.2 %collective-permute-start.3 = (bf16[2,512,512]{2,1,0:T(8,128)(2,1)S(1)}, bf16[2,512,512]{2,1,0:T(8,128)(2,1)S(1)}, u32[]{:S(2)}, u32[]{:S(2)}) collective-permute-start(bf16[2,512,512]{2,1,0:T(8,128)(2,1)S(1)} %get-tuple-element.42.refs_6_), channel_id=1, source_target_pairs={{16,24},{17,25},{18,26},{19,27},{20,28},{21,29},{22,30},{23,31},{8... | collective-permute-start | bytes 3145736 | tf_op jit(solution)/shard_map/ppermute | solution.py:284
  4.0 7.0 %collective-permute-start = (bf16[2,128,512]{2,1,0:T(8,128)(2,1)S(1)}, bf16[2,128,512]{2,1,0:T(8,128)(2,1)S(1)}, u32[]{:S(2)}, u32[]{:S(2)}) collective-permute-start(bf16[2,128,512]{2,1,0:T(8,128)(2,1)S(1)} %get-tuple-element.39), channel_id=1, source_target_pairs={{24,26},{16,8},{8,16},{0,2},{25,27},{17,9},{9,17},{1,3},{26,24},{1... | collective-permute-start | bytes 786440 | tf_op jit(solution)/shard_map/ppermute | solution.py:365
  6.6 8.2 %collective-permute-start.1 = (bf16[2,128,512]{2,1,0:T(8,128)(2,1)S(1)}, bf16[2,128,512]{2,1,0:T(8,128)(2,1)S(1)}, u32[]{:S(2)}, u32[]{:S(2)}) collective-permute-start(bf16[2,128,512]{2,1,0:T(8,128)(2,1)S(1)} %get-tuple-element.40), channel_id=1, source_target_pairs={{24,16},{16,24},{8,9},{0,1},{25,17},{17,25},{9,8},{1,0},{26,28},{1... | collective-permute-start | bytes 786440 | tf_op jit(solution)/shard_map/ppermute | solution.py:365
  8.2 9.5 %collective-permute-start.2 = (bf16[2,128,512]{2,1,0:T(8,128)(2,1)S(1)}, bf16[2,128,512]{2,1,0:T(8,128)(2,1)S(1)}, u32[]{:S(2)}, u32[]{:S(2)}) collective-permute-start(bf16[2,128,512]{2,1,0:T(8,128)(2,1)S(1)} %get-tuple-element.41), channel_id=1, source_target_pairs={{24,25},{16,8},{8,16},{0,1},{25,24},{17,9},{9,17},{1,0},{26,27},{1... | collective-permute-start | bytes 786440 | tf_op jit(solution)/shard_map/ppermute | solution.py:365
  18.6 6.4 %collective-permute-start.4 = (bf16[2,128,512]{2,1,0:T(8,128)(2,1)S(1)}, bf16[2,128,512]{2,1,0:T(8,128)(2,1)S(1)}, u32[]{:S(2)}, u32[]{:S(2)}) collective-permute-start(bf16[2,128,512]{2,1,0:T(8,128)(2,1)S(1)} %get-tuple-element.45), channel_id=1, source_target_pairs={{24,26},{16,8},{8,16},{0,2},{25,27},{17,9},{9,17},{1,3},{26,24},{1... | collective-permute-start | bytes 786440 | tf_op jit(solution)/shard_map/ppermute | solution.py:365
  18.7 6.4 %collective-permute-start.5 = (bf16[2,128,512]{2,1,0:T(8,128)(2,1)S(1)}, bf16[2,128,512]{2,1,0:T(8,128)(2,1)S(1)}, u32[]{:S(2)}, u32[]{:S(2)}) collective-permute-start(bf16[2,128,512]{2,1,0:T(8,128)(2,1)S(1)} %get-tuple-element.46), channel_id=1, source_target_pairs={{24,16},{16,24},{8,9},{0,1},{25,17},{17,25},{9,8},{1,0},{26,28},{1... | collective-permute-start | bytes 786440 | tf_op jit(solution)/shard_map/ppermute | solution.py:365
  20.3 7.7 %collective-permute-start.6 = (bf16[2,128,512]{2,1,0:T(8,128)(2,1)S(1)}, bf16[2,128,512]{2,1,0:T(8,128)(2,1)S(1)}, u32[]{:S(2)}, u32[]{:S(2)}) collective-permute-start(bf16[2,128,512]{2,1,0:T(8,128)(2,1)S(1)} %get-tuple-element.47), channel_id=1, source_target_pairs={{24,25},{16,8},{8,16},{0,1},{25,24},{17,9},{9,17},{1,0},{26,27},{1... | collective-permute-start | bytes 786440 | tf_op jit(solution)/shard_map/ppermute | solution.py:365
  28.3 10.5 %collective-permute-start.7 = (bf16[512,512]{1,0:T(8,128)(2,1)S(1)}, bf16[512,512]{1,0:T(8,128)(2,1)S(1)}, u32[]{:S(2)}, u32[]{:S(2)}) collective-permute-start(bf16[512,512]{1,0:T(8,128)(2,1)S(1)} %shard_map.90.top_ref), channel_id=1, source_target_pairs={{24,0},{25,1},{26,2},{27,3},{28,4},{29,5},{30,6},{31,7}} | collective-permute-start | bytes 1572872 | tf_op jit(solution)/shard_map/ppermute | solution.py:284
  39.6 3.4 %copy-start = (bf16[1,2,1,1,256,512]{5,4,3,2,1,0:T(8,128)(2,1)S(1)}, bf16[1,2,1,1,256,512]{5,4,3,2,1,0:T(8,128)(2,1)}, u32[]{:S(2)}) copy-start(bf16[1,2,1,1,256,512]{5,4,3,2,1,0:T(8,128)(2,1)} %param.7) | copy-start | bytes 1572868
  39.6 8.8 %collective-permute-start.11 = (bf16[512,512]{1,0:T(8,128)(2,1)S(1)}, bf16[512,512]{1,0:T(8,128)(2,1)S(1)}, u32[]{:S(2)}, u32[]{:S(2)}) collective-permute-start(bf16[512,512]{1,0:T(8,128)(2,1)S(1)} %shard_map.94), channel_id=1, source_target_pairs={{24,16},{25,17},{26,18},{27,19},{28,20},{29,21},{30,22},{31,23},{0... | collective-permute-start | bytes 1572872 | tf_op jit(solution)/shard_map/ppermute | solution.py:284
  39.7 6.4 %collective-permute-start.8 = (bf16[2,128,512]{2,1,0:T(8,128)(2,1)S(1)}, bf16[2,128,512]{2,1,0:T(8,128)(2,1)S(1)}, u32[]{:S(2)}, u32[]{:S(2)}) collective-permute-start(bf16[2,128,512]{2,1,0:T(8,128)(2,1)S(1)} %get-tuple-element.49), channel_id=1, source_target_pairs={{0,2},{8,9},{16,24},{24,16},{1,3},{9,8},{17,25},{25,17},{2,0},{10,... | collective-permute-start | bytes 786440 | tf_op jit(solution)/shard_map/ppermute | solution.py:365
  41.4 4.7 %collective-permute-start.9 = (bf16[2,128,512]{2,1,0:T(8,128)(2,1)S(1)}, bf16[2,128,512]{2,1,0:T(8,128)(2,1)S(1)}, u32[]{:S(2)}, u32[]{:S(2)}) collective-permute-start(bf16[2,128,512]{2,1,0:T(8,128)(2,1)S(1)} %get-tuple-element.50), channel_id=1, source_target_pairs={{0,8},{8,0},{16,17},{24,25},{1,9},{9,1},{17,16},{25,24},{2,4},{10,... | collective-permute-start | bytes 786440 | tf_op jit(solution)/shard_map/ppermute | solution.py:365
  41.4 7.0 %collective-permute-start.10 = (bf16[2,128,512]{2,1,0:T(8,128)(2,1)S(1)}, bf16[2,128,512]{2,1,0:T(8,128)(2,1)S(1)}, u32[]{:S(2)}, u32[]{:S(2)}) collective-permute-start(bf16[2,128,512]{2,1,0:T(8,128)(2,1)S(1)} %get-tuple-element.51), channel_id=1, source_target_pairs={{0,1},{8,16},{16,8},{24,25},{1,0},{9,17},{17,9},{25,24},{2,3},{10,... | collective-permute-start | bytes 786440 | tf_op jit(solution)/shard_map/ppermute | solution.py:365
  50.1 6.4 %collective-permute-start.14 = (bf16[256,512]{1,0:T(8,128)(2,1)S(1)}, bf16[256,512]{1,0:T(8,128)(2,1)S(1)}, u32[]{:S(2)}, u32[]{:S(2)}) collective-permute-start(bf16[256,512]{1,0:T(8,128)(2,1)S(1)} %get-tuple-element.59), channel_id=1, source_target_pairs={{0,1},{1,0},{2,3},{3,2},{4,5},{5,4},{6,7},{7,6},{8,10},{9,11},{10,... | collective-permute-start | bytes 786440 | tf_op jit(solution)/shard_map/ppermute | solution.py:448
  51.7 17.0 %collective-permute-start.16 = (bf16[512,512]{1,0:T(8,128)(2,1)S(1)}, bf16[512,512]{1,0:T(8,128)(2,1)S(1)}, u32[]{:S(2)}, u32[]{:S(2)}) collective-permute-start(bf16[512,512]{1,0:T(8,128)(2,1)S(1)} %shard_map.96), channel_id=1, source_target_pairs={{24,16},{25,17},{26,18},{27,19},{28,20},{29,21},{30,22},{31,23},{0... | collective-permute-start | bytes 1572872 | tf_op jit(solution)/shard_map/ppermute | solution.py:284
  53.3 12.0 %collective-permute-start.12 = (bf16[2,128,512]{2,1,0:T(8,128)(2,1)S(1)}, bf16[2,128,512]{2,1,0:T(8,128)(2,1)S(1)}, u32[]{:S(2)}, u32[]{:S(2)}) collective-permute-start(bf16[2,128,512]{2,1,0:T(8,128)(2,1)S(1)} %get-tuple-element.56), channel_id=1, source_target_pairs={{0,2},{8,16},{16,8},{24,26},{1,3},{9,17},{17,9},{25,27},{2,0},{10,... | collective-permute-start | bytes 786440 | tf_op jit(solution)/shard_map/ppermute | solution.py:365
  54.1 11.1 %collective-permute-start.13 = (bf16[2,128,512]{2,1,0:T(8,128)(2,1)S(1)}, bf16[2,128,512]{2,1,0:T(8,128)(2,1)S(1)}, u32[]{:S(2)}, u32[]{:S(2)}) collective-permute-start(bf16[2,128,512]{2,1,0:T(8,128)(2,1)S(1)} %get-tuple-element.57), channel_id=1, source_target_pairs={{0,8},{8,0},{16,17},{24,25},{1,9},{9,1},{17,16},{25,24},{2,4},{10,... | collective-permute-start | bytes 786440 | tf_op jit(solution)/shard_map/ppermute | solution.py:365
  56.6 12.2 %collective-permute-start.15 = (bf16[2,128,512]{2,1,0:T(8,128)(2,1)S(1)}, bf16[2,128,512]{2,1,0:T(8,128)(2,1)S(1)}, u32[]{:S(2)}, u32[]{:S(2)}) collective-permute-start(bf16[2,128,512]{2,1,0:T(8,128)(2,1)S(1)} %get-tuple-element.60), channel_id=1, source_target_pairs={{0,1},{8,16},{16,8},{24,25},{1,0},{9,17},{17,9},{25,24},{2,3},{10,... | collective-permute-start | bytes 786440 | tf_op jit(solution)/shard_map/ppermute | solution.py:365
  58.2 5.3 %collective-permute-start.17 = (bf16[128,512]{1,0:T(8,128)(2,1)S(1)}, bf16[128,512]{1,0:T(8,128)(2,1)S(1)}, u32[]{:S(2)}, u32[]{:S(2)}) collective-permute-start(bf16[128,512]{1,0:T(8,128)(2,1)S(1)} %get-tuple-element.65), channel_id=1, source_target_pairs={{0,2},{1,3},{2,0},{3,1},{4,6},{5,7},{6,4},{7,5},{8,9},{9,8},{10,11... | collective-permute-start | bytes 393224 | tf_op jit(solution)/shard_map/ppermute | solution.py:460
  63.5 5.2 %collective-permute-start.18 = (bf16[64,512]{1,0:T(8,128)(2,1)S(1)}, bf16[64,512]{1,0:T(8,128)(2,1)S(1)}, u32[]{:S(2)}, u32[]{:S(2)}) collective-permute-start(bf16[64,512]{1,0:T(8,128)(2,1)S(1)} %get-tuple-element.67), channel_id=1, source_target_pairs={{0,4},{1,5},{2,6},{3,7},{4,0},{5,1},{6,2},{7,3},{8,12},{9,13},{10,... | collective-permute-start | bytes 196616 | tf_op jit(solution)/shard_map/ppermute | solution.py:466

commit v13 on v11

--- a/solution.py
+++ b/solution.py
@@ -272,9 +272,11 @@
     def flat(section, x, y):
         return (section * rows + x) * columns + y
 
-    def to_sections(value, moves, back=True):
+    def to_sections(value, moves, back=True, crossed=False):
         if back:
-            moves = moves + [(target, source) for source, target in moves]
+            returns = [source for source, _ in moves]
+            returns = returns[::-1] if crossed else returns
+            moves = moves + [(target, source) for (_, target), source in zip(moves, returns)]
         pairs = [
             (flat(source, x, y), flat(target, x, y))
             for source, target in moves
@@ -296,19 +298,26 @@
                 paired = place in places
                 facing = places.get(place, place)
                 near = (facing, y) if axis == "tx" else (x, facing)
-                aside = (x, y ^ 1) if columns % 2 == 0 else (x, y)
-                moves = {}
-                if paired or sections != 4:
-                    moves[lead] = (lead, near)
+                aside = (x, y ^ 1) if axis == "tx" else (x ^ 1, y)
+                if aside[0] >= rows or aside[1] >= columns:
+                    aside = (x, y)
+                beside = (x ^ 1, y) if rows % 2 == 0 else (x, y)
+                here = (x, y)
+                moves = {lead: (lead, near if paired else aside)}
                 if sections != 4:
-                    moves.update((p, (q, (x, y))) for p, q in zip(others, others[1:] + others[:1]))
-                elif paired and spread and axis == "tx" and first == 0 and aside != (x, y):
-                    moves.update({buddy: (buddy, aside), inner: (outer, (x, y)), outer: (inner, (x, y))})
-                elif paired:
-                    moves.update({buddy: (inner, (x, y)), inner: (buddy, (x, y)), outer: (outer, near)})
+                    moves.update((p, (q, here)) for p, q in zip(others, others[1:] + others[:1]))
+                elif not spread and axis == "tx":
+                    moves.update({buddy: (inner, here), inner: (buddy, here)})
+                    moves[outer] = (outer, beside if first else aside)
+                elif not spread:
+                    moves.update({inner: (outer, here), outer: (inner, here), buddy: (buddy, beside)})
+                elif not paired:
+                    for p, q in ((lead, buddy), (inner, outer)):
+                        moves.update({p: (q, here), q: (p, here)})
+                elif axis == "tx" and first == 0 and aside != here:
+                    moves.update({buddy: (buddy, aside), inner: (outer, here), outer: (inner, here)})
                 else:
-                    for p, q in ((lead, buddy), (inner, outer)):
-                        moves.update({p: (q, (x, y)), q: (p, (x, y))})
+                    moves.update({buddy: (inner, here), inner: (buddy, here), outer: (outer, near)})
                 pairs += [(flat(p, x, y), flat(q, *tile)) for p, (q, tile) in moves.items()]
         return pairs
 
@@ -395,7 +404,7 @@
         moves = [(top - step, top)] + ([(step, 0)] if step < lower else [])
         layers.append(to_sections(layer, moves))
 
-    def fetch_home(values):
+    def fetch_home(values, crossed=False):
         got = None
         for step in range(1, upper):
             moves = [(top, top - step)]
@@ -405,7 +414,7 @@
                 value = call(
                     functools.partial(choose_kernel, top), [value, values[step]], [whole], 0
                 )[0]
-            new = to_sections(value, moves)
+            new = to_sections(value, moves, crossed=crossed)
             takes = here == top - step
             if step < lower:
                 takes = takes | (here == step)
@@ -461,14 +470,14 @@
         got = lax.ppermute(parcel, AXES, splits[-1][1])
         result, summed = call(
             functools.partial(last_kernel, top, count, scale),
-            [mask, total, *arrived, results[top], fetch_home(results), kept, got],
+            [mask, total, *arrived, results[top], fetch_home(results, True), kept, got],
             [whole, (kept.shape, F32)], 0, jax.ShapeDtypeStruct,
         )
     else:
         summed = scale * lax.psum_scatter(pieces[0], ("tx", "ty"), scatter_dimension=0, tiled=True)
         result = call(
             functools.partial(last_kernel, top, count, None),
-            [mask, total, *arrived, results[top], fetch_home(results)], [whole], 0,
+            [mask, total, *arrived, results[top], fetch_home(results, True)], [whole], 0,
             jax.ShapeDtypeStruct,
         )[0]
     return (summed[None], result.reshape(1, batches, 1, 1, nodes, width))

time: 67.4 us -> 65.7 us (0.975); the launches traced: 67.2 us -> 64.4 us
  starting transfers between devices: 27.6 us -> 20 us
  waiting for transfers between devices: 29.8 us -> 34.6 us
    ppermute x12, starting transfers between devices: 17.1 us -> 12.5 us  [exchange(): lax.ppermute(out, AXES, route[section])]
    ppermute x4, waiting for transfers between devices: 9.21 us -> 11.7 us  [to_sections(): return lax.ppermute(value, AXES, pairs)]
    ppermute x2, waiting for transfers between devices: 3.48 us -> 5.52 us  [per_device(): got = lax.ppermute(parcel, AXES, pairs)]
    ppermute x2, starting transfers between devices: 5.42 us -> 3.58 us  [per_device(): got = lax.ppermute(parcel, AXES, pairs)]
    ppermute x1, starting transfers between devices: 3.08 us -> 1.99 us  [per_device(): got = lax.ppermute(parcel, AXES, splits[-1][1])]
    ppermute x12, waiting for transfers between devices: 13.5 us -> 14.2 us  [exchange(): lax.ppermute(out, AXES, route[section])]
where the time goes in v13:
time: 65.7 us; the launch traced here: 64.4 us
  waiting for transfers between devices  34.6 us (53%)
  starting transfers between devices  20 us (30%)
  Pallas kernels  9.01 us (14%)
  between operations  0.78 us (1%)
    ppermute x12, waiting for transfers between devices, exchange(): lax.ppermute(out, AXES, route[section])  14.2 us
    ppermute x12, starting transfers between devices, exchange(): lax.ppermute(out, AXES, route[section])  12.5 us
    ppermute x4, waiting for transfers between devices, to_sections(): return lax.ppermute(value, AXES, pairs)  11.7 us
    pallas_call x14, Pallas kernels, call(): pl.pallas_call(body, out_shape=[kind(shape, dtype) for shape, dtype in ou...  9.01 us
    ppermute x2, waiting for transfers between devices, per_device(): got = lax.ppermute(parcel, AXES, pairs)  5.52 us
    ppermute x2, starting transfers between devices, per_device(): got = lax.ppermute(parcel, AXES, pairs)  3.58 us
    ppermute x1, waiting for transfers between devices, per_device(): got = lax.ppermute(parcel, AXES, splits[-1][1])  3.23 us
    ppermute x1, starting transfers between devices, per_device(): got = lax.ppermute(parcel, AXES, splits[-1][1])  1.99 us
  transfers between devices with their start and end apart: 19, of which 10 were waited for; matrix products, arithmetic and copies ran while one was open for 0% of the time, Pallas kernels for 2%

profile of v13, /device:TPU:0, one launch (start us, length us, event | category | flops | bytes accessed | tf_op | source)
XLA Modules:
  0.0 64.4 jit_solution(2358829658487960092)
XLA Ops:
  0.6 2.8 %shard_map.86 = (bf16[2,512,512]{2,1,0:T(8,128)(2,1)S(1)}, bf16[2,640,256]{2,1,0:T(8,128)(2,1)S(1)}, f32[12,1,512]{2,1,0:T(1,128)S(1)}, bf16[512,512]{1,0:T(8,12...) custom-call(bf16[512,512]{1,0:T(8,128)(2,1)} %bitcast.11, ...), custom_call_target="tpu_custom_call" | custom-call | flops 738197504 | bytes 5922944 | tf_op jit(solution)/shard_map/pallas_call | solution.py:254
  3.5 0.5 collective-permute-start.3
  4.0 2.6 %collective-permute-start = (bf16[2,128,512]{2,1,0:T(8,128)(2,1)S(1)}, bf16[2,128,512]{2,1,0:T(8,128)(2,1)S(1)}, u32[]{:S(2)}, u32[]{:S(2)}) collective-permute-start(bf16[2,128,512]{2,1,0:T(8,128)(2,1)S(1)} %get-tuple-element.37), channel_id=1, source_target_pairs={{24,26},{16,8},{8,16},{0,1},{25,27},{17,9},{9,17},{1,0},{26,24},{1... | collective-permute-start | bytes 786440 | tf_op jit(solution)/shard_map/ppermute | solution.py:372
  6.6 1.6 %collective-permute-start.1 = (bf16[2,128,512]{2,1,0:T(8,128)(2,1)S(1)}, bf16[2,128,512]{2,1,0:T(8,128)(2,1)S(1)}, u32[]{:S(2)}, u32[]{:S(2)}) collective-permute-start(bf16[2,128,512]{2,1,0:T(8,128)(2,1)S(1)} %get-tuple-element.38), channel_id=1, source_target_pairs={{24,25},{16,8},{8,16},{0,2},{25,24},{17,9},{9,17},{1,3},{26,28},{1... | collective-permute-start | bytes 786440 | tf_op jit(solution)/shard_map/ppermute | solution.py:372
  8.2 0.3 shard_map.87.total_ref
  8.5 2.5 %collective-permute-done.refs_0_ = bf16[2,128,512]{2,1,0:T(8,128)(2,1)S(1)} collective-permute-done((bf16[2,128,512]{2,1,0:T(8,128)(2,1)S(1)}, bf16[2,128,512]{2,1,0:T(8,128)(2,1)S(1)}, u32[]{:S(2)}, u32[]{:S(2)}) %collective-permute-start) | collective-permute-done | bytes 262176 | tf_op jit(solution)/shard_map/ppermute | solution.py:372
  10.9 2.0 %collective-permute-done.1.refs_1_ = bf16[2,128,512]{2,1,0:T(8,128)(2,1)S(1)} collective-permute-done((bf16[2,128,512]{2,1,0:T(8,128)(2,1)S(1)}, bf16[2,128,512]{2,1,0:T(8,128)(2,1)S(1)}, u32[]{:S(2)}, u32[]{:S(2)}) %collective-permute-start.1) | collective-permute-done | bytes 262176 | tf_op jit(solution)/shard_map/ppermute | solution.py:372
  13.0 0.9 %shard_map.88 = (bf16[512,512]{1,0:T(8,128)(2,1)S(1)}, bf16[512,512]{1,0:T(8,128)(2,1)S(1)}, bf16[512,512]{1,0:T(8,128)(2,1)S(1)}, bf16[2,128,512]{2,1,0:T(8,128...) custom-call(f32[12,1,512]{2,1,0:T(1,128)S(1)} %get-tuple-element.34.mask_ref, ...), custom_call_target="tpu_custom_call" | custom-call | flops 469762048 | bytes 5922816 | tf_op jit(solution)/shard_map/pallas_call | solution.py:254
  14.0 2.0 %collective-permute-start.5 = (bf16[2,128,512]{2,1,0:T(8,128)(2,1)S(1)}, bf16[2,128,512]{2,1,0:T(8,128)(2,1)S(1)}, u32[]{:S(2)}, u32[]{:S(2)}) collective-permute-start(bf16[2,128,512]{2,1,0:T(8,128)(2,1)S(1)} %get-tuple-element.44), channel_id=1, source_target_pairs={{24,25},{16,8},{8,16},{0,2},{25,24},{17,9},{9,17},{1,3},{26,28},{1... | collective-permute-start | bytes 786440 | tf_op jit(solution)/shard_map/ppermute | solution.py:372
  16.0 0.3 collective-permute-start.6
  16.7 3.6 %collective-permute-done.4.refs_0_ = bf16[2,128,512]{2,1,0:T(8,128)(2,1)S(1)} collective-permute-done((bf16[2,128,512]{2,1,0:T(8,128)(2,1)S(1)}, bf16[2,128,512]{2,1,0:T(8,128)(2,1)S(1)}, u32[]{:S(2)}, u32[]{:S(2)}) %collective-permute-start.4) | collective-permute-done | bytes 262176 | tf_op jit(solution)/shard_map/ppermute | solution.py:372
  20.4 0.4 shard_map.90.top_ref
  20.7 1.3 %collective-permute-start.7 = (bf16[512,512]{1,0:T(8,128)(2,1)S(1)}, bf16[512,512]{1,0:T(8,128)(2,1)S(1)}, u32[]{:S(2)}, u32[]{:S(2)}) collective-permute-start(bf16[512,512]{1,0:T(8,128)(2,1)S(1)} %shard_map.90.top_ref), channel_id=1, source_target_pairs={{24,0},{25,1},{26,2},{27,3},{28,4},{29,5},{30,6},{31,7}} | collective-permute-start | bytes 1572872 | tf_op jit(solution)/shard_map/ppermute | solution.py:286
  22.0 11.7 %collective-permute-done.7.upstream_ref = bf16[512,512]{1,0:T(8,128)(2,1)S(1)} collective-permute-done((bf16[512,512]{1,0:T(8,128)(2,1)S(1)}, bf16[512,512]{1,0:T(8,128)(2,1)S(1)}, u32[]{:S(2)}, u32[]{:S(2)}) %collective-permute-start.7) | collective-permute-done | bytes 524320 | tf_op jit(solution)/shard_map/ppermute | solution.py:286
  33.7 0.8 %shard_map.91 = (bf16[512,512]{1,0:T(8,128)(2,1)S(1)}, bf16[512,512]{1,0:T(8,128)(2,1)S(1)}, bf16[2,128,512]{2,1,0:T(8,128)(2,1)S(1)}, bf16[2,128,512]{2,1,0:T(8,128)(2,1)S(1)}, bf16[2,128,512]{2,1,0:T(8,128)(2,1)S(1)}) custom-call(bf16[2,512,512]{2,1,0:T(8,128)(2,1)S(1)} %collective-permute-done.3.refs_3_.layer_ref, ...), custom_call_target="tpu_custom_call" | custom-call | flops 469762048 | bytes 4063232 | tf_op jit(solution)/shard_map/pallas_call | solution.py:254
  34.6 0.4 collective-permute-start.8
  35.1 1.3 %collective-permute-start.9 = (bf16[2,128,512]{2,1,0:T(8,128)(2,1)S(1)}, bf16[2,128,512]{2,1,0:T(8,128)(2,1)S(1)}, u32[]{:S(2)}, u32[]{:S(2)}) collective-permute-start(bf16[2,128,512]{2,1,0:T(8,128)(2,1)S(1)} %get-tuple-element.48), channel_id=1, source_target_pairs={{0,8},{8,0},{16,24},{24,16},{1,9},{9,1},{17,25},{25,17},{2,4},{10,... | collective-permute-start | bytes 786440 | tf_op jit(solution)/shard_map/ppermute | solution.py:372
  36.4 0.5 collective-permute-start.10
  37.1 0.3 shard_map.92.total_ref
  37.4 3.7 %collective-permute-done.8.refs_0_ = bf16[2,128,512]{2,1,0:T(8,128)(2,1)S(1)} collective-permute-done((bf16[2,128,512]{2,1,0:T(8,128)(2,1)S(1)}, bf16[2,128,512]{2,1,0:T(8,128)(2,1)S(1)}, u32[]{:S(2)}, u32[]{:S(2)}) %collective-permute-start.8) | collective-permute-done | bytes 262176 | tf_op jit(solution)/shard_map/ppermute | solution.py:372
  41.1 2.3 %collective-permute-done.10.refs_2_ = bf16[2,128,512]{2,1,0:T(8,128)(2,1)S(1)} collective-permute-done((bf16[2,128,512]{2,1,0:T(8,128)(2,1)S(1)}, bf16[2,128,512]{2,1,0:T(8,128)(2,1)S(1)}, u32[]{:S(2)}, u32[]{:S(2)}) %collective-permute-start.10) | collective-permute-done | bytes 262176 | tf_op jit(solution)/shard_map/ppermute | solution.py:372
  43.3 1.7 %shard_map.95 = (bf16[512,512]{1,0:T(8,128)(2,1)S(1)}, f32[512,512]{1,0:T(8,128)S(1)}, bf16[2,128,512]{2,1,0:T(8,128)(2,1)S(1)}, bf16[2,128,512]{2,1,0:T(8,128)(...) custom-call(f32[12,1,512]{2,1,0:T(1,128)S(1)} %get-tuple-element.34.mask_ref, ...), custom_call_target="tpu_custom_call" | custom-call | flops 872415232 | bytes 8282112 | tf_op jit(solution)/shard_map/pallas_call | solution.py:254
  45.1 1.6 %collective-permute-start.16 = (bf16[256,512]{1,0:T(8,128)(2,1)S(1)}, bf16[256,512]{1,0:T(8,128)(2,1)S(1)}, u32[]{:S(2)}, u32[]{:S(2)}) collective-permute-start(bf16[256,512]{1,0:T(8,128)(2,1)S(1)} %get-tuple-element.59), channel_id=1, source_target_pairs={{0,1},{1,0},{2,3},{3,2},{4,5},{5,4},{6,7},{7,6},{8,10},{9,11},{10,... | collective-permute-start | bytes 786440 | tf_op jit(solution)/shard_map/ppermute | solution.py:464
  46.7 1.5 %collective-permute-start.12 = (bf16[2,128,512]{2,1,0:T(8,128)(2,1)S(1)}, bf16[2,128,512]{2,1,0:T(8,128)(2,1)S(1)}, u32[]{:S(2)}, u32[]{:S(2)}) collective-permute-start(bf16[2,128,512]{2,1,0:T(8,128)(2,1)S(1)} %get-tuple-element.54), channel_id=1, source_target_pairs={{0,2},{8,16},{16,8},{24,25},{1,3},{9,17},{17,9},{25,24},{2,0},{10,... | collective-permute-start | bytes 786440 | tf_op jit(solution)/shard_map/ppermute | solution.py:372
  48.2 0.9 %collective-permute-start.13 = (bf16[2,128,512]{2,1,0:T(8,128)(2,1)S(1)}, bf16[2,128,512]{2,1,0:T(8,128)(2,1)S(1)}, u32[]{:S(2)}, u32[]{:S(2)}) collective-permute-start(bf16[2,128,512]{2,1,0:T(8,128)(2,1)S(1)} %get-tuple-element.55), channel_id=1, source_target_pairs={{0,1},{8,16},{16,8},{24,26},{1,0},{9,17},{17,9},{25,27},{2,4},{10,... | collective-permute-start | bytes 786440 | tf_op jit(solution)/shard_map/ppermute | solution.py:372
  49.1 1.1 %collective-permute-start.14 = (bf16[2,128,512]{2,1,0:T(8,128)(2,1)S(1)}, bf16[2,128,512]{2,1,0:T(8,128)(2,1)S(1)}, u32[]{:S(2)}, u32[]{:S(2)}) collective-permute-start(bf16[2,128,512]{2,1,0:T(8,128)(2,1)S(1)} %get-tuple-element.56), channel_id=1, source_target_pairs={{0,1},{16,24},{24,16},{8,10},{1,0},{17,25},{25,17},{9,11},{2,3},{1... | collective-permute-start | bytes 786440 | tf_op jit(solution)/shard_map/ppermute | solution.py:372
  50.3 1.3 %collective-permute-done.16.got_ref = bf16[256,512]{1,0:T(8,128)(2,1)S(1)} collective-permute-done((bf16[256,512]{1,0:T(8,128)(2,1)S(1)}, bf16[256,512]{1,0:T(8,128)(2,1)S(1)}, u32[]{:S(2)}, u32[]{:S(2)}) %collective-permute-start.16) | collective-permute-done | bytes 262176 | tf_op jit(solution)/shard_map/ppermute | solution.py:464
  51.6 2.0 %collective-permute-start.17 = (bf16[128,512]{1,0:T(8,128)(2,1)S(1)}, bf16[128,512]{1,0:T(8,128)(2,1)S(1)}, u32[]{:S(2)}, u32[]{:S(2)}) collective-permute-start(bf16[128,512]{1,0:T(8,128)(2,1)S(1)} %get-tuple-element.61), channel_id=1, source_target_pairs={{0,2},{1,3},{2,0},{3,1},{4,6},{5,7},{6,4},{7,5},{8,9},{9,8},{10,11... | collective-permute-start | bytes 393224 | tf_op jit(solution)/shard_map/ppermute | solution.py:464
  53.6 4.2 %collective-permute-done.17.got_ref = bf16[128,512]{1,0:T(8,128)(2,1)S(1)} collective-permute-done((bf16[128,512]{1,0:T(8,128)(2,1)S(1)}, bf16[128,512]{1,0:T(8,128)(2,1)S(1)}, u32[]{:S(2)}, u32[]{:S(2)}) %collective-permute-start.17) | collective-permute-done | bytes 131104 | tf_op jit(solution)/shard_map/ppermute | solution.py:464
  57.9 2.0 %collective-permute-start.18 = (bf16[64,512]{1,0:T(8,128)(2,1)S(1)}, bf16[64,512]{1,0:T(8,128)(2,1)S(1)}, u32[]{:S(2)}, u32[]{:S(2)}) collective-permute-start(bf16[64,512]{1,0:T(8,128)(2,1)S(1)} %get-tuple-element.63), channel_id=1, source_target_pairs={{0,4},{1,5},{2,6},{3,7},{4,0},{5,1},{6,2},{7,3},{8,12},{9,13},{10,... | collective-permute-start | bytes 196616 | tf_op jit(solution)/shard_map/ppermute | solution.py:470
  59.9 3.2 %collective-permute-done.18.refs_6_ = bf16[64,512]{1,0:T(8,128)(2,1)S(1)} collective-permute-done((bf16[64,512]{1,0:T(8,128)(2,1)S(1)}, bf16[64,512]{1,0:T(8,128)(2,1)S(1)}, u32[]{:S(2)}, u32[]{:S(2)}) %collective-permute-start.18) | collective-permute-done | bytes 65568 | tf_op jit(solution)/shard_map/ppermute | solution.py:470
  63.2 1.2 %shard_map.99 = (bf16[512,512]{1,0:T(8,128)(2,1)}, f32[64,512]{1,0:T(8,128)}) custom-call(f32[12,1,512]{2,1,0:T(1,128)S(1)} %get-tuple-element.34.mask_ref, f32[512,512]{1,0:T(8,128)S(1)} %get-tuple-element.53.total_ref, bf16[2,128,512]{2,1,0:T(8,128)(2,1)S(1)} %collective-permute-done.12.refs_0_, bf16[2,128,512]{2,1,0:T(8,128)(2,1)S(1)} %collective-permute-done.13.refs_1_, ...), custom_call_target="tpu_custom_call" | custom-call | bytes 3760128 | tf_op jit(solution)/shard_map/pallas_call | solution.py:254
  (24 shorter events, 1.1 us)
Async XLA Ops:
  0.6 7.5 %copy-start.1 = (bf16[2,1,1,256,512]{4,3,2,1,0:T(8,128)(2,1)S(1)}, bf16[2,1,1,256,512]{4,3,2,1,0:T(8,128)(2,1)}, u32[]{:S(2)}) copy-start(bf16[2,1,1,256,512]{4,3,2,1,0:T(8,128)(2,1)} %param.8) | copy-start | bytes 1572868
  3.5 9.5 %collective-permute-start.3 = (bf16[2,512,512]{2,1,0:T(8,128)(2,1)S(1)}, bf16[2,512,512]{2,1,0:T(8,128)(2,1)S(1)}, u32[]{:S(2)}, u32[]{:S(2)}) collective-permute-start(bf16[2,512,512]{2,1,0:T(8,128)(2,1)S(1)} %get-tuple-element.40.refs_6_), channel_id=1, source_target_pairs={{16,24},{17,25},{18,26},{19,27},{20,28},{21,29},{22,30},{23,31},{8... | collective-permute-start | bytes 3145736 | tf_op jit(solution)/shard_map/ppermute | solution.py:286
  4.0 6.9 %collective-permute-start = (bf16[2,128,512]{2,1,0:T(8,128)(2,1)S(1)}, bf16[2,128,512]{2,1,0:T(8,128)(2,1)S(1)}, u32[]{:S(2)}, u32[]{:S(2)}) collective-permute-start(bf16[2,128,512]{2,1,0:T(8,128)(2,1)S(1)} %get-tuple-element.37), channel_id=1, source_target_pairs={{24,26},{16,8},{8,16},{0,1},{25,27},{17,9},{9,17},{1,0},{26,24},{1... | collective-permute-start | bytes 786440 | tf_op jit(solution)/shard_map/ppermute | solution.py:372
  6.6 6.4 %collective-permute-start.1 = (bf16[2,128,512]{2,1,0:T(8,128)(2,1)S(1)}, bf16[2,128,512]{2,1,0:T(8,128)(2,1)S(1)}, u32[]{:S(2)}, u32[]{:S(2)}) collective-permute-start(bf16[2,128,512]{2,1,0:T(8,128)(2,1)S(1)} %get-tuple-element.38), channel_id=1, source_target_pairs={{24,25},{16,8},{8,16},{0,2},{25,24},{17,9},{9,17},{1,3},{26,28},{1... | collective-permute-start | bytes 786440 | tf_op jit(solution)/shard_map/ppermute | solution.py:372
  8.2 4.8 %collective-permute-start.2 = (bf16[2,128,512]{2,1,0:T(8,128)(2,1)S(1)}, bf16[2,128,512]{2,1,0:T(8,128)(2,1)S(1)}, u32[]{:S(2)}, u32[]{:S(2)}) collective-permute-start(bf16[2,128,512]{2,1,0:T(8,128)(2,1)S(1)} %get-tuple-element.39), channel_id=1, source_target_pairs={{24,25},{8,0},{0,8},{16,18},{25,24},{9,1},{1,9},{17,19},{26,27},{1... | collective-permute-start | bytes 786440 | tf_op jit(solution)/shard_map/ppermute | solution.py:372
  13.9 6.4 %collective-permute-start.4 = (bf16[2,128,512]{2,1,0:T(8,128)(2,1)S(1)}, bf16[2,128,512]{2,1,0:T(8,128)(2,1)S(1)}, u32[]{:S(2)}, u32[]{:S(2)}) collective-permute-start(bf16[2,128,512]{2,1,0:T(8,128)(2,1)S(1)} %get-tuple-element.43), channel_id=1, source_target_pairs={{24,26},{16,8},{8,16},{0,1},{25,27},{17,9},{9,17},{1,0},{26,24},{1... | collective-permute-start | bytes 786440 | tf_op jit(solution)/shard_map/ppermute | solution.py:372
  14.0 6.4 %collective-permute-start.5 = (bf16[2,128,512]{2,1,0:T(8,128)(2,1)S(1)}, bf16[2,128,512]{2,1,0:T(8,128)(2,1)S(1)}, u32[]{:S(2)}, u32[]{:S(2)}) collective-permute-start(bf16[2,128,512]{2,1,0:T(8,128)(2,1)S(1)} %get-tuple-element.44), channel_id=1, source_target_pairs={{24,25},{16,8},{8,16},{0,2},{25,24},{17,9},{9,17},{1,3},{26,28},{1... | collective-permute-start | bytes 786440 | tf_op jit(solution)/shard_map/ppermute | solution.py:372
  16.0 4.4 %collective-permute-start.6 = (bf16[2,128,512]{2,1,0:T(8,128)(2,1)S(1)}, bf16[2,128,512]{2,1,0:T(8,128)(2,1)S(1)}, u32[]{:S(2)}, u32[]{:S(2)}) collective-permute-start(bf16[2,128,512]{2,1,0:T(8,128)(2,1)S(1)} %get-tuple-element.45), channel_id=1, source_target_pairs={{24,25},{8,0},{0,8},{16,18},{25,24},{9,1},{1,9},{17,19},{26,27},{1... | collective-permute-start | bytes 786440 | tf_op jit(solution)/shard_map/ppermute | solution.py:372
  20.7 13.0 %collective-permute-start.7 = (bf16[512,512]{1,0:T(8,128)(2,1)S(1)}, bf16[512,512]{1,0:T(8,128)(2,1)S(1)}, u32[]{:S(2)}, u32[]{:S(2)}) collective-permute-start(bf16[512,512]{1,0:T(8,128)(2,1)S(1)} %shard_map.90.top_ref), channel_id=1, source_target_pairs={{24,0},{25,1},{26,2},{27,3},{28,4},{29,5},{30,6},{31,7}} | collective-permute-start | bytes 1572872 | tf_op jit(solution)/shard_map/ppermute | solution.py:286
  34.5 2.4 %copy-start = (bf16[1,2,1,1,256,512]{5,4,3,2,1,0:T(8,128)(2,1)S(1)}, bf16[1,2,1,1,256,512]{5,4,3,2,1,0:T(8,128)(2,1)}, u32[]{:S(2)}) copy-start(bf16[1,2,1,1,256,512]{5,4,3,2,1,0:T(8,128)(2,1)} %param.7) | copy-start | bytes 1572868
  34.5 8.8 %collective-permute-start.11 = (bf16[512,512]{1,0:T(8,128)(2,1)S(1)}, bf16[512,512]{1,0:T(8,128)(2,1)S(1)}, u32[]{:S(2)}, u32[]{:S(2)}) collective-permute-start(bf16[512,512]{1,0:T(8,128)(2,1)S(1)} %shard_map.94), channel_id=1, source_target_pairs={{24,16},{25,17},{26,18},{27,19},{28,20},{29,21},{30,22},{31,23},{0... | collective-permute-start | bytes 1572872 | tf_op jit(solution)/shard_map/ppermute | solution.py:286
  34.6 6.4 %collective-permute-start.8 = (bf16[2,128,512]{2,1,0:T(8,128)(2,1)S(1)}, bf16[2,128,512]{2,1,0:T(8,128)(2,1)S(1)}, u32[]{:S(2)}, u32[]{:S(2)}) collective-permute-start(bf16[2,128,512]{2,1,0:T(8,128)(2,1)S(1)} %get-tuple-element.47), channel_id=1, source_target_pairs={{0,2},{8,9},{16,24},{24,16},{1,3},{9,8},{17,25},{25,17},{2,0},{10,... | collective-permute-start | bytes 786440 | tf_op jit(solution)/shard_map/ppermute | solution.py:372
  35.1 6.0 %collective-permute-start.9 = (bf16[2,128,512]{2,1,0:T(8,128)(2,1)S(1)}, bf16[2,128,512]{2,1,0:T(8,128)(2,1)S(1)}, u32[]{:S(2)}, u32[]{:S(2)}) collective-permute-start(bf16[2,128,512]{2,1,0:T(8,128)(2,1)S(1)} %get-tuple-element.48), channel_id=1, source_target_pairs={{0,8},{8,0},{16,24},{24,16},{1,9},{9,1},{17,25},{25,17},{2,4},{10,... | collective-permute-start | bytes 786440 | tf_op jit(solution)/shard_map/ppermute | solution.py:372
  36.4 7.0 %collective-permute-start.10 = (bf16[2,128,512]{2,1,0:T(8,128)(2,1)S(1)}, bf16[2,128,512]{2,1,0:T(8,128)(2,1)S(1)}, u32[]{:S(2)}, u32[]{:S(2)}) collective-permute-start(bf16[2,128,512]{2,1,0:T(8,128)(2,1)S(1)} %get-tuple-element.49), channel_id=1, source_target_pairs={{0,1},{8,16},{16,8},{24,25},{1,0},{9,17},{17,9},{25,24},{2,3},{10,... | collective-permute-start | bytes 786440 | tf_op jit(solution)/shard_map/ppermute | solution.py:372
  45.1 18.1 %collective-permute-start.15 = (bf16[512,512]{1,0:T(8,128)(2,1)S(1)}, bf16[512,512]{1,0:T(8,128)(2,1)S(1)}, u32[]{:S(2)}, u32[]{:S(2)}) collective-permute-start(bf16[512,512]{1,0:T(8,128)(2,1)S(1)} %shard_map.96), channel_id=1, source_target_pairs={{24,16},{25,17},{26,18},{27,19},{28,20},{29,21},{30,22},{31,23},{0... | collective-permute-start | bytes 1572872 | tf_op jit(solution)/shard_map/ppermute | solution.py:286
  45.1 6.4 %collective-permute-start.16 = (bf16[256,512]{1,0:T(8,128)(2,1)S(1)}, bf16[256,512]{1,0:T(8,128)(2,1)S(1)}, u32[]{:S(2)}, u32[]{:S(2)}) collective-permute-start(bf16[256,512]{1,0:T(8,128)(2,1)S(1)} %get-tuple-element.59), channel_id=1, source_target_pairs={{0,1},{1,0},{2,3},{3,2},{4,5},{5,4},{6,7},{7,6},{8,10},{9,11},{10,... | collective-permute-start | bytes 786440 | tf_op jit(solution)/shard_map/ppermute | solution.py:464
  46.7 13.2 %collective-permute-start.12 = (bf16[2,128,512]{2,1,0:T(8,128)(2,1)S(1)}, bf16[2,128,512]{2,1,0:T(8,128)(2,1)S(1)}, u32[]{:S(2)}, u32[]{:S(2)}) collective-permute-start(bf16[2,128,512]{2,1,0:T(8,128)(2,1)S(1)} %get-tuple-element.54), channel_id=1, source_target_pairs={{0,2},{8,16},{16,8},{24,25},{1,3},{9,17},{17,9},{25,24},{2,0},{10,... | collective-permute-start | bytes 786440 | tf_op jit(solution)/shard_map/ppermute | solution.py:372
  48.2 11.7 %collective-permute-start.13 = (bf16[2,128,512]{2,1,0:T(8,128)(2,1)S(1)}, bf16[2,128,512]{2,1,0:T(8,128)(2,1)S(1)}, u32[]{:S(2)}, u32[]{:S(2)}) collective-permute-start(bf16[2,128,512]{2,1,0:T(8,128)(2,1)S(1)} %get-tuple-element.55), channel_id=1, source_target_pairs={{0,1},{8,16},{16,8},{24,26},{1,0},{9,17},{17,9},{25,27},{2,4},{10,... | collective-permute-start | bytes 786440 | tf_op jit(solution)/shard_map/ppermute | solution.py:372
  49.1 10.8 %collective-permute-start.14 = (bf16[2,128,512]{2,1,0:T(8,128)(2,1)S(1)}, bf16[2,128,512]{2,1,0:T(8,128)(2,1)S(1)}, u32[]{:S(2)}, u32[]{:S(2)}) collective-permute-start(bf16[2,128,512]{2,1,0:T(8,128)(2,1)S(1)} %get-tuple-element.56), channel_id=1, source_target_pairs={{0,1},{16,24},{24,16},{8,10},{1,0},{17,25},{25,17},{9,11},{2,3},{1... | collective-permute-start | bytes 786440 | tf_op jit(solution)/shard_map/ppermute | solution.py:372
  51.6 6.2 %collective-permute-start.17 = (bf16[128,512]{1,0:T(8,128)(2,1)S(1)}, bf16[128,512]{1,0:T(8,128)(2,1)S(1)}, u32[]{:S(2)}, u32[]{:S(2)}) collective-permute-start(bf16[128,512]{1,0:T(8,128)(2,1)S(1)} %get-tuple-element.61), channel_id=1, source_target_pairs={{0,2},{1,3},{2,0},{3,1},{4,6},{5,7},{6,4},{7,5},{8,9},{9,8},{10,11... | collective-permute-start | bytes 393224 | tf_op jit(solution)/shard_map/ppermute | solution.py:464
  57.9 5.2 %collective-permute-start.18 = (bf16[64,512]{1,0:T(8,128)(2,1)S(1)}, bf16[64,512]{1,0:T(8,128)(2,1)S(1)}, u32[]{:S(2)}, u32[]{:S(2)}) collective-permute-start(bf16[64,512]{1,0:T(8,128)(2,1)S(1)} %get-tuple-element.63), channel_id=1, source_target_pairs={{0,4},{1,5},{2,6},{3,7},{4,0},{5,1},{6,2},{7,3},{8,12},{9,13},{10,... | collective-permute-start | bytes 196616 | tf_op jit(solution)/shard_map/ppermute | solution.py:470

commit v14 on v13

--- a/solution.py
+++ b/solution.py
@@ -470,14 +470,14 @@
         got = lax.ppermute(parcel, AXES, splits[-1][1])
         result, summed = call(
             functools.partial(last_kernel, top, count, scale),
-            [mask, total, *arrived, results[top], fetch_home(results, True), kept, got],
+            [mask, total, *arrived, results[top], fetch_home(results), kept, got],
             [whole, (kept.shape, F32)], 0, jax.ShapeDtypeStruct,
         )
     else:
         summed = scale * lax.psum_scatter(pieces[0], ("tx", "ty"), scatter_dimension=0, tiled=True)
         result = call(
             functools.partial(last_kernel, top, count, None),
-            [mask, total, *arrived, results[top], fetch_home(results, True)], [whole], 0,
+            [mask, total, *arrived, results[top], fetch_home(results)], [whole], 0,
             jax.ShapeDtypeStruct,
         )[0]
     return (summed[None], result.reshape(1, batches, 1, 1, nodes, width))

time: 65.7 us -> 66.2 us (level); the launches traced: 64.4 us -> 66.1 us
  waiting for transfers between devices: 34.6 us -> 36.4 us
    ppermute x1, waiting for transfers between devices: 3.23 us -> 4.89 us  [per_device(): got = lax.ppermute(parcel, AXES, splits[-1][1])]
where the time goes in v14:
time: 66.2 us; the launch traced here: 66.1 us
  waiting for transfers between devices  36.4 us (55%)
  starting transfers between devices  19.9 us (30%)
  Pallas kernels  9.01 us (14%)
  between operations  0.78 us (1%)
    ppermute x12, waiting for transfers between devices, exchange(): lax.ppermute(out, AXES, route[section])  14.2 us
    ppermute x12, starting transfers between devices, exchange(): lax.ppermute(out, AXES, route[section])  12.5 us
    ppermute x4, waiting for transfers between devices, to_sections(): return lax.ppermute(value, AXES, pairs)  11.7 us
    pallas_call x14, Pallas kernels, call(): pl.pallas_call(body, out_shape=[kind(shape, dtype) for shape, dtype in ou...  9.01 us
    ppermute x2, waiting for transfers between devices, per_device(): got = lax.ppermute(parcel, AXES, pairs)  5.68 us
    ppermute x1, waiting for transfers between devices, per_device(): got = lax.ppermute(parcel, AXES, splits[-1][1])  4.89 us
    ppermute x2, starting transfers between devices, per_device(): got = lax.ppermute(parcel, AXES, pairs)  3.58 us
    ppermute x4, starting transfers between devices, to_sections(): return lax.ppermute(value, AXES, pairs)  1.95 us
  transfers between devices with their start and end apart: 19, of which 10 were waited for; matrix products, arithmetic and copies ran while one was open for 0% of the time, Pallas kernels for 2%

profile of v14, /device:TPU:0, one launch (start us, length us, event | category | flops | bytes accessed | tf_op | source)
XLA Modules:
  0.0 66.1 jit_solution(17963044955222583836)
XLA Ops:
  0.6 2.8 %shard_map.86 = (bf16[2,512,512]{2,1,0:T(8,128)(2,1)S(1)}, bf16[2,640,256]{2,1,0:T(8,128)(2,1)S(1)}, f32[12,1,512]{2,1,0:T(1,128)S(1)}, bf16[512,512]{1,0:T(8,12...) custom-call(bf16[512,512]{1,0:T(8,128)(2,1)} %bitcast.11, ...), custom_call_target="tpu_custom_call" | custom-call | flops 738197504 | bytes 5922944 | tf_op jit(solution)/shard_map/pallas_call | solution.py:254
  3.5 0.5 collective-permute-start.3
  4.0 2.6 %collective-permute-start = (bf16[2,128,512]{2,1,0:T(8,128)(2,1)S(1)}, bf16[2,128,512]{2,1,0:T(8,128)(2,1)S(1)}, u32[]{:S(2)}, u32[]{:S(2)}) collective-permute-start(bf16[2,128,512]{2,1,0:T(8,128)(2,1)S(1)} %get-tuple-element.37), channel_id=1, source_target_pairs={{24,26},{16,8},{8,16},{0,1},{25,27},{17,9},{9,17},{1,0},{26,24},{1... | collective-permute-start | bytes 786440 | tf_op jit(solution)/shard_map/ppermute | solution.py:372
  6.6 1.6 %collective-permute-start.1 = (bf16[2,128,512]{2,1,0:T(8,128)(2,1)S(1)}, bf16[2,128,512]{2,1,0:T(8,128)(2,1)S(1)}, u32[]{:S(2)}, u32[]{:S(2)}) collective-permute-start(bf16[2,128,512]{2,1,0:T(8,128)(2,1)S(1)} %get-tuple-element.38), channel_id=1, source_target_pairs={{24,25},{16,8},{8,16},{0,2},{25,24},{17,9},{9,17},{1,3},{26,28},{1... | collective-permute-start | bytes 786440 | tf_op jit(solution)/shard_map/ppermute | solution.py:372
  8.2 0.3 shard_map.87.total_ref
  8.5 2.5 %collective-permute-done.refs_0_ = bf16[2,128,512]{2,1,0:T(8,128)(2,1)S(1)} collective-permute-done((bf16[2,128,512]{2,1,0:T(8,128)(2,1)S(1)}, bf16[2,128,512]{2,1,0:T(8,128)(2,1)S(1)}, u32[]{:S(2)}, u32[]{:S(2)}) %collective-permute-start) | collective-permute-done | bytes 262176 | tf_op jit(solution)/shard_map/ppermute | solution.py:372
  10.9 2.0 %collective-permute-done.1.refs_1_ = bf16[2,128,512]{2,1,0:T(8,128)(2,1)S(1)} collective-permute-done((bf16[2,128,512]{2,1,0:T(8,128)(2,1)S(1)}, bf16[2,128,512]{2,1,0:T(8,128)(2,1)S(1)}, u32[]{:S(2)}, u32[]{:S(2)}) %collective-permute-start.1) | collective-permute-done | bytes 262176 | tf_op jit(solution)/shard_map/ppermute | solution.py:372
  13.0 0.9 %shard_map.88 = (bf16[512,512]{1,0:T(8,128)(2,1)S(1)}, bf16[512,512]{1,0:T(8,128)(2,1)S(1)}, bf16[512,512]{1,0:T(8,128)(2,1)S(1)}, bf16[2,128,512]{2,1,0:T(8,128...) custom-call(f32[12,1,512]{2,1,0:T(1,128)S(1)} %get-tuple-element.34.mask_ref, ...), custom_call_target="tpu_custom_call" | custom-call | flops 469762048 | bytes 5922816 | tf_op jit(solution)/shard_map/pallas_call | solution.py:254
  14.0 2.0 %collective-permute-start.5 = (bf16[2,128,512]{2,1,0:T(8,128)(2,1)S(1)}, bf16[2,128,512]{2,1,0:T(8,128)(2,1)S(1)}, u32[]{:S(2)}, u32[]{:S(2)}) collective-permute-start(bf16[2,128,512]{2,1,0:T(8,128)(2,1)S(1)} %get-tuple-element.44), channel_id=1, source_target_pairs={{24,25},{16,8},{8,16},{0,2},{25,24},{17,9},{9,17},{1,3},{26,28},{1... | collective-permute-start | bytes 786440 | tf_op jit(solution)/shard_map/ppermute | solution.py:372
  16.0 0.3 collective-permute-start.6
  16.7 3.6 %collective-permute-done.4.refs_0_ = bf16[2,128,512]{2,1,0:T(8,128)(2,1)S(1)} collective-permute-done((bf16[2,128,512]{2,1,0:T(8,128)(2,1)S(1)}, bf16[2,128,512]{2,1,0:T(8,128)(2,1)S(1)}, u32[]{:S(2)}, u32[]{:S(2)}) %collective-permute-start.4) | collective-permute-done | bytes 262176 | tf_op jit(solution)/shard_map/ppermute | solution.py:372
  20.4 0.4 shard_map.90.top_ref
  20.7 1.3 %collective-permute-start.7 = (bf16[512,512]{1,0:T(8,128)(2,1)S(1)}, bf16[512,512]{1,0:T(8,128)(2,1)S(1)}, u32[]{:S(2)}, u32[]{:S(2)}) collective-permute-start(bf16[512,512]{1,0:T(8,128)(2,1)S(1)} %shard_map.90.top_ref), channel_id=1, source_target_pairs={{24,0},{25,1},{26,2},{27,3},{28,4},{29,5},{30,6},{31,7}} | collective-permute-start | bytes 1572872 | tf_op jit(solution)/shard_map/ppermute | solution.py:286
  22.0 11.7 %collective-permute-done.7.upstream_ref = bf16[512,512]{1,0:T(8,128)(2,1)S(1)} collective-permute-done((bf16[512,512]{1,0:T(8,128)(2,1)S(1)}, bf16[512,512]{1,0:T(8,128)(2,1)S(1)}, u32[]{:S(2)}, u32[]{:S(2)}) %collective-permute-start.7) | collective-permute-done | bytes 524320 | tf_op jit(solution)/shard_map/ppermute | solution.py:286
  33.7 0.8 %shard_map.91 = (bf16[512,512]{1,0:T(8,128)(2,1)S(1)}, bf16[512,512]{1,0:T(8,128)(2,1)S(1)}, bf16[2,128,512]{2,1,0:T(8,128)(2,1)S(1)}, bf16[2,128,512]{2,1,0:T(8,128)(2,1)S(1)}, bf16[2,128,512]{2,1,0:T(8,128)(2,1)S(1)}) custom-call(bf16[2,512,512]{2,1,0:T(8,128)(2,1)S(1)} %collective-permute-done.3.refs_3_.layer_ref, ...), custom_call_target="tpu_custom_call" | custom-call | flops 469762048 | bytes 4063232 | tf_op jit(solution)/shard_map/pallas_call | solution.py:254
  34.6 0.4 collective-permute-start.8
  35.1 1.3 %collective-permute-start.9 = (bf16[2,128,512]{2,1,0:T(8,128)(2,1)S(1)}, bf16[2,128,512]{2,1,0:T(8,128)(2,1)S(1)}, u32[]{:S(2)}, u32[]{:S(2)}) collective-permute-start(bf16[2,128,512]{2,1,0:T(8,128)(2,1)S(1)} %get-tuple-element.48), channel_id=1, source_target_pairs={{0,8},{8,0},{16,24},{24,16},{1,9},{9,1},{17,25},{25,17},{2,4},{10,... | collective-permute-start | bytes 786440 | tf_op jit(solution)/shard_map/ppermute | solution.py:372
  36.4 0.5 collective-permute-start.10
  37.1 0.3 shard_map.92.total_ref
  37.4 3.7 %collective-permute-done.8.refs_0_ = bf16[2,128,512]{2,1,0:T(8,128)(2,1)S(1)} collective-permute-done((bf16[2,128,512]{2,1,0:T(8,128)(2,1)S(1)}, bf16[2,128,512]{2,1,0:T(8,128)(2,1)S(1)}, u32[]{:S(2)}, u32[]{:S(2)}) %collective-permute-start.8) | collective-permute-done | bytes 262176 | tf_op jit(solution)/shard_map/ppermute | solution.py:372
  41.1 2.3 %collective-permute-done.10.refs_2_ = bf16[2,128,512]{2,1,0:T(8,128)(2,1)S(1)} collective-permute-done((bf16[2,128,512]{2,1,0:T(8,128)(2,1)S(1)}, bf16[2,128,512]{2,1,0:T(8,128)(2,1)S(1)}, u32[]{:S(2)}, u32[]{:S(2)}) %collective-permute-start.10) | collective-permute-done | bytes 262176 | tf_op jit(solution)/shard_map/ppermute | solution.py:372
  43.3 1.7 %shard_map.95 = (bf16[512,512]{1,0:T(8,128)(2,1)S(1)}, f32[512,512]{1,0:T(8,128)S(1)}, bf16[2,128,512]{2,1,0:T(8,128)(2,1)S(1)}, bf16[2,128,512]{2,1,0:T(8,128)(...) custom-call(f32[12,1,512]{2,1,0:T(1,128)S(1)} %get-tuple-element.34.mask_ref, ...), custom_call_target="tpu_custom_call" | custom-call | flops 872415232 | bytes 8282112 | tf_op jit(solution)/shard_map/pallas_call | solution.py:254
  45.2 1.6 %collective-permute-start.16 = (bf16[256,512]{1,0:T(8,128)(2,1)S(1)}, bf16[256,512]{1,0:T(8,128)(2,1)S(1)}, u32[]{:S(2)}, u32[]{:S(2)}) collective-permute-start(bf16[256,512]{1,0:T(8,128)(2,1)S(1)} %get-tuple-element.59), channel_id=1, source_target_pairs={{0,1},{1,0},{2,3},{3,2},{4,5},{5,4},{6,7},{7,6},{8,10},{9,11},{10,... | collective-permute-start | bytes 786440 | tf_op jit(solution)/shard_map/ppermute | solution.py:464
  46.8 1.5 %collective-permute-start.12 = (bf16[2,128,512]{2,1,0:T(8,128)(2,1)S(1)}, bf16[2,128,512]{2,1,0:T(8,128)(2,1)S(1)}, u32[]{:S(2)}, u32[]{:S(2)}) collective-permute-start(bf16[2,128,512]{2,1,0:T(8,128)(2,1)S(1)} %get-tuple-element.54), channel_id=1, source_target_pairs={{0,2},{8,16},{16,8},{24,25},{1,3},{9,17},{17,9},{25,24},{2,0},{10,... | collective-permute-start | bytes 786440 | tf_op jit(solution)/shard_map/ppermute | solution.py:372
  48.3 0.9 %collective-permute-start.13 = (bf16[2,128,512]{2,1,0:T(8,128)(2,1)S(1)}, bf16[2,128,512]{2,1,0:T(8,128)(2,1)S(1)}, u32[]{:S(2)}, u32[]{:S(2)}) collective-permute-start(bf16[2,128,512]{2,1,0:T(8,128)(2,1)S(1)} %get-tuple-element.55), channel_id=1, source_target_pairs={{0,1},{8,16},{16,8},{24,26},{1,0},{9,17},{17,9},{25,27},{2,4},{10,... | collective-permute-start | bytes 786440 | tf_op jit(solution)/shard_map/ppermute | solution.py:372
  49.2 1.1 %collective-permute-start.14 = (bf16[2,128,512]{2,1,0:T(8,128)(2,1)S(1)}, bf16[2,128,512]{2,1,0:T(8,128)(2,1)S(1)}, u32[]{:S(2)}, u32[]{:S(2)}) collective-permute-start(bf16[2,128,512]{2,1,0:T(8,128)(2,1)S(1)} %get-tuple-element.56), channel_id=1, source_target_pairs={{0,1},{16,24},{24,16},{8,10},{1,0},{17,25},{25,17},{9,11},{2,3},{1... | collective-permute-start | bytes 786440 | tf_op jit(solution)/shard_map/ppermute | solution.py:372
  50.3 1.3 %collective-permute-done.16.got_ref = bf16[256,512]{1,0:T(8,128)(2,1)S(1)} collective-permute-done((bf16[256,512]{1,0:T(8,128)(2,1)S(1)}, bf16[256,512]{1,0:T(8,128)(2,1)S(1)}, u32[]{:S(2)}, u32[]{:S(2)}) %collective-permute-start.16) | collective-permute-done | bytes 262176 | tf_op jit(solution)/shard_map/ppermute | solution.py:464
  51.7 2.0 %collective-permute-start.17 = (bf16[128,512]{1,0:T(8,128)(2,1)S(1)}, bf16[128,512]{1,0:T(8,128)(2,1)S(1)}, u32[]{:S(2)}, u32[]{:S(2)}) collective-permute-start(bf16[128,512]{1,0:T(8,128)(2,1)S(1)} %get-tuple-element.61), channel_id=1, source_target_pairs={{0,2},{1,3},{2,0},{3,1},{4,6},{5,7},{6,4},{7,5},{8,9},{9,8},{10,11... | collective-permute-start | bytes 393224 | tf_op jit(solution)/shard_map/ppermute | solution.py:464
  53.7 4.4 %collective-permute-done.17.got_ref = bf16[128,512]{1,0:T(8,128)(2,1)S(1)} collective-permute-done((bf16[128,512]{1,0:T(8,128)(2,1)S(1)}, bf16[128,512]{1,0:T(8,128)(2,1)S(1)}, u32[]{:S(2)}, u32[]{:S(2)}) %collective-permute-start.17) | collective-permute-done | bytes 131104 | tf_op jit(solution)/shard_map/ppermute | solution.py:464
  58.1 1.8 %collective-permute-start.18 = (bf16[64,512]{1,0:T(8,128)(2,1)S(1)}, bf16[64,512]{1,0:T(8,128)(2,1)S(1)}, u32[]{:S(2)}, u32[]{:S(2)}) collective-permute-start(bf16[64,512]{1,0:T(8,128)(2,1)S(1)} %get-tuple-element.63), channel_id=1, source_target_pairs={{0,4},{1,5},{2,6},{3,7},{4,0},{5,1},{6,2},{7,3},{8,12},{9,13},{10,... | collective-permute-start | bytes 196616 | tf_op jit(solution)/shard_map/ppermute | solution.py:470
  60.0 4.9 %collective-permute-done.18.refs_6_ = bf16[64,512]{1,0:T(8,128)(2,1)S(1)} collective-permute-done((bf16[64,512]{1,0:T(8,128)(2,1)S(1)}, bf16[64,512]{1,0:T(8,128)(2,1)S(1)}, u32[]{:S(2)}, u32[]{:S(2)}) %collective-permute-start.18) | collective-permute-done | bytes 65568 | tf_op jit(solution)/shard_map/ppermute | solution.py:470
  64.9 1.2 %shard_map.99 = (bf16[512,512]{1,0:T(8,128)(2,1)}, f32[64,512]{1,0:T(8,128)}) custom-call(f32[12,1,512]{2,1,0:T(1,128)S(1)} %get-tuple-element.34.mask_ref, f32[512,512]{1,0:T(8,128)S(1)} %get-tuple-element.53.total_ref, bf16[2,128,512]{2,1,0:T(8,128)(2,1)S(1)} %collective-permute-done.12.refs_0_, bf16[2,128,512]{2,1,0:T(8,128)(2,1)S(1)} %collective-permute-done.13.refs_1_, ...), custom_call_target="tpu_custom_call" | custom-call | bytes 3760128 | tf_op jit(solution)/shard_map/pallas_call | solution.py:254
  (24 shorter events, 1.1 us)
Async XLA Ops:
  0.6 7.5 %copy-start.1 = (bf16[2,1,1,256,512]{4,3,2,1,0:T(8,128)(2,1)S(1)}, bf16[2,1,1,256,512]{4,3,2,1,0:T(8,128)(2,1)}, u32[]{:S(2)}) copy-start(bf16[2,1,1,256,512]{4,3,2,1,0:T(8,128)(2,1)} %param.8) | copy-start | bytes 1572868
  3.5 9.5 %collective-permute-start.3 = (bf16[2,512,512]{2,1,0:T(8,128)(2,1)S(1)}, bf16[2,512,512]{2,1,0:T(8,128)(2,1)S(1)}, u32[]{:S(2)}, u32[]{:S(2)}) collective-permute-start(bf16[2,512,512]{2,1,0:T(8,128)(2,1)S(1)} %get-tuple-element.40.refs_6_), channel_id=1, source_target_pairs={{16,24},{17,25},{18,26},{19,27},{20,28},{21,29},{22,30},{23,31},{8... | collective-permute-start | bytes 3145736 | tf_op jit(solution)/shard_map/ppermute | solution.py:286
  4.0 6.9 %collective-permute-start = (bf16[2,128,512]{2,1,0:T(8,128)(2,1)S(1)}, bf16[2,128,512]{2,1,0:T(8,128)(2,1)S(1)}, u32[]{:S(2)}, u32[]{:S(2)}) collective-permute-start(bf16[2,128,512]{2,1,0:T(8,128)(2,1)S(1)} %get-tuple-element.37), channel_id=1, source_target_pairs={{24,26},{16,8},{8,16},{0,1},{25,27},{17,9},{9,17},{1,0},{26,24},{1... | collective-permute-start | bytes 786440 | tf_op jit(solution)/shard_map/ppermute | solution.py:372
  6.6 6.4 %collective-permute-start.1 = (bf16[2,128,512]{2,1,0:T(8,128)(2,1)S(1)}, bf16[2,128,512]{2,1,0:T(8,128)(2,1)S(1)}, u32[]{:S(2)}, u32[]{:S(2)}) collective-permute-start(bf16[2,128,512]{2,1,0:T(8,128)(2,1)S(1)} %get-tuple-element.38), channel_id=1, source_target_pairs={{24,25},{16,8},{8,16},{0,2},{25,24},{17,9},{9,17},{1,3},{26,28},{1... | collective-permute-start | bytes 786440 | tf_op jit(solution)/shard_map/ppermute | solution.py:372
  8.2 4.8 %collective-permute-start.2 = (bf16[2,128,512]{2,1,0:T(8,128)(2,1)S(1)}, bf16[2,128,512]{2,1,0:T(8,128)(2,1)S(1)}, u32[]{:S(2)}, u32[]{:S(2)}) collective-permute-start(bf16[2,128,512]{2,1,0:T(8,128)(2,1)S(1)} %get-tuple-element.39), channel_id=1, source_target_pairs={{24,25},{8,0},{0,8},{16,18},{25,24},{9,1},{1,9},{17,19},{26,27},{1... | collective-permute-start | bytes 786440 | tf_op jit(solution)/shard_map/ppermute | solution.py:372
  13.9 6.4 %collective-permute-start.4 = (bf16[2,128,512]{2,1,0:T(8,128)(2,1)S(1)}, bf16[2,128,512]{2,1,0:T(8,128)(2,1)S(1)}, u32[]{:S(2)}, u32[]{:S(2)}) collective-permute-start(bf16[2,128,512]{2,1,0:T(8,128)(2,1)S(1)} %get-tuple-element.43), channel_id=1, source_target_pairs={{24,26},{16,8},{8,16},{0,1},{25,27},{17,9},{9,17},{1,0},{26,24},{1... | collective-permute-start | bytes 786440 | tf_op jit(solution)/shard_map/ppermute | solution.py:372
  14.0 6.4 %collective-permute-start.5 = (bf16[2,128,512]{2,1,0:T(8,128)(2,1)S(1)}, bf16[2,128,512]{2,1,0:T(8,128)(2,1)S(1)}, u32[]{:S(2)}, u32[]{:S(2)}) collective-permute-start(bf16[2,128,512]{2,1,0:T(8,128)(2,1)S(1)} %get-tuple-element.44), channel_id=1, source_target_pairs={{24,25},{16,8},{8,16},{0,2},{25,24},{17,9},{9,17},{1,3},{26,28},{1... | collective-permute-start | bytes 786440 | tf_op jit(solution)/shard_map/ppermute | solution.py:372
  16.0 4.4 %collective-permute-start.6 = (bf16[2,128,512]{2,1,0:T(8,128)(2,1)S(1)}, bf16[2,128,512]{2,1,0:T(8,128)(2,1)S(1)}, u32[]{:S(2)}, u32[]{:S(2)}) collective-permute-start(bf16[2,128,512]{2,1,0:T(8,128)(2,1)S(1)} %get-tuple-element.45), channel_id=1, source_target_pairs={{24,25},{8,0},{0,8},{16,18},{25,24},{9,1},{1,9},{17,19},{26,27},{1... | collective-permute-start | bytes 786440 | tf_op jit(solution)/shard_map/ppermute | solution.py:372
  20.7 13.0 %collective-permute-start.7 = (bf16[512,512]{1,0:T(8,128)(2,1)S(1)}, bf16[512,512]{1,0:T(8,128)(2,1)S(1)}, u32[]{:S(2)}, u32[]{:S(2)}) collective-permute-start(bf16[512,512]{1,0:T(8,128)(2,1)S(1)} %shard_map.90.top_ref), channel_id=1, source_target_pairs={{24,0},{25,1},{26,2},{27,3},{28,4},{29,5},{30,6},{31,7}} | collective-permute-start | bytes 1572872 | tf_op jit(solution)/shard_map/ppermute | solution.py:286
  34.5 2.4 %copy-start = (bf16[1,2,1,1,256,512]{5,4,3,2,1,0:T(8,128)(2,1)S(1)}, bf16[1,2,1,1,256,512]{5,4,3,2,1,0:T(8,128)(2,1)}, u32[]{:S(2)}) copy-start(bf16[1,2,1,1,256,512]{5,4,3,2,1,0:T(8,128)(2,1)} %param.7) | copy-start | bytes 1572868
  34.5 8.8 %collective-permute-start.11 = (bf16[512,512]{1,0:T(8,128)(2,1)S(1)}, bf16[512,512]{1,0:T(8,128)(2,1)S(1)}, u32[]{:S(2)}, u32[]{:S(2)}) collective-permute-start(bf16[512,512]{1,0:T(8,128)(2,1)S(1)} %shard_map.94), channel_id=1, source_target_pairs={{24,16},{25,17},{26,18},{27,19},{28,20},{29,21},{30,22},{31,23},{0... | collective-permute-start | bytes 1572872 | tf_op jit(solution)/shard_map/ppermute | solution.py:286
  34.6 6.4 %collective-permute-start.8 = (bf16[2,128,512]{2,1,0:T(8,128)(2,1)S(1)}, bf16[2,128,512]{2,1,0:T(8,128)(2,1)S(1)}, u32[]{:S(2)}, u32[]{:S(2)}) collective-permute-start(bf16[2,128,512]{2,1,0:T(8,128)(2,1)S(1)} %get-tuple-element.47), channel_id=1, source_target_pairs={{0,2},{8,9},{16,24},{24,16},{1,3},{9,8},{17,25},{25,17},{2,0},{10,... | collective-permute-start | bytes 786440 | tf_op jit(solution)/shard_map/ppermute | solution.py:372
  35.1 6.0 %collective-permute-start.9 = (bf16[2,128,512]{2,1,0:T(8,128)(2,1)S(1)}, bf16[2,128,512]{2,1,0:T(8,128)(2,1)S(1)}, u32[]{:S(2)}, u32[]{:S(2)}) collective-permute-start(bf16[2,128,512]{2,1,0:T(8,128)(2,1)S(1)} %get-tuple-element.48), channel_id=1, source_target_pairs={{0,8},{8,0},{16,24},{24,16},{1,9},{9,1},{17,25},{25,17},{2,4},{10,... | collective-permute-start | bytes 786440 | tf_op jit(solution)/shard_map/ppermute | solution.py:372
  36.4 7.0 %collective-permute-start.10 = (bf16[2,128,512]{2,1,0:T(8,128)(2,1)S(1)}, bf16[2,128,512]{2,1,0:T(8,128)(2,1)S(1)}, u32[]{:S(2)}, u32[]{:S(2)}) collective-permute-start(bf16[2,128,512]{2,1,0:T(8,128)(2,1)S(1)} %get-tuple-element.49), channel_id=1, source_target_pairs={{0,1},{8,16},{16,8},{24,25},{1,0},{9,17},{17,9},{25,24},{2,3},{10,... | collective-permute-start | bytes 786440 | tf_op jit(solution)/shard_map/ppermute | solution.py:372
  45.1 19.8 %collective-permute-start.15 = (bf16[512,512]{1,0:T(8,128)(2,1)S(1)}, bf16[512,512]{1,0:T(8,128)(2,1)S(1)}, u32[]{:S(2)}, u32[]{:S(2)}) collective-permute-start(bf16[512,512]{1,0:T(8,128)(2,1)S(1)} %shard_map.96), channel_id=1, source_target_pairs={{24,16},{25,17},{26,18},{27,19},{28,20},{29,21},{30,22},{31,23},{0... | collective-permute-start | bytes 1572872 | tf_op jit(solution)/shard_map/ppermute | solution.py:286
  45.2 6.4 %collective-permute-start.16 = (bf16[256,512]{1,0:T(8,128)(2,1)S(1)}, bf16[256,512]{1,0:T(8,128)(2,1)S(1)}, u32[]{:S(2)}, u32[]{:S(2)}) collective-permute-start(bf16[256,512]{1,0:T(8,128)(2,1)S(1)} %get-tuple-element.59), channel_id=1, source_target_pairs={{0,1},{1,0},{2,3},{3,2},{4,5},{5,4},{6,7},{7,6},{8,10},{9,11},{10,... | collective-permute-start | bytes 786440 | tf_op jit(solution)/shard_map/ppermute | solution.py:464
  46.8 13.2 %collective-permute-start.12 = (bf16[2,128,512]{2,1,0:T(8,128)(2,1)S(1)}, bf16[2,128,512]{2,1,0:T(8,128)(2,1)S(1)}, u32[]{:S(2)}, u32[]{:S(2)}) collective-permute-start(bf16[2,128,512]{2,1,0:T(8,128)(2,1)S(1)} %get-tuple-element.54), channel_id=1, source_target_pairs={{0,2},{8,16},{16,8},{24,25},{1,3},{9,17},{17,9},{25,24},{2,0},{10,... | collective-permute-start | bytes 786440 | tf_op jit(solution)/shard_map/ppermute | solution.py:372
  48.3 11.7 %collective-permute-start.13 = (bf16[2,128,512]{2,1,0:T(8,128)(2,1)S(1)}, bf16[2,128,512]{2,1,0:T(8,128)(2,1)S(1)}, u32[]{:S(2)}, u32[]{:S(2)}) collective-permute-start(bf16[2,128,512]{2,1,0:T(8,128)(2,1)S(1)} %get-tuple-element.55), channel_id=1, source_target_pairs={{0,1},{8,16},{16,8},{24,26},{1,0},{9,17},{17,9},{25,27},{2,4},{10,... | collective-permute-start | bytes 786440 | tf_op jit(solution)/shard_map/ppermute | solution.py:372
  49.2 10.8 %collective-permute-start.14 = (bf16[2,128,512]{2,1,0:T(8,128)(2,1)S(1)}, bf16[2,128,512]{2,1,0:T(8,128)(2,1)S(1)}, u32[]{:S(2)}, u32[]{:S(2)}) collective-permute-start(bf16[2,128,512]{2,1,0:T(8,128)(2,1)S(1)} %get-tuple-element.56), channel_id=1, source_target_pairs={{0,1},{16,24},{24,16},{8,10},{1,0},{17,25},{25,17},{9,11},{2,3},{1... | collective-permute-start | bytes 786440 | tf_op jit(solution)/shard_map/ppermute | solution.py:372
  51.7 6.4 %collective-permute-start.17 = (bf16[128,512]{1,0:T(8,128)(2,1)S(1)}, bf16[128,512]{1,0:T(8,128)(2,1)S(1)}, u32[]{:S(2)}, u32[]{:S(2)}) collective-permute-start(bf16[128,512]{1,0:T(8,128)(2,1)S(1)} %get-tuple-element.61), channel_id=1, source_target_pairs={{0,2},{1,3},{2,0},{3,1},{4,6},{5,7},{6,4},{7,5},{8,9},{9,8},{10,11... | collective-permute-start | bytes 393224 | tf_op jit(solution)/shard_map/ppermute | solution.py:464
  58.1 6.7 %collective-permute-start.18 = (bf16[64,512]{1,0:T(8,128)(2,1)S(1)}, bf16[64,512]{1,0:T(8,128)(2,1)S(1)}, u32[]{:S(2)}, u32[]{:S(2)}) collective-permute-start(bf16[64,512]{1,0:T(8,128)(2,1)S(1)} %get-tuple-element.63), channel_id=1, source_target_pairs={{0,4},{1,5},{2,6},{3,7},{4,0},{5,1},{6,2},{7,3},{8,12},{9,13},{10,... | collective-permute-start | bytes 196616 | tf_op jit(solution)/shard_map/ppermute | solution.py:470
